TPU v7x, 32 devices: a whole 2x2x4 slice. The times are simulated.
32 devices in a mesh: groups: 2 (over y), seq: 4 (over z), tensor: 2 (over x), pipe: 2 (over core).
Axes of the slice: x: 2, y: 2, z: 4, core: 2. Of those that a mesh axis runs over, the one named last changes fastest.
Arguments:
- out_grad: bfloat16 [4, 1536, 3072], P(('groups', 'pipe'), 'seq', 'tensor'), parts along dimension 0, may hold values from -6 to 6
- queries: bfloat16 [4, 1536, 3072], P(('groups', 'pipe'), 'seq', 'tensor'), parts along dimension 0, may hold values from -0.3 to 0.3
- keys: bfloat16 [4, 1536, 3072], P(('groups', 'pipe'), 'seq', 'tensor'), parts along dimension 0, may hold values from -0.45 to 0.45
- main_out: bfloat16 [4, 512, 3072], P(('groups', 'pipe'), 'seq', 'tensor'), parts along dimension 0, may hold values from -6 to 6
- main_in_grad: bfloat16 [4, 512, 3072], P(('groups', 'pipe'), 'seq', 'tensor'), parts along dimension 0, may hold values from -6 to 6
- boundaries: int32 [4, 512], P(('groups', 'pipe')), parts along dimension 0, may hold values from 0 to 1535, as said below
- query_weight: bfloat16 [3072, 3072], P('seq', 'tensor'), may hold values from -0.109375 to 0.109375
- key_weight: bfloat16 [3072, 3072], P('seq', 'tensor'), may hold values from -0.109375 to 0.109375
Outputs:
- byte_grad: bfloat16 [4, 1536, 3072], P(('groups', 'pipe'), 'seq', 'tensor'), parts along dimension 0
- main_grad: bfloat16 [4, 512, 3072], P(('groups', 'pipe'), 'seq', 'tensor'), parts along dimension 0
There are 2 independent parts, one for each index of `groups`. A program takes and returns all parts, laid end to end along the dimension named above; an argument that names none is the same for every part. Nothing has to cross between parts.
Inputs may be any that keep to these rules, and one draw needn't show every extreme that they name: `boundaries`: each row holds 512 strictly increasing byte positions, the first 0. Every span c that holds a byte of shard i (bytes i * 384 to (i + 1) * 384 - 1) has c // 128 within 2 of i, and in every sequence some span is exactly 2 away.
All inputs are finite; a program needn't handle non-finite values.
Results may differ from a plain program's by a relative error of at most 0.008.
Values may be sent and summed in bfloat16 or wider, within the bound.
No kernel may reach another device: no remote copies, remote signals or barrier semaphores. Data moves between devices by JAX's collectives and lax.ppermute only.
A program may use at most 128 MiB of HBM per device.

v0:
```python
import jax
import jax.numpy as jnp
from jax import lax
from jax.sharding import PartitionSpec as P

epsilon = 1e-06


def passed_along(x, axis, by):
    length = lax.axis_size(axis)
    pairs = [(i, i + by) for i in range(length) if 0 <= i + by < length]
    return lax.ppermute(x, axis, pairs)


def shards(out_grad, queries, keys, main_out, main_in_grad, boundaries, query_weight, key_weight):
    cotangent = out_grad[0]
    query_rows = queries[0]
    key_rows = keys[0]
    bounds_row = boundaries[0]
    row_count = cotangent.shape[0]
    span_rows = main_out.shape[1]
    shard_index = lax.axis_index("seq")
    seq_count = lax.axis_size("seq")
    positions = shard_index * row_count + jnp.arange(row_count, dtype=jnp.int32)
    span_of = jnp.searchsorted(bounds_row, positions, side="right") - 1
    starts = jnp.take(bounds_row, span_of) == positions
    window_out, window_grad = (
        lax.all_gather(main_out[0], "seq", axis=0, tiled=True),
        lax.all_gather(main_in_grad[0], "seq", axis=0, tiled=True),
    )
    window_rows = window_out.shape[0]
    selector = span_of[:, None] == jnp.arange(window_rows, dtype=jnp.int32)[None, :]
    picker = selector.astype(jnp.bfloat16)
    upsampled = jnp.dot(picker, window_out, preferred_element_type=jnp.float32)
    start_picker = (selector & starts[:, None]).astype(jnp.bfloat16)
    start_grad = jnp.dot(start_picker, window_grad, preferred_element_type=jnp.float32)
    last_key = passed_along(key_rows[-1:], "seq", 1)
    prev_keys = jnp.concatenate([last_key, key_rows[:-1]], 0)
    query_wide = query_rows.astype(jnp.float32)
    prev_wide = prev_keys.astype(jnp.float32)
    cotangent_wide = cotangent.astype(jnp.float32)
    cross_part = jnp.sum(query_wide * prev_wide, 1)
    query_part = jnp.sum(query_wide * query_wide, 1)
    key_part = jnp.sum(prev_wide * prev_wide, 1)
    conf_part = jnp.sum(cotangent_wide * upsampled, 1)
    cross_sum, query_sum, key_sum = lax.psum((cross_part, query_part, key_part), "tensor")
    conf_grad = lax.psum(conf_part, "tensor")
    query_scale = lax.rsqrt(query_sum + epsilon)
    key_scale = lax.rsqrt(key_sum + epsilon)
    cosine = cross_sum * query_scale * key_scale
    probability = jnp.where(positions == 0, 1.0, 0.5 * (1.0 - cosine))
    confidence = jnp.where(starts, probability, 1.0 - probability)
    conf_high = confidence.astype(jnp.bfloat16)
    conf_low = (confidence - conf_high.astype(jnp.float32)).astype(jnp.bfloat16)
    zero_weight = jnp.zeros((), jnp.bfloat16)
    weight_high = jnp.where(selector, conf_high[:, None], zero_weight)
    weight_low = jnp.where(selector, conf_low[:, None], zero_weight)
    contract = (((0,), (0,)), ((), ()))
    span_terms = lax.dot_general(
        weight_high, cotangent, contract, preferred_element_type=jnp.float32
    )
    span_terms = span_terms + lax.dot_general(
        weight_low, cotangent, contract, preferred_element_type=jnp.float32
    )
    received = lax.all_to_all(
        span_terms.reshape(seq_count, span_rows, span_terms.shape[1]).astype(jnp.bfloat16),
        "seq",
        split_axis=0,
        concat_axis=0,
        tiled=True,
    ).astype(jnp.float32)
    span_sums = jnp.sum(received, 0)
    main_grad = span_sums.astype(jnp.bfloat16)[None]
    sign = jnp.where(starts, 1.0, -1.0)
    cos_grad = jnp.where(positions == 0, 0.0, -0.5 * sign * conf_grad)
    both_scale = (query_scale * key_scale)[:, None]
    query_grad = (
        cos_grad[:, None]
        * (prev_wide * both_scale - (cosine * query_scale * query_scale)[:, None] * query_wide)
    ).astype(jnp.bfloat16)
    prev_grad = (
        cos_grad[:, None]
        * (query_wide * both_scale - (cosine * key_scale * key_scale)[:, None] * prev_wide)
    ).astype(jnp.bfloat16)
    next_grad = passed_along(prev_grad[:1], "seq", -1)
    key_grad = jnp.concatenate([prev_grad[1:], next_grad], 0)
    pieces = lax.all_gather((query_weight, key_weight), "seq", axis=0, tiled=True)
    partial_value = jnp.dot(query_grad, pieces[0].T, preferred_element_type=jnp.float32) + jnp.dot(
        key_grad, pieces[1].T, preferred_element_type=jnp.float32
    )
    routing = lax.psum_scatter(
        partial_value.astype(jnp.bfloat16), "tensor", scatter_dimension=1, tiled=True
    ).astype(jnp.float32)
    byte_grad = (cotangent_wide + start_grad + routing).astype(jnp.bfloat16)[None]
    return (byte_grad, main_grad)


def solution(mesh):
    return jax.shard_map(
        shards,
        mesh=mesh,
        in_specs=(
            P(("groups", "pipe"), "seq", "tensor"),
            P(("groups", "pipe"), "seq", "tensor"),
            P(("groups", "pipe"), "seq", "tensor"),
            P(("groups", "pipe"), "seq", "tensor"),
            P(("groups", "pipe"), "seq", "tensor"),
            P(("groups", "pipe"), None),
            P("seq", "tensor"),
            P("seq", "tensor"),
        ),
        out_specs=(P(("groups", "pipe"), "seq", "tensor"), P(("groups", "pipe"), "seq", "tensor")),
        check_vma=False,
    )
```

profile of v0, /device:TPU:0, one launch (start us, length us, event | category | flops | bytes accessed | tf_op | source)
XLA Modules:
  0.0 479.5 jit_solution(7597488558393478875)
XLA Ops:
  7.2 0.0 all-gather.13.cloned.1.call-start
  7.2 0.7 all-gather.13.cloned.1.call-update
  7.9 0.0 all-gather.7.cloned.1.call-start
  8.0 0.7 all-gather.7.cloned.1.call-update
  8.7 0.0 all-gather.9.cloned.1.call-start
  8.7 0.7 all-gather.9.cloned.1.call-update
  9.4 0.0 all-gather.11.cloned.1.call-start
  9.5 0.6 slice_bitcast_fusion.1
  10.1 5.5 %collective-permute-start = (bf16[1,1536]{1,0:T(2,128)(2,1)}, bf16[1,1536]{1,0:T(2,128)(2,1)}, u32[]{:S(2)}, u32[]{:S(2)}) collective-permute-start(bf16[1,1536]{1,0:T(2,128)(2,1)} %slice_bitcast_fusion.1), channel_id=1, source_target_pairs={{0,4},{4,8},{8,12},{1,5},{5,9},{9,13},{2,6},{6,10},{10,14},{3,7},{... | collective-permute-start | bytes 9224 | tf_op jit(solution)/shard_map/ppermute | solution.py:12
  15.6 0.0 all-gather.11.cloned.1.call-update
  15.6 0.0 reduce-scatter.2.cloned.1.call-start
  15.7 0.1 slice_bitcast_fusion
  15.8 0.0 copy-start.2
  15.8 28.9 %while.24 = (s32[]{:T(128)}, u32[384]{0:T(512)S(1)}, u32[384]{0:T(512)S(1)}, s32[512]{0:T(512)S(1)}, s32[]{:T(128)}, /*index=5*/s32[]{:T(128)}, s32[]{:T(128)}, s32[]{}) while((s32[]{:T(128)}, u32[384]{0:T(512)S(1)}, u32[384]{0:T(512)S(1)}, s32[512]{0:T(512)S(1)}, s32[]{:T(128)}, /*index=5*/s32[]{:T(128)}, s32[]{:T(128)}, s32[]{}) %tuple.59), condition=%wide.region_1.2_spmd.clone, body=%wide.region_0.1_spmd.clone.sunk | while | flops 8324 | bytes 29553 | solution.py:25
  15.8 2.8 gather_fusion
  18.7 2.8 gather_fusion
  21.6 2.8 gather_fusion
  24.5 2.8 gather_fusion
  27.4 2.8 gather_fusion
  30.3 2.8 gather_fusion
  33.2 2.8 gather_fusion
  36.1 2.8 gather_fusion
  39.0 2.8 gather_fusion
  41.8 2.8 gather_fusion
  44.7 3.9 gather_fusion.1
  48.7 2.4 fusion.3
  51.1 2.9 fusion.14
  54.0 5.7 %all-reduce = (f32[384]{0:T(512)}, f32[384]{0:T(512)}, f32[384]{0:T(512)}, f32[384]{0:T(512)}) all-reduce(f32[384]{0:T(512)S(1)} %get-tuple-element.90, f32[384]{0:T(512)} %get-tuple-element.91, f32[384]{0:T(512)S(1)} %get-tuple-element.89, f32[384]{0:T(512)} %fusion.14), channel_id=1, replica_groups=mesh['groups'=2,'seq'=4,'tensor'=2,'pipe'=2] {'tensor'}, use_global_device_ids=true, to_apply=%region_9.10 | all-reduce | flops 1536 | bytes 12288 | tf_op jit(solution)/shard_map/psum | solution.py:46
  59.7 1.3 subtract_convert_fusion
  61.0 1.3 fusion.50
  62.3 1.5 fusion.9
  63.8 1.3 slice.28
  65.1 0.6 slice.29
  65.7 1.3 collective-permute-start.1
  66.9 149.8 %all-gather.7.cloned.1.call-done = bf16[3072,1536]{1,0:T(8,128)(2,1)} async-done(((bf16[768,1536]{1,0:T(8,128)(2,1)}), bf16[3072,1536]{1,0:T(8,128)(2,1)}) %all-gather.7.cloned.1.call-update) | async-done | bytes 9437200 | tf_op jit(solution)/shard_map/all_gather | solution.py:87
  216.7 10.1 %fusion.18 = f32[384,3072]{1,0:T(8,128)} fusion(bf16[3072,1536]{1,0:T(8,128)(2,1)} %all-gather.7.cloned.1.call-done, bf16[1,384,1536]{2,1,0:T(8,128)(2,1)S(1)} %copy-done.2, f32[384]{0:T(512)} %get-tuple-element.114, f32[384]{0:T(512)S(1)} %get-tuple-element.111, f32[384]{0:T(512)S(1)} %get-tuple-element.117, bf16[383,1536]{1,0:T(8,128)(2,1)S(1)} %slice_bitcast_fusion, ...), kind=kOutput, calls=%fused_computation.34 | convolution fusion | flops 3629776896 | bytes 16519680 | tf_op jit(solution)/shard_map/dot_general | solution.py:88
  226.8 156.5 %all-gather.9.cloned.1.call-done = bf16[3072,1536]{1,0:T(8,128)(2,1)} async-done(((bf16[768,1536]{1,0:T(8,128)(2,1)}), bf16[3072,1536]{1,0:T(8,128)(2,1)}) %all-gather.9.cloned.1.call-update) | async-done | bytes 9437200 | tf_op jit(solution)/shard_map/all_gather | solution.py:87
  383.3 10.7 %add_convert_fusion = bf16[384,3072]{1,0:T(8,128)(2,1)} fusion(f32[384,3072]{1,0:T(8,128)} %fusion.18, bf16[3072,1536]{1,0:T(8,128)(2,1)} %all-gather.9.cloned.1.call-done, bf16[1,1536]{1,0:T(2,128)(2,1)} %collective-permute-done.1, bf16[383,1536]{1,0:T(8,128)(2,1)} %slice.28), kind=kOutput, calls=%fused_computation.8 | convolution fusion | flops 3628597248 | bytes 17694720 | tf_op jit(solution)/shard_map/dot_general | solution.py:88
  394.1 0.0 reduce-scatter.2.cloned.1.call-update
  394.1 1.1 fusion.25
  395.2 2.3 fusion.2
  397.6 4.5 all-to-all-start
  402.0 33.3 %all-gather.11.cloned.1.call-done = bf16[1,512,1536]{2,1,0:T(8,128)(2,1)} async-done(((bf16[1,128,1536]{2,1,0:T(8,128)(2,1)}), bf16[1,512,1536]{2,1,0:T(8,128)(2,1)}) %all-gather.11.cloned.1.call-update) | async-done | bytes 1572880 | tf_op jit(solution)/shard_map/all_gather | solution.py:29
  435.4 2.2 convolution_add_fusion.1
  437.6 15.9 %all-to-all-done = bf16[4,128,1536]{2,1,0:T(8,128)(2,1)} async-done(((bf16[4,128,1536]{2,1,0:T(8,128)(2,1)}), bf16[4,128,1536]{2,1,0:T(8,128)(2,1)}, u32[]{:S(2)}, u32[]{:S(2)}) %all-to-all-start) | async-done | bytes 1572896 | tf_op jit(solution)/shard_map/all_to_all | solution.py:65
  453.5 2.5 reduce_sum.52
  456.0 14.4 %reduce-scatter.2.cloned.1.call-done = bf16[384,1536]{1,0:T(8,128)(2,1)} async-done(((bf16[384,3072]{1,0:T(8,128)(2,1)}), bf16[384,1536]{1,0:T(8,128)(2,1)}) %reduce-scatter.2.cloned.1.call-update) | async-done | bytes 1179664 | tf_op jit(solution)/shard_map/reduce_scatter | solution.py:91
  470.4 2.6 fusion.17
  (70 shorter events, 0.5 us)
Async XLA Ops:
  7.2 43.9 %all-gather.13.cloned.1.call-start = ((), (), s32[]{:S(2)}) async-start(), calls=%async_computation.6 | async-start | bytes 1966080 | tf_op jit(solution)/shard_map/all_gather | solution.py:28
  7.9 1.6 copy-start.3
  7.9 208.8 %all-gather.7.cloned.1.call-start = ((), (), s32[]{:S(2)}) async-start(), calls=%async_computation.2 | async-start | bytes 11796480 | tf_op jit(solution)/shard_map/all_gather | solution.py:87
  8.7 7.1 %copy-start = (s32[1,512]{1,0:T(1,128)S(1)}, s32[1,512]{1,0:T(1,128)}, u32[]{:S(2)}) copy-start(s32[1,512]{1,0:T(1,128)} %param.15) | copy-start | bytes 6148
  8.7 374.7 %all-gather.9.cloned.1.call-start = ((), (), s32[]{:S(2)}) async-start(), calls=%async_computation.3 | async-start | bytes 11796480 | tf_op jit(solution)/shard_map/all_gather | solution.py:87
  9.4 426.0 %all-gather.11.cloned.1.call-start = ((), (), s32[]{:S(2)}) async-start(), calls=%async_computation.5 | async-start | bytes 1966080 | tf_op jit(solution)/shard_map/all_gather | solution.py:29
  10.1 38.6 %collective-permute-start = (bf16[1,1536]{1,0:T(2,128)(2,1)}, bf16[1,1536]{1,0:T(2,128)(2,1)}, u32[]{:S(2)}, u32[]{:S(2)}) collective-permute-start(bf16[1,1536]{1,0:T(2,128)(2,1)} %slice_bitcast_fusion.1), channel_id=1, source_target_pairs={{0,4},{4,8},{8,12},{1,5},{5,9},{9,13},{2,6},{6,10},{10,14},{3,7},{... | collective-permute-start | bytes 9224 | tf_op jit(solution)/shard_map/ppermute | solution.py:12
  15.6 454.8 %reduce-scatter.2.cloned.1.call-start = ((), (), s32[]{:S(2)}) async-start(), calls=%async_computation.4 | async-start | bytes 3538944 | tf_op jit(solution)/shard_map/reduce_scatter | solution.py:91
  15.8 32.9 %copy-start.2 = (bf16[1,384,1536]{2,1,0:T(8,128)(2,1)S(1)}, bf16[1,384,1536]{2,1,0:T(8,128)(2,1)}, u32[]{:S(2)}) copy-start(bf16[1,384,1536]{2,1,0:T(8,128)(2,1)} %param.11) | copy-start | bytes 3538948
  44.7 6.4 %copy-start.1 = (bf16[1,384,1536]{2,1,0:T(8,128)(2,1)S(1)}, bf16[1,384,1536]{2,1,0:T(8,128)(2,1)}, u32[]{:S(2)}) copy-start(bf16[1,384,1536]{2,1,0:T(8,128)(2,1)} %param.10) | copy-start | bytes 3538948
  61.0 1.3 copy-start.4
  65.7 161.2 %collective-permute-start.1 = (bf16[1,1536]{1,0:T(2,128)(2,1)}, bf16[1,1536]{1,0:T(2,128)(2,1)}, u32[]{:S(2)}, u32[]{:S(2)}) collective-permute-start(bf16[1,1536]{1,0:T(2,128)(2,1)} %slice.29), channel_id=1, source_target_pairs={{4,0},{8,4},{12,8},{5,1},{9,5},{13,9},{6,2},{10,6},{14,10},{7,3},{... | collective-permute-start | bytes 9224 | tf_op jit(solution)/shard_map/ppermute | solution.py:12
  394.1 1.1 copy-start.6
  397.6 37.8 %copy-start.5 = (pred[384]{0:T(512)(128)(4,1)S(1)}, pred[384]{0:T(512)(128)(4,1)}, u32[]{:S(2)}) copy-start(pred[384]{0:T(512)(128)(4,1)} %copy-done.4) | copy-start | bytes 1156
  397.6 56.0 %all-to-all-start = ((bf16[4,128,1536]{2,1,0:T(8,128)(2,1)}), bf16[4,128,1536]{2,1,0:T(8,128)(2,1)}, u32[]{:S(2)}, u32[]{:S(2)}) async-start(bf16[4,128,1536]{2,1,0:T(8,128)(2,1)} %bitcast.9), calls=%async_computation.1 | async-start | bytes 3145728 | tf_op jit(solution)/shard_map/all_to_all | solution.py:65
Sparse Core Ops, SparseCore 0:
  9.6 39.7 all-gather.12
  51.0 165.7 all-gather.6
  218.3 164.9 all-gather.8
  384.8 50.5 all-gather.10
  437.5 32.8 reduce-scatter.1
where the time goes:
time: 480 us
  waiting for transfers between devices  372 us (78%)
  local copies, waits for them, and re-layouts  34.5 us (7%)
  matrix products  29.4 us (6%)
  between operations  13.9 us (3%)
  other arithmetic  12 us (2%)
  starting transfers between devices  11.5 us (2%)
  blocking collectives  5.69 us (1%)
    all_gather x2, waiting for transfers between devices, shards(): lax.all_gather((query_weight, key_weight), 'seq', axis=0, tiled=True)  306 us
    all_gather x1, waiting for transfers between devices, shards(): lax.all_gather(main_in_grad[0], 'seq', axis=0, tiled=True)  33.3 us
    gather x10, local copies, waits for them, and re-layouts, shards(): span_of = jnp.searchsorted(bounds_row, positions, side='right') - 1  28 us
    all_to_all x1, waiting for transfers between devices, shards(): lax.all_to_all(span_terms.reshape(seq_count, span_rows, span_terms.shape[...  15.9 us
    reduce_scatter x1, waiting for transfers between devices, shards(): lax.psum_scatter(partial_value.astype(jnp.bfloat16), 'tensor', scatter_di...  14.4 us
    dot_general x1, matrix products, shards(): jnp.dot(key_grad, pieces[1].T, preferred_element_type=jnp.float32)  10.7 us
    dot_general x1, matrix products, shards(): jnp.dot(query_grad, pieces[0].T, preferred_element_type=jnp.float32)  10.1 us
  transfers between devices with their start and end apart: 8, of which 5 were waited for; matrix products, arithmetic and copies ran while one was open for 15% of the time, Pallas kernels for 0%

commit v1 on v0

--- a/solution.py
+++ b/solution.py
@@ -22,8 +22,8 @@
     shard_index = lax.axis_index("seq")
     seq_count = lax.axis_size("seq")
     positions = shard_index * row_count + jnp.arange(row_count, dtype=jnp.int32)
-    span_of = jnp.searchsorted(bounds_row, positions, side="right") - 1
-    starts = jnp.take(bounds_row, span_of) == positions
+    span_of = jnp.sum((bounds_row[None, :] <= positions[:, None]).astype(jnp.int32), 1) - 1
+    starts = jnp.any(bounds_row[None, :] == positions[:, None], 1)
     window_out, window_grad = (
         lax.all_gather(main_out[0], "seq", axis=0, tiled=True),
         lax.all_gather(main_in_grad[0], "seq", axis=0, tiled=True),
@@ -84,7 +84,17 @@
     ).astype(jnp.bfloat16)
     next_grad = passed_along(prev_grad[:1], "seq", -1)
     key_grad = jnp.concatenate([prev_grad[1:], next_grad], 0)
-    pieces = lax.all_gather((query_weight, key_weight), "seq", axis=0, tiled=True)
+    part_rows = query_weight.shape[0] // (lax.axis_size("groups") * lax.axis_size("pipe"))
+    part_index = lax.axis_index("groups") * lax.axis_size("pipe") + lax.axis_index("pipe")
+    pieces = [
+        lax.all_gather(
+            lax.dynamic_slice_in_dim(weight, part_index * part_rows, part_rows, 0),
+            ("seq", "groups", "pipe"),
+            axis=0,
+            tiled=True,
+        )
+        for weight in (query_weight, key_weight)
+    ]
     partial_value = jnp.dot(query_grad, pieces[0].T, preferred_element_type=jnp.float32) + jnp.dot(
         key_grad, pieces[1].T, preferred_element_type=jnp.float32
     )

time: 480 us -> 312 us (0.65)
  waiting for transfers between devices: 372 us -> 225 us
  local copies, waits for them, and re-layouts: 34.5 us -> 9.5 us
    all_gather x2, waiting for transfers between devices: 306 us -> 137 us  [shards(): lax.all_gather(lax.dynamic_slice_in_dim(weight, part_index * part_rows, p...]
    gather x11 -> x0, local copies, waits for them, and re-layouts: 31.9 us -> none  [the longest x10 28 us: shards(): span_of = jnp.searchsorted(bounds_row, positions, side='right') - 1]
    all_gather x1, waiting for transfers between devices: 0.01 us -> 24.5 us  [shards(): lax.all_gather(main_out[0], 'seq', axis=0, tiled=True)]
  transfers between devices with their start and end apart: 8 -> 8, of which waited for: 5 -> 6; matrix products, arithmetic and copies ran while one was open for 15% -> 17% of each run, Pallas kernels for 0% -> 0%
where the time goes in v1:
time: 312 us; the launch traced here: 311 us
  waiting for transfers between devices  225 us (72%)
  matrix products  31.4 us (10%)
  other arithmetic  15 us (5%)
  between operations  13.9 us (4%)
  starting transfers between devices  10.9 us (3%)
  local copies, waits for them, and re-layouts  9.5 us (3%)
  blocking collectives  5.69 us (2%)
    all_gather x2, waiting for transfers between devices, shards(): lax.all_gather(lax.dynamic_slice_in_dim(weight, part_index * part_rows, p...  137 us
    all_gather x1, waiting for transfers between devices, shards(): lax.all_gather(main_in_grad[0], 'seq', axis=0, tiled=True)  33.1 us
    all_gather x1, waiting for transfers between devices, shards(): lax.all_gather(main_out[0], 'seq', axis=0, tiled=True)  24.5 us
    reduce_scatter x1, waiting for transfers between devices, shards(): lax.psum_scatter(partial_value.astype(jnp.bfloat16), 'tensor', scatter_di...  14.7 us
    all_to_all x1, waiting for transfers between devices, shards(): lax.all_to_all(span_terms.reshape(seq_count, span_rows, span_terms.shape[...  14.6 us
    dot_general x1, matrix products, shards(): jnp.dot(key_grad, pieces[1].T, preferred_element_type=jnp.float32)  10.8 us
    dot_general x1, matrix products, shards(): jnp.dot(query_grad, pieces[0].T, preferred_element_type=jnp.float32)  10.6 us
  transfers between devices with their start and end apart: 8, of which 6 were waited for; matrix products, arithmetic and copies ran while one was open for 17% of the time, Pallas kernels for 0%

profile of v1, /device:TPU:0, one launch (start us, length us, event | category | flops | bytes accessed | tf_op | source)
XLA Modules:
  0.0 311.2 jit_solution(8867071752037706211)
XLA Ops:
  7.2 0.0 copy-start
  7.2 0.0 all-gather.13.cloned.1.call-start
  7.2 0.7 all-gather.13.cloned.1.call-update
  7.9 0.0 all-gather.7.cloned.1.call-start
  8.0 0.9 copy-done
  8.8 0.8 constant_dynamic-slice_fusion.1
  9.7 0.0 all-gather.7.cloned.1.call-update
  9.7 0.0 copy-start.5
  9.7 0.0 all-gather.9.cloned.1.call-start
  9.8 1.9 constant_dynamic-slice_fusion
  11.7 0.0 all-gather.9.cloned.1.call-update
  11.7 0.0 all-gather.11.cloned.1.call-start
  11.8 1.3 slice_bitcast_fusion.1
  13.1 4.9 %collective-permute-start = (bf16[1,1536]{1,0:T(2,128)(2,1)}, bf16[1,1536]{1,0:T(2,128)(2,1)S(1)}, u32[]{:S(2)}, u32[]{:S(2)}) collective-permute-start(bf16[1,1536]{1,0:T(2,128)(2,1)} %slice_bitcast_fusion.1), channel_id=1, source_target_pairs={{0,4},{4,8},{8,12},{1,5},{5,9},{9,13},{2,6},{6,10},{10,14},{3,7},{... | collective-permute-start | bytes 9224 | tf_op jit(solution)/shard_map/ppermute | solution.py:12
  18.0 0.0 all-gather.11.cloned.1.call-update
  18.1 0.0 copy-start.1
  18.1 0.0 reduce-scatter.2.cloned.1.call-start
  18.1 2.5 slice_bitcast_fusion
  20.6 0.0 copy-done.5
  20.6 0.2 convert_reduce_fusion
  20.9 0.7 compare_reduce_fusion
  21.6 0.0 collective-permute-done
  21.6 3.3 %fusion.1 = (f32[384]{0:T(512)S(1)}, f32[384]{0:T(512)}, f32[384]{0:T(512)}) fusion(bf16[383,1536]{1,0:T(8,128)(2,1)} %slice_bitcast_fusion, bf16[1,1536]{1,0:T(2,128)(2,1)S(1)} %collective-permute-done, bf16[1,384,1536]{2,1,0:T(8,128)(2,1)} %param.9), kind=kLoop, calls=%fused_computation.12 | loop fusion | flops 6486912 | bytes 2363904 | tf_op jit(solution)/shard_map/reduce_sum | solution.py:44
  24.9 24.5 %all-gather.13.cloned.1.call-done = bf16[1,512,1536]{2,1,0:T(8,128)(2,1)} async-done(((bf16[1,128,1536]{2,1,0:T(8,128)(2,1)}), bf16[1,512,1536]{2,1,0:T(8,128)(2,1)}) %all-gather.13.cloned.1.call-update) | async-done | bytes 1572880 | tf_op jit(solution)/shard_map/all_gather | solution.py:28
  49.4 2.9 fusion.12
  52.3 5.7 %all-reduce = (f32[384]{0:T(512)}, f32[384]{0:T(512)}, f32[384]{0:T(512)}, f32[384]{0:T(512)}) all-reduce(f32[384]{0:T(512)} %get-tuple-element.3, f32[384]{0:T(512)} %get-tuple-element.4, f32[384]{0:T(512)S(1)} %get-tuple-element.2, f32[384]{0:T(512)} %fusion.12), channel_id=1, replica_groups=mesh['groups'=2,'seq'=4,'tensor'=2,'pipe'=2] {'tensor'}, use_global_device_ids=true, to_apply=%region_9.0 | all-reduce | flops 1536 | bytes 12288 | tf_op jit(solution)/shard_map/psum | solution.py:46
  58.0 1.2 subtract_convert_fusion
  59.3 1.3 fusion.44
  60.5 2.4 fusion.7
  62.9 1.4 slice.24
  64.3 0.0 copy-done.2
  64.3 0.6 slice.25
  64.9 1.3 collective-permute-start.1
  66.2 66.0 %all-gather.7.cloned.1.call-done = bf16[3072,1536]{1,0:T(8,128)(2,1)} async-done(((bf16[192,1536]{1,0:T(8,128)(2,1)}), bf16[3072,1536]{1,0:T(8,128)(2,1)}) %all-gather.7.cloned.1.call-update) | async-done | bytes 9437200 | tf_op jit(solution)/shard_map/all_gather | solution.py:90
  132.2 10.6 %fusion.16 = f32[384,3072]{1,0:T(8,128)} fusion(bf16[3072,1536]{1,0:T(8,128)(2,1)} %all-gather.7.cloned.1.call-done, bf16[1,384,1536]{2,1,0:T(8,128)(2,1)} %param.9, f32[384]{0:T(512)} %get-tuple-element.14, f32[384]{0:T(512)} %copy-done.2, f32[384]{0:T(512)} %copy-done.3, bf16[383,1536]{1,0:T(8,128)(2,1)} %slice_bitcast_fusion, ...), kind=kOutput, calls=%fused_computation.26 | convolution fusion | flops 3629776896 | bytes 16519680 | tf_op jit(solution)/shard_map/dot_general | solution.py:98
  142.8 0.0 collective-permute-done.1
  142.8 71.3 %all-gather.9.cloned.1.call-done = bf16[3072,1536]{1,0:T(8,128)(2,1)} async-done(((bf16[192,1536]{1,0:T(8,128)(2,1)}), bf16[3072,1536]{1,0:T(8,128)(2,1)}) %all-gather.9.cloned.1.call-update) | async-done | bytes 9437200 | tf_op jit(solution)/shard_map/all_gather | solution.py:90
  214.1 10.8 %add_convert_fusion = bf16[384,3072]{1,0:T(8,128)(2,1)} fusion(f32[384,3072]{1,0:T(8,128)} %fusion.16, bf16[3072,1536]{1,0:T(8,128)(2,1)} %all-gather.9.cloned.1.call-done, bf16[1,1536]{1,0:T(2,128)(2,1)} %collective-permute-done.1, bf16[383,1536]{1,0:T(8,128)(2,1)} %slice.24), kind=kOutput, calls=%fused_computation | convolution fusion | flops 3628597248 | bytes 17694720 | tf_op jit(solution)/shard_map/dot_general | solution.py:98
  224.9 0.0 reduce-scatter.2.cloned.1.call-update
  224.9 1.1 fusion.23
  226.0 2.3 fusion
  228.4 4.5 %all-to-all-start = ((bf16[4,128,1536]{2,1,0:T(8,128)(2,1)}), bf16[4,128,1536]{2,1,0:T(8,128)(2,1)}, u32[]{:S(2)}, u32[]{:S(2)}) async-start(bf16[4,128,1536]{2,1,0:T(8,128)(2,1)} %bitcast.35), calls=%async_computation.1 | async-start | bytes 3145728 | tf_op jit(solution)/shard_map/all_to_all | solution.py:65
  232.8 33.1 %all-gather.11.cloned.1.call-done = bf16[1,512,1536]{2,1,0:T(8,128)(2,1)} async-done(((bf16[1,128,1536]{2,1,0:T(8,128)(2,1)}), bf16[1,512,1536]{2,1,0:T(8,128)(2,1)}) %all-gather.11.cloned.1.call-update) | async-done | bytes 1572880 | tf_op jit(solution)/shard_map/all_gather | solution.py:29
  265.9 3.7 %convolution_add_fusion.1 = f32[384,1536]{1,0:T(8,128)} fusion(bf16[1,512,1536]{2,1,0:T(8,128)(2,1)} %all-gather.11.cloned.1.call-done, bf16[1,384,1536]{2,1,0:T(8,128)(2,1)S(1)} %copy-done.1, s32[384]{0:T(512)S(1)} %broadcast_add_fusion, pred[384]{0:T(512)(128)(4,1)S(1)} %copy-done.4), kind=kOutput, calls=%fused_computation.10 | convolution fusion | flops 605552640 | bytes 5113728 | tf_op jit(solution)/shard_map/dot_general | solution.py:36
  269.6 14.6 %all-to-all-done = bf16[4,128,1536]{2,1,0:T(8,128)(2,1)} async-done(((bf16[4,128,1536]{2,1,0:T(8,128)(2,1)}), bf16[4,128,1536]{2,1,0:T(8,128)(2,1)}, u32[]{:S(2)}, u32[]{:S(2)}) %all-to-all-start) | async-done | bytes 1572896 | tf_op jit(solution)/shard_map/all_to_all | solution.py:65
  284.2 2.5 reduce_sum.62
  286.7 14.7 %reduce-scatter.2.cloned.1.call-done = bf16[384,1536]{1,0:T(8,128)(2,1)} async-done(((bf16[384,3072]{1,0:T(8,128)(2,1)}), bf16[384,1536]{1,0:T(8,128)(2,1)}) %reduce-scatter.2.cloned.1.call-update) | async-done | bytes 1179664 | tf_op jit(solution)/shard_map/reduce_scatter | solution.py:101
  301.4 3.3 %fusion.15 = bf16[1,384,1536]{2,1,0:T(8,128)(2,1)} fusion(f32[384,1536]{1,0:T(8,128)} %convolution_add_fusion.1, bf16[384,1536]{1,0:T(8,128)(2,1)} %reduce-scatter.2.cloned.1.call-done), kind=kLoop, calls=%fused_computation.25 | loop fusion | flops 1769472 | bytes 4718592 | tf_op jit(solution)/shard_map/broadcast_in_dim | solution.py:104
  (10 shorter events, 0.0 us)
Async XLA Ops:
  7.2 1.7 copy-start
  7.2 42.2 %all-gather.13.cloned.1.call-start = ((), (), s32[]{:S(2)}) async-start(), calls=%async_computation.6 | async-start | bytes 1966080 | tf_op jit(solution)/shard_map/all_gather | solution.py:28
  7.9 124.2 %all-gather.7.cloned.1.call-start = ((), (), s32[]{:S(2)}) async-start(), calls=%async_computation.2 | async-start | bytes 10027008 | tf_op jit(solution)/shard_map/all_gather | solution.py:90
  9.7 10.9 %copy-start.5 = (s32[1,512]{1,0:T(1,128)S(1)}, s32[1,512]{1,0:T(1,128)}, u32[]{:S(2)}) copy-start(s32[1,512]{1,0:T(1,128)} %param.13) | copy-start | bytes 6148
  9.7 204.3 %all-gather.9.cloned.1.call-start = ((), (), s32[]{:S(2)}) async-start(), calls=%async_computation.3 | async-start | bytes 10027008 | tf_op jit(solution)/shard_map/all_gather | solution.py:90
  11.7 254.2 %all-gather.11.cloned.1.call-start = ((), (), s32[]{:S(2)}) async-start(), calls=%async_computation.5 | async-start | bytes 1966080 | tf_op jit(solution)/shard_map/all_gather | solution.py:29
  13.1 8.5 %collective-permute-start = (bf16[1,1536]{1,0:T(2,128)(2,1)}, bf16[1,1536]{1,0:T(2,128)(2,1)S(1)}, u32[]{:S(2)}, u32[]{:S(2)}) collective-permute-start(bf16[1,1536]{1,0:T(2,128)(2,1)} %slice_bitcast_fusion.1), channel_id=1, source_target_pairs={{0,4},{4,8},{8,12},{1,5},{5,9},{9,13},{2,6},{6,10},{10,14},{3,7},{... | collective-permute-start | bytes 9224 | tf_op jit(solution)/shard_map/ppermute | solution.py:12
  18.1 31.3 %copy-start.1 = (bf16[1,384,1536]{2,1,0:T(8,128)(2,1)S(1)}, bf16[1,384,1536]{2,1,0:T(8,128)(2,1)}, u32[]{:S(2)}) copy-start(bf16[1,384,1536]{2,1,0:T(8,128)(2,1)} %param.8) | copy-start | bytes 3538948
  18.1 283.3 %reduce-scatter.2.cloned.1.call-start = ((), (), s32[]{:S(2)}) async-start(), calls=%async_computation.4 | async-start | bytes 3538944 | tf_op jit(solution)/shard_map/reduce_scatter | solution.py:101
  59.3 5.0 %copy-start.2 = (f32[384]{0:T(512)}, f32[384]{0:T(512)S(1)}, u32[]{:S(2)}) copy-start(f32[384]{0:T(512)S(1)} %get-tuple-element.11) | copy-start | bytes 4612
  59.3 5.0 %copy-start.3 = (f32[384]{0:T(512)}, f32[384]{0:T(512)S(1)}, u32[]{:S(2)}) copy-start(f32[384]{0:T(512)S(1)} %get-tuple-element.15) | copy-start | bytes 4612
  64.9 77.9 %collective-permute-start.1 = (bf16[1,1536]{1,0:T(2,128)(2,1)}, bf16[1,1536]{1,0:T(2,128)(2,1)}, u32[]{:S(2)}, u32[]{:S(2)}) collective-permute-start(bf16[1,1536]{1,0:T(2,128)(2,1)} %slice.25), channel_id=1, source_target_pairs={{4,0},{8,4},{12,8},{5,1},{9,5},{13,9},{6,2},{10,6},{14,10},{7,3},{... | collective-permute-start | bytes 9224 | tf_op jit(solution)/shard_map/ppermute | solution.py:12
  224.9 1.1 copy-start.6
  228.3 37.6 %copy-start.4 = (pred[384]{0:T(512)(128)(4,1)S(1)}, pred[384]{0:T(512)(128)(4,1)}, u32[]{:S(2)}) copy-start(pred[384]{0:T(512)(128)(4,1)} %compare_reduce_fusion) | copy-start | bytes 1156
  228.4 55.8 %all-to-all-start = ((bf16[4,128,1536]{2,1,0:T(8,128)(2,1)}), bf16[4,128,1536]{2,1,0:T(8,128)(2,1)}, u32[]{:S(2)}, u32[]{:S(2)}) async-start(bf16[4,128,1536]{2,1,0:T(8,128)(2,1)} %bitcast.35), calls=%async_computation.1 | async-start | bytes 3145728 | tf_op jit(solution)/shard_map/all_to_all | solution.py:65
Sparse Core Ops, SparseCore 0:
  9.6 39.7 all-gather.12
  51.7 80.4 all-gather.6
  134.4 79.5 all-gather.8
  215.5 50.3 all-gather.10
  268.0 33.3 reduce-scatter.1

commit v2 on v0

v2 whole, which is shorter than its diff:
```python
import jax
import jax.numpy as jnp
from jax import lax
from jax.sharding import PartitionSpec as P

epsilon = 1e-06


def passed_along(x, axis, by):
    length = lax.axis_size(axis)
    pairs = [(i, i + by) for i in range(length) if 0 <= i + by < length]
    return lax.ppermute(x, axis, pairs)


reach = 2


def swapped(x, axis):
    length = lax.axis_size(axis)
    return lax.ppermute(x, axis, [(i, length - 1 - i) for i in range(length)])


def window_of(block):
    pieces = []
    for offset in range(-reach, reach + 1):
        pieces.append(block if offset == 0 else passed_along(block, "seq", -offset))
    return jnp.concatenate(pieces, 0)


def after(value, *others):
    return lax.optimization_barrier((value,) + others)[0]


def product(rows, weight):
    return lax.dot_general(
        rows, weight, (((1,), (1,)), ((), ())), preferred_element_type=jnp.float32
    )


def shards(out_grad, queries, keys, main_out, main_in_grad, boundaries, query_weight, key_weight):
    cotangent = out_grad[0]
    query_rows = queries[0]
    key_rows = keys[0]
    bounds_row = boundaries[0]
    row_count = cotangent.shape[0]
    span_rows = main_out.shape[1]
    shard_index = lax.axis_index("seq")
    seq_count = lax.axis_size("seq")
    tensor_count = lax.axis_size("tensor")
    tensor_index = lax.axis_index("tensor")
    group_index = lax.axis_index("groups")
    part_rows = query_weight.shape[0] // (lax.axis_size("groups") * lax.axis_size("pipe"))
    part_index = group_index * lax.axis_size("pipe") + lax.axis_index("pipe")
    query_part_weight, key_part_weight = [
        lax.all_gather(
            lax.dynamic_slice_in_dim(weight, part_index * part_rows, part_rows, 0),
            ("seq", "pipe"),
            axis=0,
            tiled=True,
        )
        for weight in (query_weight, key_weight)
    ]
    last_key = passed_along(key_rows[-1:], "seq", 1)
    window_out = window_of(main_out[0])
    positions = shard_index * row_count + jnp.arange(row_count, dtype=jnp.int32)
    span_of = jnp.sum((bounds_row[None, :] <= positions[:, None]).astype(jnp.int32), 1) - 1
    starts = jnp.any(bounds_row[None, :] == positions[:, None], 1)
    place = span_of - (shard_index - reach) * span_rows
    window_rows = window_out.shape[0]
    selector = place[:, None] == jnp.arange(window_rows, dtype=jnp.int32)[None, :]
    upsampled = jnp.dot(selector.astype(jnp.bfloat16), window_out, preferred_element_type=jnp.float32)
    prev_keys = jnp.concatenate([last_key, key_rows[:-1]], 0)
    query_wide = query_rows.astype(jnp.float32)
    prev_wide = prev_keys.astype(jnp.float32)
    cotangent_wide = cotangent.astype(jnp.float32)
    cross_part = jnp.sum(query_wide * prev_wide, 1)
    query_part = jnp.sum(query_wide * query_wide, 1)
    key_part = jnp.sum(prev_wide * prev_wide, 1)
    conf_part = jnp.sum(cotangent_wide * upsampled, 1)
    cross_sum, query_sum, key_sum, conf_grad = lax.psum(
        (cross_part, query_part, key_part, conf_part), "tensor"
    )
    query_scale = lax.rsqrt(query_sum + epsilon)
    key_scale = lax.rsqrt(key_sum + epsilon)
    cosine = cross_sum * query_scale * key_scale
    probability = jnp.where(positions == 0, 1.0, 0.5 * (1.0 - cosine))
    confidence = jnp.where(starts, probability, 1.0 - probability)
    sign = jnp.where(starts, 1.0, -1.0)
    cos_grad = jnp.where(positions == 0, 0.0, -0.5 * sign * conf_grad)
    both_scale = (query_scale * key_scale)[:, None]
    query_grad = (
        cos_grad[:, None]
        * (prev_wide * both_scale - (cosine * query_scale * query_scale)[:, None] * query_wide)
    ).astype(jnp.bfloat16)
    prev_grad = (
        cos_grad[:, None]
        * (query_wide * both_scale - (cosine * key_scale * key_scale)[:, None] * prev_wide)
    ).astype(jnp.bfloat16)
    next_grad = passed_along(prev_grad[:1], "seq", -1)
    query_grad_other = swapped(query_grad, "groups")
    key_grad = jnp.concatenate([prev_grad[1:], next_grad], 0)
    key_grad_other = swapped(key_grad, "groups")

    conf_high = confidence.astype(jnp.bfloat16)
    conf_low = (confidence - conf_high.astype(jnp.float32)).astype(jnp.bfloat16)
    zero_weight = jnp.zeros((), jnp.bfloat16)
    weight_high = jnp.where(selector, conf_high[:, None], zero_weight)
    weight_low = jnp.where(selector, conf_low[:, None], zero_weight)
    contract = (((0,), (0,)), ((), ()))
    span_terms = lax.dot_general(
        weight_high, cotangent, contract, preferred_element_type=jnp.float32
    )
    span_terms = span_terms + lax.dot_general(
        weight_low, cotangent, contract, preferred_element_type=jnp.float32
    )
    grad_block = after(main_in_grad[0], query_part_weight)
    window_grad = window_of(grad_block)
    start_picker = (selector & starts[:, None]).astype(jnp.bfloat16)
    start_grad = jnp.dot(start_picker, window_grad, preferred_element_type=jnp.float32)
    span_sums = span_terms[reach * span_rows : (reach + 1) * span_rows]
    for offset in range(-reach, reach + 1):
        if offset != 0:
            block = span_terms[(reach + offset) * span_rows : (reach + offset + 1) * span_rows]
            block = block.astype(jnp.bfloat16)
            span_sums = span_sums + passed_along(block, "seq", offset).astype(jnp.float32)
    main_grad = span_sums.astype(jnp.bfloat16)[None]

    def partial(query_side, key_side, query_block, key_block):
        total = product(query_side, query_block) + product(key_side, key_block)
        return total.astype(jnp.bfloat16)

    block_rows = query_part_weight.shape[0] // tensor_count
    if tensor_count == 2:

        def half(weight, index):
            return lax.dynamic_slice_in_dim(weight, index * block_rows, block_rows, 0)

        query_far, key_far = half(query_part_weight, 1 - tensor_index), half(key_part_weight, 1 - tensor_index)
        query_near, key_near = half(query_part_weight, tensor_index), half(key_part_weight, tensor_index)
        other_in = swapped(partial(query_grad_other, key_grad_other, query_far, key_far), "tensor")
        own_in = swapped(partial(query_grad, key_grad, query_far, key_far), "tensor")
        other_near = partial(query_grad_other, key_grad_other, query_near, key_near)
        own_near = partial(query_grad, key_grad, query_near, key_near)
        other_sum = other_near.astype(jnp.float32) + other_in.astype(jnp.float32)
        own_sum = own_near.astype(jnp.float32) + own_in.astype(jnp.float32)
    else:
        other_sum = lax.psum_scatter(
            partial(query_grad_other, key_grad_other, query_part_weight, key_part_weight),
            "tensor",
            scatter_dimension=1,
            tiled=True,
        )
        own_sum = lax.psum_scatter(
            partial(query_grad, key_grad, query_part_weight, key_part_weight),
            "tensor",
            scatter_dimension=1,
            tiled=True,
        ).astype(jnp.float32)
    from_other = swapped(other_sum.astype(jnp.bfloat16), "groups").astype(jnp.float32)
    first = jnp.where(group_index == 0, own_sum, from_other)
    second = jnp.where(group_index == 0, from_other, own_sum)
    width = part_rows * lax.axis_size("pipe")
    columns = []
    for start in range(0, block_rows, width):
        columns += [first[:, start : start + width], second[:, start : start + width]]
    routing = jnp.concatenate(columns, 1)
    byte_grad = (cotangent_wide + start_grad + routing).astype(jnp.bfloat16)[None]
    return (byte_grad, main_grad)


def solution(mesh):
    return jax.shard_map(
        shards,
        mesh=mesh,
        in_specs=(
            P(("groups", "pipe"), "seq", "tensor"),
            P(("groups", "pipe"), "seq", "tensor"),
            P(("groups", "pipe"), "seq", "tensor"),
            P(("groups", "pipe"), "seq", "tensor"),
            P(("groups", "pipe"), "seq", "tensor"),
            P(("groups", "pipe"), None),
            P("seq", "tensor"),
            P("seq", "tensor"),
        ),
        out_specs=(P(("groups", "pipe"), "seq", "tensor"), P(("groups", "pipe"), "seq", "tensor")),
        check_vma=False,
    )
```

time: 480 us -> 227 us (0.47)
  waiting for transfers between devices: 372 us -> 83.6 us
  starting transfers between devices: 11.5 us -> 63.1 us
  local copies, waits for them, and re-layouts: 34.5 us -> 19.9 us
    all_gather x4 -> x2, waiting for transfers between devices: 340 us -> 0.02 us  [shards(): lax.all_gather(lax.dynamic_slice_in_dim(weight, part_index * part_rows, p...]
    ppermute x2 -> x14, waiting for transfers between devices: 0.01 us -> 71.1 us  [passed_along(): return lax.ppermute(x, axis, pairs)]
    ppermute x2 -> x14, starting transfers between devices: 6.79 us -> 56.4 us  [passed_along(): return lax.ppermute(x, axis, pairs)]
    gather x11 -> x0, local copies, waits for them, and re-layouts: 31.9 us -> none  [the longest x10 28 us: shards(): span_of = jnp.searchsorted(bounds_row, positions, side='right') - 1]
    all_to_all x1 -> x0, waiting for transfers between devices: 15.9 us -> none  [shards(): lax.all_to_all(span_terms.reshape(seq_count, span_rows, span_terms.shape[...]
    reduce_scatter x1 -> x0, waiting for transfers between devices: 14.4 us -> none  [shards(): lax.psum_scatter(partial_value.astype(jnp.bfloat16), 'tensor', scatter_di...]
    ppermute x0 -> x5, waiting for transfers between devices: none -> 12.4 us  [swapped(): return lax.ppermute(x, axis, [(i, length - 1 - i) for i in range(length)])]
    unnamed x14 -> x28, local copies, waits for them, and re-layouts: 0.03 us -> 10.9 us
  transfers between devices with their start and end apart: 8 -> 21, of which waited for: 5 -> 7; matrix products, arithmetic and copies ran while one was open for 15% -> 22% of each run, Pallas kernels for 0% -> 0%
where the time goes in v2:
time: 227 us; the launch traced here: 225 us
  waiting for transfers between devices  83.6 us (37%)
  starting transfers between devices  63.1 us (28%)
  matrix products  26.6 us (12%)
  local copies, waits for them, and re-layouts  19.9 us (9%)
  between operations  14.4 us (6%)
  other arithmetic  12 us (5%)
  blocking collectives  5.68 us (3%)
    ppermute x14, waiting for transfers between devices, passed_along(): return lax.ppermute(x, axis, pairs)  71.1 us
    ppermute x14, starting transfers between devices, passed_along(): return lax.ppermute(x, axis, pairs)  56.4 us
    dot_general x8, matrix products, product(): lax.dot_general(rows, weight, (((1,), (1,)), ((), ())), preferred_element...  17.7 us
    ppermute x5, waiting for transfers between devices, swapped(): return lax.ppermute(x, axis, [(i, length - 1 - i) for i in range(length)])  12.4 us
    unnamed x28, local copies, waits for them, and re-layouts  10.9 us
    ppermute x5, starting transfers between devices, swapped(): return lax.ppermute(x, axis, [(i, length - 1 - i) for i in range(length)])  6.67 us
    psum x1, blocking collectives, shards(): lax.psum((cross_part, query_part, key_part, conf_part), 'tensor')  5.68 us
  transfers between devices with their start and end apart: 21, of which 7 were waited for; matrix products, arithmetic and copies ran while one was open for 22% of the time, Pallas kernels for 0%

profile of v2, /device:TPU:0, one launch (start us, length us, event | category | flops | bytes accessed | tf_op | source)
XLA Modules:
  0.0 225.4 jit_solution(201163370230000530)
XLA Ops:
  7.2 1.6 copy-done
  9.8 1.9 constant_dynamic-slice_fusion
  11.7 6.7 %collective-permute-start.4 = (bf16[128,1536]{1,0:T(8,128)(2,1)}, bf16[128,1536]{1,0:T(8,128)(2,1)}, u32[]{:S(2)}, u32[]{:S(2)}) collective-permute-start(bf16[128,1536]{1,0:T(8,128)(2,1)} %bitcast.3), channel_id=1, source_target_pairs={{0,8},{4,12},{1,9},{5,13},{2,10},{6,14},{3,11},{7,15},{16,24},{20,... | collective-permute-start | bytes 1179656 | tf_op jit(solution)/shard_map/ppermute | solution.py:12
  18.4 4.2 %collective-permute-start.5 = (bf16[128,1536]{1,0:T(8,128)(2,1)}, bf16[128,1536]{1,0:T(8,128)(2,1)}, u32[]{:S(2)}, u32[]{:S(2)}) collective-permute-start(bf16[128,1536]{1,0:T(8,128)(2,1)} %bitcast.3), channel_id=1, source_target_pairs={{0,4},{4,8},{8,12},{1,5},{5,9},{9,13},{2,6},{6,10},{10,14},{3,7},{... | collective-permute-start | bytes 1179656 | tf_op jit(solution)/shard_map/ppermute | solution.py:12
  22.7 1.3 collective-permute-start.6
  24.0 1.3 collective-permute-start.7
  25.3 1.3 slice_bitcast_fusion.1
  26.6 4.5 %collective-permute-start.8 = (bf16[1,1536]{1,0:T(2,128)(2,1)}, bf16[1,1536]{1,0:T(2,128)(2,1)S(1)}, u32[]{:S(2)}, u32[]{:S(2)}) collective-permute-start(bf16[1,1536]{1,0:T(2,128)(2,1)} %slice_bitcast_fusion.1), channel_id=1, source_target_pairs={{0,4},{4,8},{8,12},{1,5},{5,9},{9,13},{2,6},{6,10},{10,14},{3,7},{... | collective-permute-start | bytes 9224 | tf_op jit(solution)/shard_map/ppermute | solution.py:12
  31.4 1.4 slice_bitcast_fusion
  33.5 16.3 %collective-permute-done.8 = bf16[1,1536]{1,0:T(2,128)(2,1)S(1)} collective-permute-done((bf16[1,1536]{1,0:T(2,128)(2,1)}, bf16[1,1536]{1,0:T(2,128)(2,1)S(1)}, u32[]{:S(2)}, u32[]{:S(2)}) %collective-permute-start.8) | collective-permute-done | bytes 3104 | tf_op jit(solution)/shard_map/ppermute | solution.py:12
  49.9 3.0 %fusion.3 = (f32[384]{0:T(512)S(1)}, f32[384]{0:T(512)}, f32[384]{0:T(512)}) fusion(bf16[383,1536]{1,0:T(8,128)(2,1)S(1)} %slice_bitcast_fusion, bf16[1,1536]{1,0:T(2,128)(2,1)S(1)} %collective-permute-done.8, bf16[1,384,1536]{2,1,0:T(8,128)(2,1)} %param.9), kind=kLoop, calls=%fused_computation.13 | loop fusion | flops 6486912 | bytes 2363904 | tf_op jit(solution)/shard_map/reduce_sum | solution.py:78
  52.8 1.1 constant_dynamic-update-slice_fusion.9
  55.0 1.1 constant_dynamic-update-slice_fusion.7
  57.1 29.8 %collective-permute-done.7 = bf16[128,1536]{1,0:T(8,128)(2,1)} collective-permute-done((bf16[128,1536]{1,0:T(8,128)(2,1)}, bf16[128,1536]{1,0:T(8,128)(2,1)}, u32[]{:S(2)}, u32[]{:S(2)}) %collective-permute-start.7) | collective-permute-done | bytes 393248 | tf_op jit(solution)/shard_map/ppermute | solution.py:12
  87.9 1.8 fusion.28
  89.7 5.7 %all-reduce = (f32[384]{0:T(512)}, f32[384]{0:T(512)}, f32[384]{0:T(512)}, f32[384]{0:T(512)}) all-reduce(f32[384]{0:T(512)} %get-tuple-element.5, f32[384]{0:T(512)} %get-tuple-element.6, f32[384]{0:T(512)S(1)} %get-tuple-element.4, f32[384]{0:T(512)} %fusion.28), channel_id=1, replica_groups=mesh['groups'=2,'seq'=4,'tensor'=2,'pipe'=2] {'tensor'}, use_global_device_ids=true, to_apply=%region_9.0 | all-reduce | flops 1536 | bytes 12288 | tf_op jit(solution)/shard_map/psum | solution.py:80
  96.8 3.9 %fusion.6 = (bf16[384,1536]{1,0:T(8,128)(2,1)}, bf16[384,1536]{1,0:T(8,128)(2,1)S(1)}) fusion(bf16[1,384,1536]{2,1,0:T(8,128)(2,1)} %param.9, f32[384]{0:T(512)S(1)} %get-tuple-element.28, f32[384]{0:T(512)S(1)} %get-tuple-element.25, f32[384]{0:T(512)S(1)} %get-tuple-element.29, bf16[383,1536]{1,0:T(8,128)(2,1)S(1)} %slice_bitcast_fusion, ...), kind=kLoop, calls=%fused_computation.16 | loop fusion | flops 8847360 | bytes 4724736 | tf_op jit(solution)/shard_map/convert_element_type | solution.py:94
  100.8 1.3 collective-permute-start.9
  102.1 1.3 fusion.69
  103.4 3.4 %fusion.106 = (bf16[640,1536]{1,0:T(8,128)(2,1)S(1)}, f32[640,1536]{1,0:T(8,128)}) fusion(f32[640,1536]{1,0:T(8,128)S(1)} %fusion.69, bf16[1,384,1536]{2,1,0:T(8,128)(2,1)S(1)} %copy-done.2, s32[384]{0:T(512)S(1)} %add_subtract_fusion, bf16[384]{0:T(512)(128)(2,1)S(1)} %get-tuple-element.11), kind=kOutput, calls=%fused_computation.120 | convolution fusion | flops 757432320 | bytes 11012352 | tf_op jit(solution)/shard_map/dot_general | solution.py:113
  106.8 1.0 fusion.103
  108.1 1.3 collective-permute-start.15
  109.5 1.3 collective-permute-start.12
  110.8 1.3 collective-permute-start.16
  112.1 5.9 %collective-permute-start.17 = (bf16[128,1536]{1,0:T(8,128)(2,1)}, bf16[128,1536]{1,0:T(8,128)(2,1)}, u32[]{:S(2)}, u32[]{:S(2)}) collective-permute-start(bf16[128,1536]{1,0:T(8,128)(2,1)} %get-tuple-element.17), channel_id=1, source_target_pairs={{0,4},{4,8},{8,12},{1,5},{5,9},{9,13},{2,6},{6,10},{10,14},{3,7},{... | collective-permute-start | bytes 1179656 | tf_op jit(solution)/shard_map/ppermute | solution.py:12
  118.0 5.9 %collective-permute-start.18 = (bf16[128,1536]{1,0:T(8,128)(2,1)}, bf16[128,1536]{1,0:T(8,128)(2,1)}, u32[]{:S(2)}, u32[]{:S(2)}) collective-permute-start(bf16[128,1536]{1,0:T(8,128)(2,1)} %get-tuple-element.16), channel_id=1, source_target_pairs={{0,8},{4,12},{1,9},{5,13},{2,10},{6,14},{3,11},{7,15},{16,24},{20,... | collective-permute-start | bytes 1179656 | tf_op jit(solution)/shard_map/ppermute | solution.py:12
  123.9 24.9 %collective-permute-done.15 = bf16[128,1536]{1,0:T(8,128)(2,1)S(1)} collective-permute-done((bf16[128,1536]{1,0:T(8,128)(2,1)S(1)}, bf16[128,1536]{1,0:T(8,128)(2,1)S(1)}, u32[]{:S(2)}, u32[]{:S(2)}) %collective-permute-start.15) | collective-permute-done | bytes 393248 | tf_op jit(solution)/shard_map/ppermute | solution.py:12
  149.6 1.5 collective-permute-start.11
  151.1 2.6 %fusion.86 = bf16[1,128,1536]{2,1,0:T(8,128)(2,1)} fusion(bf16[128,1536]{1,0:T(8,128)(2,1)} %collective-permute-done.18, bf16[128,1536]{1,0:T(8,128)(2,1)} %collective-permute-done.17, bf16[128,1536]{1,0:T(8,128)(2,1)} %collective-permute-done.16, bf16[128,1536]{1,0:T(8,128)(2,1)} %copy-done.6, f32[640,1536]{1,0:T(8,128)} %get-tuple-element.31), kind=kLoop, calls=%fused_computation.76 | loop fusion | flops 1769472 | bytes 2752512 | tf_op jit(solution)/shard_map/broadcast_in_dim | solution.py:126
  153.7 15.4 %collective-permute-start = (bf16[128,1536]{1,0:T(8,128)(2,1)}, bf16[128,1536]{1,0:T(8,128)(2,1)}, u32[]{:S(2)}, u32[]{:S(2)}) collective-permute-start(bf16[128,1536]{1,0:T(8,128)(2,1)} %bitcast.37), channel_id=1, source_target_pairs={{0,8},{4,12},{1,9},{5,13},{2,10},{6,14},{3,11},{7,15},{16,24},{20,... | collective-permute-start | bytes 1179656 | tf_op jit(solution)/shard_map/ppermute | solution.py:12
  169.1 4.5 %collective-permute-start.1 = (bf16[128,1536]{1,0:T(8,128)(2,1)}, bf16[128,1536]{1,0:T(8,128)(2,1)}, u32[]{:S(2)}, u32[]{:S(2)}) collective-permute-start(bf16[128,1536]{1,0:T(8,128)(2,1)} %bitcast.38), channel_id=1, source_target_pairs={{0,4},{4,8},{8,12},{1,5},{5,9},{9,13},{2,6},{6,10},{10,14},{3,7},{... | collective-permute-start | bytes 1179656 | tf_op jit(solution)/shard_map/ppermute | solution.py:12
  173.7 1.3 collective-permute-start.2
  175.0 1.5 collective-permute-start.3
  176.5 3.3 %fusion.12 = f32[384,768]{1,0:T(8,128)S(1)} fusion(bf16[384,1536]{1,0:T(8,128)(2,1)} %collective-permute-done.12, bf16[1536,1536]{1,0:T(8,128)(2,1)} %all-gather.5.cloned.1.call-done, s32[]{:T(128)S(6)} %select_n.51), kind=kOutput, calls=%fused_computation.22 | convolution fusion | flops 905969664 | bytes 4718596 | tf_op jit(solution)/shard_map/dot_general | solution.py:35
  179.9 2.5 %fusion.41 = bf16[384,768]{1,0:T(8,128)(2,1)S(1)} fusion(f32[384,768]{1,0:T(8,128)S(1)} %fusion.12, bf16[384,1536]{1,0:T(8,128)(2,1)} %collective-permute-done.11, bf16[1536,1536]{1,0:T(8,128)(2,1)S(1)} %copy-done.4, s32[]{:T(128)S(6)} %select_n.51), kind=kOutput, calls=%fused_computation.45 | convolution fusion | flops 906559488 | bytes 5308420 | tf_op jit(solution)/shard_map/dot_general | solution.py:35
  182.4 1.7 collective-permute-start.13
  184.2 1.1 fusion.14
  185.3 2.4 %fusion.44 = bf16[384,768]{1,0:T(8,128)(2,1)S(1)} fusion(f32[384,768]{1,0:T(8,128)S(1)} %fusion.14, bf16[384,1536]{1,0:T(8,128)(2,1)} %get-tuple-element.13, bf16[1536,1536]{1,0:T(8,128)(2,1)S(1)} %copy-done.4, s32[]{:T(128)S(6)} %select_n.51), kind=kOutput, calls=%fused_computation.46 | convolution fusion | flops 906559488 | bytes 5308420 | tf_op jit(solution)/shard_map/dot_general | solution.py:35
  187.7 2.4 %fusion.20 = f32[384,768]{1,0:T(8,128)S(1)} fusion(bf16[384,1536]{1,0:T(8,128)(2,1)} %collective-permute-done.12, bf16[1536,1536]{1,0:T(8,128)(2,1)S(1)} %copy-done.9, s32[]{:T(128)S(6)} %select_n.50), kind=kOutput, calls=%fused_computation.30 | convolution fusion | flops 905969664 | bytes 4718596 | tf_op jit(solution)/shard_map/dot_general | solution.py:35
  190.1 1.1 fusion.22
  193.7 5.0 %collective-permute-done.13 = bf16[384,768]{1,0:T(8,128)(2,1)S(1)} collective-permute-done((bf16[384,768]{1,0:T(8,128)(2,1)S(1)}, bf16[384,768]{1,0:T(8,128)(2,1)S(1)}, u32[]{:S(2)}, u32[]{:S(2)}) %collective-permute-start.13) | collective-permute-done | bytes 589856 | tf_op jit(solution)/shard_map/ppermute | solution.py:20
  198.8 2.4 %fusion.56 = bf16[384,768]{1,0:T(8,128)(2,1)S(1)} fusion(f32[384,768]{1,0:T(8,128)S(1)} %fusion.20, bf16[384,1536]{1,0:T(8,128)(2,1)} %collective-permute-done.11, bf16[1536,1536]{1,0:T(8,128)(2,1)S(1)} %copy-done.4, s32[]{:T(128)S(6)} %select_n.50, bf16[384,768]{1,0:T(8,128)(2,1)S(1)} %collective-permute-done.13), kind=kOutput, calls=%fused_computation.50 | convolution fusion | flops 907739136 | bytes 5898244 | tf_op jit(solution)/shard_map/dot_general | solution.py:35
  201.2 1.7 collective-permute-start.14
  205.0 4.3 %collective-permute-done.10 = bf16[384,768]{1,0:T(8,128)(2,1)S(1)} collective-permute-done((bf16[384,768]{1,0:T(8,128)(2,1)S(1)}, bf16[384,768]{1,0:T(8,128)(2,1)S(1)}, u32[]{:S(2)}, u32[]{:S(2)}) %collective-permute-start.10) | collective-permute-done | bytes 589856 | tf_op jit(solution)/shard_map/ppermute | solution.py:20
  209.3 3.1 %collective-permute-done.14 = bf16[384,768]{1,0:T(8,128)(2,1)S(1)} collective-permute-done((bf16[384,768]{1,0:T(8,128)(2,1)S(1)}, bf16[384,768]{1,0:T(8,128)(2,1)S(1)}, u32[]{:S(2)}, u32[]{:S(2)}) %collective-permute-start.14) | collective-permute-done | bytes 589856 | tf_op jit(solution)/shard_map/ppermute | solution.py:20
  212.4 2.5 %convert_select_fusion.1 = (f32[384,768]{1,0:T(8,128)S(1)}, f32[384,768]{1,0:T(8,128)S(1)}) fusion(bf16[384,768]{1,0:T(8,128)(2,1)S(1)} %collective-permute-done.14, pred[]{:T(512)S(6)} %eq.16, bf16[384,768]{1,0:T(8,128)(2,1)S(1)} %collective-permute-done.10, f32[384,768]{1,0:T(8,128)S(1)} %fusion.22, bf16[384,1536]{1,0:T(8,128)(2,1)} %get-tuple-element.13, ...), kind=kOutput, calls=%fused_computation.39 | convolution fusion | flops 908328960 | bytes 8257541 | tf_op jit(solution)/shard_map/dot_general | solution.py:35
  215.1 1.1 copy-done.3
  216.2 2.4 %fusion.2 = bf16[1,384,1536]{2,1,0:T(8,128)(2,1)} fusion(bf16[640,1536]{1,0:T(8,128)(2,1)S(1)} %constant_dynamic-update-slice_fusion, f32[384,384]{1,0:T(8,128)S(1)} %get-tuple-element.32, f32[384,384]{1,0:T(8,128)S(1)} %get-tuple-element.22, f32[384,384]{1,0:T(8,128)S(1)} %get-tuple-element.33, f32[384,384]{1,0:T(8,128)S(1)} %get-tuple-element.21, ...), kind=kOutput, calls=%fused_computation.12 | convolution fusion | flops 759595008 | bytes 6686592 | tf_op jit(solution)/shard_map/dot_general | solution.py:119
  (57 shorter events, 12.5 us)
Async XLA Ops:
  7.2 1.7 copy-start
  7.2 24.0 %copy-start.7 = (s32[1,512]{1,0:T(1,128)S(1)}, s32[1,512]{1,0:T(1,128)}, u32[]{:S(2)}) copy-start(s32[1,512]{1,0:T(1,128)} %param.13) | copy-start | bytes 6148
  7.2 146.5 %all-gather.3.cloned.1.call-start = ((), (), s32[]{:S(2)}) async-start(), calls=%async_computation | async-start | bytes 5308416 | tf_op jit(solution)/shard_map/all_gather | solution.py:55
  9.7 166.7 %all-gather.5.cloned.1.call-start = ((), (), s32[]{:S(2)}) async-start(), calls=%async_computation.1 | async-start | bytes 5308416 | tf_op jit(solution)/shard_map/all_gather | solution.py:55
  11.7 41.1 %collective-permute-start.4 = (bf16[128,1536]{1,0:T(8,128)(2,1)}, bf16[128,1536]{1,0:T(8,128)(2,1)}, u32[]{:S(2)}, u32[]{:S(2)}) collective-permute-start(bf16[128,1536]{1,0:T(8,128)(2,1)} %bitcast.3), channel_id=1, source_target_pairs={{0,8},{4,12},{1,9},{5,13},{2,10},{6,14},{3,11},{7,15},{16,24},{20,... | collective-permute-start | bytes 1179656 | tf_op jit(solution)/shard_map/ppermute | solution.py:12
  18.4 35.5 %collective-permute-start.5 = (bf16[128,1536]{1,0:T(8,128)(2,1)}, bf16[128,1536]{1,0:T(8,128)(2,1)}, u32[]{:S(2)}, u32[]{:S(2)}) collective-permute-start(bf16[128,1536]{1,0:T(8,128)(2,1)} %bitcast.3), channel_id=1, source_target_pairs={{0,4},{4,8},{8,12},{1,5},{5,9},{9,13},{2,6},{6,10},{10,14},{3,7},{... | collective-permute-start | bytes 1179656 | tf_op jit(solution)/shard_map/ppermute | solution.py:12
  22.7 33.4 %collective-permute-start.6 = (bf16[128,1536]{1,0:T(8,128)(2,1)}, bf16[128,1536]{1,0:T(8,128)(2,1)}, u32[]{:S(2)}, u32[]{:S(2)}) collective-permute-start(bf16[128,1536]{1,0:T(8,128)(2,1)} %bitcast.3), channel_id=1, source_target_pairs={{4,0},{8,4},{12,8},{5,1},{9,5},{13,9},{6,2},{10,6},{14,10},{7,3},{... | collective-permute-start | bytes 1179656 | tf_op jit(solution)/shard_map/ppermute | solution.py:12
  24.0 62.9 %collective-permute-start.7 = (bf16[128,1536]{1,0:T(8,128)(2,1)}, bf16[128,1536]{1,0:T(8,128)(2,1)}, u32[]{:S(2)}, u32[]{:S(2)}) collective-permute-start(bf16[128,1536]{1,0:T(8,128)(2,1)} %bitcast.3), channel_id=1, source_target_pairs={{8,0},{12,4},{9,1},{13,5},{10,2},{14,6},{11,3},{15,7},{24,16},{28,... | collective-permute-start | bytes 1179656 | tf_op jit(solution)/shard_map/ppermute | solution.py:12
  26.6 23.3 %collective-permute-start.8 = (bf16[1,1536]{1,0:T(2,128)(2,1)}, bf16[1,1536]{1,0:T(2,128)(2,1)S(1)}, u32[]{:S(2)}, u32[]{:S(2)}) collective-permute-start(bf16[1,1536]{1,0:T(2,128)(2,1)} %slice_bitcast_fusion.1), channel_id=1, source_target_pairs={{0,4},{4,8},{8,12},{1,5},{5,9},{9,13},{2,6},{6,10},{10,14},{3,7},{... | collective-permute-start | bytes 9224 | tf_op jit(solution)/shard_map/ppermute | solution.py:12
  52.8 35.1 %copy-start.1 = (bf16[1,384,1536]{2,1,0:T(8,128)(2,1)S(1)}, bf16[1,384,1536]{2,1,0:T(8,128)(2,1)}, u32[]{:S(2)}) copy-start(bf16[1,384,1536]{2,1,0:T(8,128)(2,1)} %param.8) | copy-start | bytes 3538948
  96.8 5.3 %copy-start.2 = (bf16[1,384,1536]{2,1,0:T(8,128)(2,1)S(1)}, bf16[1,384,1536]{2,1,0:T(8,128)(2,1)}, u32[]{:S(2)}) copy-start(bf16[1,384,1536]{2,1,0:T(8,128)(2,1)} %param.8) | copy-start | bytes 3538948
  100.8 8.6 %collective-permute-start.9 = (bf16[1,1536]{1,0:T(2,128)(2,1)S(1)}, bf16[1,1536]{1,0:T(2,128)(2,1)S(1)}, u32[]{:S(2)}, u32[]{:S(2)}) collective-permute-start(bf16[1,1536]{1,0:T(2,128)(2,1)S(1)} %slice.65), channel_id=1, source_target_pairs={{4,0},{8,4},{12,8},{5,1},{9,5},{13,9},{6,2},{10,6},{14,10},{7,3},{... | collective-permute-start | bytes 9224 | tf_op jit(solution)/shard_map/ppermute | solution.py:12
  108.1 40.7 %collective-permute-start.15 = (bf16[128,1536]{1,0:T(8,128)(2,1)S(1)}, bf16[128,1536]{1,0:T(8,128)(2,1)S(1)}, u32[]{:S(2)}, u32[]{:S(2)}) collective-permute-start(bf16[128,1536]{1,0:T(8,128)(2,1)S(1)} %get-tuple-element.15), channel_id=1, source_target_pairs={{8,0},{12,4},{9,1},{13,5},{10,2},{14,6},{11,3},{15,7},{24,16},{28,... | collective-permute-start | bytes 1179656 | tf_op jit(solution)/shard_map/ppermute | solution.py:12
  109.5 65.5 %collective-permute-start.12 = (bf16[384,1536]{1,0:T(8,128)(2,1)S(1)}, bf16[384,1536]{1,0:T(8,128)(2,1)}, u32[]{:S(2)}, u32[]{:S(2)}) collective-permute-start(bf16[384,1536]{1,0:T(8,128)(2,1)S(1)} %pad_maximum_fusion.1), channel_id=1, source_target_pairs={{0,16},{16,0},{1,17},{17,1},{2,18},{18,2},{3,19},{19,3},{4,20},{20... | collective-permute-start | bytes 3538952 | tf_op jit(solution)/shard_map/ppermute | solution.py:20
  110.8 40.2 %collective-permute-start.16 = (bf16[128,1536]{1,0:T(8,128)(2,1)}, bf16[128,1536]{1,0:T(8,128)(2,1)}, u32[]{:S(2)}, u32[]{:S(2)}) collective-permute-start(bf16[128,1536]{1,0:T(8,128)(2,1)} %get-tuple-element.18), channel_id=1, source_target_pairs={{4,0},{8,4},{12,8},{5,1},{9,5},{13,9},{6,2},{10,6},{14,10},{7,3},{... | collective-permute-start | bytes 1179656 | tf_op jit(solution)/shard_map/ppermute | solution.py:12
  112.1 39.0 %collective-permute-start.17 = (bf16[128,1536]{1,0:T(8,128)(2,1)}, bf16[128,1536]{1,0:T(8,128)(2,1)}, u32[]{:S(2)}, u32[]{:S(2)}) collective-permute-start(bf16[128,1536]{1,0:T(8,128)(2,1)} %get-tuple-element.17), channel_id=1, source_target_pairs={{0,4},{4,8},{8,12},{1,5},{5,9},{9,13},{2,6},{6,10},{10,14},{3,7},{... | collective-permute-start | bytes 1179656 | tf_op jit(solution)/shard_map/ppermute | solution.py:12
  118.0 33.1 %collective-permute-start.18 = (bf16[128,1536]{1,0:T(8,128)(2,1)}, bf16[128,1536]{1,0:T(8,128)(2,1)}, u32[]{:S(2)}, u32[]{:S(2)}) collective-permute-start(bf16[128,1536]{1,0:T(8,128)(2,1)} %get-tuple-element.16), channel_id=1, source_target_pairs={{0,8},{4,12},{1,9},{5,13},{2,10},{6,14},{3,11},{7,15},{16,24},{20,... | collective-permute-start | bytes 1179656 | tf_op jit(solution)/shard_map/ppermute | solution.py:12
  148.8 0.8 copy-start.6
  149.6 30.2 %collective-permute-start.11 = (bf16[384,1536]{1,0:T(8,128)(2,1)}, bf16[384,1536]{1,0:T(8,128)(2,1)}, u32[]{:S(2)}, u32[]{:S(2)}) collective-permute-start(bf16[384,1536]{1,0:T(8,128)(2,1)} %get-tuple-element.13), channel_id=1, source_target_pairs={{0,16},{16,0},{1,17},{17,1},{2,18},{18,2},{3,19},{19,3},{4,20},{20... | collective-permute-start | bytes 3538952 | tf_op jit(solution)/shard_map/ppermute | solution.py:20
  153.7 37.5 %collective-permute-start = (bf16[128,1536]{1,0:T(8,128)(2,1)}, bf16[128,1536]{1,0:T(8,128)(2,1)}, u32[]{:S(2)}, u32[]{:S(2)}) collective-permute-start(bf16[128,1536]{1,0:T(8,128)(2,1)} %bitcast.37), channel_id=1, source_target_pairs={{0,8},{4,12},{1,9},{5,13},{2,10},{6,14},{3,11},{7,15},{16,24},{20,... | collective-permute-start | bytes 1179656 | tf_op jit(solution)/shard_map/ppermute | solution.py:12
  169.1 23.5 %collective-permute-start.1 = (bf16[128,1536]{1,0:T(8,128)(2,1)}, bf16[128,1536]{1,0:T(8,128)(2,1)}, u32[]{:S(2)}, u32[]{:S(2)}) collective-permute-start(bf16[128,1536]{1,0:T(8,128)(2,1)} %bitcast.38), channel_id=1, source_target_pairs={{0,4},{4,8},{8,12},{1,5},{5,9},{9,13},{2,6},{6,10},{10,14},{3,7},{... | collective-permute-start | bytes 1179656 | tf_op jit(solution)/shard_map/ppermute | solution.py:12
  173.7 29.3 %collective-permute-start.2 = (bf16[128,1536]{1,0:T(8,128)(2,1)}, bf16[128,1536]{1,0:T(8,128)(2,1)}, u32[]{:S(2)}, u32[]{:S(2)}) collective-permute-start(bf16[128,1536]{1,0:T(8,128)(2,1)} %bitcast.39), channel_id=1, source_target_pairs={{4,0},{8,4},{12,8},{5,1},{9,5},{13,9},{6,2},{10,6},{14,10},{7,3},{... | collective-permute-start | bytes 1179656 | tf_op jit(solution)/shard_map/ppermute | solution.py:12
  175.0 29.0 %collective-permute-start.3 = (bf16[128,1536]{1,0:T(8,128)(2,1)}, bf16[128,1536]{1,0:T(8,128)(2,1)}, u32[]{:S(2)}, u32[]{:S(2)}) collective-permute-start(bf16[128,1536]{1,0:T(8,128)(2,1)} %bitcast.40), channel_id=1, source_target_pairs={{8,0},{12,4},{9,1},{13,5},{10,2},{14,6},{11,3},{15,7},{24,16},{28,... | collective-permute-start | bytes 1179656 | tf_op jit(solution)/shard_map/ppermute | solution.py:12
  176.5 3.4 %copy-start.4 = (bf16[1536,1536]{1,0:T(8,128)(2,1)S(1)}, bf16[1536,1536]{1,0:T(8,128)(2,1)}, u32[]{:S(2)}) copy-start(bf16[1536,1536]{1,0:T(8,128)(2,1)} %all-gather.3.cloned.1.call-done) | copy-start | bytes 14155780
  179.8 4.4 %copy-start.9 = (bf16[1536,1536]{1,0:T(8,128)(2,1)S(1)}, bf16[1536,1536]{1,0:T(8,128)(2,1)}, u32[]{:S(2)}) copy-start(bf16[1536,1536]{1,0:T(8,128)(2,1)} %all-gather.5.cloned.1.call-done) | copy-start | bytes 14155780
  182.4 16.3 %collective-permute-start.13 = (bf16[384,768]{1,0:T(8,128)(2,1)S(1)}, bf16[384,768]{1,0:T(8,128)(2,1)S(1)}, u32[]{:S(2)}, u32[]{:S(2)}) collective-permute-start(bf16[384,768]{1,0:T(8,128)(2,1)S(1)} %fusion.41), channel_id=1, source_target_pairs={{0,2},{2,0},{1,3},{3,1},{4,6},{6,4},{5,7},{7,5},{8,10},{10,8},{9,1... | collective-permute-start | bytes 1769480 | tf_op jit(solution)/shard_map/ppermute | solution.py:20
  191.2 18.1 %collective-permute-start.10 = (bf16[384,768]{1,0:T(8,128)(2,1)S(1)}, bf16[384,768]{1,0:T(8,128)(2,1)S(1)}, u32[]{:S(2)}, u32[]{:S(2)}) collective-permute-start(bf16[384,768]{1,0:T(8,128)(2,1)S(1)} %fusion.44), channel_id=1, source_target_pairs={{0,2},{2,0},{1,3},{3,1},{4,6},{6,4},{5,7},{7,5},{8,10},{10,8},{9,1... | collective-permute-start | bytes 1769480 | tf_op jit(solution)/shard_map/ppermute | solution.py:20
  193.7 9.2 %copy-start.5 = (bf16[1,128,1536]{2,1,0:T(8,128)(2,1)S(1)}, bf16[1,128,1536]{2,1,0:T(8,128)(2,1)}, u32[]{:S(2)}) copy-start(bf16[1,128,1536]{2,1,0:T(8,128)(2,1)} %param.12) | copy-start | bytes 1179652
  201.2 11.2 %collective-permute-start.14 = (bf16[384,768]{1,0:T(8,128)(2,1)S(1)}, bf16[384,768]{1,0:T(8,128)(2,1)S(1)}, u32[]{:S(2)}, u32[]{:S(2)}) collective-permute-start(bf16[384,768]{1,0:T(8,128)(2,1)S(1)} %fusion.56), channel_id=1, source_target_pairs={{0,16},{16,0},{1,17},{17,1},{2,18},{18,2},{3,19},{19,3},{4,20},{20... | collective-permute-start | bytes 1769480 | tf_op jit(solution)/shard_map/ppermute | solution.py:20
  214.9 1.3 copy-start.3
  214.9 1.3 copy-start.8
Sparse Core Ops, SparseCore 0:
  9.8 79.3 all-gather.2
  90.8 71.3 all-gather.4

commit v3 on v0

v3 whole, which is shorter than its diff:
```python
import jax
import jax.numpy as jnp
from jax import lax
from jax.sharding import PartitionSpec as P

epsilon = 1e-06


def passed_along(x, axis, by):
    length = lax.axis_size(axis)
    pairs = [(i, i + by) for i in range(length) if 0 <= i + by < length]
    return lax.ppermute(x, axis, pairs)


reach = 2


def swapped(x, axis):
    length = lax.axis_size(axis)
    return lax.ppermute(x, axis, [(i, length - 1 - i) for i in range(length)])


def passed_across(x, by):
    group_count, length = lax.axis_size("groups"), lax.axis_size("seq")
    pairs = [
        (g * length + i, (group_count - 1 - g) * length + i + by)
        for g in range(group_count)
        for i in range(length)
        if 0 <= i + by < length
    ]
    return lax.ppermute(x, ("groups", "seq"), pairs)


def window_of(block):
    right = passed_along(block, "seq", 1)
    left = passed_along(block, "seq", -1)
    far_right = passed_along(right, "seq", 1)
    far_left = passed_along(left, "seq", -1)
    return jnp.concatenate([far_right, right, block, left, far_left], 0)


def after(value, *others):
    return lax.optimization_barrier((value,) + others)[0]


def product(rows, weight):
    return lax.dot_general(
        rows, weight, (((1,), (1,)), ((), ())), preferred_element_type=jnp.float32
    )


def shards(out_grad, queries, keys, main_out, main_in_grad, boundaries, query_weight, key_weight):
    cotangent = out_grad[0]
    query_rows = queries[0]
    key_rows = keys[0]
    bounds_row = boundaries[0]
    row_count = cotangent.shape[0]
    span_rows = main_out.shape[1]
    shard_index = lax.axis_index("seq")
    seq_count = lax.axis_size("seq")
    tensor_count = lax.axis_size("tensor")
    tensor_index = lax.axis_index("tensor")
    group_index = lax.axis_index("groups")
    pipe_index = lax.axis_index("pipe")
    group_rows = query_weight.shape[0] // lax.axis_size("groups")
    half_cols = query_weight.shape[1] // lax.axis_size("pipe")

    def columns(x, index):
        return lax.dynamic_slice_in_dim(x, index * half_cols, half_cols, 1)

    first_rows = group_rows * 2 // 3 // 16 * 16
    cuts = [(0, first_rows), (first_rows, group_rows)]
    own_weights = []
    for low, high in cuts:
        piece = jnp.concatenate(
            [
                lax.dynamic_slice(
                    weight,
                    (group_index * group_rows + low, pipe_index * half_cols),
                    (high - low, half_cols),
                )
                for weight in (query_weight, key_weight)
            ],
            1,
        )
        own_weights.append(lax.all_gather(piece, "seq", axis=0, tiled=True))
    window_out = window_of(main_out[0])
    last_key = passed_along(key_rows[-1:], "seq", 1)
    next_query = passed_along(query_rows[:1], "seq", -1)
    query_other = swapped(query_rows, "groups")
    key_other = swapped(key_rows, "groups")
    last_key_other = passed_across(key_rows[-1:], 1)
    next_query_other = passed_across(query_rows[:1], -1)
    other_weights = [swapped(weight, "pipe") for weight in own_weights]

    positions = shard_index * row_count + jnp.arange(row_count, dtype=jnp.int32)
    span_of = jnp.sum((bounds_row[None, :] <= positions[:, None]).astype(jnp.int32), 1) - 1
    starts = jnp.any(bounds_row[None, :] == positions[:, None], 1)
    place = span_of - (shard_index - reach) * span_rows
    window_rows = window_out.shape[0]
    selector = place[:, None] == jnp.arange(window_rows, dtype=jnp.int32)[None, :]
    upsampled = jnp.dot(selector.astype(jnp.bfloat16), window_out, preferred_element_type=jnp.float32)
    prev_keys = jnp.concatenate([last_key, key_rows[:-1]], 0)
    query_wide = query_rows.astype(jnp.float32)
    prev_wide = prev_keys.astype(jnp.float32)
    cotangent_wide = cotangent.astype(jnp.float32)
    sums = jnp.stack(
        [
            jnp.sum(query_wide * prev_wide, 1),
            jnp.sum(query_wide * query_wide, 1),
            jnp.sum(prev_wide * prev_wide, 1),
            jnp.sum(cotangent_wide * upsampled, 1),
        ]
    )
    if tensor_count == 2:
        sums = sums + swapped(sums, "tensor")
    else:
        sums = lax.psum(sums, "tensor")
    cross_sum, query_sum, key_sum, conf_grad = sums
    query_scale = lax.rsqrt(query_sum + epsilon)
    key_scale = lax.rsqrt(key_sum + epsilon)
    cosine = cross_sum * query_scale * key_scale
    probability = jnp.where(positions == 0, 1.0, 0.5 * (1.0 - cosine))
    confidence = jnp.where(starts, probability, 1.0 - probability)
    sign = jnp.where(starts, 1.0, -1.0)
    cos_grad = jnp.where(positions == 0, 0.0, -0.5 * sign * conf_grad)
    factors = jnp.stack(
        [
            cos_grad * (query_scale * key_scale),
            cos_grad * (cosine * query_scale * query_scale),
            cos_grad * (cosine * key_scale * key_scale),
        ]
    )
    next_factors = passed_along(factors[:, :1], "seq", -1)
    factors_other = swapped(factors, "groups")
    next_factors_other = passed_across(factors[:, :1], -1)

    def grads(queries_here, keys_here, key_before, query_after, here, after_here, index):
        previous = jnp.concatenate([columns(key_before, index), columns(keys_here, index)[:-1]], 0)
        current = columns(queries_here, index)
        following = jnp.concatenate([current[1:], columns(query_after, index)], 0)
        ahead = jnp.concatenate([here[:, 1:], after_here], 1)
        query_grad = here[0][:, None] * previous.astype(jnp.float32)
        query_grad = query_grad - here[1][:, None] * current.astype(jnp.float32)
        key_grad = ahead[0][:, None] * following.astype(jnp.float32)
        key_grad = key_grad - ahead[2][:, None] * columns(keys_here, index).astype(jnp.float32)
        return jnp.concatenate([query_grad.astype(jnp.bfloat16), key_grad.astype(jnp.bfloat16)], 1)

    def both_grads(index):
        own = grads(query_rows, key_rows, last_key, next_query, factors, next_factors, index)
        other = grads(
            query_other,
            key_other,
            last_key_other,
            next_query_other,
            factors_other,
            next_factors_other,
            index,
        )
        return jnp.concatenate([own, other], 0)

    own_side, other_side = both_grads(pipe_index), both_grads(1 - pipe_index)

    conf_high = confidence.astype(jnp.bfloat16)
    conf_low = (confidence - conf_high.astype(jnp.float32)).astype(jnp.bfloat16)
    zero_weight = jnp.zeros((), jnp.bfloat16)
    weight_high = jnp.where(selector, conf_high[:, None], zero_weight)
    weight_low = jnp.where(selector, conf_low[:, None], zero_weight)
    contract = (((0,), (0,)), ((), ()))
    span_terms = lax.dot_general(
        weight_high, cotangent, contract, preferred_element_type=jnp.float32
    )
    span_terms = span_terms + lax.dot_general(
        weight_low, cotangent, contract, preferred_element_type=jnp.float32
    )
    terms = [span_terms[i * span_rows : (i + 1) * span_rows] for i in range(2 * reach + 1)]

    def moved(block, by):
        return passed_along(block.astype(jnp.bfloat16), "seq", by).astype(jnp.float32)

    span_sums = terms[2] + moved(terms[3] + moved(terms[4], 1), 1) + moved(terms[1] + moved(terms[0], -1), -1)
    main_grad = span_sums.astype(jnp.bfloat16)[None]
    grad_block = after(main_in_grad[0], own_weights[0])
    window_grad = window_of(grad_block)
    start_picker = (selector & starts[:, None]).astype(jnp.bfloat16)
    start_grad = jnp.dot(start_picker, window_grad, preferred_element_type=jnp.float32)

    def partial(own_weight, other_weight):
        total = product(own_side, own_weight) + product(other_side, other_weight)
        return total.astype(jnp.bfloat16)

    pieces = []
    for own_weight, other_weight in zip(own_weights, other_weights):
        block_rows = own_weight.shape[0] // tensor_count
        if tensor_count == 2:

            def half(index):
                return [
                    lax.dynamic_slice_in_dim(weight, index * block_rows, block_rows, 0)
                    for weight in (own_weight, other_weight)
                ]

            incoming = swapped(partial(*half(1 - tensor_index)), "tensor").astype(jnp.float32)
            total = partial(*half(tensor_index)).astype(jnp.float32) + incoming
        else:
            total = lax.psum_scatter(
                partial(own_weight, other_weight), "tensor", scatter_dimension=1, tiled=True
            ).astype(jnp.float32)
        own = total[:row_count]
        arrived = swapped(total[row_count:].astype(jnp.bfloat16), "groups").astype(jnp.float32)
        pieces.append(
            [jnp.where(group_index == 0, own, arrived), jnp.where(group_index == 0, arrived, own)]
        )
    widths = [high - low for low, high in cuts]
    routing = jnp.concatenate(
        [
            piece[group][:, s * width : (s + 1) * width]
            for s in range(seq_count // tensor_count)
            for group in range(2)
            for piece, width in zip(pieces, widths)
        ],
        1,
    )
    byte_grad = (cotangent_wide + start_grad + routing).astype(jnp.bfloat16)[None]
    return (byte_grad, main_grad)


def solution(mesh):
    return jax.shard_map(
        shards,
        mesh=mesh,
        in_specs=(
            P(("groups", "pipe"), "seq", "tensor"),
            P(("groups", "pipe"), "seq", "tensor"),
            P(("groups", "pipe"), "seq", "tensor"),
            P(("groups", "pipe"), "seq", "tensor"),
            P(("groups", "pipe"), "seq", "tensor"),
            P(("groups", "pipe"), None),
            P("seq", "tensor"),
            P("seq", "tensor"),
        ),
        out_specs=(P(("groups", "pipe"), "seq", "tensor"), P(("groups", "pipe"), "seq", "tensor")),
        check_vma=False,
    )
```

time: 480 us -> 210 us (0.44)
  waiting for transfers between devices: 372 us -> 74.6 us
  starting transfers between devices: 11.5 us -> 57.9 us
  local copies, waits for them, and re-layouts: 34.5 us -> 22.4 us
  matrix products: 29.4 us -> 19.3 us
  other arithmetic: 12 us -> 19.5 us
  blocking collectives: 5.69 us -> 0 us
    all_gather x4 -> x2, waiting for transfers between devices: 340 us -> 19.8 us  [shards(): own_weights.append(lax.all_gather(piece, 'seq', axis=0, tiled=True))]
    ppermute x0 -> x13, waiting for transfers between devices: none -> 36.2 us  [the longest x10 36.2 us: swapped(): return lax.ppermute(x, axis, [(i, length - 1 - i) for i in range(length)])]
    ppermute x2 -> x15, starting transfers between devices: 6.79 us -> 40.6 us  [passed_along(): return lax.ppermute(x, axis, pairs)]
    gather x11 -> x0, local copies, waits for them, and re-layouts: 31.9 us -> none  [the longest x10 28 us: shards(): span_of = jnp.searchsorted(bounds_row, positions, side='right') - 1]
    ppermute x2 -> x15, waiting for transfers between devices: 0.01 us -> 18.5 us  [passed_along(): return lax.ppermute(x, axis, pairs)]
    ppermute x0 -> x13, starting transfers between devices: none -> 17.2 us  [the longest x10 10.4 us: swapped(): return lax.ppermute(x, axis, [(i, length - 1 - i) for i in range(length)])]
    all_to_all x1 -> x0, waiting for transfers between devices: 15.9 us -> none  [shards(): lax.all_to_all(span_terms.reshape(seq_count, span_rows, span_terms.shape[...]
    reduce_scatter x1 -> x0, waiting for transfers between devices: 14.4 us -> none  [shards(): lax.psum_scatter(partial_value.astype(jnp.bfloat16), 'tensor', scatter_di...]
  transfers between devices with their start and end apart: 8 -> 30, of which waited for: 5 -> 12; matrix products, arithmetic and copies ran while one was open for 15% -> 26% of each run, Pallas kernels for 0% -> 0%
where the time goes in v3:
time: 210 us; the launch traced here: 208 us
  waiting for transfers between devices  74.6 us (36%)
  starting transfers between devices  57.9 us (28%)
  local copies, waits for them, and re-layouts  22.4 us (11%)
  other arithmetic  19.5 us (9%)
  matrix products  19.3 us (9%)
  between operations  14.7 us (7%)
    ppermute x15, starting transfers between devices, passed_along(): return lax.ppermute(x, axis, pairs)  40.6 us
    ppermute x10, waiting for transfers between devices, swapped(): return lax.ppermute(x, axis, [(i, length - 1 - i) for i in range(length)])  36.2 us
    all_gather x2, waiting for transfers between devices, shards(): own_weights.append(lax.all_gather(piece, 'seq', axis=0, tiled=True))  19.8 us
    ppermute x15, waiting for transfers between devices, passed_along(): return lax.ppermute(x, axis, pairs)  18.5 us
    dot_general x8, matrix products, product(): lax.dot_general(rows, weight, (((1,), (1,)), ((), ())), preferred_element...  11.3 us
    ppermute x10, starting transfers between devices, swapped(): return lax.ppermute(x, axis, [(i, length - 1 - i) for i in range(length)])  10.4 us
    ppermute x3, starting transfers between devices, passed_across(): return lax.ppermute(x, ('groups', 'seq'), pairs)  6.84 us
    convert_element_type x2, other arithmetic, grads(): key_grad.astype(jnp.bfloat16)  5.51 us
  transfers between devices with their start and end apart: 30, of which 12 were waited for; matrix products, arithmetic and copies ran while one was open for 26% of the time, Pallas kernels for 0%

profile of v3, /device:TPU:0, one launch (start us, length us, event | category | flops | bytes accessed | tf_op | source)
XLA Modules:
  0.0 208.4 jit_solution(15118100395618475811)
XLA Ops:
  10.1 5.7 %collective-permute-start.5 = (bf16[128,1536]{1,0:T(8,128)(2,1)}, bf16[128,1536]{1,0:T(8,128)(2,1)}, u32[]{:S(2)}, u32[]{:S(2)}) collective-permute-start(bf16[128,1536]{1,0:T(8,128)(2,1)} %bitcast.6), channel_id=1, source_target_pairs={{0,4},{4,8},{8,12},{1,5},{5,9},{9,13},{2,6},{6,10},{10,14},{3,7},{... | collective-permute-start | bytes 1179656 | tf_op jit(solution)/shard_map/ppermute | solution.py:12
  17.1 1.3 slice_bitcast_fusion.2
  18.4 4.5 %collective-permute-start.4 = (bf16[1,1536]{1,0:T(2,128)(2,1)}, bf16[1,1536]{1,0:T(2,128)(2,1)S(1)}, u32[]{:S(2)}, u32[]{:S(2)}) collective-permute-start(bf16[1,1536]{1,0:T(2,128)(2,1)} %slice_bitcast_fusion.2), channel_id=1, source_target_pairs={{0,4},{4,8},{8,12},{1,5},{5,9},{9,13},{2,6},{6,10},{10,14},{3,7},{... | collective-permute-start | bytes 9224 | tf_op jit(solution)/shard_map/ppermute | solution.py:12
  23.0 4.3 %collective-permute-start.13 = (bf16[1,1536]{1,0:T(2,128)(2,1)}, bf16[1,1536]{1,0:T(2,128)(2,1)}, u32[]{:S(2)}, u32[]{:S(2)}) collective-permute-start(bf16[1,1536]{1,0:T(2,128)(2,1)} %slice_bitcast_fusion.2), channel_id=1, source_target_pairs={{0,20},{4,24},{8,28},{16,4},{20,8},{24,12},{1,21},{5,25},{9,29},{1... | collective-permute-start | bytes 9224 | tf_op jit(solution)/shard_map/ppermute | solution.py:31
  36.9 1.7 dynamic-slice_bitcast_fusion
  38.6 1.3 collective-permute-start.17
  39.9 5.2 %collective-permute-start.6 = (bf16[128,1536]{1,0:T(8,128)(2,1)}, bf16[128,1536]{1,0:T(8,128)(2,1)S(1)}, u32[]{:S(2)}, u32[]{:S(2)}) collective-permute-start(bf16[128,1536]{1,0:T(8,128)(2,1)} %collective-permute-done.5), channel_id=1, source_target_pairs={{0,4},{4,8},{8,12},{1,5},{5,9},{9,13},{2,6},{6,10},{10,14},{3,7},{... | collective-permute-start | bytes 1179656 | tf_op jit(solution)/shard_map/ppermute | solution.py:12
  50.9 1.4 collective-permute-start.8
  52.3 5.6 %collective-permute-done.6 = bf16[128,1536]{1,0:T(8,128)(2,1)S(1)} collective-permute-done((bf16[128,1536]{1,0:T(8,128)(2,1)}, bf16[128,1536]{1,0:T(8,128)(2,1)S(1)}, u32[]{:S(2)}, u32[]{:S(2)}) %collective-permute-start.6) | collective-permute-done | bytes 393248 | tf_op jit(solution)/shard_map/ppermute | solution.py:12
  61.0 1.4 collective-permute-done.8
  63.7 1.6 collective-permute-start.9
  65.9 1.5 collective-permute-done.9
  68.6 1.3 fusion.34
  70.0 3.3 %fusion.84 = (bf16[640,1536]{1,0:T(8,128)(2,1)S(1)}, f32[640,1536]{1,0:T(8,128)}) fusion(f32[640,1536]{1,0:T(8,128)S(1)} %fusion.34, bf16[1,384,1536]{2,1,0:T(8,128)(2,1)S(1)} %copy-done.3, s32[384]{0:T(512)S(1)} %add_subtract_fusion, bf16[384]{0:T(512)(128)(2,1)S(1)} %get-tuple-element.17), kind=kOutput, calls=%fused_computation.173 | convolution fusion | flops 757432320 | bytes 11012352 | tf_op jit(solution)/shard_map/dot_general | solution.py:173
  75.7 1.5 collective-permute-start.12
  78.5 3.0 %fusion.28 = (bf16[384,768]{1,0:T(8,128)(2,1)}, bf16[384,768]{1,0:T(8,128)(2,1)}) fusion(bf16[383,768]{1,0:T(8,128)(2,1)} %get-tuple-element.35, bf16[1,768]{1,0:T(2,128)(2,1)} %get-tuple-element.50, bf16[1,384,1536]{2,1,0:T(8,128)(2,1)S(1)} %copy-done, s32[]{:T(128)S(6)} %select_n.148, f32[384]{0:T(512)} %get-tuple-element.48, f32[384]{0:T(512)} %get-tuple-element.49, ...), kind=kLoop, calls=%fused_computation.38 | loop fusion | flops 5308416 | bytes 3542024 | tf_op jit(solution)/shard_map/convert_element_type | solution.py:147
  81.5 1.4 collective-permute-done.10
  84.3 2.3 %fusion.26 = (bf16[384,768]{1,0:T(8,128)(2,1)}, bf16[384,768]{1,0:T(8,128)(2,1)}) fusion(bf16[1,768]{1,0:T(2,128)(2,1)} %get-tuple-element.52, bf16[383,768]{1,0:T(8,128)(2,1)S(1)} %copy-done.4, bf16[1,384,1536]{2,1,0:T(8,128)(2,1)S(1)} %copy-done.1, s32[]{:T(128)S(6)} %select_n.148, f32[384]{0:T(512)S(1)} %get-tuple-element.8, f32[384]{0:T(512)S(1)} %get-tuple-element.7, ...), kind=kLoop, calls=%fused_computation.35 | loop fusion | flops 5308416 | bytes 3542024 | tf_op jit(solution)/shard_map/convert_element_type | solution.py:147
  86.5 11.8 %collective-permute-done.12 = f32[3,384]{1,0:T(4,128)S(1)} collective-permute-done((f32[3,384]{1,0:T(4,128)S(1)}, f32[3,384]{1,0:T(4,128)S(1)}, u32[]{:S(2)}, u32[]{:S(2)}) %collective-permute-start.12) | collective-permute-done | bytes 4640 | tf_op jit(solution)/shard_map/ppermute | solution.py:20
  98.3 4.4 %collective-permute-start.24 = (bf16[128,1536]{1,0:T(8,128)(2,1)}, bf16[128,1536]{1,0:T(8,128)(2,1)}, u32[]{:S(2)}, u32[]{:S(2)}) collective-permute-start(bf16[128,1536]{1,0:T(8,128)(2,1)} %get-tuple-element.23), channel_id=1, source_target_pairs={{0,4},{4,8},{8,12},{1,5},{5,9},{9,13},{2,6},{6,10},{10,14},{3,7},{... | collective-permute-start | bytes 1179656 | tf_op jit(solution)/shard_map/ppermute | solution.py:12
  102.8 1.5 collective-permute-start.26
  105.5 1.9 fusion.83
  107.3 1.3 constant_dynamic-slice_fusion
  108.7 19.8 %all-gather.3.cloned.1.call-done = bf16[1024,1536]{1,0:T(8,128)(2,1)} async-done(((bf16[256,1536]{1,0:T(8,128)(2,1)}), bf16[1024,1536]{1,0:T(8,128)(2,1)}) %all-gather.3.cloned.1.call-update) | async-done | bytes 3145744 | tf_op jit(solution)/shard_map/all_gather | solution.py:86
  128.4 3.2 %subtract_convert_fusion = (bf16[384,768]{1,0:T(8,128)(2,1)S(1)}, bf16[384,768]{1,0:T(8,128)(2,1)S(1)}, bf16[384,768]{1,0:T(8,128)(2,1)S(1)}, bf16[384,768]{1,0:T(8,128)(2,1)S(1)}) fusion(bf16[1,768]{1,0:T(2,128)(2,1)S(1)} %get-tuple-element.56, bf16[383,768]{1,0:T(8,128)(2,1)S(1)} %get-tuple-element.41, bf16[384,1536]{1,0:T(8,128)(2,1)} %collective-permute-done.14, ...), kind=kLoop, calls=%fused_computation.48 | loop fusion | flops 10616832 | bytes 7084040 | tf_op jit(solution)/shard_map/convert_element_type | solution.py:147
  133.0 2.1 %fusion.24 = bf16[768,256]{1,0:T(8,128)(2,1)S(1)} fusion(f32[768,256]{1,0:T(8,128)S(1)} %fusion.45, bf16[512,1536]{1,0:T(8,128)(2,1)} %collective-permute-done.21, s32[]{:T(128)S(6)} %select_n.154, bf16[384,768]{1,0:T(8,128)(2,1)S(1)} %get-tuple-element.33, bf16[384,768]{1,0:T(8,128)(2,1)S(1)} %get-tuple-element.63, bf16[384,768]{1,0:T(8,128)(2,1)S(1)} %copy-done.7, ...), kind=kOutput, calls=%fused_computation.31 | convolution fusion | flops 613810176 | bytes 4325380 | tf_op jit(solution)/shard_map/dot_general | solution.py:47
  135.1 1.5 collective-permute-start.22
  136.6 1.3 fusion.41
  138.0 2.1 %collective-permute-start.25 = (bf16[128,1536]{1,0:T(8,128)(2,1)S(1)}, bf16[128,1536]{1,0:T(8,128)(2,1)S(1)}, u32[]{:S(2)}, u32[]{:S(2)}) collective-permute-start(bf16[128,1536]{1,0:T(8,128)(2,1)S(1)} %get-tuple-element.21), channel_id=1, source_target_pairs={{0,4},{4,8},{8,12},{1,5},{5,9},{9,13},{2,6},{6,10},{10,14},{3,7},{... | collective-permute-start | bytes 1179656 | tf_op jit(solution)/shard_map/ppermute | solution.py:12
  140.1 1.3 collective-permute-start.27
  142.2 4.4 %collective-permute-done.22 = bf16[768,256]{1,0:T(8,128)(2,1)S(1)} collective-permute-done((bf16[768,256]{1,0:T(8,128)(2,1)S(1)}, bf16[768,256]{1,0:T(8,128)(2,1)S(1)}, u32[]{:S(2)}, u32[]{:S(2)}) %collective-permute-start.22) | collective-permute-done | bytes 393248 | tf_op jit(solution)/shard_map/ppermute | solution.py:20
  146.6 1.9 fusion.23
  148.6 1.5 collective-permute-start.23
  150.1 3.5 %collective-permute-done.27 = bf16[128,1536]{1,0:T(8,128)(2,1)S(1)} collective-permute-done((bf16[128,1536]{1,0:T(8,128)(2,1)S(1)}, bf16[128,1536]{1,0:T(8,128)(2,1)S(1)}, u32[]{:S(2)}, u32[]{:S(2)}) %collective-permute-start.27) | collective-permute-done | bytes 393248 | tf_op jit(solution)/shard_map/ppermute | solution.py:12
  154.5 3.7 %collective-permute-start = (bf16[128,1536]{1,0:T(8,128)(2,1)S(1)}, bf16[128,1536]{1,0:T(8,128)(2,1)S(1)}, u32[]{:S(2)}, u32[]{:S(2)}) collective-permute-start(bf16[128,1536]{1,0:T(8,128)(2,1)S(1)} %bitcast.51), channel_id=1, source_target_pairs={{0,4},{4,8},{8,12},{1,5},{5,9},{9,13},{2,6},{6,10},{10,14},{3,7},{... | collective-permute-start | bytes 1179656 | tf_op jit(solution)/shard_map/ppermute | solution.py:12
  158.3 1.3 collective-permute-start.2
  159.6 1.4 fusion.8
  161.0 4.7 %collective-permute-done = bf16[128,1536]{1,0:T(8,128)(2,1)S(1)} collective-permute-done((bf16[128,1536]{1,0:T(8,128)(2,1)S(1)}, bf16[128,1536]{1,0:T(8,128)(2,1)S(1)}, u32[]{:S(2)}, u32[]{:S(2)}) %collective-permute-start) | collective-permute-done | bytes 393248 | tf_op jit(solution)/shard_map/ppermute | solution.py:12
  165.8 4.4 %collective-permute-start.1 = (bf16[128,1536]{1,0:T(8,128)(2,1)S(1)}, bf16[128,1536]{1,0:T(8,128)(2,1)S(1)}, u32[]{:S(2)}, u32[]{:S(2)}) collective-permute-start(bf16[128,1536]{1,0:T(8,128)(2,1)S(1)} %collective-permute-done), channel_id=1, source_target_pairs={{0,4},{4,8},{8,12},{1,5},{5,9},{9,13},{2,6},{6,10},{10,14},{3,7},{... | collective-permute-start | bytes 1179656 | tf_op jit(solution)/shard_map/ppermute | solution.py:12
  170.2 1.4 add_convert_fusion
  172.2 1.4 fusion.12
  173.6 1.3 collective-permute-start.3
  174.9 1.9 collective-permute-done.1
  176.9 12.1 %collective-permute-done.19 = bf16[768,512]{1,0:T(8,128)(2,1)S(1)} collective-permute-done((bf16[768,512]{1,0:T(8,128)(2,1)S(1)}, bf16[768,512]{1,0:T(8,128)(2,1)S(1)}, u32[]{:S(2)}, u32[]{:S(2)}) %collective-permute-start.19) | collective-permute-done | bytes 786464 | tf_op jit(solution)/shard_map/ppermute | solution.py:20
  189.0 1.4 convert_add_fusion
  190.5 1.5 collective-permute-start.20
  192.0 6.5 %collective-permute-done.20 = bf16[384,512]{1,0:T(8,128)(2,1)S(1)} collective-permute-done((bf16[384,512]{1,0:T(8,128)(2,1)S(1)}, bf16[384,512]{1,0:T(8,128)(2,1)S(1)}, u32[]{:S(2)}, u32[]{:S(2)}) %collective-permute-start.20) | collective-permute-done | bytes 393248 | tf_op jit(solution)/shard_map/ppermute | solution.py:20
  199.4 2.2 %fusion.2 = bf16[1,384,1536]{2,1,0:T(8,128)(2,1)} fusion(f32[384,1536]{1,0:T(8,128)S(1)} %slice_dynamic-update-slice_fusion.4, bf16[640,1536]{1,0:T(8,128)(2,1)S(1)} %constant_dynamic-update-slice_fusion, bf16[1,384,1536]{2,1,0:T(8,128)(2,1)S(1)} %copy-done.3, s32[384]{0:T(512)S(1)} %add_subtract_fusion, pred[384]{0:T(512)(128)(4,1)S(1)} %copy-done.15), kind=kOutput, calls=%fused_computation.8 | convolution fusion | flops 757825536 | bytes 6686592 | tf_op jit(solution)/shard_map/dot_general | solution.py:186
  (130 shorter events, 36.7 us)
Async XLA Ops:
  7.2 20.1 %copy-start = (bf16[1,384,1536]{2,1,0:T(8,128)(2,1)S(1)}, bf16[1,384,1536]{2,1,0:T(8,128)(2,1)}, u32[]{:S(2)}) copy-start(bf16[1,384,1536]{2,1,0:T(8,128)(2,1)} %param.9) | copy-start | bytes 3538948
  7.2 67.6 %all-gather.5.cloned.1.call-start = ((), (), s32[]{:S(2)}) async-start(), calls=%async_computation.1 | async-start | bytes 1966080 | tf_op jit(solution)/shard_map/all_gather | solution.py:86
  10.0 118.4 %all-gather.3.cloned.1.call-start = ((), (), s32[]{:S(2)}) async-start(), calls=%async_computation | async-start | bytes 3932160 | tf_op jit(solution)/shard_map/all_gather | solution.py:86
  10.1 29.8 %collective-permute-start.5 = (bf16[128,1536]{1,0:T(8,128)(2,1)}, bf16[128,1536]{1,0:T(8,128)(2,1)}, u32[]{:S(2)}, u32[]{:S(2)}) collective-permute-start(bf16[128,1536]{1,0:T(8,128)(2,1)} %bitcast.6), channel_id=1, source_target_pairs={{0,4},{4,8},{8,12},{1,5},{5,9},{9,13},{2,6},{6,10},{10,14},{3,7},{... | collective-permute-start | bytes 1179656 | tf_op jit(solution)/shard_map/ppermute | solution.py:12
  15.8 35.1 %collective-permute-start.7 = (bf16[128,1536]{1,0:T(8,128)(2,1)}, bf16[128,1536]{1,0:T(8,128)(2,1)}, u32[]{:S(2)}, u32[]{:S(2)}) collective-permute-start(bf16[128,1536]{1,0:T(8,128)(2,1)} %bitcast.6), channel_id=1, source_target_pairs={{4,0},{8,4},{12,8},{5,1},{9,5},{13,9},{6,2},{10,6},{14,10},{7,3},{... | collective-permute-start | bytes 1179656 | tf_op jit(solution)/shard_map/ppermute | solution.py:12
  18.4 20.2 %collective-permute-start.4 = (bf16[1,1536]{1,0:T(2,128)(2,1)}, bf16[1,1536]{1,0:T(2,128)(2,1)S(1)}, u32[]{:S(2)}, u32[]{:S(2)}) collective-permute-start(bf16[1,1536]{1,0:T(2,128)(2,1)} %slice_bitcast_fusion.2), channel_id=1, source_target_pairs={{0,4},{4,8},{8,12},{1,5},{5,9},{9,13},{2,6},{6,10},{10,14},{3,7},{... | collective-permute-start | bytes 9224 | tf_op jit(solution)/shard_map/ppermute | solution.py:12
  23.0 26.0 %collective-permute-start.13 = (bf16[1,1536]{1,0:T(2,128)(2,1)}, bf16[1,1536]{1,0:T(2,128)(2,1)}, u32[]{:S(2)}, u32[]{:S(2)}) collective-permute-start(bf16[1,1536]{1,0:T(2,128)(2,1)} %slice_bitcast_fusion.2), channel_id=1, source_target_pairs={{0,20},{4,24},{8,28},{16,4},{20,8},{24,12},{1,21},{5,25},{9,29},{1... | collective-permute-start | bytes 9224 | tf_op jit(solution)/shard_map/ppermute | solution.py:31
  27.8 19.0 %collective-permute-start.11 = (bf16[1,1536]{1,0:T(2,128)(2,1)}, bf16[1,1536]{1,0:T(2,128)(2,1)}, u32[]{:S(2)}, u32[]{:S(2)}) collective-permute-start(bf16[1,1536]{1,0:T(2,128)(2,1)} %slice_bitcast_fusion.1), channel_id=1, source_target_pairs={{4,0},{8,4},{12,8},{5,1},{9,5},{13,9},{6,2},{10,6},{14,10},{7,3},{... | collective-permute-start | bytes 9224 | tf_op jit(solution)/shard_map/ppermute | solution.py:12
  29.1 3.1 %copy-start.1 = (bf16[1,384,1536]{2,1,0:T(8,128)(2,1)S(1)}, bf16[1,384,1536]{2,1,0:T(8,128)(2,1)}, u32[]{:S(2)}) copy-start(bf16[1,384,1536]{2,1,0:T(8,128)(2,1)} %param.10) | copy-start | bytes 3538948
  32.2 0.7 copy-start.12
  33.1 0.5 copy-start.13
  38.6 26.7 %collective-permute-start.17 = (bf16[1,1536]{1,0:T(2,128)(2,1)}, bf16[1,1536]{1,0:T(2,128)(2,1)S(1)}, u32[]{:S(2)}, u32[]{:S(2)}) collective-permute-start(bf16[1,1536]{1,0:T(2,128)(2,1)} %slice_bitcast_fusion.1), channel_id=1, source_target_pairs={{4,16},{8,20},{12,24},{20,0},{24,4},{28,8},{5,17},{9,21},{13,25},{... | collective-permute-start | bytes 9224 | tf_op jit(solution)/shard_map/ppermute | solution.py:31
  39.9 18.1 %collective-permute-start.6 = (bf16[128,1536]{1,0:T(8,128)(2,1)}, bf16[128,1536]{1,0:T(8,128)(2,1)S(1)}, u32[]{:S(2)}, u32[]{:S(2)}) collective-permute-start(bf16[128,1536]{1,0:T(8,128)(2,1)} %collective-permute-done.5), channel_id=1, source_target_pairs={{0,4},{4,8},{8,12},{1,5},{5,9},{9,13},{2,6},{6,10},{10,14},{3,7},{... | collective-permute-start | bytes 1179656 | tf_op jit(solution)/shard_map/ppermute | solution.py:12
  46.8 58.7 %collective-permute-start.15 = (bf16[384,1536]{1,0:T(8,128)(2,1)S(1)}, bf16[384,1536]{1,0:T(8,128)(2,1)}, u32[]{:S(2)}, u32[]{:S(2)}) collective-permute-start(bf16[384,1536]{1,0:T(8,128)(2,1)S(1)} %bitcast.49), channel_id=1, source_target_pairs={{0,16},{16,0},{1,17},{17,1},{2,18},{18,2},{3,19},{19,3},{4,20},{20... | collective-permute-start | bytes 3538952 | tf_op jit(solution)/shard_map/ppermute | solution.py:20
  48.9 58.4 %collective-permute-start.14 = (bf16[384,1536]{1,0:T(8,128)(2,1)S(1)}, bf16[384,1536]{1,0:T(8,128)(2,1)}, u32[]{:S(2)}, u32[]{:S(2)}) collective-permute-start(bf16[384,1536]{1,0:T(8,128)(2,1)S(1)} %bitcast.50), channel_id=1, source_target_pairs={{0,16},{16,0},{1,17},{17,1},{2,18},{18,2},{3,19},{19,3},{4,20},{20... | collective-permute-start | bytes 3538952 | tf_op jit(solution)/shard_map/ppermute | solution.py:20
  50.9 11.6 %copy-start.3 = (bf16[1,384,1536]{2,1,0:T(8,128)(2,1)S(1)}, bf16[1,384,1536]{2,1,0:T(8,128)(2,1)}, u32[]{:S(2)}) copy-start(bf16[1,384,1536]{2,1,0:T(8,128)(2,1)} %param.8) | copy-start | bytes 3538948
  50.9 11.5 %collective-permute-start.8 = (bf16[128,1536]{1,0:T(8,128)(2,1)}, bf16[128,1536]{1,0:T(8,128)(2,1)S(1)}, u32[]{:S(2)}, u32[]{:S(2)}) collective-permute-start(bf16[128,1536]{1,0:T(8,128)(2,1)} %collective-permute-done.7), channel_id=1, source_target_pairs={{4,0},{8,4},{12,8},{5,1},{9,5},{13,9},{6,2},{10,6},{14,10},{7,3},{... | collective-permute-start | bytes 1179656 | tf_op jit(solution)/shard_map/ppermute | solution.py:12
  62.4 5.0 %copy-start.11 = (f32[384]{0:T(512)S(1)}, f32[384]{0:T(512)}, u32[]{:S(2)}) copy-start(f32[384]{0:T(512)} %select_multiply_fusion) | copy-start | bytes 4612
  62.5 5.6 %copy-start.14 = (pred[384]{0:T(512)(128)(4,1)S(1)}, pred[384]{0:T(512)(128)(4,1)}, u32[]{:S(2)}) copy-start(pred[384]{0:T(512)(128)(4,1)} %copy-done.13) | copy-start | bytes 1156
  63.7 3.7 %collective-permute-start.9 = (f32[4,384]{1,0:T(4,128)S(1)}, f32[4,384]{1,0:T(4,128)S(1)}, u32[]{:S(2)}, u32[]{:S(2)}) collective-permute-start(f32[4,384]{1,0:T(4,128)S(1)} %pad_maximum_fusion.3), channel_id=1, source_target_pairs={{0,2},{2,0},{1,3},{3,1},{4,6},{6,4},{5,7},{7,5},{8,10},{10,8},{9,1... | collective-permute-start | bytes 18440 | tf_op jit(solution)/shard_map/ppermute | solution.py:20
  74.8 9.5 %copy-start.4 = (bf16[383,768]{1,0:T(8,128)(2,1)S(1)}, bf16[383,768]{1,0:T(8,128)(2,1)}, u32[]{:S(2)}) copy-start(bf16[383,768]{1,0:T(8,128)(2,1)} %get-tuple-element.37) | copy-start | bytes 1764868
  74.8 9.5 %copy-start.5 = (bf16[383,768]{1,0:T(8,128)(2,1)S(1)}, bf16[383,768]{1,0:T(8,128)(2,1)}, u32[]{:S(2)}) copy-start(bf16[383,768]{1,0:T(8,128)(2,1)} %get-tuple-element.38) | copy-start | bytes 1764868
  74.8 57.8 %collective-permute-start.21 = (bf16[512,1536]{1,0:T(8,128)(2,1)}, bf16[512,1536]{1,0:T(8,128)(2,1)}, u32[]{:S(2)}, u32[]{:S(2)}) collective-permute-start(bf16[512,1536]{1,0:T(8,128)(2,1)} %all-gather.5.cloned.1.call-done), channel_id=1, source_target_pairs={{0,1},{1,0},{2,3},{3,2},{4,5},{5,4},{6,7},{7,6},{8,9},{9,8},{10,11... | collective-permute-start | bytes 4718600 | tf_op jit(solution)/shard_map/ppermute | solution.py:20
  75.7 22.6 %collective-permute-start.12 = (f32[3,384]{1,0:T(4,128)S(1)}, f32[3,384]{1,0:T(4,128)S(1)}, u32[]{:S(2)}, u32[]{:S(2)}) collective-permute-start(f32[3,384]{1,0:T(4,128)S(1)} %pad_maximum_fusion.4), channel_id=1, source_target_pairs={{0,16},{16,0},{1,17},{17,1},{2,18},{18,2},{3,19},{19,3},{4,20},{20... | collective-permute-start | bytes 13832 | tf_op jit(solution)/shard_map/ppermute | solution.py:20
  77.2 5.6 %collective-permute-start.10 = (f32[3,1]{1,0:T(4,128)S(1)}, f32[3,1]{1,0:T(4,128)S(1)}, u32[]{:S(2)}, u32[]{:S(2)}) collective-permute-start(f32[3,1]{1,0:T(4,128)S(1)} %slice.192), channel_id=1, source_target_pairs={{4,0},{8,4},{12,8},{5,1},{9,5},{13,9},{6,2},{10,6},{14,10},{7,3},{... | collective-permute-start | bytes 44 | tf_op jit(solution)/shard_map/ppermute | solution.py:12
  82.9 19.9 %collective-permute-start.16 = (f32[3,1]{1,0:T(4,128)S(1)}, f32[3,1]{1,0:T(4,128)S(1)}, u32[]{:S(2)}, u32[]{:S(2)}) collective-permute-start(f32[3,1]{1,0:T(4,128)S(1)} %slice.192), channel_id=1, source_target_pairs={{4,16},{8,20},{12,24},{20,0},{24,4},{28,8},{5,17},{9,21},{13,25},{... | collective-permute-start | bytes 44 | tf_op jit(solution)/shard_map/ppermute | solution.py:31
  98.3 38.3 %collective-permute-start.24 = (bf16[128,1536]{1,0:T(8,128)(2,1)}, bf16[128,1536]{1,0:T(8,128)(2,1)}, u32[]{:S(2)}, u32[]{:S(2)}) collective-permute-start(bf16[128,1536]{1,0:T(8,128)(2,1)} %get-tuple-element.23), channel_id=1, source_target_pairs={{0,4},{4,8},{8,12},{1,5},{5,9},{9,13},{2,6},{6,10},{10,14},{3,7},{... | collective-permute-start | bytes 1179656 | tf_op jit(solution)/shard_map/ppermute | solution.py:12
  102.8 33.9 %collective-permute-start.26 = (bf16[128,1536]{1,0:T(8,128)(2,1)}, bf16[128,1536]{1,0:T(8,128)(2,1)}, u32[]{:S(2)}, u32[]{:S(2)}) collective-permute-start(bf16[128,1536]{1,0:T(8,128)(2,1)} %get-tuple-element.24), channel_id=1, source_target_pairs={{4,0},{8,4},{12,8},{5,1},{9,5},{13,9},{6,2},{10,6},{14,10},{7,3},{... | collective-permute-start | bytes 1179656 | tf_op jit(solution)/shard_map/ppermute | solution.py:12
  128.4 41.7 %collective-permute-start.18 = (bf16[1024,1536]{1,0:T(8,128)(2,1)}, bf16[1024,1536]{1,0:T(8,128)(2,1)S(1)}, u32[]{:S(2)}, u32[]{:S(2)}) collective-permute-start(bf16[1024,1536]{1,0:T(8,128)(2,1)} %all-gather.3.cloned.1.call-done), channel_id=1, source_target_pairs={{0,1},{1,0},{2,3},{3,2},{4,5},{5,4},{6,7},{7,6},{8,9},{9,8},{10,11... | collective-permute-start | bytes 9437192 | tf_op jit(solution)/shard_map/ppermute | solution.py:20
  128.4 3.3 %copy-start.8 = (bf16[384,768]{1,0:T(8,128)(2,1)S(1)}, bf16[384,768]{1,0:T(8,128)(2,1)}, u32[]{:S(2)}) copy-start(bf16[384,768]{1,0:T(8,128)(2,1)} %get-tuple-element.28) | copy-start | bytes 1769476
  128.4 3.3 %copy-start.9 = (bf16[384,768]{1,0:T(8,128)(2,1)S(1)}, bf16[384,768]{1,0:T(8,128)(2,1)}, u32[]{:S(2)}) copy-start(bf16[384,768]{1,0:T(8,128)(2,1)} %get-tuple-element.30) | copy-start | bytes 1769476
  128.4 3.3 %copy-start.17 = (bf16[512,1536]{1,0:T(8,128)(2,1)S(1)}, bf16[512,1536]{1,0:T(8,128)(2,1)}, u32[]{:S(2)}) copy-start(bf16[512,1536]{1,0:T(8,128)(2,1)} %all-gather.5.cloned.1.call-done) | copy-start | bytes 4718596
  131.7 1.1 copy-start.6
  131.7 1.2 copy-start.7
  133.0 3.6 %copy-start.2 = (f32[640,1536]{1,0:T(8,128)S(1)}, f32[640,1536]{1,0:T(8,128)}, u32[]{:S(2)}) copy-start(f32[640,1536]{1,0:T(8,128)} %get-tuple-element.61) | copy-start | bytes 11796484
  135.1 11.6 %collective-permute-start.22 = (bf16[768,256]{1,0:T(8,128)(2,1)S(1)}, bf16[768,256]{1,0:T(8,128)(2,1)S(1)}, u32[]{:S(2)}, u32[]{:S(2)}) collective-permute-start(bf16[768,256]{1,0:T(8,128)(2,1)S(1)} %fusion.24), channel_id=1, source_target_pairs={{0,2},{2,0},{1,3},{3,1},{4,6},{6,4},{5,7},{7,5},{8,10},{10,8},{9,1... | collective-permute-start | bytes 1179656 | tf_op jit(solution)/shard_map/ppermute | solution.py:20
  138.0 12.2 %collective-permute-start.25 = (bf16[128,1536]{1,0:T(8,128)(2,1)S(1)}, bf16[128,1536]{1,0:T(8,128)(2,1)S(1)}, u32[]{:S(2)}, u32[]{:S(2)}) collective-permute-start(bf16[128,1536]{1,0:T(8,128)(2,1)S(1)} %get-tuple-element.21), channel_id=1, source_target_pairs={{0,4},{4,8},{8,12},{1,5},{5,9},{9,13},{2,6},{6,10},{10,14},{3,7},{... | collective-permute-start | bytes 1179656 | tf_op jit(solution)/shard_map/ppermute | solution.py:12
  140.1 13.5 %collective-permute-start.27 = (bf16[128,1536]{1,0:T(8,128)(2,1)S(1)}, bf16[128,1536]{1,0:T(8,128)(2,1)S(1)}, u32[]{:S(2)}, u32[]{:S(2)}) collective-permute-start(bf16[128,1536]{1,0:T(8,128)(2,1)S(1)} %get-tuple-element.22), channel_id=1, source_target_pairs={{4,0},{8,4},{12,8},{5,1},{9,5},{13,9},{6,2},{10,6},{14,10},{7,3},{... | collective-permute-start | bytes 1179656 | tf_op jit(solution)/shard_map/ppermute | solution.py:12
  148.6 6.0 %copy-start.10 = (bf16[1,128,1536]{2,1,0:T(8,128)(2,1)S(1)}, bf16[1,128,1536]{2,1,0:T(8,128)(2,1)}, u32[]{:S(2)}) copy-start(bf16[1,128,1536]{2,1,0:T(8,128)(2,1)} %param.12) | copy-start | bytes 1179652
  148.6 11.0 %copy-start.16 = (bf16[1024,1536]{1,0:T(8,128)(2,1)S(1)}, bf16[1024,1536]{1,0:T(8,128)(2,1)}, u32[]{:S(2)}) copy-start(bf16[1024,1536]{1,0:T(8,128)(2,1)} %all-gather.3.cloned.1.call-done) | copy-start | bytes 9437188
  148.6 9.6 %collective-permute-start.23 = (bf16[384,256]{1,0:T(8,128)(2,1)S(1)}, bf16[384,256]{1,0:T(8,128)(2,1)S(1)}, u32[]{:S(2)}, u32[]{:S(2)}) collective-permute-start(bf16[384,256]{1,0:T(8,128)(2,1)S(1)} %slice.246), channel_id=1, source_target_pairs={{0,16},{16,0},{1,17},{17,1},{2,18},{18,2},{3,19},{19,3},{4,20},{20... | collective-permute-start | bytes 589832 | tf_op jit(solution)/shard_map/ppermute | solution.py:20
  154.5 11.2 %collective-permute-start = (bf16[128,1536]{1,0:T(8,128)(2,1)S(1)}, bf16[128,1536]{1,0:T(8,128)(2,1)S(1)}, u32[]{:S(2)}, u32[]{:S(2)}) collective-permute-start(bf16[128,1536]{1,0:T(8,128)(2,1)S(1)} %bitcast.51), channel_id=1, source_target_pairs={{0,4},{4,8},{8,12},{1,5},{5,9},{9,13},{2,6},{6,10},{10,14},{3,7},{... | collective-permute-start | bytes 1179656 | tf_op jit(solution)/shard_map/ppermute | solution.py:12
  158.3 15.3 %collective-permute-start.2 = (bf16[128,1536]{1,0:T(8,128)(2,1)S(1)}, bf16[128,1536]{1,0:T(8,128)(2,1)S(1)}, u32[]{:S(2)}, u32[]{:S(2)}) collective-permute-start(bf16[128,1536]{1,0:T(8,128)(2,1)S(1)} %bitcast.52), channel_id=1, source_target_pairs={{4,0},{8,4},{12,8},{5,1},{9,5},{13,9},{6,2},{10,6},{14,10},{7,3},{... | collective-permute-start | bytes 1179656 | tf_op jit(solution)/shard_map/ppermute | solution.py:12
  165.8 11.0 %collective-permute-start.1 = (bf16[128,1536]{1,0:T(8,128)(2,1)S(1)}, bf16[128,1536]{1,0:T(8,128)(2,1)S(1)}, u32[]{:S(2)}, u32[]{:S(2)}) collective-permute-start(bf16[128,1536]{1,0:T(8,128)(2,1)S(1)} %collective-permute-done), channel_id=1, source_target_pairs={{0,4},{4,8},{8,12},{1,5},{5,9},{9,13},{2,6},{6,10},{10,14},{3,7},{... | collective-permute-start | bytes 1179656 | tf_op jit(solution)/shard_map/ppermute | solution.py:12
  171.6 17.4 %collective-permute-start.19 = (bf16[768,512]{1,0:T(8,128)(2,1)S(1)}, bf16[768,512]{1,0:T(8,128)(2,1)S(1)}, u32[]{:S(2)}, u32[]{:S(2)}) collective-permute-start(bf16[768,512]{1,0:T(8,128)(2,1)S(1)} %add_convert_fusion), channel_id=1, source_target_pairs={{0,2},{2,0},{1,3},{3,1},{4,6},{6,4},{5,7},{7,5},{8,10},{10,8},{9,1... | collective-permute-start | bytes 2359304 | tf_op jit(solution)/shard_map/ppermute | solution.py:20
  173.6 18.4 %collective-permute-start.3 = (bf16[128,1536]{1,0:T(8,128)(2,1)S(1)}, bf16[128,1536]{1,0:T(8,128)(2,1)S(1)}, u32[]{:S(2)}, u32[]{:S(2)}) collective-permute-start(bf16[128,1536]{1,0:T(8,128)(2,1)S(1)} %collective-permute-done.2), channel_id=1, source_target_pairs={{4,0},{8,4},{12,8},{5,1},{9,5},{13,9},{6,2},{10,6},{14,10},{7,3},{... | collective-permute-start | bytes 1179656 | tf_op jit(solution)/shard_map/ppermute | solution.py:12
  190.5 8.0 %collective-permute-start.20 = (bf16[384,512]{1,0:T(8,128)(2,1)S(1)}, bf16[384,512]{1,0:T(8,128)(2,1)S(1)}, u32[]{:S(2)}, u32[]{:S(2)}) collective-permute-start(bf16[384,512]{1,0:T(8,128)(2,1)S(1)} %slice.245), channel_id=1, source_target_pairs={{0,16},{16,0},{1,17},{17,1},{2,18},{18,2},{3,19},{19,3},{4,20},{20... | collective-permute-start | bytes 1179656 | tf_op jit(solution)/shard_map/ppermute | solution.py:20
  198.7 0.6 copy-start.15
Sparse Core Ops, SparseCore 0:
  10.1 44.4 all-gather.4
  56.8 71.5 all-gather.2

commit v4 on v3

--- a/solution.py
+++ b/solution.py
@@ -1,6 +1,7 @@
 import jax
 import jax.numpy as jnp
 from jax import lax
+from jax.experimental import pallas as pl
 from jax.sharding import PartitionSpec as P
 
 epsilon = 1e-06
@@ -31,16 +32,35 @@
     return lax.ppermute(x, ("groups", "seq"), pairs)
 
 
-def window_of(block):
-    right = passed_along(block, "seq", 1)
-    left = passed_along(block, "seq", -1)
-    far_right = passed_along(right, "seq", 1)
-    far_left = passed_along(left, "seq", -1)
-    return jnp.concatenate([far_right, right, block, left, far_left], 0)
+def passed_on(x, axis, by, came_from):
+    length = lax.axis_size(axis)
+    pairs = [
+        (i, i + by) for i in range(length) if 0 <= i + by < length and 0 <= i + came_from < length
+    ]
+    return lax.ppermute(x, axis, pairs)
+
+
+def neighbours(block):
+    return passed_along(block, "seq", 1), passed_along(block, "seq", -1)
+
+
+def second_neighbours(right, left):
+    return passed_on(right, "seq", 1, -1), passed_on(left, "seq", -1, 1)
 
 
 def after(value, *others):
-    return lax.optimization_barrier((value,) + others)[0]
+    def kernel(*refs):
+        del refs
+
+    anywhere = pl.BlockSpec(memory_space=pl.ANY)
+    return pl.pallas_call(
+        kernel,
+        out_shape=jax.ShapeDtypeStruct(value.shape, value.dtype),
+        in_specs=[anywhere] * (1 + len(others)),
+        out_specs=anywhere,
+        input_output_aliases={0: 0},
+        name="after",
+    )(value, *others)
 
 
 def product(rows, weight):
@@ -70,6 +90,9 @@
 
     first_rows = group_rows * 2 // 3 // 16 * 16
     cuts = [(0, first_rows), (first_rows, group_rows)]
+    out_right, out_left = neighbours(main_out[0])
+    query_other = swapped(query_rows, "groups")
+    key_other = swapped(key_rows, "groups")
     own_weights = []
     for low, high in cuts:
         piece = jnp.concatenate(
@@ -83,15 +106,18 @@
             ],
             1,
         )
+        if own_weights:
+            piece = after(piece, out_right)
         own_weights.append(lax.all_gather(piece, "seq", axis=0, tiled=True))
-    window_out = window_of(main_out[0])
+    out_far_right, out_far_left = second_neighbours(out_right, out_left)
+    out_far_left = after(out_far_left, query_other, key_other)
+    window_out = jnp.concatenate(
+        [out_far_right, out_right, main_out[0], out_left, out_far_left], 0
+    )
     last_key = passed_along(key_rows[-1:], "seq", 1)
     next_query = passed_along(query_rows[:1], "seq", -1)
-    query_other = swapped(query_rows, "groups")
-    key_other = swapped(key_rows, "groups")
     last_key_other = passed_across(key_rows[-1:], 1)
     next_query_other = passed_across(query_rows[:1], -1)
-    other_weights = [swapped(weight, "pipe") for weight in own_weights]
 
     positions = shard_index * row_count + jnp.arange(row_count, dtype=jnp.int32)
     span_of = jnp.sum((bounds_row[None, :] <= positions[:, None]).astype(jnp.int32), 1) - 1
@@ -175,13 +201,18 @@
     )
     terms = [span_terms[i * span_rows : (i + 1) * span_rows] for i in range(2 * reach + 1)]
 
-    def moved(block, by):
-        return passed_along(block.astype(jnp.bfloat16), "seq", by).astype(jnp.float32)
-
-    span_sums = terms[2] + moved(terms[3] + moved(terms[4], 1), 1) + moved(terms[1] + moved(terms[0], -1), -1)
+    def moved(block, by, further):
+        moved_block = passed_on(block.astype(jnp.bfloat16), "seq", by, further)
+        return moved_block.astype(jnp.float32)
+
+    span_sums = terms[2] + moved(terms[3] + moved(terms[4], 1, 2), 1, 1)
+    span_sums = span_sums + moved(terms[1] + moved(terms[0], -1, -2), -1, -1)
     main_grad = span_sums.astype(jnp.bfloat16)[None]
-    grad_block = after(main_in_grad[0], own_weights[0])
-    window_grad = window_of(grad_block)
+    grad_right, grad_left = neighbours(after(main_in_grad[0], own_weights[0]))
+    grad_far_right, grad_far_left = second_neighbours(grad_right, grad_left)
+    window_grad = jnp.concatenate(
+        [grad_far_right, grad_right, main_in_grad[0], grad_left, grad_far_left], 0
+    )
     start_picker = (selector & starts[:, None]).astype(jnp.bfloat16)
     start_grad = jnp.dot(start_picker, window_grad, preferred_element_type=jnp.float32)
 
@@ -190,7 +221,11 @@
         return total.astype(jnp.bfloat16)
 
     pieces = []
-    for own_weight, other_weight in zip(own_weights, other_weights):
+    far_part = None
+    for own_weight in own_weights:
+        if far_part is not None:
+            own_weight = after(own_weight, far_part)
+        other_weight = swapped(own_weight, "pipe")
         block_rows = own_weight.shape[0] // tensor_count
         if tensor_count == 2:
 
@@ -200,14 +235,18 @@
                     for weight in (own_weight, other_weight)
                 ]
 
-            incoming = swapped(partial(*half(1 - tensor_index)), "tensor").astype(jnp.float32)
+            far_part = partial(*half(1 - tensor_index))
+            incoming = swapped(far_part, "tensor").astype(jnp.float32)
             total = partial(*half(tensor_index)).astype(jnp.float32) + incoming
         else:
             total = lax.psum_scatter(
                 partial(own_weight, other_weight), "tensor", scatter_dimension=1, tiled=True
             ).astype(jnp.float32)
         own = total[:row_count]
-        arrived = swapped(total[row_count:].astype(jnp.bfloat16), "groups").astype(jnp.float32)
+        returned = total[row_count:].astype(jnp.bfloat16)
+        if not pieces:
+            returned = after(returned, grad_right, grad_left)
+        arrived = swapped(returned, "groups").astype(jnp.float32)
         pieces.append(
             [jnp.where(group_index == 0, own, arrived), jnp.where(group_index == 0, arrived, own)]
         )

time: 210 us -> 236 us (1.12)
  the two profiles are of different devices: /device:TPU:0 before, /device:TPU:16 now
where the time goes in v4:
time: 236 us; the launch traced here: 235 us
  waiting for transfers between devices  75.2 us (32%)
  starting transfers between devices  61.7 us (26%)
  local copies, waits for them, and re-layouts  33.4 us (14%)
  matrix products  29.5 us (12%)
  other arithmetic  20.1 us (9%)
  between operations  15.1 us (6%)
    ppermute x10, waiting for transfers between devices, swapped(): return lax.ppermute(x, axis, [(i, length - 1 - i) for i in range(length)])  40.2 us
    ppermute x8, waiting for transfers between devices, passed_on(): return lax.ppermute(x, axis, pairs)  32.5 us
    ppermute x8, starting transfers between devices, passed_on(): return lax.ppermute(x, axis, pairs)  25.7 us
    dot_general x8, matrix products, product(): lax.dot_general(rows, weight, (((1,), (1,)), ((), ())), preferred_element...  18.8 us
    ppermute x7, starting transfers between devices, passed_along(): return lax.ppermute(x, axis, pairs)  18.4 us
    unnamed x132, local copies, waits for them, and re-layouts  12.3 us
    ppermute x3, starting transfers between devices, passed_across(): return lax.ppermute(x, ('groups', 'seq'), pairs)  10.6 us
    ppermute x10, starting transfers between devices, swapped(): return lax.ppermute(x, axis, [(i, length - 1 - i) for i in range(length)])  6.88 us
  transfers between devices with their start and end apart: 30, of which 12 were waited for; matrix products, arithmetic and copies ran while one was open for 31% of the time, Pallas kernels for 0%

profile of v4, /device:TPU:16, one launch (start us, length us, event | category | flops | bytes accessed | tf_op | source)
XLA Modules:
  0.0 235.1 jit_solution(15103093696185321941)
XLA Ops:
  10.5 3.5 %collective-permute-start.5 = (bf16[128,1536]{1,0:T(8,128)(2,1)}, bf16[128,1536]{1,0:T(8,128)(2,1)}, u32[]{:S(2)}, u32[]{:S(2)}) collective-permute-start(bf16[128,1536]{1,0:T(8,128)(2,1)} %bitcast.6), channel_id=1, source_target_pairs={{0,4},{4,8},{8,12},{1,5},{5,9},{9,13},{2,6},{6,10},{10,14},{3,7},{... | collective-permute-start | bytes 1179656 | tf_op jit(solution)/shard_map/ppermute | solution.py:13
  14.0 2.4 %collective-permute-start.7 = (bf16[128,1536]{1,0:T(8,128)(2,1)}, bf16[128,1536]{1,0:T(8,128)(2,1)}, u32[]{:S(2)}, u32[]{:S(2)}) collective-permute-start(bf16[128,1536]{1,0:T(8,128)(2,1)} %bitcast.6), channel_id=1, source_target_pairs={{4,0},{8,4},{12,8},{5,1},{9,5},{13,9},{6,2},{10,6},{14,10},{7,3},{... | collective-permute-start | bytes 1179656 | tf_op jit(solution)/shard_map/ppermute | solution.py:13
  17.0 4.2 %collective-permute-start.4 = (bf16[1,1536]{1,0:T(2,128)(2,1)}, bf16[1,1536]{1,0:T(2,128)(2,1)S(1)}, u32[]{:S(2)}, u32[]{:S(2)}) collective-permute-start(bf16[1,1536]{1,0:T(2,128)(2,1)} %slice_bitcast_fusion.2), channel_id=1, source_target_pairs={{0,4},{4,8},{8,12},{1,5},{5,9},{9,13},{2,6},{6,10},{10,14},{3,7},{... | collective-permute-start | bytes 9224 | tf_op jit(solution)/shard_map/ppermute | solution.py:13
  21.2 2.2 collective-permute-start.15
  24.1 4.5 %collective-permute-start.17 = (bf16[1,1536]{1,0:T(2,128)(2,1)}, bf16[1,1536]{1,0:T(2,128)(2,1)}, u32[]{:S(2)}, u32[]{:S(2)}) collective-permute-start(bf16[1,1536]{1,0:T(2,128)(2,1)} %slice_bitcast_fusion.1), channel_id=1, source_target_pairs={{4,16},{8,20},{12,24},{20,0},{24,4},{28,8},{5,17},{9,21},{13,25},{... | collective-permute-start | bytes 9224 | tf_op jit(solution)/shard_map/ppermute | solution.py:32
  31.7 1.7 dynamic-slice_bitcast_fusion
  33.4 1.8 copy.32.refs_0_
  35.2 2.2 collective-permute-start.13
  38.5 3.7 %collective-permute-start.6 = (bf16[128,1536]{1,0:T(8,128)(2,1)}, bf16[128,1536]{1,0:T(8,128)(2,1)}, u32[]{:S(2)}, u32[]{:S(2)}) collective-permute-start(bf16[128,1536]{1,0:T(8,128)(2,1)} %collective-permute-done.5.refs_1_), channel_id=1, source_target_pairs={{4,8},{8,12},{5,9},{9,13},{6,10},{10,14},{7,11},{11,15},{20,24},{2... | collective-permute-start | bytes 1179656 | tf_op jit(solution)/shard_map/ppermute | solution.py:40
  42.7 1.5 collective-permute-start.9
  48.0 3.0 %collective-permute-start.8 = (bf16[128,1536]{1,0:T(8,128)(2,1)}, bf16[128,1536]{1,0:T(8,128)(2,1)S(1)}, u32[]{:S(2)}, u32[]{:S(2)}) collective-permute-start(bf16[128,1536]{1,0:T(8,128)(2,1)} %collective-permute-done.7), channel_id=1, source_target_pairs={{4,0},{8,4},{5,1},{9,5},{6,2},{10,6},{7,3},{11,7},{20,16},{24,20},... | collective-permute-start | bytes 1179656 | tf_op jit(solution)/shard_map/ppermute | solution.py:40
  51.0 24.4 %collective-permute-done.6 = bf16[128,1536]{1,0:T(8,128)(2,1)} collective-permute-done((bf16[128,1536]{1,0:T(8,128)(2,1)}, bf16[128,1536]{1,0:T(8,128)(2,1)}, u32[]{:S(2)}, u32[]{:S(2)}) %collective-permute-start.6) | collective-permute-done | bytes 393248 | tf_op jit(solution)/shard_map/ppermute | solution.py:40
  81.1 12.8 %collective-permute-done.10.refs_2_ = bf16[384,1536]{1,0:T(8,128)(2,1)} collective-permute-done((bf16[384,1536]{1,0:T(8,128)(2,1)S(1)}, bf16[384,1536]{1,0:T(8,128)(2,1)}, u32[]{:S(2)}, u32[]{:S(2)}) %collective-permute-start.10) | collective-permute-done | bytes 1179680 | tf_op jit(solution)/shard_map/ppermute | solution.py:21
  93.9 1.8 constant_dynamic-update-slice_fusion.5
  95.7 3.2 %fusion.14 = f32[384]{0:T(512)S(1)} fusion(bf16[640,1536]{1,0:T(8,128)(2,1)} %constant_dynamic-update-slice_fusion.5, bf16[1,384,1536]{2,1,0:T(8,128)(2,1)} %param.8, s32[384]{0:T(512)S(1)} %add_subtract_fusion), kind=kOutput, calls=%fused_computation.25 | convolution fusion | flops 756989568 | bytes 3148800 | tf_op jit(solution)/shard_map/dot_general | solution.py:128
  98.9 1.6 collective-permute-start.11
  100.5 1.6 fusion.83
  102.1 2.4 %constant_dynamic-slice_fusion = (bf16[383,768]{1,0:T(8,128)(2,1)}, bf16[383,768]{1,0:T(8,128)(2,1)}) fusion(bf16[384,1536]{1,0:T(8,128)(2,1)} %collective-permute-done.10.refs_2_, s32[]{:T(128)S(6)} %select_n.148, s32[]{:T(128)} %select_n.142), kind=kLoop, calls=%fused_computation.112 | loop fusion | bytes 2353160 | tf_op jit(solution)/shard_map/slice | solution.py:165
  105.2 3.9 %collective-permute-start.16 = (f32[3,1]{1,0:T(4,128)}, f32[3,1]{1,0:T(4,128)}, u32[]{:S(2)}, u32[]{:S(2)}) collective-permute-start(f32[3,1]{1,0:T(4,128)} %slice.192), channel_id=1, source_target_pairs={{4,16},{8,20},{12,24},{20,0},{24,4},{28,8},{5,17},{9,21},{13,25},{... | collective-permute-start | bytes 44 | tf_op jit(solution)/shard_map/ppermute | solution.py:32
  109.1 1.9 collective-permute-start.12
  113.6 4.0 %fusion.84 = (bf16[640,1536]{1,0:T(8,128)(2,1)}, f32[640,1536]{1,0:T(8,128)}) fusion(f32[640,1536]{1,0:T(8,128)S(1)} %fusion.34, bf16[1,384,1536]{2,1,0:T(8,128)(2,1)S(1)} %copy-done.4, s32[384]{0:T(512)S(1)} %add_subtract_fusion, bf16[384]{0:T(512)(128)(2,1)S(1)} %get-tuple-element.15), kind=kOutput, calls=%fused_computation.173 | convolution fusion | flops 757432320 | bytes 11012352 | tf_op jit(solution)/shard_map/dot_general | solution.py:199
  118.9 1.4 collective-permute-start.24
  120.3 4.6 %collective-permute-start.26 = (bf16[128,1536]{1,0:T(8,128)(2,1)S(1)}, bf16[128,1536]{1,0:T(8,128)(2,1)S(1)}, u32[]{:S(2)}, u32[]{:S(2)}) collective-permute-start(bf16[128,1536]{1,0:T(8,128)(2,1)S(1)} %get-tuple-element.22), channel_id=1, source_target_pairs={{8,4},{12,8},{9,5},{13,9},{10,6},{14,10},{11,7},{15,11},{24,20},{2... | collective-permute-start | bytes 1179656 | tf_op jit(solution)/shard_map/ppermute | solution.py:40
  124.9 2.4 %fusion.28 = (bf16[384,768]{1,0:T(8,128)(2,1)}, bf16[384,768]{1,0:T(8,128)(2,1)}) fusion(bf16[383,768]{1,0:T(8,128)(2,1)S(1)} %copy-done.13, bf16[1,768]{1,0:T(2,128)(2,1)S(1)} %copy-done.50, bf16[1,384,1536]{2,1,0:T(8,128)(2,1)S(1)} %copy-done, s32[]{:T(128)S(6)} %select_n.148, f32[384]{0:T(512)} %get-tuple-element.46, f32[384]{0:T(512)} %get-tuple-element.47, ...), kind=kLoop, calls=%fused_computation.38 | loop fusion | flops 5308416 | bytes 3542024 | tf_op jit(solution)/shard_map/convert_element_type | solution.py:173
  128.8 1.5 fusion.26
  133.7 2.5 %fusion.41 = (bf16[128,1536]{1,0:T(8,128)(2,1)}, bf16[128,1536]{1,0:T(8,128)(2,1)}) fusion(f32[640,1536]{1,0:T(8,128)} %get-tuple-element.59, bf16[128,1536]{1,0:T(8,128)(2,1)S(1)} %collective-permute-done.24, bf16[128,1536]{1,0:T(8,128)(2,1)S(1)} %collective-permute-done.26), kind=kLoop, calls=%fused_computation.62 | loop fusion | flops 1179648 | bytes 3145728 | tf_op jit(solution)/shard_map/convert_element_type | solution.py:205
  136.1 4.3 %collective-permute-start.27 = (bf16[128,1536]{1,0:T(8,128)(2,1)}, bf16[128,1536]{1,0:T(8,128)(2,1)}, u32[]{:S(2)}, u32[]{:S(2)}) collective-permute-start(bf16[128,1536]{1,0:T(8,128)(2,1)} %get-tuple-element.20), channel_id=1, source_target_pairs={{4,0},{8,4},{12,8},{5,1},{9,5},{13,9},{6,2},{10,6},{14,10},{7,3},{... | collective-permute-start | bytes 1179656 | tf_op jit(solution)/shard_map/ppermute | solution.py:40
  140.4 2.3 collective-permute-start.25
  142.8 3.8 %subtract_convert_fusion = (bf16[384,768]{1,0:T(8,128)(2,1)}, bf16[384,768]{1,0:T(8,128)(2,1)}, bf16[384,768]{1,0:T(8,128)(2,1)}, bf16[384,768]{1,0:T(8,128)(2,1)}) fusion(bf16[1,768]{1,0:T(2,128)(2,1)S(1)} %copy-done.46, bf16[383,768]{1,0:T(8,128)(2,1)S(1)} %copy-done.7, bf16[384,1536]{1,0:T(8,128)(2,1)} %collective-permute-done.10.refs_2_, ...), kind=kLoop, calls=%fused_computation.48 | loop fusion | flops 10616832 | bytes 7084040 | tf_op jit(solution)/shard_map/convert_element_type | solution.py:173
  146.7 2.4 %collective-permute-start = (bf16[128,1536]{1,0:T(8,128)(2,1)}, bf16[128,1536]{1,0:T(8,128)(2,1)S(1)}, u32[]{:S(2)}, u32[]{:S(2)}) collective-permute-start(bf16[128,1536]{1,0:T(8,128)(2,1)} %after.5), channel_id=1, source_target_pairs={{0,4},{4,8},{8,12},{1,5},{5,9},{9,13},{2,6},{6,10},{10,14},{3,7},{... | collective-permute-start | bytes 1179656 | tf_op jit(solution)/shard_map/ppermute | solution.py:13
  149.0 5.5 %collective-permute-done.25 = bf16[128,1536]{1,0:T(8,128)(2,1)} collective-permute-done((bf16[128,1536]{1,0:T(8,128)(2,1)}, bf16[128,1536]{1,0:T(8,128)(2,1)}, u32[]{:S(2)}, u32[]{:S(2)}) %collective-permute-start.25) | collective-permute-done | bytes 393248 | tf_op jit(solution)/shard_map/ppermute | solution.py:40
  154.5 2.2 fusion.57
  156.7 1.9 collective-permute-start.2
  158.7 2.4 %collective-permute-done.refs_1_ = bf16[128,1536]{1,0:T(8,128)(2,1)S(1)} collective-permute-done((bf16[128,1536]{1,0:T(8,128)(2,1)}, bf16[128,1536]{1,0:T(8,128)(2,1)S(1)}, u32[]{:S(2)}, u32[]{:S(2)}) %collective-permute-start) | collective-permute-done | bytes 393248 | tf_op jit(solution)/shard_map/ppermute | solution.py:13
  161.0 2.6 %collective-permute-start.1 = (bf16[128,1536]{1,0:T(8,128)(2,1)S(1)}, bf16[128,1536]{1,0:T(8,128)(2,1)S(1)}, u32[]{:S(2)}, u32[]{:S(2)}) collective-permute-start(bf16[128,1536]{1,0:T(8,128)(2,1)S(1)} %collective-permute-done.refs_1_), channel_id=1, source_target_pairs={{4,8},{8,12},{5,9},{9,13},{6,10},{10,14},{7,11},{11,15},{20,24},{2... | collective-permute-start | bytes 1179656 | tf_op jit(solution)/shard_map/ppermute | solution.py:40
  163.7 3.0 %fusion.8 = f32[768,512]{1,0:T(8,128)S(1)} fusion(bf16[1024,1536]{1,0:T(8,128)(2,1)} %all-gather.3.cloned.1.call-done.refs_1_, s32[]{:T(128)S(6)} %select_n.149, bf16[384,768]{1,0:T(8,128)(2,1)S(1)} %copy-done.23, bf16[384,768]{1,0:T(8,128)(2,1)S(1)} %copy-done.24, bf16[384,768]{1,0:T(8,128)(2,1)S(1)} %copy-done.37, bf16[384,768]{1,0:T(8,128)(2,1)S(1)} %copy-done.31), kind=kOutput, calls=%fused_computation.18 | convolution fusion | flops 1217396736 | bytes 5505028 | tf_op jit(solution)/shard_map/dot_general | solution.py:67
  166.7 2.6 %fusion.12 = f32[768,512]{1,0:T(8,128)} fusion(bf16[1024,1536]{1,0:T(8,128)(2,1)S(1)} %copy-done.6, s32[]{:T(128)S(6)} %select_n.147, bf16[384,768]{1,0:T(8,128)(2,1)S(1)} %copy-done.23, bf16[384,768]{1,0:T(8,128)(2,1)S(1)} %copy-done.24, bf16[384,768]{1,0:T(8,128)(2,1)S(1)} %copy-done.38, bf16[384,768]{1,0:T(8,128)(2,1)S(1)} %copy-done.32), kind=kOutput, calls=%fused_computation.23 | convolution fusion | flops 1217396736 | bytes 5505028 | tf_op jit(solution)/shard_map/dot_general | solution.py:67
  169.3 4.0 %collective-permute-start.3 = (bf16[128,1536]{1,0:T(8,128)(2,1)S(1)}, bf16[128,1536]{1,0:T(8,128)(2,1)}, u32[]{:S(2)}, u32[]{:S(2)}) collective-permute-start(bf16[128,1536]{1,0:T(8,128)(2,1)S(1)} %collective-permute-done.2.refs_2_), channel_id=1, source_target_pairs={{4,0},{8,4},{5,1},{9,5},{6,2},{10,6},{7,3},{11,7},{20,16},{24,20},... | collective-permute-start | bytes 1179656 | tf_op jit(solution)/shard_map/ppermute | solution.py:40
  174.1 3.7 %add_convert_fusion.refs_1_ = bf16[768,512]{1,0:T(8,128)(2,1)} fusion(f32[768,512]{1,0:T(8,128)S(1)} %fusion.8, bf16[1024,1536]{1,0:T(8,128)(2,1)} %collective-permute-done.18, s32[]{:T(128)S(6)} %select_n.149, bf16[384,768]{1,0:T(8,128)(2,1)S(1)} %copy-done.25, bf16[384,768]{1,0:T(8,128)(2,1)S(1)} %copy-done.28, bf16[384,768]{1,0:T(8,128)(2,1)S(1)} %copy-done.40, ...), kind=kOutput, calls=%fused_computation.15 | convolution fusion | flops 1218183168 | bytes 6291460 | tf_op jit(solution)/shard_map/dot_general | solution.py:67
  181.3 1.8 constant_dynamic-update-slice_fusion
  183.1 15.6 %collective-permute-done.19 = bf16[768,512]{1,0:T(8,128)(2,1)S(1)} collective-permute-done((bf16[768,512]{1,0:T(8,128)(2,1)S(1)}, bf16[768,512]{1,0:T(8,128)(2,1)S(1)}, u32[]{:S(2)}, u32[]{:S(2)}) %collective-permute-start.19) | collective-permute-done | bytes 786464 | tf_op jit(solution)/shard_map/ppermute | solution.py:21
  198.7 3.3 %convert_add_fusion = f32[768,512]{1,0:T(8,128)S(1)} fusion(bf16[768,512]{1,0:T(8,128)(2,1)S(1)} %collective-permute-done.19, f32[768,512]{1,0:T(8,128)} %fusion.12, bf16[1024,1536]{1,0:T(8,128)(2,1)} %collective-permute-done.18, s32[]{:T(128)S(6)} %select_n.147, bf16[384,768]{1,0:T(8,128)(2,1)S(1)} %copy-done.26, bf16[384,768]{1,0:T(8,128)(2,1)S(1)} %copy-done.29, ...), kind=kOutput, calls=%fused_computation.14 | convolution fusion | flops 1219362816 | bytes 7864324 | tf_op jit(solution)/shard_map/dot_general | solution.py:67
  203.5 2.7 %fusion.44 = f32[768,256]{1,0:T(8,128)S(1)} fusion(bf16[512,1536]{1,0:T(8,128)(2,1)} %collective-permute-done.21, s32[]{:T(128)S(6)} %select_n.154, bf16[384,768]{1,0:T(8,128)(2,1)S(1)} %copy-done.27, bf16[384,768]{1,0:T(8,128)(2,1)} %get-tuple-element.61, bf16[384,768]{1,0:T(8,128)(2,1)} %get-tuple-element.27, bf16[384,768]{1,0:T(8,128)(2,1)} %get-tuple-element.25), kind=kOutput, calls=%fused_computation.68 | convolution fusion | flops 613416960 | bytes 3932164 | tf_op jit(solution)/shard_map/dot_general | solution.py:67
  207.7 5.7 %collective-permute-done.20 = bf16[384,512]{1,0:T(8,128)(2,1)S(1)} collective-permute-done((bf16[384,512]{1,0:T(8,128)(2,1)}, bf16[384,512]{1,0:T(8,128)(2,1)S(1)}, u32[]{:S(2)}, u32[]{:S(2)}) %collective-permute-start.20) | collective-permute-done | bytes 393248 | tf_op jit(solution)/shard_map/ppermute | solution.py:21
  213.4 1.3 convert_select_fusion
  214.7 1.9 fusion.47
  219.3 4.8 %collective-permute-done.23 = bf16[384,256]{1,0:T(8,128)(2,1)S(1)} collective-permute-done((bf16[384,256]{1,0:T(8,128)(2,1)S(1)}, bf16[384,256]{1,0:T(8,128)(2,1)S(1)}, u32[]{:S(2)}, u32[]{:S(2)}) %collective-permute-start.23) | collective-permute-done | bytes 196640 | tf_op jit(solution)/shard_map/ppermute | solution.py:21
  226.1 2.2 fusion.2
  (218 shorter events, 39.8 us)
Async XLA Ops:
  7.2 110.4 %all-gather.3.cloned.1.call-start = ((), (), s32[]{:S(2)}) async-start(), calls=%async_computation | async-start | bytes 3932160 | tf_op jit(solution)/shard_map/all_gather | solution.py:111
  7.2 16.3 %copy-start = (bf16[1,384,1536]{2,1,0:T(8,128)(2,1)S(1)}, bf16[1,384,1536]{2,1,0:T(8,128)(2,1)}, u32[]{:S(2)}) copy-start(bf16[1,384,1536]{2,1,0:T(8,128)(2,1)} %param.9) | copy-start | bytes 3538948
  8.4 20.2 %copy-start.54 = (s32[1,512]{1,0:T(1,128)S(1)}, s32[1,512]{1,0:T(1,128)}, u32[]{:S(2)}) copy-start(s32[1,512]{1,0:T(1,128)} %param.13) | copy-start | bytes 6148
  10.5 167.4 %all-gather.5.cloned.1.call-start = ((), (), s32[]{:S(2)}) async-start(), calls=%async_computation.1 | async-start | bytes 1966080 | tf_op jit(solution)/shard_map/all_gather | solution.py:111
  10.5 27.9 %collective-permute-start.5 = (bf16[128,1536]{1,0:T(8,128)(2,1)}, bf16[128,1536]{1,0:T(8,128)(2,1)}, u32[]{:S(2)}, u32[]{:S(2)}) collective-permute-start(bf16[128,1536]{1,0:T(8,128)(2,1)} %bitcast.6), channel_id=1, source_target_pairs={{0,4},{4,8},{8,12},{1,5},{5,9},{9,13},{2,6},{6,10},{10,14},{3,7},{... | collective-permute-start | bytes 1179656 | tf_op jit(solution)/shard_map/ppermute | solution.py:13
  14.0 34.0 %collective-permute-start.7 = (bf16[128,1536]{1,0:T(8,128)(2,1)}, bf16[128,1536]{1,0:T(8,128)(2,1)}, u32[]{:S(2)}, u32[]{:S(2)}) collective-permute-start(bf16[128,1536]{1,0:T(8,128)(2,1)} %bitcast.6), channel_id=1, source_target_pairs={{4,0},{8,4},{12,8},{5,1},{9,5},{13,9},{6,2},{10,6},{14,10},{7,3},{... | collective-permute-start | bytes 1179656 | tf_op jit(solution)/shard_map/ppermute | solution.py:13
  17.0 18.2 %collective-permute-start.4 = (bf16[1,1536]{1,0:T(2,128)(2,1)}, bf16[1,1536]{1,0:T(2,128)(2,1)S(1)}, u32[]{:S(2)}, u32[]{:S(2)}) collective-permute-start(bf16[1,1536]{1,0:T(2,128)(2,1)} %slice_bitcast_fusion.2), channel_id=1, source_target_pairs={{0,4},{4,8},{8,12},{1,5},{5,9},{9,13},{2,6},{6,10},{10,14},{3,7},{... | collective-permute-start | bytes 9224 | tf_op jit(solution)/shard_map/ppermute | solution.py:13
  21.2 24.3 %collective-permute-start.15 = (bf16[1,1536]{1,0:T(2,128)(2,1)}, bf16[1,1536]{1,0:T(2,128)(2,1)}, u32[]{:S(2)}, u32[]{:S(2)}) collective-permute-start(bf16[1,1536]{1,0:T(2,128)(2,1)} %slice_bitcast_fusion.2), channel_id=1, source_target_pairs={{0,20},{4,24},{8,28},{16,4},{20,8},{24,12},{1,21},{5,25},{9,29},{1... | collective-permute-start | bytes 9224 | tf_op jit(solution)/shard_map/ppermute | solution.py:32
  24.1 18.6 %collective-permute-start.17 = (bf16[1,1536]{1,0:T(2,128)(2,1)}, bf16[1,1536]{1,0:T(2,128)(2,1)}, u32[]{:S(2)}, u32[]{:S(2)}) collective-permute-start(bf16[1,1536]{1,0:T(2,128)(2,1)} %slice_bitcast_fusion.1), channel_id=1, source_target_pairs={{4,16},{8,20},{12,24},{20,0},{24,4},{28,8},{5,17},{9,21},{13,25},{... | collective-permute-start | bytes 9224 | tf_op jit(solution)/shard_map/ppermute | solution.py:32
  35.2 12.2 %collective-permute-start.13 = (bf16[1,1536]{1,0:T(2,128)(2,1)}, bf16[1,1536]{1,0:T(2,128)(2,1)S(1)}, u32[]{:S(2)}, u32[]{:S(2)}) collective-permute-start(bf16[1,1536]{1,0:T(2,128)(2,1)} %slice_bitcast_fusion.1), channel_id=1, source_target_pairs={{4,0},{8,4},{12,8},{5,1},{9,5},{13,9},{6,2},{10,6},{14,10},{7,3},{... | collective-permute-start | bytes 9224 | tf_op jit(solution)/shard_map/ppermute | solution.py:13
  38.5 36.9 %collective-permute-start.6 = (bf16[128,1536]{1,0:T(8,128)(2,1)}, bf16[128,1536]{1,0:T(8,128)(2,1)}, u32[]{:S(2)}, u32[]{:S(2)}) collective-permute-start(bf16[128,1536]{1,0:T(8,128)(2,1)} %collective-permute-done.5.refs_1_), channel_id=1, source_target_pairs={{4,8},{8,12},{5,9},{9,13},{6,10},{10,14},{7,11},{11,15},{20,24},{2... | collective-permute-start | bytes 1179656 | tf_op jit(solution)/shard_map/ppermute | solution.py:40
  42.7 37.6 %collective-permute-start.9 = (bf16[384,1536]{1,0:T(8,128)(2,1)S(1)}, bf16[384,1536]{1,0:T(8,128)(2,1)S(1)}, u32[]{:S(2)}, u32[]{:S(2)}) collective-permute-start(bf16[384,1536]{1,0:T(8,128)(2,1)S(1)} %bitcast.50), channel_id=1, source_target_pairs={{0,16},{16,0},{1,17},{17,1},{2,18},{18,2},{3,19},{19,3},{4,20},{20... | collective-permute-start | bytes 3538952 | tf_op jit(solution)/shard_map/ppermute | solution.py:21
  45.6 48.3 %collective-permute-start.10 = (bf16[384,1536]{1,0:T(8,128)(2,1)S(1)}, bf16[384,1536]{1,0:T(8,128)(2,1)}, u32[]{:S(2)}, u32[]{:S(2)}) collective-permute-start(bf16[384,1536]{1,0:T(8,128)(2,1)S(1)} %bitcast.51), channel_id=1, source_target_pairs={{0,16},{16,0},{1,17},{17,1},{2,18},{18,2},{3,19},{19,3},{4,20},{20... | collective-permute-start | bytes 3538952 | tf_op jit(solution)/shard_map/ppermute | solution.py:21
  48.0 32.4 %collective-permute-start.8 = (bf16[128,1536]{1,0:T(8,128)(2,1)}, bf16[128,1536]{1,0:T(8,128)(2,1)S(1)}, u32[]{:S(2)}, u32[]{:S(2)}) collective-permute-start(bf16[128,1536]{1,0:T(8,128)(2,1)} %collective-permute-done.7), channel_id=1, source_target_pairs={{4,0},{8,4},{5,1},{9,5},{6,2},{10,6},{7,3},{11,7},{20,16},{24,20},... | collective-permute-start | bytes 1179656 | tf_op jit(solution)/shard_map/ppermute | solution.py:40
  81.1 12.8 %copy-start.2 = (bf16[384,1536]{1,0:T(8,128)(2,1)}, bf16[384,1536]{1,0:T(8,128)(2,1)S(1)}, u32[]{:S(2)}) copy-start(bf16[384,1536]{1,0:T(8,128)(2,1)S(1)} %collective-permute-done.9.refs_1_) | copy-start | bytes 3538948
  98.9 12.7 %copy-start.56 = (pred[384]{0:T(512)(128)(4,1)S(1)}, pred[384]{0:T(512)(128)(4,1)}, u32[]{:S(2)}) copy-start(pred[384]{0:T(512)(128)(4,1)} %copy-done.55) | copy-start | bytes 1156
  98.9 13.3 %copy-start.4 = (bf16[1,384,1536]{2,1,0:T(8,128)(2,1)S(1)}, bf16[1,384,1536]{2,1,0:T(8,128)(2,1)}, u32[]{:S(2)}) copy-start(bf16[1,384,1536]{2,1,0:T(8,128)(2,1)} %param.8) | copy-start | bytes 3538948
  98.9 5.6 %collective-permute-start.11 = (f32[4,384]{1,0:T(4,128)S(1)}, f32[4,384]{1,0:T(4,128)S(1)}, u32[]{:S(2)}, u32[]{:S(2)}) collective-permute-start(f32[4,384]{1,0:T(4,128)S(1)} %pad_maximum_fusion.3), channel_id=1, source_target_pairs={{0,2},{2,0},{1,3},{3,1},{4,6},{6,4},{5,7},{7,5},{8,10},{10,8},{9,1... | collective-permute-start | bytes 18440 | tf_op jit(solution)/shard_map/ppermute | solution.py:21
  105.2 25.8 %collective-permute-start.16 = (f32[3,1]{1,0:T(4,128)}, f32[3,1]{1,0:T(4,128)}, u32[]{:S(2)}, u32[]{:S(2)}) collective-permute-start(f32[3,1]{1,0:T(4,128)} %slice.192), channel_id=1, source_target_pairs={{4,16},{8,20},{12,24},{20,0},{24,4},{28,8},{5,17},{9,21},{13,25},{... | collective-permute-start | bytes 44 | tf_op jit(solution)/shard_map/ppermute | solution.py:32
  109.1 18.3 %collective-permute-start.12 = (f32[3,1]{1,0:T(4,128)}, f32[3,1]{1,0:T(4,128)}, u32[]{:S(2)}, u32[]{:S(2)}) collective-permute-start(f32[3,1]{1,0:T(4,128)} %slice.192), channel_id=1, source_target_pairs={{4,0},{8,4},{12,8},{5,1},{9,5},{13,9},{6,2},{10,6},{14,10},{7,3},{... | collective-permute-start | bytes 44 | tf_op jit(solution)/shard_map/ppermute | solution.py:13
  117.6 56.5 %collective-permute-start.18 = (bf16[1024,1536]{1,0:T(8,128)(2,1)}, bf16[1024,1536]{1,0:T(8,128)(2,1)}, u32[]{:S(2)}, u32[]{:S(2)}) collective-permute-start(bf16[1024,1536]{1,0:T(8,128)(2,1)} %all-gather.3.cloned.1.call-done.refs_1_), channel_id=1, source_target_pairs={{0,1},{1,0},{2,3},{3,2},{4,5},{5,4},{6,7},{7,6},{8,9},{9,8},{10,11... | collective-permute-start | bytes 9437192 | tf_op jit(solution)/shard_map/ppermute | solution.py:21
  118.9 13.5 %collective-permute-start.24 = (bf16[128,1536]{1,0:T(8,128)(2,1)S(1)}, bf16[128,1536]{1,0:T(8,128)(2,1)S(1)}, u32[]{:S(2)}, u32[]{:S(2)}) collective-permute-start(bf16[128,1536]{1,0:T(8,128)(2,1)S(1)} %get-tuple-element.21), channel_id=1, source_target_pairs={{0,4},{4,8},{1,5},{5,9},{2,6},{6,10},{3,7},{7,11},{16,20},{20,24},... | collective-permute-start | bytes 1179656 | tf_op jit(solution)/shard_map/ppermute | solution.py:40
  120.3 13.3 %collective-permute-start.26 = (bf16[128,1536]{1,0:T(8,128)(2,1)S(1)}, bf16[128,1536]{1,0:T(8,128)(2,1)S(1)}, u32[]{:S(2)}, u32[]{:S(2)}) collective-permute-start(bf16[128,1536]{1,0:T(8,128)(2,1)S(1)} %get-tuple-element.22), channel_id=1, source_target_pairs={{8,4},{12,8},{9,5},{13,9},{10,6},{14,10},{11,7},{15,11},{24,20},{2... | collective-permute-start | bytes 1179656 | tf_op jit(solution)/shard_map/ppermute | solution.py:40
  127.3 3.6 %collective-permute-start.14 = (f32[3,384]{1,0:T(4,128)S(1)}, f32[3,384]{1,0:T(4,128)S(1)}, u32[]{:S(2)}, u32[]{:S(2)}) collective-permute-start(f32[3,384]{1,0:T(4,128)S(1)} %pad_maximum_fusion.4), channel_id=1, source_target_pairs={{0,16},{16,0},{1,17},{17,1},{2,18},{18,2},{3,19},{19,3},{4,20},{20... | collective-permute-start | bytes 13832 | tf_op jit(solution)/shard_map/ppermute | solution.py:21
  130.3 12.5 %copy-start.46 = (bf16[1,768]{1,0:T(2,128)(2,1)S(1)}, bf16[1,768]{1,0:T(2,128)(2,1)}, u32[]{:S(2)}) copy-start(bf16[1,768]{1,0:T(2,128)(2,1)} %get-tuple-element.54) | copy-start | bytes 4612
  130.3 12.5 %copy-start.47 = (bf16[1,768]{1,0:T(2,128)(2,1)S(1)}, bf16[1,768]{1,0:T(2,128)(2,1)}, u32[]{:S(2)}) copy-start(bf16[1,768]{1,0:T(2,128)(2,1)} %get-tuple-element.55) | copy-start | bytes 4612
  130.3 12.5 %copy-start.48 = (bf16[1,768]{1,0:T(2,128)(2,1)S(1)}, bf16[1,768]{1,0:T(2,128)(2,1)}, u32[]{:S(2)}) copy-start(bf16[1,768]{1,0:T(2,128)(2,1)} %get-tuple-element.52) | copy-start | bytes 4612
  130.3 12.5 %copy-start.49 = (bf16[1,768]{1,0:T(2,128)(2,1)S(1)}, bf16[1,768]{1,0:T(2,128)(2,1)}, u32[]{:S(2)}) copy-start(bf16[1,768]{1,0:T(2,128)(2,1)} %get-tuple-element.53) | copy-start | bytes 4612
  136.1 12.9 %collective-permute-start.27 = (bf16[128,1536]{1,0:T(8,128)(2,1)}, bf16[128,1536]{1,0:T(8,128)(2,1)}, u32[]{:S(2)}, u32[]{:S(2)}) collective-permute-start(bf16[128,1536]{1,0:T(8,128)(2,1)} %get-tuple-element.20), channel_id=1, source_target_pairs={{4,0},{8,4},{12,8},{5,1},{9,5},{13,9},{6,2},{10,6},{14,10},{7,3},{... | collective-permute-start | bytes 1179656 | tf_op jit(solution)/shard_map/ppermute | solution.py:40
  140.4 14.1 %collective-permute-start.25 = (bf16[128,1536]{1,0:T(8,128)(2,1)}, bf16[128,1536]{1,0:T(8,128)(2,1)}, u32[]{:S(2)}, u32[]{:S(2)}) collective-permute-start(bf16[128,1536]{1,0:T(8,128)(2,1)} %get-tuple-element.19), channel_id=1, source_target_pairs={{0,4},{4,8},{8,12},{1,5},{5,9},{9,13},{2,6},{6,10},{10,14},{3,7},{... | collective-permute-start | bytes 1179656 | tf_op jit(solution)/shard_map/ppermute | solution.py:40
  146.6 17.0 %copy-start.31 = (bf16[384,768]{1,0:T(8,128)(2,1)S(1)}, bf16[384,768]{1,0:T(8,128)(2,1)}, u32[]{:S(2)}) copy-start(bf16[384,768]{1,0:T(8,128)(2,1)} %get-tuple-element.26) | copy-start | bytes 1769476
  146.6 17.0 %copy-start.37 = (bf16[384,768]{1,0:T(8,128)(2,1)S(1)}, bf16[384,768]{1,0:T(8,128)(2,1)}, u32[]{:S(2)}) copy-start(bf16[384,768]{1,0:T(8,128)(2,1)} %get-tuple-element.28) | copy-start | bytes 1769476
  146.6 17.0 %copy-start.23 = (bf16[384,768]{1,0:T(8,128)(2,1)S(1)}, bf16[384,768]{1,0:T(8,128)(2,1)}, u32[]{:S(2)}) copy-start(bf16[384,768]{1,0:T(8,128)(2,1)} %get-tuple-element.32) | copy-start | bytes 1769476
  146.7 17.0 %copy-start.24 = (bf16[384,768]{1,0:T(8,128)(2,1)S(1)}, bf16[384,768]{1,0:T(8,128)(2,1)}, u32[]{:S(2)}) copy-start(bf16[384,768]{1,0:T(8,128)(2,1)} %get-tuple-element.60) | copy-start | bytes 1769476
  146.7 14.3 %collective-permute-start = (bf16[128,1536]{1,0:T(8,128)(2,1)}, bf16[128,1536]{1,0:T(8,128)(2,1)S(1)}, u32[]{:S(2)}, u32[]{:S(2)}) collective-permute-start(bf16[128,1536]{1,0:T(8,128)(2,1)} %after.5), channel_id=1, source_target_pairs={{0,4},{4,8},{8,12},{1,5},{5,9},{9,13},{2,6},{6,10},{10,14},{3,7},{... | collective-permute-start | bytes 1179656 | tf_op jit(solution)/shard_map/ppermute | solution.py:13
  156.7 12.6 %collective-permute-start.2 = (bf16[128,1536]{1,0:T(8,128)(2,1)S(1)}, bf16[128,1536]{1,0:T(8,128)(2,1)S(1)}, u32[]{:S(2)}, u32[]{:S(2)}) collective-permute-start(bf16[128,1536]{1,0:T(8,128)(2,1)S(1)} %copy-done.20), channel_id=1, source_target_pairs={{4,0},{8,4},{12,8},{5,1},{9,5},{13,9},{6,2},{10,6},{14,10},{7,3},{... | collective-permute-start | bytes 1179656 | tf_op jit(solution)/shard_map/ppermute | solution.py:13
  161.0 17.0 %copy-start.17 = (bf16[128,1536]{1,0:T(8,128)(2,1)}, bf16[128,1536]{1,0:T(8,128)(2,1)S(1)}, u32[]{:S(2)}) copy-start(bf16[128,1536]{1,0:T(8,128)(2,1)S(1)} %collective-permute-done.refs_1_) | copy-start | bytes 1179652
  161.0 12.3 %collective-permute-start.1 = (bf16[128,1536]{1,0:T(8,128)(2,1)S(1)}, bf16[128,1536]{1,0:T(8,128)(2,1)S(1)}, u32[]{:S(2)}, u32[]{:S(2)}) collective-permute-start(bf16[128,1536]{1,0:T(8,128)(2,1)S(1)} %collective-permute-done.refs_1_), channel_id=1, source_target_pairs={{4,8},{8,12},{5,9},{9,13},{6,10},{10,14},{7,11},{11,15},{20,24},{2... | collective-permute-start | bytes 1179656 | tf_op jit(solution)/shard_map/ppermute | solution.py:40
  169.3 11.9 %collective-permute-start.3 = (bf16[128,1536]{1,0:T(8,128)(2,1)S(1)}, bf16[128,1536]{1,0:T(8,128)(2,1)}, u32[]{:S(2)}, u32[]{:S(2)}) collective-permute-start(bf16[128,1536]{1,0:T(8,128)(2,1)S(1)} %collective-permute-done.2.refs_2_), channel_id=1, source_target_pairs={{4,0},{8,4},{5,1},{9,5},{6,2},{10,6},{7,3},{11,7},{20,16},{24,20},... | collective-permute-start | bytes 1179656 | tf_op jit(solution)/shard_map/ppermute | solution.py:40
  177.9 20.8 %copy-start.26 = (bf16[384,768]{1,0:T(8,128)(2,1)S(1)}, bf16[384,768]{1,0:T(8,128)(2,1)}, u32[]{:S(2)}) copy-start(bf16[384,768]{1,0:T(8,128)(2,1)} %get-tuple-element.31) | copy-start | bytes 1769476
  177.9 20.8 %copy-start.29 = (bf16[384,768]{1,0:T(8,128)(2,1)S(1)}, bf16[384,768]{1,0:T(8,128)(2,1)}, u32[]{:S(2)}) copy-start(bf16[384,768]{1,0:T(8,128)(2,1)} %get-tuple-element.61) | copy-start | bytes 1769476
  177.9 20.8 %copy-start.35 = (bf16[384,768]{1,0:T(8,128)(2,1)S(1)}, bf16[384,768]{1,0:T(8,128)(2,1)}, u32[]{:S(2)}) copy-start(bf16[384,768]{1,0:T(8,128)(2,1)} %get-tuple-element.25) | copy-start | bytes 1769476
  177.9 20.8 %copy-start.41 = (bf16[384,768]{1,0:T(8,128)(2,1)S(1)}, bf16[384,768]{1,0:T(8,128)(2,1)}, u32[]{:S(2)}) copy-start(bf16[384,768]{1,0:T(8,128)(2,1)} %get-tuple-element.27) | copy-start | bytes 1769476
  177.9 25.5 %collective-permute-start.21 = (bf16[512,1536]{1,0:T(8,128)(2,1)}, bf16[512,1536]{1,0:T(8,128)(2,1)}, u32[]{:S(2)}, u32[]{:S(2)}) collective-permute-start(bf16[512,1536]{1,0:T(8,128)(2,1)} %after.9), channel_id=1, source_target_pairs={{0,1},{1,0},{2,3},{3,2},{4,5},{5,4},{6,7},{7,6},{8,9},{9,8},{10,11... | collective-permute-start | bytes 4718600 | tf_op jit(solution)/shard_map/ppermute | solution.py:21
  179.1 19.6 %collective-permute-start.19 = (bf16[768,512]{1,0:T(8,128)(2,1)S(1)}, bf16[768,512]{1,0:T(8,128)(2,1)S(1)}, u32[]{:S(2)}, u32[]{:S(2)}) collective-permute-start(bf16[768,512]{1,0:T(8,128)(2,1)S(1)} %copy-done.22), channel_id=1, source_target_pairs={{0,2},{2,0},{1,3},{3,1},{4,6},{6,4},{5,7},{7,5},{8,10},{10,8},{9,1... | collective-permute-start | bytes 2359304 | tf_op jit(solution)/shard_map/ppermute | solution.py:21
  202.9 10.5 %collective-permute-start.20 = (bf16[384,512]{1,0:T(8,128)(2,1)}, bf16[384,512]{1,0:T(8,128)(2,1)S(1)}, u32[]{:S(2)}, u32[]{:S(2)}) collective-permute-start(bf16[384,512]{1,0:T(8,128)(2,1)} %after.7), channel_id=1, source_target_pairs={{0,16},{16,0},{1,17},{17,1},{2,18},{18,2},{3,19},{19,3},{4,20},{20... | collective-permute-start | bytes 1179656 | tf_op jit(solution)/shard_map/ppermute | solution.py:21
  207.1 10.4 %collective-permute-start.22 = (bf16[768,256]{1,0:T(8,128)(2,1)S(1)}, bf16[768,256]{1,0:T(8,128)(2,1)S(1)}, u32[]{:S(2)}, u32[]{:S(2)}) collective-permute-start(bf16[768,256]{1,0:T(8,128)(2,1)S(1)} %fusion.24), channel_id=1, source_target_pairs={{0,2},{2,0},{1,3},{3,1},{4,6},{6,4},{5,7},{7,5},{8,10},{10,8},{9,1... | collective-permute-start | bytes 1179656 | tf_op jit(solution)/shard_map/ppermute | solution.py:21
  218.3 5.7 %collective-permute-start.23 = (bf16[384,256]{1,0:T(8,128)(2,1)S(1)}, bf16[384,256]{1,0:T(8,128)(2,1)S(1)}, u32[]{:S(2)}, u32[]{:S(2)}) collective-permute-start(bf16[384,256]{1,0:T(8,128)(2,1)S(1)} %slice.246), channel_id=1, source_target_pairs={{0,16},{16,0},{1,17},{17,1},{2,18},{18,2},{3,19},{19,3},{4,20},{20... | collective-permute-start | bytes 589832 | tf_op jit(solution)/shard_map/ppermute | solution.py:21
  (42 other events, 259.0 us)
Sparse Core Ops, SparseCore 0:
  10.6 73.4 all-gather.2
  85.7 37.3 all-gather.4

commit v5 on v4

--- a/solution.py
+++ b/solution.py
@@ -2,6 +2,7 @@
 import jax.numpy as jnp
 from jax import lax
 from jax.experimental import pallas as pl
+from jax.experimental.pallas import tpu as pltpu
 from jax.sharding import PartitionSpec as P
 
 epsilon = 1e-06
@@ -19,17 +20,6 @@
 def swapped(x, axis):
     length = lax.axis_size(axis)
     return lax.ppermute(x, axis, [(i, length - 1 - i) for i in range(length)])
-
-
-def passed_across(x, by):
-    group_count, length = lax.axis_size("groups"), lax.axis_size("seq")
-    pairs = [
-        (g * length + i, (group_count - 1 - g) * length + i + by)
-        for g in range(group_count)
-        for i in range(length)
-        if 0 <= i + by < length
-    ]
-    return lax.ppermute(x, ("groups", "seq"), pairs)
 
 
 def passed_on(x, axis, by, came_from):
@@ -38,10 +28,6 @@
         (i, i + by) for i in range(length) if 0 <= i + by < length and 0 <= i + came_from < length
     ]
     return lax.ppermute(x, axis, pairs)
-
-
-def neighbours(block):
-    return passed_along(block, "seq", 1), passed_along(block, "seq", -1)
 
 
 def second_neighbours(right, left):
@@ -61,6 +47,57 @@
         input_output_aliases={0: 0},
         name="after",
     )(value, *others)
+
+
+def byte_sums_kernel(shard_ref, bounds_ref, cotangent_ref, query_ref, key_ref, *refs):
+    blocks, out_ref = refs[:-1], refs[-1]
+    rows, width = query_ref.shape
+    span_rows = blocks[reach].shape[0]
+    shard = shard_ref[0]
+    row = lax.broadcasted_iota(jnp.int32, (rows, 1), 0)
+    held = (bounds_ref[...] <= shard * rows + row).astype(jnp.float32)
+    span_of = jnp.sum(held, 1, keepdims=True).astype(jnp.int32) - 1
+    place = span_of - (shard - reach) * span_rows
+    column = lax.broadcasted_iota(jnp.int32, (rows, span_rows), 1)
+    pickers = [
+        (place - i * span_rows == column).astype(jnp.float32).astype(jnp.bfloat16)
+        for i in range(len(blocks))
+    ]
+    last_row = blocks[reach - 1].shape[0] - 1
+    tile = 384
+    totals = [jnp.zeros((rows, 128), jnp.float32)] * 4
+    for start in range(0, width, tile):
+        cols = pl.ds(start, tile)
+        upsampled = jnp.zeros((rows, tile), jnp.float32)
+        for picker, block in zip(pickers, blocks):
+            upsampled = upsampled + jnp.dot(
+                picker, block[:span_rows, cols], preferred_element_type=jnp.float32
+            )
+        query = query_ref[:, cols].astype(jnp.float32)
+        previous = pltpu.roll(key_ref[:, cols].astype(jnp.float32), 1, 0)
+        edge = blocks[reach - 1][last_row - 15 :, cols].astype(jnp.float32)[15:16]
+        previous = jnp.where(row == 0, edge, previous)
+        cotangent = cotangent_ref[:, cols].astype(jnp.float32)
+        terms = [query * previous, query * query, previous * previous, cotangent * upsampled]
+        for piece in range(0, tile, 128):
+            totals = [
+                total + term[:, piece : piece + 128] for total, term in zip(totals, terms)
+            ]
+    lines = [jnp.sum(total.T, 0, keepdims=True) for total in totals]
+    out_ref[...] = jnp.concatenate(lines + [jnp.zeros((4, rows), jnp.float32)], 0)
+
+
+def byte_sums(shard_index, bounds, cotangent, query_rows, key_rows, blocks):
+    rows = query_rows.shape[0]
+    vmem = pl.BlockSpec(memory_space=pltpu.VMEM)
+    return pl.pallas_call(
+        byte_sums_kernel,
+        out_shape=jax.ShapeDtypeStruct((8, rows), jnp.float32),
+        in_specs=[pl.BlockSpec(memory_space=pltpu.SMEM)] + [vmem] * (4 + len(blocks)),
+        out_specs=vmem,
+        compiler_params=pltpu.CompilerParams(vmem_limit_bytes=40 * 1024 * 1024),
+        name="byte_sums",
+    )(shard_index[None], bounds, cotangent, query_rows, key_rows, *blocks)
 
 
 def product(rows, weight):
@@ -90,7 +127,8 @@
 
     first_rows = group_rows * 2 // 3 // 16 * 16
     cuts = [(0, first_rows), (first_rows, group_rows)]
-    out_right, out_left = neighbours(main_out[0])
+    out_right = passed_along(jnp.concatenate([main_out[0], key_rows[-16:]], 0), "seq", 1)
+    out_left = passed_along(jnp.concatenate([main_out[0], query_rows[:16]], 0), "seq", -1)
     query_other = swapped(query_rows, "groups")
     key_other = swapped(key_rows, "groups")
     own_weights = []
@@ -110,39 +148,24 @@
             piece = after(piece, out_right)
         own_weights.append(lax.all_gather(piece, "seq", axis=0, tiled=True))
     out_far_right, out_far_left = second_neighbours(out_right, out_left)
-    out_far_left = after(out_far_left, query_other, key_other)
-    window_out = jnp.concatenate(
-        [out_far_right, out_right, main_out[0], out_left, out_far_left], 0
-    )
-    last_key = passed_along(key_rows[-1:], "seq", 1)
-    next_query = passed_along(query_rows[:1], "seq", -1)
-    last_key_other = passed_across(key_rows[-1:], 1)
-    next_query_other = passed_across(query_rows[:1], -1)
+    last_key, next_query = out_right[-1:], out_left[span_rows : span_rows + 1]
+    edges_other = swapped(jnp.concatenate([last_key, next_query], 0), "groups")
+    last_key_other, next_query_other = edges_other[:1], edges_other[1:]
+    blocks = [out_far_right, out_right, main_out[0], out_left, out_far_left]
+    sums = byte_sums(shard_index, boundaries, cotangent, query_rows, key_rows, blocks)
 
     positions = shard_index * row_count + jnp.arange(row_count, dtype=jnp.int32)
     span_of = jnp.sum((bounds_row[None, :] <= positions[:, None]).astype(jnp.int32), 1) - 1
     starts = jnp.any(bounds_row[None, :] == positions[:, None], 1)
     place = span_of - (shard_index - reach) * span_rows
-    window_rows = window_out.shape[0]
+    window_rows = (2 * reach + 1) * span_rows
     selector = place[:, None] == jnp.arange(window_rows, dtype=jnp.int32)[None, :]
-    upsampled = jnp.dot(selector.astype(jnp.bfloat16), window_out, preferred_element_type=jnp.float32)
-    prev_keys = jnp.concatenate([last_key, key_rows[:-1]], 0)
-    query_wide = query_rows.astype(jnp.float32)
-    prev_wide = prev_keys.astype(jnp.float32)
     cotangent_wide = cotangent.astype(jnp.float32)
-    sums = jnp.stack(
-        [
-            jnp.sum(query_wide * prev_wide, 1),
-            jnp.sum(query_wide * query_wide, 1),
-            jnp.sum(prev_wide * prev_wide, 1),
-            jnp.sum(cotangent_wide * upsampled, 1),
-        ]
-    )
     if tensor_count == 2:
         sums = sums + swapped(sums, "tensor")
     else:
         sums = lax.psum(sums, "tensor")
-    cross_sum, query_sum, key_sum, conf_grad = sums
+    cross_sum, query_sum, key_sum, conf_grad = sums[:4]
     query_scale = lax.rsqrt(query_sum + epsilon)
     key_scale = lax.rsqrt(key_sum + epsilon)
     cosine = cross_sum * query_scale * key_scale
@@ -158,14 +181,14 @@
         ]
     )
     next_factors = passed_along(factors[:, :1], "seq", -1)
+    factors = jnp.concatenate([factors, next_factors], 1)
     factors_other = swapped(factors, "groups")
-    next_factors_other = passed_across(factors[:, :1], -1)
-
-    def grads(queries_here, keys_here, key_before, query_after, here, after_here, index):
+
+    def grads(queries_here, keys_here, key_before, query_after, here, index):
         previous = jnp.concatenate([columns(key_before, index), columns(keys_here, index)[:-1]], 0)
         current = columns(queries_here, index)
         following = jnp.concatenate([current[1:], columns(query_after, index)], 0)
-        ahead = jnp.concatenate([here[:, 1:], after_here], 1)
+        ahead, here = here[:, 1:], here[:, :-1]
         query_grad = here[0][:, None] * previous.astype(jnp.float32)
         query_grad = query_grad - here[1][:, None] * current.astype(jnp.float32)
         key_grad = ahead[0][:, None] * following.astype(jnp.float32)
@@ -173,47 +196,48 @@
         return jnp.concatenate([query_grad.astype(jnp.bfloat16), key_grad.astype(jnp.bfloat16)], 1)
 
     def both_grads(index):
-        own = grads(query_rows, key_rows, last_key, next_query, factors, next_factors, index)
+        own = grads(query_rows, key_rows, last_key, next_query, factors, index)
         other = grads(
             query_other,
             key_other,
             last_key_other,
             next_query_other,
             factors_other,
-            next_factors_other,
             index,
         )
         return jnp.concatenate([own, other], 0)
 
     own_side, other_side = both_grads(pipe_index), both_grads(1 - pipe_index)
 
-    conf_high = confidence.astype(jnp.bfloat16)
-    conf_low = (confidence - conf_high.astype(jnp.float32)).astype(jnp.bfloat16)
-    zero_weight = jnp.zeros((), jnp.bfloat16)
-    weight_high = jnp.where(selector, conf_high[:, None], zero_weight)
-    weight_low = jnp.where(selector, conf_low[:, None], zero_weight)
-    contract = (((0,), (0,)), ((), ()))
-    span_terms = lax.dot_general(
-        weight_high, cotangent, contract, preferred_element_type=jnp.float32
-    )
-    span_terms = span_terms + lax.dot_general(
-        weight_low, cotangent, contract, preferred_element_type=jnp.float32
-    )
-    terms = [span_terms[i * span_rows : (i + 1) * span_rows] for i in range(2 * reach + 1)]
-
-    def moved(block, by, further):
-        moved_block = passed_on(block.astype(jnp.bfloat16), "seq", by, further)
-        return moved_block.astype(jnp.float32)
-
-    span_sums = terms[2] + moved(terms[3] + moved(terms[4], 1, 2), 1, 1)
-    span_sums = span_sums + moved(terms[1] + moved(terms[0], -1, -2), -1, -1)
-    main_grad = span_sums.astype(jnp.bfloat16)[None]
-    grad_right, grad_left = neighbours(after(main_in_grad[0], own_weights[0]))
-    grad_far_right, grad_far_left = second_neighbours(grad_right, grad_left)
-    window_grad = jnp.concatenate(
-        [grad_far_right, grad_right, main_in_grad[0], grad_left, grad_far_left], 0
-    )
-    start_picker = (selector & starts[:, None]).astype(jnp.bfloat16)
+    def span_part(ready):
+        conf_high = confidence.astype(jnp.bfloat16)
+        conf_low = (confidence - conf_high.astype(jnp.float32)).astype(jnp.bfloat16)
+        zero_weight = jnp.zeros((), jnp.bfloat16)
+        weight_high = jnp.where(selector, conf_high[:, None], zero_weight)
+        weight_low = jnp.where(selector, conf_low[:, None], zero_weight)
+        contract = (((0,), (0,)), ((), ()))
+        span_terms = lax.dot_general(
+            weight_high, cotangent, contract, preferred_element_type=jnp.float32
+        )
+        span_terms = span_terms + lax.dot_general(
+            weight_low, cotangent, contract, preferred_element_type=jnp.float32
+        )
+        terms = [span_terms[i * span_rows : (i + 1) * span_rows] for i in range(2 * reach + 1)]
+
+        def moved(block, by, further):
+            moved_block = passed_on(block.astype(jnp.bfloat16), "seq", by, further)
+            return moved_block.astype(jnp.float32)
+
+        outer = after(jnp.stack([terms[0], terms[4]]).astype(jnp.bfloat16), ready)
+        span_sums = terms[2] + moved(terms[3] + moved(outer[1], 1, 2), 1, 1)
+        span_sums = span_sums + moved(terms[1] + moved(outer[0], -1, -2), -1, -1)
+        return span_sums.astype(jnp.bfloat16)[None]
+
+    window_grad = lax.all_gather(
+        after(main_in_grad[0], own_weights[0]), "seq", axis=0, tiled=True
+    )
+    span_index = jnp.arange(window_grad.shape[0], dtype=jnp.int32)
+    start_picker = ((span_of[:, None] == span_index[None, :]) & starts[:, None]).astype(jnp.bfloat16)
     start_grad = jnp.dot(start_picker, window_grad, preferred_element_type=jnp.float32)
 
     def partial(own_weight, other_weight):
@@ -221,7 +245,7 @@
         return total.astype(jnp.bfloat16)
 
     pieces = []
-    far_part = None
+    far_part, main_grad = None, None
     for own_weight in own_weights:
         if far_part is not None:
             own_weight = after(own_weight, far_part)
@@ -244,8 +268,8 @@
             ).astype(jnp.float32)
         own = total[:row_count]
         returned = total[row_count:].astype(jnp.bfloat16)
-        if not pieces:
-            returned = after(returned, grad_right, grad_left)
+        if main_grad is None:
+            main_grad = span_part(returned)
         arrived = swapped(returned, "groups").astype(jnp.float32)
         pieces.append(
             [jnp.where(group_index == 0, own, arrived), jnp.where(group_index == 0, arrived, own)]

time: 236 us -> 211 us (0.89)
  the two profiles are of different devices: /device:TPU:16 before, /device:TPU:0 now
where the time goes in v5:
time: 211 us; the launch traced here: 210 us
  waiting for transfers between devices  89.2 us (42%)
  starting transfers between devices  40.8 us (19%)
  matrix products  23.1 us (11%)
  other arithmetic  19.4 us (9%)
  local copies, waits for them, and re-layouts  19.3 us (9%)
  between operations  14.6 us (7%)
  Pallas kernels  3.62 us (2%)
    ppermute x11, waiting for transfers between devices, swapped(): return lax.ppermute(x, axis, [(i, length - 1 - i) for i in range(length)])  35.7 us
    ppermute x6, waiting for transfers between devices, passed_on(): return lax.ppermute(x, axis, pairs)  33.9 us
    ppermute x6, starting transfers between devices, passed_on(): return lax.ppermute(x, axis, pairs)  19.3 us
    dot_general x8, matrix products, product(): lax.dot_general(rows, weight, (((1,), (1,)), ((), ())), preferred_element...  15.3 us
    ppermute x11, starting transfers between devices, swapped(): return lax.ppermute(x, axis, [(i, length - 1 - i) for i in range(length)])  12.3 us
    ppermute x3, waiting for transfers between devices, passed_along(): return lax.ppermute(x, axis, pairs)  9.93 us
    all_gather x2, waiting for transfers between devices, shards(): own_weights.append(lax.all_gather(piece, 'seq', axis=0, tiled=True))  9.56 us
    ppermute x3, starting transfers between devices, passed_along(): return lax.ppermute(x, axis, pairs)  9.06 us
  transfers between devices with their start and end apart: 23, of which 11 were waited for; matrix products, arithmetic and copies ran while one was open for 24% of the time, Pallas kernels for 2%

profile of v5, /device:TPU:0, one launch (start us, length us, event | category | flops | bytes accessed | tf_op | source)
XLA Modules:
  0.0 210.0 jit_solution(5393872191753921374)
XLA Ops:
  7.2 2.0 copy.38
  9.2 1.0 dynamic_slice.89
  10.2 1.0 dynamic_slice.88
  13.3 1.3 collective-permute-start.2
  14.6 6.3 %collective-permute-start = (bf16[144,1536]{1,0:T(8,128)(2,1)}, bf16[144,1536]{1,0:T(8,128)(2,1)}, u32[]{:S(2)}, u32[]{:S(2)}) collective-permute-start(bf16[144,1536]{1,0:T(8,128)(2,1)} %get-tuple-element.42), channel_id=1, source_target_pairs={{0,4},{4,8},{8,12},{1,5},{5,9},{9,13},{2,6},{6,10},{10,14},{3,7},{... | collective-permute-start | bytes 1327112 | tf_op jit(solution)/shard_map/ppermute | solution.py:14
  20.9 2.0 collective-permute-start.9
  23.5 1.1 dynamic-slice_bitcast_fusion.1
  24.6 1.7 dynamic-slice_bitcast_fusion
  28.2 7.4 %collective-permute-done.2.refs_3_ = bf16[144,1536]{1,0:T(8,128)(2,1)} collective-permute-done((bf16[144,1536]{1,0:T(8,128)(2,1)}, bf16[144,1536]{1,0:T(8,128)(2,1)}, u32[]{:S(2)}, u32[]{:S(2)}) %collective-permute-start.2) | collective-permute-done | bytes 442400 | tf_op jit(solution)/shard_map/ppermute | solution.py:14
  38.5 2.0 collective-permute-start.7
  42.4 1.3 collective-permute-start.3
  43.7 30.1 %collective-permute-done.7 = bf16[2,1536]{1,0:T(2,128)(2,1)S(1)} collective-permute-done((bf16[2,1536]{1,0:T(2,128)(2,1)}, bf16[2,1536]{1,0:T(2,128)(2,1)S(1)}, u32[]{:S(2)}, u32[]{:S(2)}) %collective-permute-start.7) | collective-permute-done | bytes 6176 | tf_op jit(solution)/shard_map/ppermute | solution.py:22
  74.4 9.7 %collective-permute-done.3.refs_4_ = bf16[144,1536]{1,0:T(8,128)(2,1)S(1)} collective-permute-done((bf16[144,1536]{1,0:T(8,128)(2,1)}, bf16[144,1536]{1,0:T(8,128)(2,1)S(1)}, u32[]{:S(2)}, u32[]{:S(2)}) %collective-permute-start.3) | collective-permute-done | bytes 442400 | tf_op jit(solution)/shard_map/ppermute | solution.py:30
  85.1 3.6 %byte_sums.1 = f32[8,384]{1,0:T(8,128)S(1)} custom-call(s32[1]{0:T(128)} %bitcast.3.shard_ref, s32[1,512]{1,0:T(1,128)S(1)} %copy-done.5, bf16[384,1536]{1,0:T(8,128)(2,1)S(1)} %bitcast.51, bf16[384,1536]{1,0:T(8,128)(2,1)S(1)} %bitcast.53, bf16[384,1536]{1,0:T(8,128)(2,1)S(1)} %bitcast.55, bf16[144,1536]{1,0:T(8,128)(2,1)S(1)} %collective-permute-done.1.refs_0_, ...), custom_call_target="tpu_custom_call" | custom-call | tf_op jit(solution)/shard_map/byte_sums/pallas_call | solution.py:93
  88.7 1.9 collective-permute-start.4
  91.2 1.3 collective-permute-done.4
  92.5 1.2 slice_reduce_fusion.7
  95.0 1.5 collective-permute-start.5
  97.2 1.3 fusion.43
  98.6 3.2 %fusion.76 = (bf16[640,1536]{1,0:T(8,128)(2,1)S(1)}, f32[640,1536]{1,0:T(8,128)}) fusion(f32[640,1536]{1,0:T(8,128)S(1)} %fusion.43, bf16[1,384,1536]{2,1,0:T(8,128)(2,1)S(1)} %copy-done, s32[384]{0:T(512)S(1)} %get-tuple-element.61, bf16[384]{0:T(512)(128)(2,1)S(1)} %get-tuple-element.12), kind=kOutput, calls=%fused_computation.160 | convolution fusion | flops 757432320 | bytes 11012352 | tf_op jit(solution)/shard_map/dot_general | solution.py:222
  101.8 1.7 collective-permute-done.5
  103.6 1.6 collective-permute-start.6
  105.3 1.9 fusion.22
  107.5 2.5 %fusion.74 = (bf16[383,768]{1,0:T(8,128)(2,1)S(1)}, bf16[383,768]{1,0:T(8,128)(2,1)S(1)}) fusion(bf16[384,1536]{1,0:T(8,128)(2,1)} %collective-permute-done.9, s32[]{:T(128)S(6)} %add.223, s32[]{:T(128)S(6)} %select_n.148, s32[]{:T(128)} %select_n.142), kind=kLoop, calls=%fused_computation.158 | loop fusion | bytes 2353164 | tf_op jit(solution)/shard_map/slice | solution.py:190
  109.9 1.3 constant_dynamic-slice_fusion
  111.3 3.2 %subtract_convert_fusion = (bf16[384,768]{1,0:T(8,128)(2,1)S(1)}, bf16[384,768]{1,0:T(8,128)(2,1)S(1)}, bf16[384,768]{1,0:T(8,128)(2,1)S(1)}, bf16[384,768]{1,0:T(8,128)(2,1)S(1)}) fusion(bf16[1,768]{1,0:T(2,128)(2,1)S(1)} %copy-done.31, bf16[383,768]{1,0:T(8,128)(2,1)S(1)} %get-tuple-element.36, bf16[384,1536]{1,0:T(8,128)(2,1)} %collective-permute-done.8, ...), kind=kLoop, calls=%fused_computation.36 | loop fusion | flops 10616832 | bytes 7084040 | tf_op jit(solution)/shard_map/convert_element_type | solution.py:196
  114.6 1.4 fusion.5
  116.1 1.4 add_convert_fusion.refs_1_
  117.8 1.5 collective-permute-start.11
  120.4 2.6 %fusion.9 = f32[768,512]{1,0:T(8,128)} fusion(bf16[1024,1536]{1,0:T(8,128)(2,1)S(1)} %copy-done.6, s32[]{:T(128)S(6)} %select_n.147, bf16[384,768]{1,0:T(8,128)(2,1)S(1)} %get-tuple-element.29, bf16[384,768]{1,0:T(8,128)(2,1)S(1)} %get-tuple-element.67, bf16[384,768]{1,0:T(8,128)(2,1)S(1)} %get-tuple-element.25, bf16[384,768]{1,0:T(8,128)(2,1)S(1)} %get-tuple-element.65), kind=kOutput, calls=%fused_computation.16 | convolution fusion | flops 1217396736 | bytes 5505028 | tf_op jit(solution)/shard_map/dot_general | solution.py:104
  123.0 9.6 %all-gather.8.cloned.1.call-done.refs_0_ = bf16[512,1536]{1,0:T(8,128)(2,1)} async-done(((bf16[128,1536]{1,0:T(8,128)(2,1)}), bf16[512,1536]{1,0:T(8,128)(2,1)}) %all-gather.8.cloned.1.call-update) | async-done | bytes 1572880 | tf_op jit(solution)/shard_map/all_gather | solution.py:149
  132.5 4.2 %collective-permute-done.11 = bf16[768,512]{1,0:T(8,128)(2,1)} collective-permute-done((bf16[768,512]{1,0:T(8,128)(2,1)S(1)}, bf16[768,512]{1,0:T(8,128)(2,1)}, u32[]{:S(2)}, u32[]{:S(2)}) %collective-permute-start.11) | collective-permute-done | bytes 786464 | tf_op jit(solution)/shard_map/ppermute | solution.py:22
  136.8 4.3 %convert_add_fusion = f32[768,512]{1,0:T(8,128)S(1)} fusion(bf16[768,512]{1,0:T(8,128)(2,1)} %collective-permute-done.11, f32[768,512]{1,0:T(8,128)} %fusion.9, bf16[1024,1536]{1,0:T(8,128)(2,1)} %copy-done.43, s32[]{:T(128)S(6)} %select_n.147, bf16[384,768]{1,0:T(8,128)(2,1)} %copy-done.26, bf16[384,768]{1,0:T(8,128)(2,1)} %copy-done.28, ...), kind=kOutput, calls=%fused_computation.7 | convolution fusion | flops 1219362816 | bytes 7864324 | tf_op jit(solution)/shard_map/dot_general | solution.py:104
  141.8 2.0 slice_bitcast_fusion.1
  143.9 6.8 %collective-permute-start.16 = (bf16[128,1536]{1,0:T(8,128)(2,1)}, bf16[128,1536]{1,0:T(8,128)(2,1)S(1)}, u32[]{:S(2)}, u32[]{:S(2)}) collective-permute-start(bf16[128,1536]{1,0:T(8,128)(2,1)} %get-tuple-element.40), channel_id=1, source_target_pairs={{0,4},{4,8},{1,5},{5,9},{2,6},{6,10},{3,7},{7,11},{16,20},{20,24},... | collective-permute-start | bytes 1179656 | tf_op jit(solution)/shard_map/ppermute | solution.py:30
  150.7 1.4 collective-permute-start.18
  152.2 1.3 convert_select_fusion
  153.5 5.4 %collective-permute-done.16 = bf16[128,1536]{1,0:T(8,128)(2,1)S(1)} collective-permute-done((bf16[128,1536]{1,0:T(8,128)(2,1)}, bf16[128,1536]{1,0:T(8,128)(2,1)S(1)}, u32[]{:S(2)}, u32[]{:S(2)}) %collective-permute-start.16) | collective-permute-done | bytes 393248 | tf_op jit(solution)/shard_map/ppermute | solution.py:30
  158.9 1.7 fusion.32
  160.8 2.1 %fusion.35 = f32[768,256]{1,0:T(8,128)S(1)} fusion(bf16[512,1536]{1,0:T(8,128)(2,1)} %collective-permute-done.13, s32[]{:T(128)S(6)} %select_n.154, bf16[384,768]{1,0:T(8,128)(2,1)S(1)} %copy-done.27, bf16[384,768]{1,0:T(8,128)(2,1)S(1)} %copy-done.29, bf16[384,768]{1,0:T(8,128)(2,1)S(1)} %copy-done.19, bf16[384,768]{1,0:T(8,128)(2,1)S(1)} %copy-done.21), kind=kOutput, calls=%fused_computation.55 | convolution fusion | flops 613416960 | bytes 3932164 | tf_op jit(solution)/shard_map/dot_general | solution.py:104
  163.9 1.6 collective-permute-start.14
  165.5 1.3 collective-permute-start.19
  166.8 7.8 %collective-permute-start.17 = (bf16[128,1536]{1,0:T(8,128)(2,1)S(1)}, bf16[128,1536]{1,0:T(8,128)(2,1)S(1)}, u32[]{:S(2)}, u32[]{:S(2)}) collective-permute-start(bf16[128,1536]{1,0:T(8,128)(2,1)S(1)} %get-tuple-element.16), channel_id=1, source_target_pairs={{0,4},{4,8},{8,12},{1,5},{5,9},{9,13},{2,6},{6,10},{10,14},{3,7},{... | collective-permute-start | bytes 1179656 | tf_op jit(solution)/shard_map/ppermute | solution.py:30
  174.7 1.9 fusion.38
  177.5 1.1 collective-permute-start.15
  178.7 18.8 %collective-permute-done.19 = bf16[128,1536]{1,0:T(8,128)(2,1)S(1)} collective-permute-done((bf16[128,1536]{1,0:T(8,128)(2,1)S(1)}, bf16[128,1536]{1,0:T(8,128)(2,1)S(1)}, u32[]{:S(2)}, u32[]{:S(2)}) %collective-permute-start.19) | collective-permute-done | bytes 393248 | tf_op jit(solution)/shard_map/ppermute | solution.py:30
  197.5 2.0 fusion.48
  200.2 3.2 %fusion.2 = bf16[1,384,1536]{2,1,0:T(8,128)(2,1)} fusion(f32[384,1536]{1,0:T(8,128)S(1)} %slice_dynamic-update-slice_fusion.4, bf16[512,1536]{1,0:T(8,128)(2,1)} %all-gather.6.cloned.1.call-done, s32[384]{0:T(512)S(1)} %copy-done.39, pred[384]{0:T(512)(128)(4,1)S(1)} %copy-done.41, bf16[1,384,1536]{2,1,0:T(8,128)(2,1)S(1)} %copy-done), kind=kOutput, calls=%fused_computation.4 | convolution fusion | flops 606732288 | bytes 6293376 | tf_op jit(solution)/shard_map/dot_general | solution.py:241
  (162 shorter events, 18.6 us)
Async XLA Ops:
  7.2 5.1 %copy-start.2 = (bf16[1,384,1536]{2,1,0:T(8,128)(2,1)S(1)}, bf16[1,384,1536]{2,1,0:T(8,128)(2,1)}, u32[]{:S(2)}) copy-start(bf16[1,384,1536]{2,1,0:T(8,128)(2,1)} %param.10) | copy-start | bytes 3538948
  7.2 5.1 %copy-start.1 = (bf16[1,384,1536]{2,1,0:T(8,128)(2,1)S(1)}, bf16[1,384,1536]{2,1,0:T(8,128)(2,1)}, u32[]{:S(2)}) copy-start(bf16[1,384,1536]{2,1,0:T(8,128)(2,1)} %param.9) | copy-start | bytes 3538948
  7.2 5.1 %copy-start.3 = (bf16[1,128,1536]{2,1,0:T(8,128)(2,1)S(1)}, bf16[1,128,1536]{2,1,0:T(8,128)(2,1)}, u32[]{:S(2)}) copy-start(bf16[1,128,1536]{2,1,0:T(8,128)(2,1)} %param.11) | copy-start | bytes 1179652
  7.2 86.5 %all-gather.4.cloned.1.call-start = ((), (), s32[]{:S(2)}) async-start(), calls=%async_computation | async-start | bytes 3932160 | tf_op jit(solution)/shard_map/all_gather | solution.py:149
  11.3 11.7 %copy-start.5 = (s32[1,512]{1,0:T(1,128)S(1)}, s32[1,512]{1,0:T(1,128)}, u32[]{:S(2)}) copy-start(s32[1,512]{1,0:T(1,128)} %bounds_ref.1) | copy-start | bytes 6148
  12.2 120.3 %all-gather.8.cloned.1.call-start = ((), (), s32[]{:S(2)}) async-start(), calls=%async_computation.2 | async-start | bytes 1966080 | tf_op jit(solution)/shard_map/all_gather | solution.py:149
  13.3 22.3 %collective-permute-start.2 = (bf16[144,1536]{1,0:T(8,128)(2,1)}, bf16[144,1536]{1,0:T(8,128)(2,1)}, u32[]{:S(2)}, u32[]{:S(2)}) collective-permute-start(bf16[144,1536]{1,0:T(8,128)(2,1)} %get-tuple-element.43), channel_id=1, source_target_pairs={{4,0},{8,4},{12,8},{5,1},{9,5},{13,9},{6,2},{10,6},{14,10},{7,3},{... | collective-permute-start | bytes 1327112 | tf_op jit(solution)/shard_map/ppermute | solution.py:14
  14.6 22.5 %collective-permute-start = (bf16[144,1536]{1,0:T(8,128)(2,1)}, bf16[144,1536]{1,0:T(8,128)(2,1)}, u32[]{:S(2)}, u32[]{:S(2)}) collective-permute-start(bf16[144,1536]{1,0:T(8,128)(2,1)} %get-tuple-element.42), channel_id=1, source_target_pairs={{0,4},{4,8},{8,12},{1,5},{5,9},{9,13},{2,6},{6,10},{10,14},{3,7},{... | collective-permute-start | bytes 1327112 | tf_op jit(solution)/shard_map/ppermute | solution.py:14
  20.9 86.5 %collective-permute-start.9 = (bf16[384,1536]{1,0:T(8,128)(2,1)S(1)}, bf16[384,1536]{1,0:T(8,128)(2,1)}, u32[]{:S(2)}, u32[]{:S(2)}) collective-permute-start(bf16[384,1536]{1,0:T(8,128)(2,1)S(1)} %bitcast.52), channel_id=1, source_target_pairs={{0,16},{16,0},{1,17},{17,1},{2,18},{18,2},{3,19},{19,3},{4,20},{20... | collective-permute-start | bytes 3538952 | tf_op jit(solution)/shard_map/ppermute | solution.py:22
  22.9 87.1 %collective-permute-start.8 = (bf16[384,1536]{1,0:T(8,128)(2,1)S(1)}, bf16[384,1536]{1,0:T(8,128)(2,1)}, u32[]{:S(2)}, u32[]{:S(2)}) collective-permute-start(bf16[384,1536]{1,0:T(8,128)(2,1)S(1)} %bitcast.54), channel_id=1, source_target_pairs={{0,16},{16,0},{1,17},{17,1},{2,18},{18,2},{3,19},{19,3},{4,20},{20... | collective-permute-start | bytes 3538952 | tf_op jit(solution)/shard_map/ppermute | solution.py:22
  24.6 59.5 %copy-start = (bf16[1,384,1536]{2,1,0:T(8,128)(2,1)S(1)}, bf16[1,384,1536]{2,1,0:T(8,128)(2,1)}, u32[]{:S(2)}) copy-start(bf16[1,384,1536]{2,1,0:T(8,128)(2,1)} %param.8) | copy-start | bytes 3538948
  38.5 35.3 %collective-permute-start.7 = (bf16[2,1536]{1,0:T(2,128)(2,1)}, bf16[2,1536]{1,0:T(2,128)(2,1)S(1)}, u32[]{:S(2)}, u32[]{:S(2)}) collective-permute-start(bf16[2,1536]{1,0:T(2,128)(2,1)} %pad_maximum_fusion.6), channel_id=1, source_target_pairs={{0,16},{16,0},{1,17},{17,1},{2,18},{18,2},{3,19},{19,3},{4,20},{20... | collective-permute-start | bytes 18440 | tf_op jit(solution)/shard_map/ppermute | solution.py:22
  41.6 158.2 %all-gather.6.cloned.1.call-start = ((), (), s32[]{:S(2)}) async-start(), calls=%async_computation.1 | async-start | bytes 1966080 | tf_op jit(solution)/shard_map/all_gather | solution.py:236
  41.7 32.7 %collective-permute-start.1 = (bf16[144,1536]{1,0:T(8,128)(2,1)}, bf16[144,1536]{1,0:T(8,128)(2,1)S(1)}, u32[]{:S(2)}, u32[]{:S(2)}) collective-permute-start(bf16[144,1536]{1,0:T(8,128)(2,1)} %collective-permute-done.refs_1_), channel_id=1, source_target_pairs={{4,8},{8,12},{5,9},{9,13},{6,10},{10,14},{7,11},{11,15},{20,24},{2... | collective-permute-start | bytes 1327112 | tf_op jit(solution)/shard_map/ppermute | solution.py:30
  42.4 41.7 %collective-permute-start.3 = (bf16[144,1536]{1,0:T(8,128)(2,1)}, bf16[144,1536]{1,0:T(8,128)(2,1)S(1)}, u32[]{:S(2)}, u32[]{:S(2)}) collective-permute-start(bf16[144,1536]{1,0:T(8,128)(2,1)} %collective-permute-done.2.refs_3_), channel_id=1, source_target_pairs={{4,0},{8,4},{5,1},{9,5},{6,2},{10,6},{7,3},{11,7},{20,16},{24,20},... | collective-permute-start | bytes 1327112 | tf_op jit(solution)/shard_map/ppermute | solution.py:30
  85.1 7.4 %copy-start.42 = (f32[384]{0:T(512)S(1)}, f32[384]{0:T(512)}, u32[]{:S(2)}) copy-start(f32[384]{0:T(512)} %select_multiply_fusion) | copy-start | bytes 4612
  88.7 3.8 %collective-permute-start.4 = (f32[8,384]{1,0:T(8,128)S(1)}, f32[8,384]{1,0:T(8,128)S(1)}, u32[]{:S(2)}, u32[]{:S(2)}) collective-permute-start(f32[8,384]{1,0:T(8,128)S(1)} %byte_sums.1), channel_id=1, source_target_pairs={{0,2},{2,0},{1,3},{3,1},{4,6},{6,4},{5,7},{7,5},{8,10},{10,8},{9,1... | collective-permute-start | bytes 36872 | tf_op jit(solution)/shard_map/ppermute | solution.py:22
  93.7 22.4 %collective-permute-start.10 = (bf16[1024,1536]{1,0:T(8,128)(2,1)}, bf16[1024,1536]{1,0:T(8,128)(2,1)S(1)}, u32[]{:S(2)}, u32[]{:S(2)}) collective-permute-start(bf16[1024,1536]{1,0:T(8,128)(2,1)} %all-gather.4.cloned.1.call-done.refs_1_), channel_id=1, source_target_pairs={{0,1},{1,0},{2,3},{3,2},{4,5},{5,4},{6,7},{7,6},{8,9},{9,8},{10,11... | collective-permute-start | bytes 9437192 | tf_op jit(solution)/shard_map/ppermute | solution.py:22
  95.0 8.6 %collective-permute-start.5 = (f32[3,1]{1,0:T(4,128)S(1)}, f32[3,1]{1,0:T(4,128)S(1)}, u32[]{:S(2)}, u32[]{:S(2)}) collective-permute-start(f32[3,1]{1,0:T(4,128)S(1)} %pad_maximum_fusion.7), channel_id=1, source_target_pairs={{4,0},{8,4},{12,8},{5,1},{9,5},{13,9},{6,2},{10,6},{14,10},{7,3},{... | collective-permute-start | bytes 44 | tf_op jit(solution)/shard_map/ppermute | solution.py:14
  98.5 6.7 %copy-start.7 = (bf16[383,768]{1,0:T(8,128)(2,1)S(1)}, bf16[383,768]{1,0:T(8,128)(2,1)}, u32[]{:S(2)}) copy-start(bf16[383,768]{1,0:T(8,128)(2,1)} %get-tuple-element.30) | copy-start | bytes 1764868
  98.5 6.7 %copy-start.8 = (bf16[383,768]{1,0:T(8,128)(2,1)S(1)}, bf16[383,768]{1,0:T(8,128)(2,1)}, u32[]{:S(2)}) copy-start(bf16[383,768]{1,0:T(8,128)(2,1)} %get-tuple-element.31) | copy-start | bytes 1764868
  98.6 6.7 %copy-start.9 = (bf16[383,768]{1,0:T(8,128)(2,1)S(1)}, bf16[383,768]{1,0:T(8,128)(2,1)}, u32[]{:S(2)}) copy-start(bf16[383,768]{1,0:T(8,128)(2,1)} %get-tuple-element.32) | copy-start | bytes 1764868
  98.6 6.7 %copy-start.10 = (bf16[383,768]{1,0:T(8,128)(2,1)S(1)}, bf16[383,768]{1,0:T(8,128)(2,1)}, u32[]{:S(2)}) copy-start(bf16[383,768]{1,0:T(8,128)(2,1)} %get-tuple-element.33) | copy-start | bytes 1764868
  98.6 6.7 %copy-start.33 = (bf16[1,768]{1,0:T(2,128)(2,1)S(1)}, bf16[1,768]{1,0:T(2,128)(2,1)}, u32[]{:S(2)}) copy-start(bf16[1,768]{1,0:T(2,128)(2,1)} %get-tuple-element.53) | copy-start | bytes 4612
  98.6 6.7 %copy-start.34 = (bf16[1,768]{1,0:T(2,128)(2,1)S(1)}, bf16[1,768]{1,0:T(2,128)(2,1)}, u32[]{:S(2)}) copy-start(bf16[1,768]{1,0:T(2,128)(2,1)} %get-tuple-element.54) | copy-start | bytes 4612
  98.6 6.7 %copy-start.35 = (bf16[1,768]{1,0:T(2,128)(2,1)S(1)}, bf16[1,768]{1,0:T(2,128)(2,1)}, u32[]{:S(2)}) copy-start(bf16[1,768]{1,0:T(2,128)(2,1)} %get-tuple-element.51) | copy-start | bytes 4612
  98.6 6.7 %copy-start.36 = (bf16[1,768]{1,0:T(2,128)(2,1)S(1)}, bf16[1,768]{1,0:T(2,128)(2,1)}, u32[]{:S(2)}) copy-start(bf16[1,768]{1,0:T(2,128)(2,1)} %get-tuple-element.52) | copy-start | bytes 4612
  103.6 3.7 %collective-permute-start.6 = (f32[3,385]{1,0:T(4,128)S(1)}, f32[3,385]{1,0:T(4,128)S(1)}, u32[]{:S(2)}, u32[]{:S(2)}) collective-permute-start(f32[3,385]{1,0:T(4,128)S(1)} %pad_maximum_fusion.5), channel_id=1, source_target_pairs={{0,16},{16,0},{1,17},{17,1},{2,18},{18,2},{3,19},{19,3},{4,20},{20... | collective-permute-start | bytes 13868 | tf_op jit(solution)/shard_map/ppermute | solution.py:22
  107.2 8.9 %copy-start.18 = (bf16[384,768]{1,0:T(8,128)(2,1)}, bf16[384,768]{1,0:T(8,128)(2,1)S(1)}, u32[]{:S(2)}) copy-start(bf16[384,768]{1,0:T(8,128)(2,1)S(1)} %get-tuple-element.24) | copy-start | bytes 1769476
  107.2 8.9 %copy-start.20 = (bf16[384,768]{1,0:T(8,128)(2,1)}, bf16[384,768]{1,0:T(8,128)(2,1)S(1)}, u32[]{:S(2)}) copy-start(bf16[384,768]{1,0:T(8,128)(2,1)S(1)} %get-tuple-element.66) | copy-start | bytes 1769476
  107.2 13.2 %copy-start.14 = (bf16[384,768]{1,0:T(8,128)(2,1)}, bf16[384,768]{1,0:T(8,128)(2,1)S(1)}, u32[]{:S(2)}) copy-start(bf16[384,768]{1,0:T(8,128)(2,1)S(1)} %get-tuple-element.25) | copy-start | bytes 1769476
  107.2 13.2 %copy-start.16 = (bf16[384,768]{1,0:T(8,128)(2,1)}, bf16[384,768]{1,0:T(8,128)(2,1)S(1)}, u32[]{:S(2)}) copy-start(bf16[384,768]{1,0:T(8,128)(2,1)S(1)} %get-tuple-element.65) | copy-start | bytes 1769476
  114.6 5.8 %copy-start.22 = (bf16[384,768]{1,0:T(8,128)(2,1)}, bf16[384,768]{1,0:T(8,128)(2,1)S(1)}, u32[]{:S(2)}) copy-start(bf16[384,768]{1,0:T(8,128)(2,1)S(1)} %get-tuple-element.29) | copy-start | bytes 1769476
  114.6 5.8 %copy-start.24 = (bf16[384,768]{1,0:T(8,128)(2,1)}, bf16[384,768]{1,0:T(8,128)(2,1)S(1)}, u32[]{:S(2)}) copy-start(bf16[384,768]{1,0:T(8,128)(2,1)S(1)} %get-tuple-element.67) | copy-start | bytes 1769476
  117.8 5.1 %copy-start.13 = (bf16[768,512]{1,0:T(8,128)(2,1)}, bf16[768,512]{1,0:T(8,128)(2,1)S(1)}, u32[]{:S(2)}) copy-start(bf16[768,512]{1,0:T(8,128)(2,1)S(1)} %add_convert_fusion.refs_1_) | copy-start | bytes 2359300
  117.8 18.9 %collective-permute-start.11 = (bf16[768,512]{1,0:T(8,128)(2,1)S(1)}, bf16[768,512]{1,0:T(8,128)(2,1)}, u32[]{:S(2)}, u32[]{:S(2)}) collective-permute-start(bf16[768,512]{1,0:T(8,128)(2,1)S(1)} %add_convert_fusion.refs_1_), channel_id=1, source_target_pairs={{0,2},{2,0},{1,3},{3,1},{4,6},{6,4},{5,7},{7,5},{8,10},{10,8},{9,1... | collective-permute-start | bytes 2359304 | tf_op jit(solution)/shard_map/ppermute | solution.py:22
  132.5 28.2 %collective-permute-start.13 = (bf16[512,1536]{1,0:T(8,128)(2,1)}, bf16[512,1536]{1,0:T(8,128)(2,1)}, u32[]{:S(2)}, u32[]{:S(2)}) collective-permute-start(bf16[512,1536]{1,0:T(8,128)(2,1)} %after.6), channel_id=1, source_target_pairs={{0,1},{1,0},{2,3},{3,2},{4,5},{5,4},{6,7},{7,6},{8,9},{9,8},{10,11... | collective-permute-start | bytes 4718600 | tf_op jit(solution)/shard_map/ppermute | solution.py:22
  141.1 11.1 %collective-permute-start.12 = (bf16[384,512]{1,0:T(8,128)(2,1)S(1)}, bf16[384,512]{1,0:T(8,128)(2,1)}, u32[]{:S(2)}, u32[]{:S(2)}) collective-permute-start(bf16[384,512]{1,0:T(8,128)(2,1)S(1)} %slice.279.refs_1_), channel_id=1, source_target_pairs={{0,16},{16,0},{1,17},{17,1},{2,18},{18,2},{3,19},{19,3},{4,20},{20... | collective-permute-start | bytes 1179656 | tf_op jit(solution)/shard_map/ppermute | solution.py:22
  143.9 15.0 %collective-permute-start.16 = (bf16[128,1536]{1,0:T(8,128)(2,1)}, bf16[128,1536]{1,0:T(8,128)(2,1)S(1)}, u32[]{:S(2)}, u32[]{:S(2)}) collective-permute-start(bf16[128,1536]{1,0:T(8,128)(2,1)} %get-tuple-element.40), channel_id=1, source_target_pairs={{0,4},{4,8},{1,5},{5,9},{2,6},{6,10},{3,7},{7,11},{16,20},{20,24},... | collective-permute-start | bytes 1179656 | tf_op jit(solution)/shard_map/ppermute | solution.py:30
  150.7 8.2 %collective-permute-start.18 = (bf16[128,1536]{1,0:T(8,128)(2,1)}, bf16[128,1536]{1,0:T(8,128)(2,1)}, u32[]{:S(2)}, u32[]{:S(2)}) collective-permute-start(bf16[128,1536]{1,0:T(8,128)(2,1)} %get-tuple-element.41), channel_id=1, source_target_pairs={{8,4},{12,8},{9,5},{13,9},{10,6},{14,10},{11,7},{15,11},{24,20},{2... | collective-permute-start | bytes 1179656 | tf_op jit(solution)/shard_map/ppermute | solution.py:30
  152.1 8.6 %copy-start.19 = (bf16[384,768]{1,0:T(8,128)(2,1)S(1)}, bf16[384,768]{1,0:T(8,128)(2,1)}, u32[]{:S(2)}) copy-start(bf16[384,768]{1,0:T(8,128)(2,1)} %copy-done.18) | copy-start | bytes 1769476
  152.1 8.6 %copy-start.21 = (bf16[384,768]{1,0:T(8,128)(2,1)S(1)}, bf16[384,768]{1,0:T(8,128)(2,1)}, u32[]{:S(2)}) copy-start(bf16[384,768]{1,0:T(8,128)(2,1)} %copy-done.20) | copy-start | bytes 1769476
  152.1 8.6 %copy-start.27 = (bf16[384,768]{1,0:T(8,128)(2,1)S(1)}, bf16[384,768]{1,0:T(8,128)(2,1)}, u32[]{:S(2)}) copy-start(bf16[384,768]{1,0:T(8,128)(2,1)} %copy-done.26) | copy-start | bytes 1769476
  152.2 8.6 %copy-start.29 = (bf16[384,768]{1,0:T(8,128)(2,1)S(1)}, bf16[384,768]{1,0:T(8,128)(2,1)}, u32[]{:S(2)}) copy-start(bf16[384,768]{1,0:T(8,128)(2,1)} %copy-done.28) | copy-start | bytes 1769476
  163.9 12.7 %collective-permute-start.14 = (bf16[768,256]{1,0:T(8,128)(2,1)S(1)}, bf16[768,256]{1,0:T(8,128)(2,1)S(1)}, u32[]{:S(2)}, u32[]{:S(2)}) collective-permute-start(bf16[768,256]{1,0:T(8,128)(2,1)S(1)} %fusion.20), channel_id=1, source_target_pairs={{0,2},{2,0},{1,3},{3,1},{4,6},{6,4},{5,7},{7,5},{8,10},{10,8},{9,1... | collective-permute-start | bytes 1179656 | tf_op jit(solution)/shard_map/ppermute | solution.py:22
  165.5 32.0 %collective-permute-start.19 = (bf16[128,1536]{1,0:T(8,128)(2,1)S(1)}, bf16[128,1536]{1,0:T(8,128)(2,1)S(1)}, u32[]{:S(2)}, u32[]{:S(2)}) collective-permute-start(bf16[128,1536]{1,0:T(8,128)(2,1)S(1)} %get-tuple-element.17), channel_id=1, source_target_pairs={{4,0},{8,4},{12,8},{5,1},{9,5},{13,9},{6,2},{10,6},{14,10},{7,3},{... | collective-permute-start | bytes 1179656 | tf_op jit(solution)/shard_map/ppermute | solution.py:30
  166.8 30.7 %collective-permute-start.17 = (bf16[128,1536]{1,0:T(8,128)(2,1)S(1)}, bf16[128,1536]{1,0:T(8,128)(2,1)S(1)}, u32[]{:S(2)}, u32[]{:S(2)}) collective-permute-start(bf16[128,1536]{1,0:T(8,128)(2,1)S(1)} %get-tuple-element.16), channel_id=1, source_target_pairs={{0,4},{4,8},{8,12},{1,5},{5,9},{9,13},{2,6},{6,10},{10,14},{3,7},{... | collective-permute-start | bytes 1179656 | tf_op jit(solution)/shard_map/ppermute | solution.py:30
  177.5 22.0 %collective-permute-start.15 = (bf16[384,256]{1,0:T(8,128)(2,1)S(1)}, bf16[384,256]{1,0:T(8,128)(2,1)S(1)}, u32[]{:S(2)}, u32[]{:S(2)}) collective-permute-start(bf16[384,256]{1,0:T(8,128)(2,1)S(1)} %slice.280), channel_id=1, source_target_pairs={{0,16},{16,0},{1,17},{17,1},{2,18},{18,2},{3,19},{19,3},{4,20},{20... | collective-permute-start | bytes 589832 | tf_op jit(solution)/shard_map/ppermute | solution.py:22
  (21 other events, 54.7 us)
Sparse Core Ops, SparseCore 0:
  12.4 77.9 all-gather.3
  92.5 40.0 all-gather.7
  152.2 45.4 all-gather.5

commit v6 on v5

--- a/solution.py
+++ b/solution.py
@@ -28,10 +28,6 @@
         (i, i + by) for i in range(length) if 0 <= i + by < length and 0 <= i + came_from < length
     ]
     return lax.ppermute(x, axis, pairs)
-
-
-def second_neighbours(right, left):
-    return passed_on(right, "seq", 1, -1), passed_on(left, "seq", -1, 1)
 
 
 def after(value, *others):
@@ -125,29 +121,22 @@
     def columns(x, index):
         return lax.dynamic_slice_in_dim(x, index * half_cols, half_cols, 1)
 
-    first_rows = group_rows * 2 // 3 // 16 * 16
-    cuts = [(0, first_rows), (first_rows, group_rows)]
+    own_piece = jnp.concatenate(
+        [
+            lax.dynamic_slice(
+                weight, (group_index * group_rows, pipe_index * half_cols), (group_rows, half_cols)
+            )
+            for weight in (query_weight, key_weight)
+        ],
+        1,
+    )
+    own_weight = lax.all_gather(own_piece, "seq", axis=0, tiled=True)
     out_right = passed_along(jnp.concatenate([main_out[0], key_rows[-16:]], 0), "seq", 1)
     out_left = passed_along(jnp.concatenate([main_out[0], query_rows[:16]], 0), "seq", -1)
+    out_far_right = passed_along(main_out[0], "seq", 2)
+    out_far_left = passed_along(main_out[0], "seq", -2)
     query_other = swapped(query_rows, "groups")
     key_other = swapped(key_rows, "groups")
-    own_weights = []
-    for low, high in cuts:
-        piece = jnp.concatenate(
-            [
-                lax.dynamic_slice(
-                    weight,
-                    (group_index * group_rows + low, pipe_index * half_cols),
-                    (high - low, half_cols),
-                )
-                for weight in (query_weight, key_weight)
-            ],
-            1,
-        )
-        if own_weights:
-            piece = after(piece, out_right)
-        own_weights.append(lax.all_gather(piece, "seq", axis=0, tiled=True))
-    out_far_right, out_far_left = second_neighbours(out_right, out_left)
     last_key, next_query = out_right[-1:], out_left[span_rows : span_rows + 1]
     edges_other = swapped(jnp.concatenate([last_key, next_query], 0), "groups")
     last_key_other, next_query_other = edges_other[:1], edges_other[1:]
@@ -195,19 +184,10 @@
         key_grad = key_grad - ahead[2][:, None] * columns(keys_here, index).astype(jnp.float32)
         return jnp.concatenate([query_grad.astype(jnp.bfloat16), key_grad.astype(jnp.bfloat16)], 1)
 
-    def both_grads(index):
-        own = grads(query_rows, key_rows, last_key, next_query, factors, index)
-        other = grads(
-            query_other,
-            key_other,
-            last_key_other,
-            next_query_other,
-            factors_other,
-            index,
-        )
-        return jnp.concatenate([own, other], 0)
-
-    own_side, other_side = both_grads(pipe_index), both_grads(1 - pipe_index)
+    own_tokens = (query_rows, key_rows, last_key, next_query, factors)
+    other_tokens = (query_other, key_other, last_key_other, next_query_other, factors_other)
+    own_sides = [grads(*own_tokens, pipe_index), grads(*own_tokens, 1 - pipe_index)]
+    other_sides = [grads(*other_tokens, pipe_index), grads(*other_tokens, 1 - pipe_index)]
 
     def span_part(ready):
         conf_high = confidence.astype(jnp.bfloat16)
@@ -234,53 +214,46 @@
         return span_sums.astype(jnp.bfloat16)[None]
 
     window_grad = lax.all_gather(
-        after(main_in_grad[0], own_weights[0]), "seq", axis=0, tiled=True
+        after(main_in_grad[0], factors_other), "seq", axis=0, tiled=True
     )
     span_index = jnp.arange(window_grad.shape[0], dtype=jnp.int32)
     start_picker = ((span_of[:, None] == span_index[None, :]) & starts[:, None]).astype(jnp.bfloat16)
     start_grad = jnp.dot(start_picker, window_grad, preferred_element_type=jnp.float32)
 
-    def partial(own_weight, other_weight):
-        total = product(own_side, own_weight) + product(other_side, other_weight)
+    main_grad = span_part(factors_other)
+
+    def partial(sides, weights):
+        total = product(sides[0], weights[0]) + product(sides[1], weights[1])
         return total.astype(jnp.bfloat16)
 
-    pieces = []
-    far_part, main_grad = None, None
-    for own_weight in own_weights:
-        if far_part is not None:
-            own_weight = after(own_weight, far_part)
-        other_weight = swapped(own_weight, "pipe")
-        block_rows = own_weight.shape[0] // tensor_count
-        if tensor_count == 2:
-
-            def half(index):
-                return [
-                    lax.dynamic_slice_in_dim(weight, index * block_rows, block_rows, 0)
-                    for weight in (own_weight, other_weight)
-                ]
-
-            far_part = partial(*half(1 - tensor_index))
-            incoming = swapped(far_part, "tensor").astype(jnp.float32)
-            total = partial(*half(tensor_index)).astype(jnp.float32) + incoming
-        else:
-            total = lax.psum_scatter(
-                partial(own_weight, other_weight), "tensor", scatter_dimension=1, tiled=True
+    block_rows = own_weight.shape[0] // tensor_count
+    if tensor_count == 2:
+
+        def both(index):
+            own = lax.dynamic_slice_in_dim(own_weight, index * block_rows, block_rows, 0)
+            return own, swapped(own, "pipe")
+
+        far, near = both(1 - tensor_index), both(tensor_index)
+        other_far = swapped(partial(other_sides, far), "tensor")
+        own_far = swapped(partial(own_sides, far), "tensor")
+        other_sum = partial(other_sides, near).astype(jnp.float32) + other_far.astype(jnp.float32)
+        own_sum = partial(own_sides, near).astype(jnp.float32) + own_far.astype(jnp.float32)
+    else:
+        weights = own_weight, swapped(own_weight, "pipe")
+        other_sum, own_sum = [
+            lax.psum_scatter(
+                partial(sides, weights), "tensor", scatter_dimension=1, tiled=True
             ).astype(jnp.float32)
-        own = total[:row_count]
-        returned = total[row_count:].astype(jnp.bfloat16)
-        if main_grad is None:
-            main_grad = span_part(returned)
-        arrived = swapped(returned, "groups").astype(jnp.float32)
-        pieces.append(
-            [jnp.where(group_index == 0, own, arrived), jnp.where(group_index == 0, arrived, own)]
-        )
-    widths = [high - low for low, high in cuts]
+            for sides in (other_sides, own_sides)
+        ]
+    arrived = swapped(other_sum.astype(jnp.bfloat16), "groups").astype(jnp.float32)
+    first = jnp.where(group_index == 0, own_sum, arrived)
+    second = jnp.where(group_index == 0, arrived, own_sum)
     routing = jnp.concatenate(
         [
-            piece[group][:, s * width : (s + 1) * width]
-            for s in range(seq_count // tensor_count)
-            for group in range(2)
-            for piece, width in zip(pieces, widths)
+            side[:, low : low + group_rows]
+            for low in range(0, block_rows, group_rows)
+            for side in (first, second)
         ],
         1,
     )

time: 211 us -> 216 us (1.024)
  other arithmetic: 19.4 us -> 15.6 us
  waiting for transfers between devices: 89.2 us -> 92.7 us
  local copies, waits for them, and re-layouts: 19.3 us -> 21.5 us
    ppermute x3 -> x5, waiting for transfers between devices: 9.93 us -> 53.7 us  [passed_along(): return lax.ppermute(x, axis, pairs)]
    ppermute x6 -> x4, waiting for transfers between devices: 33.9 us -> 4.71 us  [passed_on(): return lax.ppermute(x, axis, pairs)]
    all_gather x3 -> x2, waiting for transfers between devices: 9.58 us -> 1.63 us  [the longest x1 1.63 us: shards(): own_weight = lax.all_gather(own_piece, 'seq', axis=0, tiled=True)]
    ppermute x3 -> x5, starting transfers between devices: 9.06 us -> 14.9 us  [passed_along(): return lax.ppermute(x, axis, pairs)]
    dynamic_slice x6 -> x5, local copies, waits for them, and re-layouts: 2.07 us -> 6.13 us  [the longest x1 4.89 us: both(): lax.dynamic_slice_in_dim(own_weight, index * block_rows, block_rows, 0)]
    ppermute x11 -> x10, waiting for transfers between devices: 35.7 us -> 32.6 us  [swapped(): return lax.ppermute(x, axis, [(i, length - 1 - i) for i in range(length)])]
    ppermute x6 -> x4, starting transfers between devices: 19.3 us -> 17.3 us  [passed_on(): return lax.ppermute(x, axis, pairs)]
    ppermute x11 -> x10, starting transfers between devices: 12.3 us -> 10.6 us  [swapped(): return lax.ppermute(x, axis, [(i, length - 1 - i) for i in range(length)])]
  transfers between devices with their start and end apart: 23 -> 21, of which waited for: 11 -> 9; matrix products, arithmetic and copies ran while one was open for 24% -> 24% of each run, Pallas kernels for 2% -> 2%
where the time goes in v6:
time: 216 us; the launch traced here: 215 us
  waiting for transfers between devices  92.7 us (43%)
  starting transfers between devices  42.9 us (20%)
  matrix products  24.1 us (11%)
  local copies, waits for them, and re-layouts  21.5 us (10%)
  other arithmetic  15.6 us (7%)
  between operations  14.5 us (7%)
  Pallas kernels  3.96 us (2%)
    ppermute x5, waiting for transfers between devices, passed_along(): return lax.ppermute(x, axis, pairs)  53.7 us
    ppermute x10, waiting for transfers between devices, swapped(): return lax.ppermute(x, axis, [(i, length - 1 - i) for i in range(length)])  32.6 us
    ppermute x4, starting transfers between devices, passed_on(): return lax.ppermute(x, axis, pairs)  17.3 us
    dot_general x8, matrix products, product(): lax.dot_general(rows, weight, (((1,), (1,)), ((), ())), preferred_element...  15.9 us
    ppermute x5, starting transfers between devices, passed_along(): return lax.ppermute(x, axis, pairs)  14.9 us
    ppermute x10, starting transfers between devices, swapped(): return lax.ppermute(x, axis, [(i, length - 1 - i) for i in range(length)])  10.6 us
    dynamic_slice x1, local copies, waits for them, and re-layouts, both(): lax.dynamic_slice_in_dim(own_weight, index * block_rows, block_rows, 0)  4.89 us
    convert_element_type x2, other arithmetic, grads(): key_grad.astype(jnp.bfloat16)  4.8 us
  transfers between devices with their start and end apart: 21, of which 9 were waited for; matrix products, arithmetic and copies ran while one was open for 24% of the time, Pallas kernels for 2%

profile of v6, /device:TPU:0, one launch (start us, length us, event | category | flops | bytes accessed | tf_op | source)
XLA Modules:
  0.0 215.3 jit_solution(12049582561543485392)
XLA Ops:
  7.2 1.8 copy.15
  11.4 6.8 %collective-permute-start = (bf16[128,1536]{1,0:T(8,128)(2,1)}, bf16[128,1536]{1,0:T(8,128)(2,1)}, u32[]{:S(2)}, u32[]{:S(2)}) collective-permute-start(bf16[128,1536]{1,0:T(8,128)(2,1)} %bitcast.6.refs_2_), channel_id=1, source_target_pairs={{0,8},{4,12},{1,9},{5,13},{2,10},{6,14},{3,11},{7,15},{16,24},{20,... | collective-permute-start | bytes 1179656 | tf_op jit(solution)/shard_map/ppermute | solution.py:14
  18.3 1.3 collective-permute-start.3
  19.6 2.0 pad_maximum_fusion.15
  21.6 4.2 %collective-permute-start.1 = (bf16[144,1536]{1,0:T(8,128)(2,1)}, bf16[144,1536]{1,0:T(8,128)(2,1)}, u32[]{:S(2)}, u32[]{:S(2)}) collective-permute-start(bf16[144,1536]{1,0:T(8,128)(2,1)} %get-tuple-element.47), channel_id=1, source_target_pairs={{0,4},{4,8},{8,12},{1,5},{5,9},{9,13},{2,6},{6,10},{10,14},{3,7},{... | collective-permute-start | bytes 1327112 | tf_op jit(solution)/shard_map/ppermute | solution.py:14
  25.9 1.3 collective-permute-start.2
  27.1 1.6 collective-permute-start.12
  29.3 1.6 dynamic-slice_bitcast_fusion
  31.5 37.4 %collective-permute-done.2.refs_3_ = bf16[144,1536]{1,0:T(8,128)(2,1)} collective-permute-done((bf16[144,1536]{1,0:T(8,128)(2,1)}, bf16[144,1536]{1,0:T(8,128)(2,1)}, u32[]{:S(2)}, u32[]{:S(2)}) %collective-permute-start.2) | collective-permute-done | bytes 442400 | tf_op jit(solution)/shard_map/ppermute | solution.py:14
  68.9 1.5 collective-permute-start.11
  73.2 4.0 %byte_sums.1 = f32[8,384]{1,0:T(8,128)S(1)} custom-call(s32[1]{0:T(128)} %bitcast.3.shard_ref, s32[1,512]{1,0:T(1,128)S(1)} %copy-done.3, bf16[384,1536]{1,0:T(8,128)(2,1)S(1)} %bitcast.63, bf16[384,1536]{1,0:T(8,128)(2,1)S(1)} %bitcast.60, bf16[384,1536]{1,0:T(8,128)(2,1)S(1)} %bitcast.62, bf16[128,1536]{1,0:T(8,128)(2,1)} %collective-permute-done.refs_0_, ...), custom_call_target="tpu_custom_call" | custom-call | tf_op jit(solution)/shard_map/byte_sums/pallas_call | solution.py:89
  77.1 1.5 collective-permute-start.4
  78.7 15.9 %collective-permute-done.10 = bf16[2,1536]{1,0:T(2,128)(2,1)S(1)} collective-permute-done((bf16[2,1536]{1,0:T(2,128)(2,1)S(1)}, bf16[2,1536]{1,0:T(2,128)(2,1)S(1)}, u32[]{:S(2)}, u32[]{:S(2)}) %collective-permute-start.10) | collective-permute-done | bytes 6176 | tf_op jit(solution)/shard_map/ppermute | solution.py:22
  95.9 1.3 collective-permute-start.5
  97.3 1.7 fusion.15
  99.0 1.3 fusion.32
  100.3 3.3 %fusion.67 = (bf16[640,1536]{1,0:T(8,128)(2,1)S(1)}, f32[640,1536]{1,0:T(8,128)}) fusion(f32[640,1536]{1,0:T(8,128)S(1)} %fusion.32, bf16[1,384,1536]{2,1,0:T(8,128)(2,1)S(1)} %copy-done.2, s32[384]{0:T(512)S(1)} %get-tuple-element.65, bf16[384]{0:T(512)(128)(2,1)S(1)} %get-tuple-element.12), kind=kOutput, calls=%fused_computation.147 | convolution fusion | flops 757432320 | bytes 11012352 | tf_op jit(solution)/shard_map/dot_general | solution.py:202
  103.7 16.4 %collective-permute-done.5 = f32[3,1]{1,0:T(4,128)S(1)} collective-permute-done((f32[3,1]{1,0:T(4,128)S(1)}, f32[3,1]{1,0:T(4,128)S(1)}, u32[]{:S(2)}, u32[]{:S(2)}) %collective-permute-start.5) | collective-permute-done | bytes 44 | tf_op jit(solution)/shard_map/ppermute | solution.py:14
  120.1 1.6 collective-permute-start.6
  122.6 1.1 collective-permute-done.6.refs_1_
  124.4 1.6 all-gather.5.cloned.1.call-done
  126.0 4.9 %constant_dynamic-slice_fusion.6 = (bf16[768,1536]{1,0:T(8,128)(2,1)}, bf16[768,1536]{1,0:T(8,128)(2,1)}) fusion(bf16[1536,1536]{1,0:T(8,128)(2,1)} %all-gather.5.cloned.1.call-done, s32[]{:T(128)S(6)} %select_n.121, s32[]{:T(128)S(6)} %select_n.119), kind=kLoop, calls=%fused_computation.90 | loop fusion | bytes 9437192 | tf_op jit(solution)/shard_map/dynamic_slice | solution.py:233
  132.0 5.7 %collective-permute-start.15 = (bf16[128,1536]{1,0:T(8,128)(2,1)}, bf16[128,1536]{1,0:T(8,128)(2,1)}, u32[]{:S(2)}, u32[]{:S(2)}) collective-permute-start(bf16[128,1536]{1,0:T(8,128)(2,1)} %get-tuple-element.44), channel_id=1, source_target_pairs={{0,4},{4,8},{1,5},{5,9},{2,6},{6,10},{3,7},{7,11},{16,20},{20,24},... | collective-permute-start | bytes 1179656 | tf_op jit(solution)/shard_map/ppermute | solution.py:30
  137.7 1.4 collective-permute-start.17
  139.3 1.6 fusion.13
  141.6 4.7 %collective-permute-done.15 = bf16[128,1536]{1,0:T(8,128)(2,1)} collective-permute-done((bf16[128,1536]{1,0:T(8,128)(2,1)}, bf16[128,1536]{1,0:T(8,128)(2,1)}, u32[]{:S(2)}, u32[]{:S(2)}) %collective-permute-start.15) | collective-permute-done | bytes 393248 | tf_op jit(solution)/shard_map/ppermute | solution.py:30
  146.3 1.8 fusion.23
  148.1 1.3 collective-permute-start.18
  149.4 8.9 %collective-permute-start.16 = (bf16[128,1536]{1,0:T(8,128)(2,1)S(1)}, bf16[128,1536]{1,0:T(8,128)(2,1)S(1)}, u32[]{:S(2)}, u32[]{:S(2)}) collective-permute-start(bf16[128,1536]{1,0:T(8,128)(2,1)S(1)} %get-tuple-element.18), channel_id=1, source_target_pairs={{0,4},{4,8},{8,12},{1,5},{5,9},{9,13},{2,6},{6,10},{10,14},{3,7},{... | collective-permute-start | bytes 1179656 | tf_op jit(solution)/shard_map/ppermute | solution.py:30
  158.3 1.9 fusion.65
  160.2 1.3 constant_dynamic-slice_fusion.1
  161.6 3.2 %subtract_convert_fusion = (bf16[384,768]{1,0:T(8,128)(2,1)S(1)}, bf16[384,768]{1,0:T(8,128)(2,1)S(1)}, bf16[384,768]{1,0:T(8,128)(2,1)S(1)}, bf16[384,768]{1,0:T(8,128)(2,1)S(1)}) fusion(bf16[1,768]{1,0:T(2,128)(2,1)S(1)} %copy-done.16, bf16[383,768]{1,0:T(8,128)(2,1)S(1)} %get-tuple-element.38, bf16[384,1536]{1,0:T(8,128)(2,1)} %collective-permute-done.11, ...), kind=kLoop, calls=%fused_computation.37 | loop fusion | flops 10616832 | bytes 7084040 | tf_op jit(solution)/shard_map/convert_element_type | solution.py:185
  164.8 1.1 fusion.29
  166.0 2.8 %fusion.28 = f32[384,768]{1,0:T(8,128)S(1)} fusion(bf16[768,1536]{1,0:T(8,128)(2,1)} %get-tuple-element.16, bf16[384,768]{1,0:T(8,128)(2,1)S(1)} %get-tuple-element.27, bf16[384,768]{1,0:T(8,128)(2,1)S(1)} %get-tuple-element.69), kind=kOutput, calls=%fused_computation.56 | convolution fusion | flops 908328960 | bytes 4718592 | tf_op jit(solution)/shard_map/dot_general | solution.py:100
  168.8 2.9 %fusion.11 = bf16[384,768]{1,0:T(8,128)(2,1)S(1)} fusion(f32[384,768]{1,0:T(8,128)S(1)} %fusion.28, bf16[768,1536]{1,0:T(8,128)(2,1)} %collective-permute-done.8, bf16[384,768]{1,0:T(8,128)(2,1)S(1)} %get-tuple-element.26, bf16[384,768]{1,0:T(8,128)(2,1)S(1)} %get-tuple-element.70), kind=kOutput, calls=%fused_computation.19 | convolution fusion | flops 908918784 | bytes 5308416 | tf_op jit(solution)/shard_map/dot_general | solution.py:100
  171.7 1.6 collective-permute-start.13
  173.3 2.9 %fusion.30 = f32[384,768]{1,0:T(8,128)S(1)} fusion(bf16[768,1536]{1,0:T(8,128)(2,1)} %get-tuple-element.16, bf16[384,768]{1,0:T(8,128)(2,1)S(1)} %copy-done.11, bf16[384,768]{1,0:T(8,128)(2,1)S(1)} %copy-done.9), kind=kOutput, calls=%fused_computation.58 | convolution fusion | flops 908328960 | bytes 4718592 | tf_op jit(solution)/shard_map/dot_general | solution.py:100
  176.2 2.8 %fusion.6 = bf16[384,768]{1,0:T(8,128)(2,1)S(1)} fusion(f32[384,768]{1,0:T(8,128)S(1)} %fusion.30, bf16[768,1536]{1,0:T(8,128)(2,1)} %collective-permute-done.8, bf16[384,768]{1,0:T(8,128)(2,1)S(1)} %copy-done.10, bf16[384,768]{1,0:T(8,128)(2,1)S(1)} %copy-done.8), kind=kOutput, calls=%fused_computation.14 | convolution fusion | flops 908918784 | bytes 5308416 | tf_op jit(solution)/shard_map/dot_general | solution.py:100
  179.5 8.5 %collective-permute-done.13 = bf16[384,768]{1,0:T(8,128)(2,1)S(1)} collective-permute-done((bf16[384,768]{1,0:T(8,128)(2,1)S(1)}, bf16[384,768]{1,0:T(8,128)(2,1)S(1)}, u32[]{:S(2)}, u32[]{:S(2)}) %collective-permute-start.13) | collective-permute-done | bytes 589856 | tf_op jit(solution)/shard_map/ppermute | solution.py:22
  188.0 1.1 fusion.10
  189.1 1.6 collective-permute-start.14
  190.7 2.0 fusion.37
  192.7 1.1 fusion.31
  193.9 4.9 %collective-permute-done.9 = bf16[384,768]{1,0:T(8,128)(2,1)S(1)} collective-permute-done((bf16[384,768]{1,0:T(8,128)(2,1)S(1)}, bf16[384,768]{1,0:T(8,128)(2,1)S(1)}, u32[]{:S(2)}, u32[]{:S(2)}) %collective-permute-start.9) | collective-permute-done | bytes 589856 | tf_op jit(solution)/shard_map/ppermute | solution.py:22
  198.8 2.1 collective-permute-done.14
  200.9 1.2 convert_select_fusion.1
  203.2 1.1 fusion.63
  204.9 3.6 %fusion.2 = bf16[1,384,1536]{2,1,0:T(8,128)(2,1)} fusion(bf16[512,1536]{1,0:T(8,128)(2,1)} %all-gather.3.cloned.1.call-done, f32[384,384]{1,0:T(8,128)S(1)} %copy-done.13, f32[384,384]{1,0:T(8,128)} %get-tuple-element.33, f32[384,384]{1,0:T(8,128)S(1)} %copy-done.12, f32[384,384]{1,0:T(8,128)} %get-tuple-element.32, s32[384]{0:T(512)S(1)} %copy-done.24, ...), kind=kOutput, calls=%fused_computation.4 | convolution fusion | flops 608501760 | bytes 6293376 | tf_op jit(solution)/shard_map/dot_general | solution.py:221
  (106 shorter events, 13.4 us)
Async XLA Ops:
  7.2 118.8 %all-gather.5.cloned.1.call-start = ((), (), s32[]{:S(2)}) async-start(), calls=%async_computation.1 | async-start | bytes 5898240 | tf_op jit(solution)/shard_map/all_gather | solution.py:133
  9.0 1.1 dynamic-slice-start
  9.0 1.2 dynamic-slice-start.1
  10.2 9.3 %copy-start.1 = (bf16[1,384,1536]{2,1,0:T(8,128)(2,1)S(1)}, bf16[1,384,1536]{2,1,0:T(8,128)(2,1)}, u32[]{:S(2)}) copy-start(bf16[1,384,1536]{2,1,0:T(8,128)(2,1)} %param.10) | copy-start | bytes 3538948
  11.3 8.2 %copy-start = (bf16[1,384,1536]{2,1,0:T(8,128)(2,1)S(1)}, bf16[1,384,1536]{2,1,0:T(8,128)(2,1)}, u32[]{:S(2)}) copy-start(bf16[1,384,1536]{2,1,0:T(8,128)(2,1)} %param.9) | copy-start | bytes 3538948
  11.3 17.4 %copy-start.3 = (s32[1,512]{1,0:T(1,128)S(1)}, s32[1,512]{1,0:T(1,128)}, u32[]{:S(2)}) copy-start(s32[1,512]{1,0:T(1,128)} %bounds_ref.1) | copy-start | bytes 6148
  11.4 192.9 %all-gather.3.cloned.1.call-start = ((), (), s32[]{:S(2)}) async-start(), calls=%async_computation | async-start | bytes 1966080 | tf_op jit(solution)/shard_map/all_gather | solution.py:216
  11.4 61.7 %collective-permute-start = (bf16[128,1536]{1,0:T(8,128)(2,1)}, bf16[128,1536]{1,0:T(8,128)(2,1)}, u32[]{:S(2)}, u32[]{:S(2)}) collective-permute-start(bf16[128,1536]{1,0:T(8,128)(2,1)} %bitcast.6.refs_2_), channel_id=1, source_target_pairs={{0,8},{4,12},{1,9},{5,13},{2,10},{6,14},{3,11},{7,15},{16,24},{20,... | collective-permute-start | bytes 1179656 | tf_op jit(solution)/shard_map/ppermute | solution.py:14
  18.3 54.9 %collective-permute-start.3 = (bf16[128,1536]{1,0:T(8,128)(2,1)}, bf16[128,1536]{1,0:T(8,128)(2,1)}, u32[]{:S(2)}, u32[]{:S(2)}) collective-permute-start(bf16[128,1536]{1,0:T(8,128)(2,1)} %bitcast.6.refs_2_), channel_id=1, source_target_pairs={{8,0},{12,4},{9,1},{13,5},{10,2},{14,6},{11,3},{15,7},{24,16},{28,... | collective-permute-start | bytes 1179656 | tf_op jit(solution)/shard_map/ppermute | solution.py:14
  21.6 49.5 %collective-permute-start.1 = (bf16[144,1536]{1,0:T(8,128)(2,1)}, bf16[144,1536]{1,0:T(8,128)(2,1)}, u32[]{:S(2)}, u32[]{:S(2)}) collective-permute-start(bf16[144,1536]{1,0:T(8,128)(2,1)} %get-tuple-element.47), channel_id=1, source_target_pairs={{0,4},{4,8},{8,12},{1,5},{5,9},{9,13},{2,6},{6,10},{10,14},{3,7},{... | collective-permute-start | bytes 1327112 | tf_op jit(solution)/shard_map/ppermute | solution.py:14
  25.9 43.0 %collective-permute-start.2 = (bf16[144,1536]{1,0:T(8,128)(2,1)}, bf16[144,1536]{1,0:T(8,128)(2,1)}, u32[]{:S(2)}, u32[]{:S(2)}) collective-permute-start(bf16[144,1536]{1,0:T(8,128)(2,1)} %get-tuple-element.46), channel_id=1, source_target_pairs={{4,0},{8,4},{12,8},{5,1},{9,5},{13,9},{6,2},{10,6},{14,10},{7,3},{... | collective-permute-start | bytes 1327112 | tf_op jit(solution)/shard_map/ppermute | solution.py:14
  27.1 122.2 %collective-permute-start.12 = (bf16[384,1536]{1,0:T(8,128)(2,1)S(1)}, bf16[384,1536]{1,0:T(8,128)(2,1)}, u32[]{:S(2)}, u32[]{:S(2)}) collective-permute-start(bf16[384,1536]{1,0:T(8,128)(2,1)S(1)} %bitcast.59), channel_id=1, source_target_pairs={{0,16},{16,0},{1,17},{17,1},{2,18},{18,2},{3,19},{19,3},{4,20},{20... | collective-permute-start | bytes 3538952 | tf_op jit(solution)/shard_map/ppermute | solution.py:22
  29.0 68.2 %copy-start.22 = (pred[384]{0:T(512)(128)(4,1)}, pred[384]{0:T(512)(128)(4,1)S(1)}, u32[]{:S(2)}) copy-start(pred[384]{0:T(512)(128)(4,1)S(1)} %compare_reduce_fusion) | copy-start | bytes 1156
  29.3 43.9 %copy-start.2 = (bf16[1,384,1536]{2,1,0:T(8,128)(2,1)S(1)}, bf16[1,384,1536]{2,1,0:T(8,128)(2,1)}, u32[]{:S(2)}) copy-start(bf16[1,384,1536]{2,1,0:T(8,128)(2,1)} %param.8) | copy-start | bytes 3538948
  68.9 91.3 %collective-permute-start.11 = (bf16[384,1536]{1,0:T(8,128)(2,1)S(1)}, bf16[384,1536]{1,0:T(8,128)(2,1)}, u32[]{:S(2)}, u32[]{:S(2)}) collective-permute-start(bf16[384,1536]{1,0:T(8,128)(2,1)S(1)} %bitcast.61), channel_id=1, source_target_pairs={{0,16},{16,0},{1,17},{17,1},{2,18},{18,2},{3,19},{19,3},{4,20},{20... | collective-permute-start | bytes 3538952 | tf_op jit(solution)/shard_map/ppermute | solution.py:22
  71.9 22.7 %collective-permute-start.10 = (bf16[2,1536]{1,0:T(2,128)(2,1)S(1)}, bf16[2,1536]{1,0:T(2,128)(2,1)S(1)}, u32[]{:S(2)}, u32[]{:S(2)}) collective-permute-start(bf16[2,1536]{1,0:T(2,128)(2,1)S(1)} %pad_maximum_fusion.17), channel_id=1, source_target_pairs={{0,16},{16,0},{1,17},{17,1},{2,18},{18,2},{3,19},{19,3},{4,20},{20... | collective-permute-start | bytes 18440 | tf_op jit(solution)/shard_map/ppermute | solution.py:22
  77.1 18.7 %collective-permute-start.4 = (f32[8,384]{1,0:T(8,128)S(1)}, f32[8,384]{1,0:T(8,128)S(1)}, u32[]{:S(2)}, u32[]{:S(2)}) collective-permute-start(f32[8,384]{1,0:T(8,128)S(1)} %byte_sums.1), channel_id=1, source_target_pairs={{0,2},{2,0},{1,3},{3,1},{4,6},{6,4},{5,7},{7,5},{8,10},{10,8},{9,1... | collective-permute-start | bytes 36872 | tf_op jit(solution)/shard_map/ppermute | solution.py:22
  95.9 24.1 %collective-permute-start.5 = (f32[3,1]{1,0:T(4,128)S(1)}, f32[3,1]{1,0:T(4,128)S(1)}, u32[]{:S(2)}, u32[]{:S(2)}) collective-permute-start(f32[3,1]{1,0:T(4,128)S(1)} %pad_maximum_fusion.18), channel_id=1, source_target_pairs={{4,0},{8,4},{12,8},{5,1},{9,5},{13,9},{6,2},{10,6},{14,10},{7,3},{... | collective-permute-start | bytes 44 | tf_op jit(solution)/shard_map/ppermute | solution.py:14
  120.1 3.7 %collective-permute-start.6 = (f32[3,385]{1,0:T(4,128)S(1)}, f32[3,385]{1,0:T(4,128)S(1)}, u32[]{:S(2)}, u32[]{:S(2)}) collective-permute-start(f32[3,385]{1,0:T(4,128)S(1)} %pad_maximum_fusion.16), channel_id=1, source_target_pairs={{0,16},{16,0},{1,17},{17,1},{2,18},{18,2},{3,19},{19,3},{4,20},{20... | collective-permute-start | bytes 13868 | tf_op jit(solution)/shard_map/ppermute | solution.py:22
  123.8 0.6 copy-start.14
  126.0 5.0 %copy-start.4 = (bf16[2,128,1536]{2,1,0:T(8,128)(2,1)S(1)}, bf16[2,128,1536]{2,1,0:T(8,128)(2,1)}, u32[]{:S(2)}) copy-start(bf16[2,128,1536]{2,1,0:T(8,128)(2,1)} %after.3) | copy-start | bytes 2359300
  130.9 8.3 %copy-start.6 = (bf16[383,768]{1,0:T(8,128)(2,1)S(1)}, bf16[383,768]{1,0:T(8,128)(2,1)}, u32[]{:S(2)}) copy-start(bf16[383,768]{1,0:T(8,128)(2,1)} %get-tuple-element.42) | copy-start | bytes 1764868
  130.9 8.3 %copy-start.7 = (bf16[383,768]{1,0:T(8,128)(2,1)S(1)}, bf16[383,768]{1,0:T(8,128)(2,1)}, u32[]{:S(2)}) copy-start(bf16[383,768]{1,0:T(8,128)(2,1)} %get-tuple-element.43) | copy-start | bytes 1764868
  130.9 8.3 %copy-start.20 = (bf16[1,768]{1,0:T(2,128)(2,1)S(1)}, bf16[1,768]{1,0:T(2,128)(2,1)}, u32[]{:S(2)}) copy-start(bf16[1,768]{1,0:T(2,128)(2,1)} %get-tuple-element.63) | copy-start | bytes 4612
  130.9 8.3 %copy-start.21 = (bf16[1,768]{1,0:T(2,128)(2,1)S(1)}, bf16[1,768]{1,0:T(2,128)(2,1)}, u32[]{:S(2)}) copy-start(bf16[1,768]{1,0:T(2,128)(2,1)} %get-tuple-element.64) | copy-start | bytes 4612
  130.9 37.8 %collective-permute-start.8 = (bf16[768,1536]{1,0:T(8,128)(2,1)}, bf16[768,1536]{1,0:T(8,128)(2,1)}, u32[]{:S(2)}, u32[]{:S(2)}) collective-permute-start(bf16[768,1536]{1,0:T(8,128)(2,1)} %get-tuple-element.16), channel_id=1, source_target_pairs={{0,1},{1,0},{2,3},{3,2},{4,5},{5,4},{6,7},{7,6},{8,9},{9,8},{10,11... | collective-permute-start | bytes 7077896 | tf_op jit(solution)/shard_map/ppermute | solution.py:22
  132.0 14.3 %collective-permute-start.15 = (bf16[128,1536]{1,0:T(8,128)(2,1)}, bf16[128,1536]{1,0:T(8,128)(2,1)}, u32[]{:S(2)}, u32[]{:S(2)}) collective-permute-start(bf16[128,1536]{1,0:T(8,128)(2,1)} %get-tuple-element.44), channel_id=1, source_target_pairs={{0,4},{4,8},{1,5},{5,9},{2,6},{6,10},{3,7},{7,11},{16,20},{20,24},... | collective-permute-start | bytes 1179656 | tf_op jit(solution)/shard_map/ppermute | solution.py:30
  137.7 8.6 %collective-permute-start.17 = (bf16[128,1536]{1,0:T(8,128)(2,1)}, bf16[128,1536]{1,0:T(8,128)(2,1)}, u32[]{:S(2)}, u32[]{:S(2)}) collective-permute-start(bf16[128,1536]{1,0:T(8,128)(2,1)} %get-tuple-element.45), channel_id=1, source_target_pairs={{8,4},{12,8},{9,5},{13,9},{10,6},{14,10},{11,7},{15,11},{24,20},{2... | collective-permute-start | bytes 1179656 | tf_op jit(solution)/shard_map/ppermute | solution.py:30
  140.8 0.7 copy-start.15
  146.3 33.2 %collective-permute-start.7 = (bf16[768,1536]{1,0:T(8,128)(2,1)}, bf16[768,1536]{1,0:T(8,128)(2,1)S(1)}, u32[]{:S(2)}, u32[]{:S(2)}) collective-permute-start(bf16[768,1536]{1,0:T(8,128)(2,1)} %get-tuple-element.17), channel_id=1, source_target_pairs={{0,1},{1,0},{2,3},{3,2},{4,5},{5,4},{6,7},{7,6},{8,9},{9,8},{10,11... | collective-permute-start | bytes 7077896 | tf_op jit(solution)/shard_map/ppermute | solution.py:22
  148.1 42.6 %collective-permute-start.18 = (bf16[128,1536]{1,0:T(8,128)(2,1)S(1)}, bf16[128,1536]{1,0:T(8,128)(2,1)S(1)}, u32[]{:S(2)}, u32[]{:S(2)}) collective-permute-start(bf16[128,1536]{1,0:T(8,128)(2,1)S(1)} %get-tuple-element.19), channel_id=1, source_target_pairs={{4,0},{8,4},{12,8},{5,1},{9,5},{13,9},{6,2},{10,6},{14,10},{7,3},{... | collective-permute-start | bytes 1179656 | tf_op jit(solution)/shard_map/ppermute | solution.py:30
  149.4 41.3 %collective-permute-start.16 = (bf16[128,1536]{1,0:T(8,128)(2,1)S(1)}, bf16[128,1536]{1,0:T(8,128)(2,1)S(1)}, u32[]{:S(2)}, u32[]{:S(2)}) collective-permute-start(bf16[128,1536]{1,0:T(8,128)(2,1)S(1)} %get-tuple-element.18), channel_id=1, source_target_pairs={{0,4},{4,8},{8,12},{1,5},{5,9},{9,13},{2,6},{6,10},{10,14},{3,7},{... | collective-permute-start | bytes 1179656 | tf_op jit(solution)/shard_map/ppermute | solution.py:30
  160.1 1.4 copy-start.16
  160.2 1.4 copy-start.17
  160.2 1.4 copy-start.18
  160.2 1.4 copy-start.19
  161.6 3.3 %copy-start.5 = (bf16[768,1536]{1,0:T(8,128)(2,1)S(1)}, bf16[768,1536]{1,0:T(8,128)(2,1)}, u32[]{:S(2)}) copy-start(bf16[768,1536]{1,0:T(8,128)(2,1)} %get-tuple-element.17) | copy-start | bytes 7077892
  168.8 4.5 %copy-start.9 = (bf16[384,768]{1,0:T(8,128)(2,1)S(1)}, bf16[384,768]{1,0:T(8,128)(2,1)}, u32[]{:S(2)}) copy-start(bf16[384,768]{1,0:T(8,128)(2,1)} %get-tuple-element.29) | copy-start | bytes 1769476
  168.8 4.5 %copy-start.11 = (bf16[384,768]{1,0:T(8,128)(2,1)S(1)}, bf16[384,768]{1,0:T(8,128)(2,1)}, u32[]{:S(2)}) copy-start(bf16[384,768]{1,0:T(8,128)(2,1)} %get-tuple-element.31) | copy-start | bytes 1769476
  171.7 16.3 %collective-permute-start.13 = (bf16[384,768]{1,0:T(8,128)(2,1)S(1)}, bf16[384,768]{1,0:T(8,128)(2,1)S(1)}, u32[]{:S(2)}, u32[]{:S(2)}) collective-permute-start(bf16[384,768]{1,0:T(8,128)(2,1)S(1)} %fusion.11), channel_id=1, source_target_pairs={{0,2},{2,0},{1,3},{3,1},{4,6},{6,4},{5,7},{7,5},{8,10},{10,8},{9,1... | collective-permute-start | bytes 1769480 | tf_op jit(solution)/shard_map/ppermute | solution.py:22
  173.3 2.9 %copy-start.8 = (bf16[384,768]{1,0:T(8,128)(2,1)S(1)}, bf16[384,768]{1,0:T(8,128)(2,1)}, u32[]{:S(2)}) copy-start(bf16[384,768]{1,0:T(8,128)(2,1)} %get-tuple-element.28) | copy-start | bytes 1769476
  173.3 2.9 %copy-start.10 = (bf16[384,768]{1,0:T(8,128)(2,1)S(1)}, bf16[384,768]{1,0:T(8,128)(2,1)}, u32[]{:S(2)}) copy-start(bf16[384,768]{1,0:T(8,128)(2,1)} %get-tuple-element.30) | copy-start | bytes 1769476
  179.0 19.8 %collective-permute-start.9 = (bf16[384,768]{1,0:T(8,128)(2,1)S(1)}, bf16[384,768]{1,0:T(8,128)(2,1)S(1)}, u32[]{:S(2)}, u32[]{:S(2)}) collective-permute-start(bf16[384,768]{1,0:T(8,128)(2,1)S(1)} %fusion.6), channel_id=1, source_target_pairs={{0,2},{2,0},{1,3},{3,1},{4,6},{6,4},{5,7},{7,5},{8,10},{10,8},{9,1... | collective-permute-start | bytes 1769480 | tf_op jit(solution)/shard_map/ppermute | solution.py:22
  189.1 11.8 %collective-permute-start.14 = (bf16[384,768]{1,0:T(8,128)(2,1)S(1)}, bf16[384,768]{1,0:T(8,128)(2,1)S(1)}, u32[]{:S(2)}, u32[]{:S(2)}) collective-permute-start(bf16[384,768]{1,0:T(8,128)(2,1)S(1)} %fusion.10), channel_id=1, source_target_pairs={{0,16},{16,0},{1,17},{17,1},{2,18},{18,2},{3,19},{19,3},{4,20},{20... | collective-permute-start | bytes 1769480 | tf_op jit(solution)/shard_map/ppermute | solution.py:22
  203.2 1.3 copy-start.12
  203.2 1.7 copy-start.13
  203.2 1.7 copy-start.23
  203.2 1.7 copy-start.24
Sparse Core Ops, SparseCore 0:
  11.5 114.4 all-gather.4
  141.0 46.4 all-gather.2

commit v7 on v5

--- a/solution.py
+++ b/solution.py
@@ -20,18 +20,6 @@
 def swapped(x, axis):
     length = lax.axis_size(axis)
     return lax.ppermute(x, axis, [(i, length - 1 - i) for i in range(length)])
-
-
-def passed_on(x, axis, by, came_from):
-    length = lax.axis_size(axis)
-    pairs = [
-        (i, i + by) for i in range(length) if 0 <= i + by < length and 0 <= i + came_from < length
-    ]
-    return lax.ppermute(x, axis, pairs)
-
-
-def second_neighbours(right, left):
-    return passed_on(right, "seq", 1, -1), passed_on(left, "seq", -1, 1)
 
 
 def after(value, *others):
@@ -100,6 +88,46 @@
     )(shard_index[None], bounds, cotangent, query_rows, key_rows, *blocks)
 
 
+def base_kernel(shard_ref, bounds_ref, cotangent_ref, *refs):
+    blocks, out_ref = refs[:-1], refs[-1]
+    rows, width = cotangent_ref.shape
+    span_rows = blocks[reach].shape[0]
+    shard = shard_ref[0]
+    position = shard * rows + lax.broadcasted_iota(jnp.int32, (rows, 1), 0)
+    held = (bounds_ref[...] <= position).astype(jnp.float32)
+    held_before = (bounds_ref[...] < position).astype(jnp.float32)
+    count = jnp.sum(held, 1, keepdims=True)
+    starts = count > jnp.sum(held_before, 1, keepdims=True)
+    place = count.astype(jnp.int32) - 1 - (shard - reach) * span_rows
+    place = jnp.where(starts, place, -1)
+    column = lax.broadcasted_iota(jnp.int32, (rows, span_rows), 1)
+    pickers = [
+        (place - i * span_rows == column).astype(jnp.float32).astype(jnp.bfloat16)
+        for i in range(len(blocks))
+    ]
+    tile = 384
+    for start in range(0, width, tile):
+        cols = pl.ds(start, tile)
+        total = cotangent_ref[:, cols].astype(jnp.float32)
+        for picker, block in zip(pickers, blocks):
+            total = total + jnp.dot(
+                picker, block[:span_rows, cols], preferred_element_type=jnp.float32
+            )
+        out_ref[:, cols] = total
+
+
+def base_of(shard_index, bounds, cotangent, blocks):
+    vmem = pl.BlockSpec(memory_space=pltpu.VMEM)
+    return pl.pallas_call(
+        base_kernel,
+        out_shape=jax.ShapeDtypeStruct(cotangent.shape, jnp.float32),
+        in_specs=[pl.BlockSpec(memory_space=pltpu.SMEM)] + [vmem] * (2 + len(blocks)),
+        out_specs=vmem,
+        compiler_params=pltpu.CompilerParams(vmem_limit_bytes=40 * 1024 * 1024),
+        name="base",
+    )(shard_index[None], bounds, cotangent, *blocks)
+
+
 def product(rows, weight):
     return lax.dot_general(
         rows, weight, (((1,), (1,)), ((), ())), preferred_element_type=jnp.float32
@@ -129,8 +157,10 @@
     cuts = [(0, first_rows), (first_rows, group_rows)]
     out_right = passed_along(jnp.concatenate([main_out[0], key_rows[-16:]], 0), "seq", 1)
     out_left = passed_along(jnp.concatenate([main_out[0], query_rows[:16]], 0), "seq", -1)
-    query_other = swapped(query_rows, "groups")
-    key_other = swapped(key_rows, "groups")
+    out_far_right = passed_along(main_out[0], "seq", 2)
+    out_far_left = passed_along(main_out[0], "seq", -2)
+    rows_other = swapped(jnp.concatenate([query_rows, key_rows], 0), "groups")
+    query_other, key_other = rows_other[:row_count], rows_other[row_count:]
     own_weights = []
     for low, high in cuts:
         piece = jnp.concatenate(
@@ -147,7 +177,6 @@
         if own_weights:
             piece = after(piece, out_right)
         own_weights.append(lax.all_gather(piece, "seq", axis=0, tiled=True))
-    out_far_right, out_far_left = second_neighbours(out_right, out_left)
     last_key, next_query = out_right[-1:], out_left[span_rows : span_rows + 1]
     edges_other = swapped(jnp.concatenate([last_key, next_query], 0), "groups")
     last_key_other, next_query_other = edges_other[:1], edges_other[1:]
@@ -160,7 +189,6 @@
     place = span_of - (shard_index - reach) * span_rows
     window_rows = (2 * reach + 1) * span_rows
     selector = place[:, None] == jnp.arange(window_rows, dtype=jnp.int32)[None, :]
-    cotangent_wide = cotangent.astype(jnp.float32)
     if tensor_count == 2:
         sums = sums + swapped(sums, "tensor")
     else:
@@ -224,28 +252,28 @@
         )
         terms = [span_terms[i * span_rows : (i + 1) * span_rows] for i in range(2 * reach + 1)]
 
-        def moved(block, by, further):
-            moved_block = passed_on(block.astype(jnp.bfloat16), "seq", by, further)
-            return moved_block.astype(jnp.float32)
-
-        outer = after(jnp.stack([terms[0], terms[4]]).astype(jnp.bfloat16), ready)
-        span_sums = terms[2] + moved(terms[3] + moved(outer[1], 1, 2), 1, 1)
-        span_sums = span_sums + moved(terms[1] + moved(outer[0], -1, -2), -1, -1)
-        return span_sums.astype(jnp.bfloat16)[None]
-
-    window_grad = lax.all_gather(
-        after(main_in_grad[0], own_weights[0]), "seq", axis=0, tiled=True
-    )
-    span_index = jnp.arange(window_grad.shape[0], dtype=jnp.int32)
-    start_picker = ((span_of[:, None] == span_index[None, :]) & starts[:, None]).astype(jnp.bfloat16)
-    start_grad = jnp.dot(start_picker, window_grad, preferred_element_type=jnp.float32)
+        def sent(i):
+            block = jnp.concatenate([main_in_grad[0], terms[i].astype(jnp.bfloat16)], 0)
+            return passed_along(after(block, ready), "seq", i - reach)
+
+        right, left, far_right, far_left = sent(3), sent(1), sent(4), sent(0)
+        span_sums = terms[reach]
+        for block in (right, left, far_right, far_left):
+            span_sums = span_sums + block[span_rows:].astype(jnp.float32)
+        base = base_of(
+            shard_index,
+            boundaries,
+            cotangent,
+            [far_right, right, main_in_grad[0], left, far_left],
+        )
+        return span_sums.astype(jnp.bfloat16)[None], base
 
     def partial(own_weight, other_weight):
         total = product(own_side, own_weight) + product(other_side, other_weight)
         return total.astype(jnp.bfloat16)
 
     pieces = []
-    far_part, main_grad = None, None
+    far_part, main_grad, base = None, None, None
     for own_weight in own_weights:
         if far_part is not None:
             own_weight = after(own_weight, far_part)
@@ -260,16 +288,19 @@
                 ]
 
             far_part = partial(*half(1 - tensor_index))
+            if base is None:
+                main_grad, base = span_part(far_part)
             incoming = swapped(far_part, "tensor").astype(jnp.float32)
             total = partial(*half(tensor_index)).astype(jnp.float32) + incoming
         else:
+            far_part = partial(own_weight, other_weight)
+            if base is None:
+                main_grad, base = span_part(far_part)
             total = lax.psum_scatter(
-                partial(own_weight, other_weight), "tensor", scatter_dimension=1, tiled=True
+                far_part, "tensor", scatter_dimension=1, tiled=True
             ).astype(jnp.float32)
         own = total[:row_count]
         returned = total[row_count:].astype(jnp.bfloat16)
-        if main_grad is None:
-            main_grad = span_part(returned)
         arrived = swapped(returned, "groups").astype(jnp.float32)
         pieces.append(
             [jnp.where(group_index == 0, own, arrived), jnp.where(group_index == 0, arrived, own)]
@@ -284,7 +315,7 @@
         ],
         1,
     )
-    byte_grad = (cotangent_wide + start_grad + routing).astype(jnp.bfloat16)[None]
+    byte_grad = (base + routing).astype(jnp.bfloat16)[None]
     return (byte_grad, main_grad)
 
 

time: 211 us -> 235 us (1.11)
  waiting for transfers between devices: 89.2 us -> 111 us
  other arithmetic: 19.4 us -> 24.1 us
  local copies, waits for them, and re-layouts: 19.3 us -> 14.9 us
    ppermute x3 -> x9, waiting for transfers between devices: 9.93 us -> 75.3 us  [passed_along(): return lax.ppermute(x, axis, pairs)]
    ppermute x6 -> x0, waiting for transfers between devices: 33.9 us -> none  [passed_on(): return lax.ppermute(x, axis, pairs)]
    ppermute x6 -> x0, starting transfers between devices: 19.3 us -> none  [passed_on(): return lax.ppermute(x, axis, pairs)]
    ppermute x3 -> x9, starting transfers between devices: 9.06 us -> 28 us  [passed_along(): return lax.ppermute(x, axis, pairs)]
    ppermute x11 -> x10, waiting for transfers between devices: 35.7 us -> 21.1 us  [swapped(): return lax.ppermute(x, axis, [(i, length - 1 - i) for i in range(length)])]
    all_gather x2, waiting for transfers between devices: 9.56 us -> 14.6 us  [shards(): own_weights.append(lax.all_gather(piece, 'seq', axis=0, tiled=True))]
    concatenate x1 -> x3, other arithmetic: 0.97 us -> 5.47 us  [the longest x1 2.03 us: shards(): jnp.concatenate([main_out[0], query_rows[:16]], 0)]
    convert_element_type x2, other arithmetic: 5.11 us -> 1.04 us  [grads(): key_grad.astype(jnp.bfloat16)]
  transfers between devices with their start and end apart: 23 -> 21, of which waited for: 11 -> 12; matrix products, arithmetic and copies ran while one was open for 24% -> 23% of each run, Pallas kernels for 2% -> 3%
where the time goes in v7:
time: 235 us; the launch traced here: 234 us
  waiting for transfers between devices  111 us (47%)
  starting transfers between devices  40.8 us (17%)
  other arithmetic  24.1 us (10%)
  matrix products  22.2 us (9%)
  local copies, waits for them, and re-layouts  14.9 us (6%)
  between operations  14.8 us (6%)
  Pallas kernels  5.97 us (3%)
    ppermute x9, waiting for transfers between devices, passed_along(): return lax.ppermute(x, axis, pairs)  75.3 us
    ppermute x9, starting transfers between devices, passed_along(): return lax.ppermute(x, axis, pairs)  28 us
    ppermute x10, waiting for transfers between devices, swapped(): return lax.ppermute(x, axis, [(i, length - 1 - i) for i in range(length)])  21.1 us
    dot_general x8, matrix products, product(): lax.dot_general(rows, weight, (((1,), (1,)), ((), ())), preferred_element...  16.9 us
    all_gather x2, waiting for transfers between devices, shards(): own_weights.append(lax.all_gather(piece, 'seq', axis=0, tiled=True))  14.6 us
    ppermute x10, starting transfers between devices, swapped(): return lax.ppermute(x, axis, [(i, length - 1 - i) for i in range(length)])  12.8 us
  transfers between devices with their start and end apart: 21, of which 12 were waited for; matrix products, arithmetic and copies ran while one was open for 23% of the time, Pallas kernels for 3%

profile of v7, /device:TPU:0, one launch (start us, length us, event | category | flops | bytes accessed | tf_op | source)
XLA Modules:
  0.0 233.7 jit_solution(7494900046019233535)
XLA Ops:
  10.5 1.3 collective-permute-start.3
  11.8 7.5 %collective-permute-start = (bf16[128,1536]{1,0:T(8,128)(2,1)}, bf16[128,1536]{1,0:T(8,128)(2,1)}, u32[]{:S(2)}, u32[]{:S(2)}) collective-permute-start(bf16[128,1536]{1,0:T(8,128)(2,1)} %bitcast.6.refs_2_), channel_id=1, source_target_pairs={{0,8},{4,12},{1,9},{5,13},{2,10},{6,14},{3,11},{7,15},{16,24},{20,... | collective-permute-start | bytes 1179656 | tf_op jit(solution)/shard_map/ppermute | solution.py:14
  19.2 2.0 pad_maximum_fusion.7
  21.3 1.3 collective-permute-start.2
  22.6 5.9 %collective-permute-start.1 = (bf16[144,1536]{1,0:T(8,128)(2,1)}, bf16[144,1536]{1,0:T(8,128)(2,1)}, u32[]{:S(2)}, u32[]{:S(2)}) collective-permute-start(bf16[144,1536]{1,0:T(8,128)(2,1)} %get-tuple-element.47), channel_id=1, source_target_pairs={{0,4},{4,8},{8,12},{1,5},{5,9},{9,13},{2,6},{6,10},{10,14},{3,7},{... | collective-permute-start | bytes 1327112 | tf_op jit(solution)/shard_map/ppermute | solution.py:14
  28.4 1.6 pad_maximum_fusion
  30.0 2.0 collective-permute-start.8
  33.6 1.7 dynamic-slice_bitcast_fusion
  37.2 26.2 %collective-permute-done.2.refs_3_ = bf16[144,1536]{1,0:T(8,128)(2,1)} collective-permute-done((bf16[144,1536]{1,0:T(8,128)(2,1)}, bf16[144,1536]{1,0:T(8,128)(2,1)}, u32[]{:S(2)}, u32[]{:S(2)}) %collective-permute-start.2) | collective-permute-done | bytes 442400 | tf_op jit(solution)/shard_map/ppermute | solution.py:14
  65.5 2.9 %collective-permute-start.7 = (bf16[2,1536]{1,0:T(2,128)(2,1)}, bf16[2,1536]{1,0:T(2,128)(2,1)}, u32[]{:S(2)}, u32[]{:S(2)}) collective-permute-start(bf16[2,1536]{1,0:T(2,128)(2,1)} %pad_maximum_fusion.10), channel_id=1, source_target_pairs={{0,16},{16,0},{1,17},{17,1},{2,18},{18,2},{3,19},{19,3},{4,20},{20... | collective-permute-start | bytes 18440 | tf_op jit(solution)/shard_map/ppermute | solution.py:22
  69.6 4.1 %byte_sums.1 = f32[8,384]{1,0:T(8,128)S(1)} custom-call(s32[1]{0:T(128)} %bitcast.shard_ref, s32[1,512]{1,0:T(1,128)S(1)} %copy-done.4, bf16[384,1536]{1,0:T(8,128)(2,1)S(1)} %bitcast.45, bf16[384,1536]{1,0:T(8,128)(2,1)S(1)} %bitcast.42, bf16[384,1536]{1,0:T(8,128)(2,1)S(1)} %bitcast.44, bf16[128,1536]{1,0:T(8,128)(2,1)} %collective-permute-done.refs_0_, ...), custom_call_target="tpu_custom_call" | custom-call | tf_op jit(solution)/shard_map/byte_sums/pallas_call | solution.py:81
  73.7 1.6 collective-permute-start.4
  75.3 7.3 %collective-permute-done.7 = bf16[2,1536]{1,0:T(2,128)(2,1)} collective-permute-done((bf16[2,1536]{1,0:T(2,128)(2,1)}, bf16[2,1536]{1,0:T(2,128)(2,1)}, u32[]{:S(2)}, u32[]{:S(2)}) %collective-permute-start.7) | collective-permute-done | bytes 6176 | tf_op jit(solution)/shard_map/ppermute | solution.py:22
  86.6 1.5 collective-permute-start.5
  88.1 1.2 multiply_multiply_fusion.3
  89.3 2.9 %fusion.20 = (bf16[384,768]{1,0:T(8,128)(2,1)}, bf16[384,768]{1,0:T(8,128)(2,1)}) fusion(bf16[383,768]{1,0:T(8,128)(2,1)} %get-tuple-element.32, bf16[1,768]{1,0:T(2,128)(2,1)} %get-tuple-element.57, bf16[1,384,1536]{2,1,0:T(8,128)(2,1)S(1)} %copy-done, s32[]{:T(128)S(6)} %select_n.151, f32[384]{0:T(512)S(1)} %get-tuple-element.55, ...), kind=kLoop, calls=%fused_computation.28 | loop fusion | flops 5308416 | bytes 3542024 | tf_op jit(solution)/shard_map/convert_element_type | solution.py:224
  92.2 1.7 all-gather.3.cloned.1.call-done
  94.8 2.1 fusion.37
  96.9 3.3 %fusion.70 = (bf16[640,1536]{1,0:T(8,128)(2,1)S(1)}, f32[640,1536]{1,0:T(8,128)}) fusion(f32[640,1536]{1,0:T(8,128)S(1)} %fusion.37, bf16[1,384,1536]{2,1,0:T(8,128)(2,1)S(1)} %copy-done.2, s32[384]{0:T(512)S(1)} %copy-done.27, bf16[384]{0:T(512)(128)(2,1)S(1)} %get-tuple-element.14), kind=kOutput, calls=%fused_computation.153 | convolution fusion | flops 757432320 | bytes 11012352 | tf_op jit(solution)/shard_map/dot_general | solution.py:250
  100.2 8.0 %collective-permute-done.5 = f32[3,1]{1,0:T(4,128)} collective-permute-done((f32[3,1]{1,0:T(4,128)}, f32[3,1]{1,0:T(4,128)}, u32[]{:S(2)}, u32[]{:S(2)}) %collective-permute-start.5) | collective-permute-done | bytes 44 | tf_op jit(solution)/shard_map/ppermute | solution.py:14
  109.8 2.8 %collective-permute-done.6 = f32[3,385]{1,0:T(4,128)S(1)} collective-permute-done((f32[3,385]{1,0:T(4,128)S(1)}, f32[3,385]{1,0:T(4,128)S(1)}, u32[]{:S(2)}, u32[]{:S(2)}) %collective-permute-start.6) | collective-permute-done | bytes 4652 | tf_op jit(solution)/shard_map/ppermute | solution.py:22
  112.7 1.8 fusion.66
  118.2 1.4 fusion.6
  119.6 1.4 add_convert_fusion.2.refs_1_
  121.4 1.5 collective-permute-start.14
  123.0 1.8 pad_maximum_fusion.1
  124.8 12.9 %all-gather.5.cloned.1.call-done.refs_0_ = bf16[512,1536]{1,0:T(8,128)(2,1)} async-done(((bf16[128,1536]{1,0:T(8,128)(2,1)}), bf16[512,1536]{1,0:T(8,128)(2,1)}) %all-gather.5.cloned.1.call-update) | async-done | bytes 1572880 | tf_op jit(solution)/shard_map/all_gather | solution.py:179
  137.7 4.3 %fusion.2 = f32[768,512]{1,0:T(8,128)} fusion(bf16[1024,1536]{1,0:T(8,128)(2,1)} %all-gather.3.cloned.1.call-done, s32[]{:T(128)S(6)} %select_n.153, bf16[384,768]{1,0:T(8,128)(2,1)} %copy-done.19, bf16[384,768]{1,0:T(8,128)(2,1)} %copy-done.23, bf16[384,768]{1,0:T(8,128)(2,1)S(1)} %copy-done.15, bf16[384,768]{1,0:T(8,128)(2,1)S(1)} %copy-done.10), kind=kOutput, calls=%fused_computation.9 | convolution fusion | flops 1217396736 | bytes 5505028 | tf_op jit(solution)/shard_map/dot_general | solution.py:132
  142.1 3.2 %collective-permute-start.10 = (bf16[256,1536]{1,0:T(8,128)(2,1)}, bf16[256,1536]{1,0:T(8,128)(2,1)S(1)}, u32[]{:S(2)}, u32[]{:S(2)}) collective-permute-start(bf16[256,1536]{1,0:T(8,128)(2,1)} %after.6), channel_id=1, source_target_pairs={{0,8},{4,12},{1,9},{5,13},{2,10},{6,14},{3,11},{7,15},{16,24},{20,... | collective-permute-start | bytes 2359304 | tf_op jit(solution)/shard_map/ppermute | solution.py:14
  145.3 1.3 collective-permute-start.12
  146.6 4.6 %collective-permute-start.11 = (bf16[256,1536]{1,0:T(8,128)(2,1)}, bf16[256,1536]{1,0:T(8,128)(2,1)S(1)}, u32[]{:S(2)}, u32[]{:S(2)}) collective-permute-start(bf16[256,1536]{1,0:T(8,128)(2,1)} %after.7), channel_id=1, source_target_pairs={{0,4},{4,8},{8,12},{1,5},{5,9},{9,13},{2,6},{6,10},{10,14},{3,7},{... | collective-permute-start | bytes 2359304 | tf_op jit(solution)/shard_map/ppermute | solution.py:14
  151.2 1.5 collective-permute-start.13
  152.7 4.0 %add_convert_fusion.1 = bf16[768,512]{1,0:T(8,128)(2,1)S(1)} fusion(f32[768,512]{1,0:T(8,128)} %fusion.2, bf16[1024,1536]{1,0:T(8,128)(2,1)} %copy-done.36, s32[]{:T(128)S(6)} %select_n.153, bf16[384,768]{1,0:T(8,128)(2,1)} %copy-done.21, bf16[384,768]{1,0:T(8,128)(2,1)} %copy-done.25, bf16[384,768]{1,0:T(8,128)(2,1)} %copy-done.17, ...), kind=kOutput, calls=%fused_computation.6 | convolution fusion | flops 1218183168 | bytes 6291460 | tf_op jit(solution)/shard_map/dot_general | solution.py:132
  156.8 1.4 convert_add_fusion
  158.2 5.2 %collective-permute-done.10.refs_0_ = bf16[256,1536]{1,0:T(8,128)(2,1)S(1)} collective-permute-done((bf16[256,1536]{1,0:T(8,128)(2,1)}, bf16[256,1536]{1,0:T(8,128)(2,1)S(1)}, u32[]{:S(2)}, u32[]{:S(2)}) %collective-permute-start.10) | collective-permute-done | bytes 786464 | tf_op jit(solution)/shard_map/ppermute | solution.py:14
  163.4 1.5 collective-permute-start.15
  164.9 2.1 collective-permute-done.12.refs_3_
  167.1 12.8 %collective-permute-done.11.refs_1_ = bf16[256,1536]{1,0:T(8,128)(2,1)S(1)} collective-permute-done((bf16[256,1536]{1,0:T(8,128)(2,1)}, bf16[256,1536]{1,0:T(8,128)(2,1)S(1)}, u32[]{:S(2)}, u32[]{:S(2)}) %collective-permute-start.11) | collective-permute-done | bytes 786464 | tf_op jit(solution)/shard_map/ppermute | solution.py:14
  179.9 20.9 %collective-permute-done.13.refs_4_ = bf16[256,1536]{1,0:T(8,128)(2,1)S(1)} collective-permute-done((bf16[256,1536]{1,0:T(8,128)(2,1)}, bf16[256,1536]{1,0:T(8,128)(2,1)S(1)}, u32[]{:S(2)}, u32[]{:S(2)}) %collective-permute-start.13) | collective-permute-done | bytes 786464 | tf_op jit(solution)/shard_map/ppermute | solution.py:14
  200.8 1.9 base.1
  202.7 2.3 fusion.42
  205.0 2.1 fusion.31
  208.1 1.5 collective-permute-start.17
  209.8 1.9 fusion.34
  211.8 6.8 %collective-permute-done.17 = bf16[768,256]{1,0:T(8,128)(2,1)S(1)} collective-permute-done((bf16[768,256]{1,0:T(8,128)(2,1)S(1)}, bf16[768,256]{1,0:T(8,128)(2,1)S(1)}, u32[]{:S(2)}, u32[]{:S(2)}) %collective-permute-start.17) | collective-permute-done | bytes 393248 | tf_op jit(solution)/shard_map/ppermute | solution.py:22
  219.5 1.5 collective-permute-start.18
  221.0 4.2 %collective-permute-done.18 = bf16[384,256]{1,0:T(8,128)(2,1)S(1)} collective-permute-done((bf16[384,256]{1,0:T(8,128)(2,1)S(1)}, bf16[384,256]{1,0:T(8,128)(2,1)S(1)}, u32[]{:S(2)}, u32[]{:S(2)}) %collective-permute-start.18) | collective-permute-done | bytes 196640 | tf_op jit(solution)/shard_map/ppermute | solution.py:22
  225.5 1.4 fusion.16
  (147 shorter events, 23.0 us)
Async XLA Ops:
  7.2 12.1 %copy-start.1 = (bf16[1,384,1536]{2,1,0:T(8,128)(2,1)S(1)}, bf16[1,384,1536]{2,1,0:T(8,128)(2,1)}, u32[]{:S(2)}) copy-start(bf16[1,384,1536]{2,1,0:T(8,128)(2,1)} %param.10) | copy-start | bytes 3538948
  7.2 12.0 %copy-start = (bf16[1,384,1536]{2,1,0:T(8,128)(2,1)S(1)}, bf16[1,384,1536]{2,1,0:T(8,128)(2,1)}, u32[]{:S(2)}) copy-start(bf16[1,384,1536]{2,1,0:T(8,128)(2,1)} %param.9) | copy-start | bytes 3538948
  7.2 86.8 %all-gather.3.cloned.1.call-start = ((), (), s32[]{:S(2)}) async-start(), calls=%async_computation | async-start | bytes 3932160 | tf_op jit(solution)/shard_map/all_gather | solution.py:179
  10.4 127.3 %all-gather.5.cloned.1.call-start = ((), (), s32[]{:S(2)}) async-start(), calls=%async_computation.1 | async-start | bytes 1966080 | tf_op jit(solution)/shard_map/all_gather | solution.py:179
  10.5 59.1 %collective-permute-start.3 = (bf16[128,1536]{1,0:T(8,128)(2,1)}, bf16[128,1536]{1,0:T(8,128)(2,1)}, u32[]{:S(2)}, u32[]{:S(2)}) collective-permute-start(bf16[128,1536]{1,0:T(8,128)(2,1)} %bitcast.6.refs_2_), channel_id=1, source_target_pairs={{8,0},{12,4},{9,1},{13,5},{10,2},{14,6},{11,3},{15,7},{24,16},{28,... | collective-permute-start | bytes 1179656 | tf_op jit(solution)/shard_map/ppermute | solution.py:14
  11.8 57.8 %collective-permute-start = (bf16[128,1536]{1,0:T(8,128)(2,1)}, bf16[128,1536]{1,0:T(8,128)(2,1)}, u32[]{:S(2)}, u32[]{:S(2)}) collective-permute-start(bf16[128,1536]{1,0:T(8,128)(2,1)} %bitcast.6.refs_2_), channel_id=1, source_target_pairs={{0,8},{4,12},{1,9},{5,13},{2,10},{6,14},{3,11},{7,15},{16,24},{20,... | collective-permute-start | bytes 1179656 | tf_op jit(solution)/shard_map/ppermute | solution.py:14
  21.3 42.1 %collective-permute-start.2 = (bf16[144,1536]{1,0:T(8,128)(2,1)}, bf16[144,1536]{1,0:T(8,128)(2,1)}, u32[]{:S(2)}, u32[]{:S(2)}) collective-permute-start(bf16[144,1536]{1,0:T(8,128)(2,1)} %get-tuple-element.46), channel_id=1, source_target_pairs={{4,0},{8,4},{12,8},{5,1},{9,5},{13,9},{6,2},{10,6},{14,10},{7,3},{... | collective-permute-start | bytes 1327112 | tf_op jit(solution)/shard_map/ppermute | solution.py:14
  22.6 41.6 %collective-permute-start.1 = (bf16[144,1536]{1,0:T(8,128)(2,1)}, bf16[144,1536]{1,0:T(8,128)(2,1)}, u32[]{:S(2)}, u32[]{:S(2)}) collective-permute-start(bf16[144,1536]{1,0:T(8,128)(2,1)} %get-tuple-element.47), channel_id=1, source_target_pairs={{0,4},{4,8},{8,12},{1,5},{5,9},{9,13},{2,6},{6,10},{10,14},{3,7},{... | collective-permute-start | bytes 1327112 | tf_op jit(solution)/shard_map/ppermute | solution.py:14
  28.4 3.6 %copy-start.4 = (s32[1,512]{1,0:T(1,128)S(1)}, s32[1,512]{1,0:T(1,128)}, u32[]{:S(2)}) copy-start(s32[1,512]{1,0:T(1,128)} %bounds_ref.3) | copy-start | bytes 6148
  30.0 82.6 %collective-permute-start.8 = (bf16[768,1536]{1,0:T(8,128)(2,1)}, bf16[768,1536]{1,0:T(8,128)(2,1)}, u32[]{:S(2)}, u32[]{:S(2)}) collective-permute-start(bf16[768,1536]{1,0:T(8,128)(2,1)} %pad_maximum_fusion), channel_id=1, source_target_pairs={{0,16},{16,0},{1,17},{17,1},{2,18},{18,2},{3,19},{19,3},{4,20},{20... | collective-permute-start | bytes 7077896 | tf_op jit(solution)/shard_map/ppermute | solution.py:22
  32.2 3.6 %copy-start.34 = (pred[384]{0:T(512)(128)(4,1)}, pred[384]{0:T(512)(128)(4,1)S(1)}, u32[]{:S(2)}) copy-start(pred[384]{0:T(512)(128)(4,1)S(1)} %compare_reduce_fusion) | copy-start | bytes 1156
  32.5 4.0 %dynamic-slice-start = ((bf16[768,1536]{1,0:T(8,128)(2,1)}, s32[]{:T(128)}, s32[]{:T(128)}), bf16[128,768]{1,0:T(8,128)(2,1)S(1)}, s32[]{:S(2)}) async-start(bf16[768,1536]{1,0:T(8,128)(2,1)} %param.14, s32[]{:T(128)} %select_n.156, s32[]{:T(128)} %select_n.147), calls=%async_computation.2 | async-start | bytes 393728 | tf_op jit(solution)/shard_map/dynamic_slice | solution.py:168
  32.5 4.0 %dynamic-slice-start.1 = ((bf16[768,1536]{1,0:T(8,128)(2,1)}, s32[]{:T(128)}, s32[]{:T(128)}), bf16[128,768]{1,0:T(8,128)(2,1)S(1)}, s32[]{:S(2)}) async-start(bf16[768,1536]{1,0:T(8,128)(2,1)} %param.15, s32[]{:T(128)} %select_n.156, s32[]{:T(128)} %select_n.147), calls=%async_computation.3 | async-start | bytes 393728 | tf_op jit(solution)/shard_map/dynamic_slice | solution.py:168
  32.5 37.1 %copy-start.2 = (bf16[1,384,1536]{2,1,0:T(8,128)(2,1)S(1)}, bf16[1,384,1536]{2,1,0:T(8,128)(2,1)}, u32[]{:S(2)}) copy-start(bf16[1,384,1536]{2,1,0:T(8,128)(2,1)} %param.8) | copy-start | bytes 3538948
  65.5 17.1 %collective-permute-start.7 = (bf16[2,1536]{1,0:T(2,128)(2,1)}, bf16[2,1536]{1,0:T(2,128)(2,1)}, u32[]{:S(2)}, u32[]{:S(2)}) collective-permute-start(bf16[2,1536]{1,0:T(2,128)(2,1)} %pad_maximum_fusion.10), channel_id=1, source_target_pairs={{0,16},{16,0},{1,17},{17,1},{2,18},{18,2},{3,19},{19,3},{4,20},{20... | collective-permute-start | bytes 18440 | tf_op jit(solution)/shard_map/ppermute | solution.py:22
  73.7 10.9 %collective-permute-start.4 = (f32[8,384]{1,0:T(8,128)S(1)}, f32[8,384]{1,0:T(8,128)}, u32[]{:S(2)}, u32[]{:S(2)}) collective-permute-start(f32[8,384]{1,0:T(8,128)S(1)} %byte_sums.1), channel_id=1, source_target_pairs={{0,2},{2,0},{1,3},{3,1},{4,6},{6,4},{5,7},{7,5},{8,10},{10,8},{9,1... | collective-permute-start | bytes 36872 | tf_op jit(solution)/shard_map/ppermute | solution.py:22
  86.6 21.5 %collective-permute-start.5 = (f32[3,1]{1,0:T(4,128)}, f32[3,1]{1,0:T(4,128)}, u32[]{:S(2)}, u32[]{:S(2)}) collective-permute-start(f32[3,1]{1,0:T(4,128)} %pad_maximum_fusion.11), channel_id=1, source_target_pairs={{4,0},{8,4},{12,8},{5,1},{9,5},{13,9},{6,2},{10,6},{14,10},{7,3},{... | collective-permute-start | bytes 44 | tf_op jit(solution)/shard_map/ppermute | solution.py:14
  93.9 25.6 %collective-permute-start.9 = (bf16[1024,1536]{1,0:T(8,128)(2,1)}, bf16[1024,1536]{1,0:T(8,128)(2,1)S(1)}, u32[]{:S(2)}, u32[]{:S(2)}) collective-permute-start(bf16[1024,1536]{1,0:T(8,128)(2,1)} %all-gather.3.cloned.1.call-done), channel_id=1, source_target_pairs={{0,1},{1,0},{2,3},{3,2},{4,5},{5,4},{6,7},{7,6},{8,9},{9,8},{10,11... | collective-permute-start | bytes 9437192 | tf_op jit(solution)/shard_map/ppermute | solution.py:22
  96.9 12.4 %copy-start.6 = (bf16[383,768]{1,0:T(8,128)(2,1)S(1)}, bf16[383,768]{1,0:T(8,128)(2,1)}, u32[]{:S(2)}) copy-start(bf16[383,768]{1,0:T(8,128)(2,1)} %get-tuple-element.34) | copy-start | bytes 1764868
  96.9 12.4 %copy-start.7 = (bf16[383,768]{1,0:T(8,128)(2,1)S(1)}, bf16[383,768]{1,0:T(8,128)(2,1)}, u32[]{:S(2)}) copy-start(bf16[383,768]{1,0:T(8,128)(2,1)} %get-tuple-element.35) | copy-start | bytes 1764868
  96.9 12.4 %copy-start.30 = (bf16[1,768]{1,0:T(2,128)(2,1)S(1)}, bf16[1,768]{1,0:T(2,128)(2,1)}, u32[]{:S(2)}) copy-start(bf16[1,768]{1,0:T(2,128)(2,1)} %get-tuple-element.59) | copy-start | bytes 4612
  96.9 12.4 %copy-start.31 = (bf16[1,768]{1,0:T(2,128)(2,1)S(1)}, bf16[1,768]{1,0:T(2,128)(2,1)}, u32[]{:S(2)}) copy-start(bf16[1,768]{1,0:T(2,128)(2,1)} %get-tuple-element.60) | copy-start | bytes 4612
  108.9 3.7 %collective-permute-start.6 = (f32[3,385]{1,0:T(4,128)S(1)}, f32[3,385]{1,0:T(4,128)S(1)}, u32[]{:S(2)}, u32[]{:S(2)}) collective-permute-start(f32[3,385]{1,0:T(4,128)S(1)} %pad_maximum_fusion.9), channel_id=1, source_target_pairs={{0,16},{16,0},{1,17},{17,1},{2,18},{18,2},{3,19},{19,3},{4,20},{20... | collective-permute-start | bytes 13868 | tf_op jit(solution)/shard_map/ppermute | solution.py:22
  109.8 6.8 %copy-start.14 = (bf16[384,768]{1,0:T(8,128)(2,1)}, bf16[384,768]{1,0:T(8,128)(2,1)S(1)}, u32[]{:S(2)}) copy-start(bf16[384,768]{1,0:T(8,128)(2,1)S(1)} %get-tuple-element.27) | copy-start | bytes 1769476
  109.8 9.8 %copy-start.17 = (bf16[384,768]{1,0:T(8,128)(2,1)}, bf16[384,768]{1,0:T(8,128)(2,1)S(1)}, u32[]{:S(2)}) copy-start(bf16[384,768]{1,0:T(8,128)(2,1)S(1)} %get-tuple-element.26) | copy-start | bytes 1769476
  115.3 2.5 %copy-start.35 = (bf16[1024,1536]{1,0:T(8,128)(2,1)S(1)}, bf16[1024,1536]{1,0:T(8,128)(2,1)}, u32[]{:S(2)}) copy-start(bf16[1024,1536]{1,0:T(8,128)(2,1)} %all-gather.3.cloned.1.call-done) | copy-start | bytes 9437188
  115.8 3.8 %copy-start.19 = (bf16[384,768]{1,0:T(8,128)(2,1)}, bf16[384,768]{1,0:T(8,128)(2,1)S(1)}, u32[]{:S(2)}) copy-start(bf16[384,768]{1,0:T(8,128)(2,1)S(1)} %get-tuple-element.31) | copy-start | bytes 1769476
  115.8 3.8 %copy-start.21 = (bf16[384,768]{1,0:T(8,128)(2,1)}, bf16[384,768]{1,0:T(8,128)(2,1)S(1)}, u32[]{:S(2)}) copy-start(bf16[384,768]{1,0:T(8,128)(2,1)S(1)} %get-tuple-element.30) | copy-start | bytes 1769476
  115.8 2.3 %copy-start.9 = (bf16[384,768]{1,0:T(8,128)(2,1)S(1)}, bf16[384,768]{1,0:T(8,128)(2,1)}, u32[]{:S(2)}) copy-start(bf16[384,768]{1,0:T(8,128)(2,1)} %get-tuple-element.25) | copy-start | bytes 1769476
  116.6 3.0 %copy-start.23 = (bf16[384,768]{1,0:T(8,128)(2,1)}, bf16[384,768]{1,0:T(8,128)(2,1)S(1)}, u32[]{:S(2)}) copy-start(bf16[384,768]{1,0:T(8,128)(2,1)S(1)} %get-tuple-element.29) | copy-start | bytes 1769476
  116.6 3.1 %copy-start.25 = (bf16[384,768]{1,0:T(8,128)(2,1)}, bf16[384,768]{1,0:T(8,128)(2,1)S(1)}, u32[]{:S(2)}) copy-start(bf16[384,768]{1,0:T(8,128)(2,1)S(1)} %get-tuple-element.28) | copy-start | bytes 1769476
  121.4 3.4 %copy-start.5 = (bf16[768,512]{1,0:T(8,128)(2,1)}, bf16[768,512]{1,0:T(8,128)(2,1)S(1)}, u32[]{:S(2)}) copy-start(bf16[768,512]{1,0:T(8,128)(2,1)S(1)} %add_convert_fusion.2.refs_1_) | copy-start | bytes 2359300
  121.4 29.8 %collective-permute-start.14 = (bf16[768,512]{1,0:T(8,128)(2,1)S(1)}, bf16[768,512]{1,0:T(8,128)(2,1)}, u32[]{:S(2)}, u32[]{:S(2)}) collective-permute-start(bf16[768,512]{1,0:T(8,128)(2,1)S(1)} %add_convert_fusion.2.refs_1_), channel_id=1, source_target_pairs={{0,2},{2,0},{1,3},{3,1},{4,6},{6,4},{5,7},{7,5},{8,10},{10,8},{9,1... | collective-permute-start | bytes 2359304 | tf_op jit(solution)/shard_map/ppermute | solution.py:22
  124.8 12.9 %copy-start.10 = (bf16[384,768]{1,0:T(8,128)(2,1)S(1)}, bf16[384,768]{1,0:T(8,128)(2,1)}, u32[]{:S(2)}) copy-start(bf16[384,768]{1,0:T(8,128)(2,1)} %get-tuple-element.25) | copy-start | bytes 1769476
  124.8 12.9 %copy-start.15 = (bf16[384,768]{1,0:T(8,128)(2,1)S(1)}, bf16[384,768]{1,0:T(8,128)(2,1)}, u32[]{:S(2)}) copy-start(bf16[384,768]{1,0:T(8,128)(2,1)} %copy-done.14) | copy-start | bytes 1769476
  137.7 67.3 %collective-permute-start.16 = (bf16[512,1536]{1,0:T(8,128)(2,1)}, bf16[512,1536]{1,0:T(8,128)(2,1)}, u32[]{:S(2)}, u32[]{:S(2)}) collective-permute-start(bf16[512,1536]{1,0:T(8,128)(2,1)} %after.11), channel_id=1, source_target_pairs={{0,1},{1,0},{2,3},{3,2},{4,5},{5,4},{6,7},{7,6},{8,9},{9,8},{10,11... | collective-permute-start | bytes 4718600 | tf_op jit(solution)/shard_map/ppermute | solution.py:22
  142.1 21.4 %collective-permute-start.10 = (bf16[256,1536]{1,0:T(8,128)(2,1)}, bf16[256,1536]{1,0:T(8,128)(2,1)S(1)}, u32[]{:S(2)}, u32[]{:S(2)}) collective-permute-start(bf16[256,1536]{1,0:T(8,128)(2,1)} %after.6), channel_id=1, source_target_pairs={{0,8},{4,12},{1,9},{5,13},{2,10},{6,14},{3,11},{7,15},{16,24},{20,... | collective-permute-start | bytes 2359304 | tf_op jit(solution)/shard_map/ppermute | solution.py:14
  145.3 21.8 %collective-permute-start.12 = (bf16[256,1536]{1,0:T(8,128)(2,1)}, bf16[256,1536]{1,0:T(8,128)(2,1)S(1)}, u32[]{:S(2)}, u32[]{:S(2)}) collective-permute-start(bf16[256,1536]{1,0:T(8,128)(2,1)} %after.8), channel_id=1, source_target_pairs={{4,0},{8,4},{12,8},{5,1},{9,5},{13,9},{6,2},{10,6},{14,10},{7,3},{... | collective-permute-start | bytes 2359304 | tf_op jit(solution)/shard_map/ppermute | solution.py:14
  146.6 33.3 %collective-permute-start.11 = (bf16[256,1536]{1,0:T(8,128)(2,1)}, bf16[256,1536]{1,0:T(8,128)(2,1)S(1)}, u32[]{:S(2)}, u32[]{:S(2)}) collective-permute-start(bf16[256,1536]{1,0:T(8,128)(2,1)} %after.7), channel_id=1, source_target_pairs={{0,4},{4,8},{8,12},{1,5},{5,9},{9,13},{2,6},{6,10},{10,14},{3,7},{... | collective-permute-start | bytes 2359304 | tf_op jit(solution)/shard_map/ppermute | solution.py:14
  151.2 49.6 %collective-permute-start.13 = (bf16[256,1536]{1,0:T(8,128)(2,1)}, bf16[256,1536]{1,0:T(8,128)(2,1)S(1)}, u32[]{:S(2)}, u32[]{:S(2)}) collective-permute-start(bf16[256,1536]{1,0:T(8,128)(2,1)} %after.9), channel_id=1, source_target_pairs={{8,0},{12,4},{9,1},{13,5},{10,2},{14,6},{11,3},{15,7},{24,16},{28,... | collective-permute-start | bytes 2359304 | tf_op jit(solution)/shard_map/ppermute | solution.py:14
  163.4 46.2 %collective-permute-start.15 = (bf16[384,512]{1,0:T(8,128)(2,1)S(1)}, bf16[384,512]{1,0:T(8,128)(2,1)S(1)}, u32[]{:S(2)}, u32[]{:S(2)}) collective-permute-start(bf16[384,512]{1,0:T(8,128)(2,1)S(1)} %slice.299), channel_id=1, source_target_pairs={{0,16},{16,0},{1,17},{17,1},{2,18},{18,2},{3,19},{19,3},{4,20},{20... | collective-permute-start | bytes 1179656 | tf_op jit(solution)/shard_map/ppermute | solution.py:22
  202.7 2.4 %copy-start.13 = (bf16[384,768]{1,0:T(8,128)(2,1)S(1)}, bf16[384,768]{1,0:T(8,128)(2,1)}, u32[]{:S(2)}) copy-start(bf16[384,768]{1,0:T(8,128)(2,1)} %get-tuple-element.24) | copy-start | bytes 1769476
  202.7 2.4 %copy-start.18 = (bf16[384,768]{1,0:T(8,128)(2,1)S(1)}, bf16[384,768]{1,0:T(8,128)(2,1)}, u32[]{:S(2)}) copy-start(bf16[384,768]{1,0:T(8,128)(2,1)} %copy-done.17) | copy-start | bytes 1769476
  202.7 2.4 %copy-start.22 = (bf16[384,768]{1,0:T(8,128)(2,1)S(1)}, bf16[384,768]{1,0:T(8,128)(2,1)}, u32[]{:S(2)}) copy-start(bf16[384,768]{1,0:T(8,128)(2,1)} %copy-done.21) | copy-start | bytes 1769476
  202.7 2.4 %copy-start.26 = (bf16[384,768]{1,0:T(8,128)(2,1)S(1)}, bf16[384,768]{1,0:T(8,128)(2,1)}, u32[]{:S(2)}) copy-start(bf16[384,768]{1,0:T(8,128)(2,1)} %copy-done.25) | copy-start | bytes 1769476
  205.0 2.3 copy-start.24
  208.1 10.5 %collective-permute-start.17 = (bf16[768,256]{1,0:T(8,128)(2,1)S(1)}, bf16[768,256]{1,0:T(8,128)(2,1)S(1)}, u32[]{:S(2)}, u32[]{:S(2)}) collective-permute-start(bf16[768,256]{1,0:T(8,128)(2,1)S(1)} %fusion.15), channel_id=1, source_target_pairs={{0,2},{2,0},{1,3},{3,1},{4,6},{6,4},{5,7},{7,5},{8,10},{10,8},{9,1... | collective-permute-start | bytes 1179656 | tf_op jit(solution)/shard_map/ppermute | solution.py:22
  219.5 5.7 %collective-permute-start.18 = (bf16[384,256]{1,0:T(8,128)(2,1)S(1)}, bf16[384,256]{1,0:T(8,128)(2,1)S(1)}, u32[]{:S(2)}, u32[]{:S(2)}) collective-permute-start(bf16[384,256]{1,0:T(8,128)(2,1)S(1)} %slice.300), channel_id=1, source_target_pairs={{0,16},{16,0},{1,17},{17,1},{2,18},{18,2},{3,19},{19,3},{4,20},{20... | collective-permute-start | bytes 589832 | tf_op jit(solution)/shard_map/ppermute | solution.py:22
  (12 other events, 18.6 us)
Sparse Core Ops, SparseCore 0:
  10.5 83.3 all-gather.2
  96.1 41.5 all-gather.4

commit v8 on v7

--- a/solution.py
+++ b/solution.py
@@ -20,6 +20,14 @@
 def swapped(x, axis):
     length = lax.axis_size(axis)
     return lax.ppermute(x, axis, [(i, length - 1 - i) for i in range(length)])
+
+
+def passed_on(x, axis, by, came_from):
+    length = lax.axis_size(axis)
+    pairs = [
+        (i, i + by) for i in range(length) if 0 <= i + by < length and 0 <= i + came_from < length
+    ]
+    return lax.ppermute(x, axis, pairs)
 
 
 def after(value, *others):
@@ -40,7 +48,7 @@
 def byte_sums_kernel(shard_ref, bounds_ref, cotangent_ref, query_ref, key_ref, *refs):
     blocks, out_ref = refs[:-1], refs[-1]
     rows, width = query_ref.shape
-    span_rows = blocks[reach].shape[0]
+    span_rows = blocks[reach].shape[0] // 2
     shard = shard_ref[0]
     row = lax.broadcasted_iota(jnp.int32, (rows, 1), 0)
     held = (bounds_ref[...] <= shard * rows + row).astype(jnp.float32)
@@ -91,7 +99,7 @@
 def base_kernel(shard_ref, bounds_ref, cotangent_ref, *refs):
     blocks, out_ref = refs[:-1], refs[-1]
     rows, width = cotangent_ref.shape
-    span_rows = blocks[reach].shape[0]
+    span_rows = blocks[reach].shape[0] // 2
     shard = shard_ref[0]
     position = shard * rows + lax.broadcasted_iota(jnp.int32, (rows, 1), 0)
     held = (bounds_ref[...] <= position).astype(jnp.float32)
@@ -111,7 +119,7 @@
         total = cotangent_ref[:, cols].astype(jnp.float32)
         for picker, block in zip(pickers, blocks):
             total = total + jnp.dot(
-                picker, block[:span_rows, cols], preferred_element_type=jnp.float32
+                picker, block[span_rows : 2 * span_rows, cols], preferred_element_type=jnp.float32
             )
         out_ref[:, cols] = total
 
@@ -155,10 +163,11 @@
 
     first_rows = group_rows * 2 // 3 // 16 * 16
     cuts = [(0, first_rows), (first_rows, group_rows)]
-    out_right = passed_along(jnp.concatenate([main_out[0], key_rows[-16:]], 0), "seq", 1)
-    out_left = passed_along(jnp.concatenate([main_out[0], query_rows[:16]], 0), "seq", -1)
-    out_far_right = passed_along(main_out[0], "seq", 2)
-    out_far_left = passed_along(main_out[0], "seq", -2)
+    pair = jnp.concatenate([main_out[0], main_in_grad[0]], 0)
+    out_right = passed_along(jnp.concatenate([pair, key_rows[-16:]], 0), "seq", 1)
+    out_left = passed_along(jnp.concatenate([pair, query_rows[:16]], 0), "seq", -1)
+    out_far_right = passed_along(pair, "seq", 2)
+    out_far_left = passed_along(pair, "seq", -2)
     rows_other = swapped(jnp.concatenate([query_rows, key_rows], 0), "groups")
     query_other, key_other = rows_other[:row_count], rows_other[row_count:]
     own_weights = []
@@ -177,10 +186,10 @@
         if own_weights:
             piece = after(piece, out_right)
         own_weights.append(lax.all_gather(piece, "seq", axis=0, tiled=True))
-    last_key, next_query = out_right[-1:], out_left[span_rows : span_rows + 1]
+    last_key, next_query = out_right[-1:], out_left[2 * span_rows : 2 * span_rows + 1]
     edges_other = swapped(jnp.concatenate([last_key, next_query], 0), "groups")
     last_key_other, next_query_other = edges_other[:1], edges_other[1:]
-    blocks = [out_far_right, out_right, main_out[0], out_left, out_far_left]
+    blocks = [out_far_right, out_right, pair, out_left, out_far_left]
     sums = byte_sums(shard_index, boundaries, cotangent, query_rows, key_rows, blocks)
 
     positions = shard_index * row_count + jnp.arange(row_count, dtype=jnp.int32)
@@ -252,28 +261,23 @@
         )
         terms = [span_terms[i * span_rows : (i + 1) * span_rows] for i in range(2 * reach + 1)]
 
-        def sent(i):
-            block = jnp.concatenate([main_in_grad[0], terms[i].astype(jnp.bfloat16)], 0)
-            return passed_along(after(block, ready), "seq", i - reach)
-
-        right, left, far_right, far_left = sent(3), sent(1), sent(4), sent(0)
-        span_sums = terms[reach]
-        for block in (right, left, far_right, far_left):
-            span_sums = span_sums + block[span_rows:].astype(jnp.float32)
-        base = base_of(
-            shard_index,
-            boundaries,
-            cotangent,
-            [far_right, right, main_in_grad[0], left, far_left],
-        )
-        return span_sums.astype(jnp.bfloat16)[None], base
+        outer = after(jnp.stack([terms[0], terms[4]]).astype(jnp.bfloat16), ready)
+        inner = jnp.stack(
+            [
+                terms[1] + passed_on(outer[0], "seq", -1, -2).astype(jnp.float32),
+                terms[3] + passed_on(outer[1], "seq", 1, 2).astype(jnp.float32),
+            ]
+        )
+        return terms[reach], inner.astype(jnp.bfloat16)
+
+    base = base_of(shard_index, boundaries, cotangent, blocks)
 
     def partial(own_weight, other_weight):
         total = product(own_side, own_weight) + product(other_side, other_weight)
         return total.astype(jnp.bfloat16)
 
     pieces = []
-    far_part, main_grad, base = None, None, None
+    far_part, span_inner = None, None
     for own_weight in own_weights:
         if far_part is not None:
             own_weight = after(own_weight, far_part)
@@ -288,14 +292,14 @@
                 ]
 
             far_part = partial(*half(1 - tensor_index))
-            if base is None:
-                main_grad, base = span_part(far_part)
+            if span_inner is None:
+                span_sums, span_inner = span_part(far_part)
             incoming = swapped(far_part, "tensor").astype(jnp.float32)
             total = partial(*half(tensor_index)).astype(jnp.float32) + incoming
         else:
             far_part = partial(own_weight, other_weight)
-            if base is None:
-                main_grad, base = span_part(far_part)
+            if span_inner is None:
+                span_sums, span_inner = span_part(far_part)
             total = lax.psum_scatter(
                 far_part, "tensor", scatter_dimension=1, tiled=True
             ).astype(jnp.float32)
@@ -305,6 +309,10 @@
         pieces.append(
             [jnp.where(group_index == 0, own, arrived), jnp.where(group_index == 0, arrived, own)]
         )
+    span_inner = after(span_inner, far_part)
+    span_sums = span_sums + passed_along(span_inner[0], "seq", -1).astype(jnp.float32)
+    span_sums = span_sums + passed_along(span_inner[1], "seq", 1).astype(jnp.float32)
+    main_grad = span_sums.astype(jnp.bfloat16)[None]
     widths = [high - low for low, high in cuts]
     routing = jnp.concatenate(
         [

time: 235 us -> 234 us (level)
  waiting for transfers between devices: 111 us -> 104 us
  local copies, waits for them, and re-layouts: 14.9 us -> 21.1 us
  other arithmetic: 24.1 us -> 19.9 us
  Pallas kernels: 5.97 us -> 8.57 us
    ppermute x10, waiting for transfers between devices: 21.1 us -> 7.26 us  [swapped(): return lax.ppermute(x, axis, [(i, length - 1 - i) for i in range(length)])]
    ppermute x9 -> x7, waiting for transfers between devices: 75.3 us -> 88.8 us  [passed_along(): return lax.ppermute(x, axis, pairs)]
    all_gather x2, waiting for transfers between devices: 14.6 us -> 5.11 us  [shards(): own_weights.append(lax.all_gather(piece, 'seq', axis=0, tiled=True))]
    ppermute x0 -> x2, starting transfers between devices: none -> 5.42 us  [passed_on(): return lax.ppermute(x, axis, pairs)]
    ppermute x10, starting transfers between devices: 12.8 us -> 9.09 us  [swapped(): return lax.ppermute(x, axis, [(i, length - 1 - i) for i in range(length)])]
    another operation x0 -> x4, other arithmetic: none -> 3.51 us  [the longest x2 2.52 us: span_part(): jnp.stack([terms[1] + passed_on(outer[0], 'seq', -1, -2).astype(jnp.float...]
    ppermute x0 -> x2, waiting for transfers between devices: none -> 2.74 us  [passed_on(): return lax.ppermute(x, axis, pairs)]
    unnamed x81 -> x117, local copies, waits for them, and re-layouts: 2.32 us -> 4.91 us
  transfers between devices with their start and end apart: 21 -> 21, of which waited for: 12 -> 8; matrix products, arithmetic and copies ran while one was open for 23% -> 22% of each run, Pallas kernels for 3% -> 4%
where the time goes in v8:
time: 234 us; the launch traced here: 233 us
  waiting for transfers between devices  104 us (44%)
  starting transfers between devices  42.4 us (18%)
  matrix products  22.2 us (9%)
  local copies, waits for them, and re-layouts  21.1 us (9%)
  other arithmetic  19.9 us (9%)
  between operations  15.1 us (6%)
  Pallas kernels  8.57 us (4%)
    ppermute x7, waiting for transfers between devices, passed_along(): return lax.ppermute(x, axis, pairs)  88.8 us
    ppermute x7, starting transfers between devices, passed_along(): return lax.ppermute(x, axis, pairs)  27.8 us
    dot_general x8, matrix products, product(): lax.dot_general(rows, weight, (((1,), (1,)), ((), ())), preferred_element...  17 us
    ppermute x10, starting transfers between devices, swapped(): return lax.ppermute(x, axis, [(i, length - 1 - i) for i in range(length)])  9.09 us
    ppermute x10, waiting for transfers between devices, swapped(): return lax.ppermute(x, axis, [(i, length - 1 - i) for i in range(length)])  7.26 us
    ppermute x2, starting transfers between devices, passed_on(): return lax.ppermute(x, axis, pairs)  5.42 us
    all_gather x2, waiting for transfers between devices, shards(): own_weights.append(lax.all_gather(piece, 'seq', axis=0, tiled=True))  5.11 us
    unnamed x117, local copies, waits for them, and re-layouts  4.91 us
  transfers between devices with their start and end apart: 21, of which 8 were waited for; matrix products, arithmetic and copies ran while one was open for 22% of the time, Pallas kernels for 4%

profile of v8, /device:TPU:0, one launch (start us, length us, event | category | flops | bytes accessed | tf_op | source)
XLA Modules:
  0.0 233.2 jit_solution(8503385770827889297)
XLA Ops:
  7.2 1.1 dynamic_slice.97
  8.4 1.2 dynamic_slice.96
  11.5 6.9 %collective-permute-start = (bf16[256,1536]{1,0:T(8,128)(2,1)}, bf16[256,1536]{1,0:T(8,128)(2,1)}, u32[]{:S(2)}, u32[]{:S(2)}) collective-permute-start(bf16[256,1536]{1,0:T(8,128)(2,1)} %pad_maximum_fusion.4.refs_2_), channel_id=1, source_target_pairs={{0,8},{4,12},{1,9},{5,13},{2,10},{6,14},{3,11},{7,15},{16,24},{20,... | collective-permute-start | bytes 2359304 | tf_op jit(solution)/shard_map/ppermute | solution.py:14
  18.4 1.3 collective-permute-start.3
  19.7 1.3 pad_maximum_fusion.3
  21.1 4.4 %collective-permute-start.1 = (bf16[272,1536]{1,0:T(8,128)(2,1)}, bf16[272,1536]{1,0:T(8,128)(2,1)}, u32[]{:S(2)}, u32[]{:S(2)}) collective-permute-start(bf16[272,1536]{1,0:T(8,128)(2,1)} %get-tuple-element.47), channel_id=1, source_target_pairs={{0,4},{4,8},{8,12},{1,5},{5,9},{9,13},{2,6},{6,10},{10,14},{3,7},{... | collective-permute-start | bytes 2506760 | tf_op jit(solution)/shard_map/ppermute | solution.py:14
  25.5 1.3 collective-permute-start.2
  26.8 1.6 pad_maximum_fusion
  28.3 1.5 collective-permute-start.8
  30.1 1.1 dynamic-slice_bitcast_fusion.1
  32.6 1.6 dynamic-slice_bitcast_fusion
  35.1 64.8 %collective-permute-done.2.refs_3_ = bf16[272,1536]{1,0:T(8,128)(2,1)} collective-permute-done((bf16[272,1536]{1,0:T(8,128)(2,1)}, bf16[272,1536]{1,0:T(8,128)(2,1)}, u32[]{:S(2)}, u32[]{:S(2)}) %collective-permute-start.2) | collective-permute-done | bytes 835616 | tf_op jit(solution)/shard_map/ppermute | solution.py:14
  102.0 1.5 collective-permute-start.7
  104.7 4.6 %byte_sums.1 = f32[8,384]{1,0:T(8,128)S(1)} custom-call(s32[1]{0:T(128)} %bitcast.shard_ref, s32[1,512]{1,0:T(1,128)S(1)} %copy-done.5, bf16[384,1536]{1,0:T(8,128)(2,1)S(1)} %bitcast.61, bf16[384,1536]{1,0:T(8,128)(2,1)S(1)} %bitcast.58, bf16[384,1536]{1,0:T(8,128)(2,1)S(1)} %bitcast.60, bf16[256,1536]{1,0:T(8,128)(2,1)} %collective-permute-done.refs_0_, ...), custom_call_target="tpu_custom_call" | custom-call | tf_op jit(solution)/shard_map/byte_sums/pallas_call | solution.py:89
  109.3 1.6 collective-permute-start.4
  110.9 4.0 %base.1 = f32[384,1536]{1,0:T(8,128)S(1)} custom-call(s32[1]{0:T(128)} %bitcast.shard_ref, s32[1,512]{1,0:T(1,128)S(1)} %copy-done.5, bf16[384,1536]{1,0:T(8,128)(2,1)S(1)} %bitcast.62, bf16[256,1536]{1,0:T(8,128)(2,1)} %collective-permute-done.refs_0_, bf16[272,1536]{1,0:T(8,128)(2,1)} %collective-permute-done.1.refs_1_, ...), custom_call_target="tpu_custom_call" | custom-call | tf_op jit(solution)/shard_map/base/pallas_call | solution.py:129
  118.3 1.5 collective-permute-start.5
  120.4 1.3 fusion.39
  121.7 3.9 %fusion.73 = (bf16[640,1536]{1,0:T(8,128)(2,1)}, f32[640,1536]{1,0:T(8,128)}) fusion(f32[640,1536]{1,0:T(8,128)S(1)} %fusion.39, bf16[1,384,1536]{2,1,0:T(8,128)(2,1)S(1)} %copy-done.2, s32[384]{0:T(512)S(1)} %copy-done.39, bf16[384]{0:T(512)(128)(2,1)S(1)} %get-tuple-element.12), kind=kOutput, calls=%fused_computation.162 | convolution fusion | flops 757432320 | bytes 11012352 | tf_op jit(solution)/shard_map/dot_general | solution.py:259
  125.8 1.2 slice_bitcast_fusion.5
  128.7 19.9 %collective-permute-done.5 = f32[3,1]{1,0:T(4,128)} collective-permute-done((f32[3,1]{1,0:T(4,128)}, f32[3,1]{1,0:T(4,128)}, u32[]{:S(2)}, u32[]{:S(2)}) %collective-permute-start.5) | collective-permute-done | bytes 44 | tf_op jit(solution)/shard_map/ppermute | solution.py:14
  150.6 2.4 %collective-permute-done.6 = f32[3,385]{1,0:T(4,128)S(1)} collective-permute-done((f32[3,385]{1,0:T(4,128)S(1)}, f32[3,385]{1,0:T(4,128)S(1)}, u32[]{:S(2)}, u32[]{:S(2)}) %collective-permute-start.6) | collective-permute-done | bytes 4652 | tf_op jit(solution)/shard_map/ppermute | solution.py:22
  153.1 1.8 fusion.70
  157.0 2.0 copy-done.53
  159.0 1.4 fusion.2
  160.4 1.4 add_convert_fusion.1.refs_1_
  162.7 2.7 %fusion.6 = f32[768,512]{1,0:T(8,128)} fusion(bf16[1024,1536]{1,0:T(8,128)(2,1)S(1)} %copy-done.53, s32[]{:T(128)S(6)} %select_n.147, bf16[384,768]{1,0:T(8,128)(2,1)S(1)} %get-tuple-element.31, bf16[384,768]{1,0:T(8,128)(2,1)S(1)} %get-tuple-element.29, bf16[384,768]{1,0:T(8,128)(2,1)S(1)} %get-tuple-element.27, bf16[384,768]{1,0:T(8,128)(2,1)S(1)} %get-tuple-element.25), kind=kOutput, calls=%fused_computation.14 | convolution fusion | flops 1217396736 | bytes 5505028 | tf_op jit(solution)/shard_map/dot_general | solution.py:140
  165.4 5.1 %all-gather.5.cloned.1.call-done.refs_0_ = bf16[512,1536]{1,0:T(8,128)(2,1)} async-done(((bf16[128,1536]{1,0:T(8,128)(2,1)}), bf16[512,1536]{1,0:T(8,128)(2,1)}) %all-gather.5.cloned.1.call-update) | async-done | bytes 1572880 | tf_op jit(solution)/shard_map/all_gather | solution.py:188
  170.5 1.3 slice_bitcast_fusion.3
  172.5 4.7 %collective-permute-start.16 = (bf16[128,1536]{1,0:T(8,128)(2,1)S(1)}, bf16[128,1536]{1,0:T(8,128)(2,1)S(1)}, u32[]{:S(2)}, u32[]{:S(2)}) collective-permute-start(bf16[128,1536]{1,0:T(8,128)(2,1)S(1)} %get-tuple-element.45), channel_id=1, source_target_pairs={{0,4},{4,8},{1,5},{5,9},{2,6},{6,10},{3,7},{7,11},{16,20},{20,24},... | collective-permute-start | bytes 1179656 | tf_op jit(solution)/shard_map/ppermute | solution.py:30
  177.2 1.4 collective-permute-done.10
  178.7 3.5 %convert_add_fusion = f32[768,512]{1,0:T(8,128)S(1)} fusion(bf16[768,512]{1,0:T(8,128)(2,1)} %collective-permute-done.10, f32[768,512]{1,0:T(8,128)} %fusion.6, bf16[1024,1536]{1,0:T(8,128)(2,1)} %copy-done.54, s32[]{:T(128)S(6)} %select_n.147, bf16[384,768]{1,0:T(8,128)(2,1)S(1)} %copy-done.31, bf16[384,768]{1,0:T(8,128)(2,1)S(1)} %copy-done.37, ...), kind=kOutput, calls=%fused_computation.5 | convolution fusion | flops 1219362816 | bytes 7864324 | tf_op jit(solution)/shard_map/dot_general | solution.py:140
  182.3 1.1 collective-permute-start.11
  183.3 2.7 %collective-permute-done.16 = bf16[128,1536]{1,0:T(8,128)(2,1)S(1)} collective-permute-done((bf16[128,1536]{1,0:T(8,128)(2,1)S(1)}, bf16[128,1536]{1,0:T(8,128)(2,1)S(1)}, u32[]{:S(2)}, u32[]{:S(2)}) %collective-permute-start.16) | collective-permute-done | bytes 393248 | tf_op jit(solution)/shard_map/ppermute | solution.py:30
  186.1 1.6 fusion.45
  188.6 3.4 %collective-permute-done.11 = bf16[384,512]{1,0:T(8,128)(2,1)S(1)} collective-permute-done((bf16[384,512]{1,0:T(8,128)(2,1)S(1)}, bf16[384,512]{1,0:T(8,128)(2,1)S(1)}, u32[]{:S(2)}, u32[]{:S(2)}) %collective-permute-start.11) | collective-permute-done | bytes 393248 | tf_op jit(solution)/shard_map/ppermute | solution.py:22
  193.2 2.1 fusion.33
  195.4 1.6 fusion.17.refs_1_
  197.0 1.5 collective-permute-start.13
  198.5 1.2 slice_bitcast_fusion.1
  199.6 11.0 %collective-permute-start.18 = (bf16[128,1536]{1,0:T(8,128)(2,1)S(1)}, bf16[128,1536]{1,0:T(8,128)(2,1)S(1)}, u32[]{:S(2)}, u32[]{:S(2)}) collective-permute-start(bf16[128,1536]{1,0:T(8,128)(2,1)S(1)} %get-tuple-element.43), channel_id=1, source_target_pairs={{0,4},{4,8},{8,12},{1,5},{5,9},{9,13},{2,6},{6,10},{10,14},{3,7},{... | collective-permute-start | bytes 1179656 | tf_op jit(solution)/shard_map/ppermute | solution.py:14
  210.7 1.6 collective-permute-start.17
  212.2 2.5 %fusion.36 = f32[768,256]{1,0:T(8,128)S(1)} fusion(bf16[512,1536]{1,0:T(8,128)(2,1)} %collective-permute-done.12, s32[]{:T(128)S(6)} %select_n.153, bf16[384,768]{1,0:T(8,128)(2,1)} %copy-done.30, bf16[384,768]{1,0:T(8,128)(2,1)} %copy-done.36, bf16[384,768]{1,0:T(8,128)(2,1)} %copy-done.25, bf16[384,768]{1,0:T(8,128)(2,1)S(1)} %copy-done.21), kind=kOutput, calls=%fused_computation.63 | convolution fusion | flops 613416960 | bytes 3932164 | tf_op jit(solution)/shard_map/dot_general | solution.py:140
  214.8 1.8 fusion.16
  217.3 4.1 %collective-permute-done.17 = bf16[128,1536]{1,0:T(8,128)(2,1)S(1)} collective-permute-done((bf16[128,1536]{1,0:T(8,128)(2,1)S(1)}, bf16[128,1536]{1,0:T(8,128)(2,1)S(1)}, u32[]{:S(2)}, u32[]{:S(2)}) %collective-permute-start.17) | collective-permute-done | bytes 393248 | tf_op jit(solution)/shard_map/ppermute | solution.py:14
  221.4 2.0 fusion.44
  223.7 1.4 copy-done.4
  225.1 1.3 fusion.18
  (185 shorter events, 22.2 us)
Async XLA Ops:
  7.2 118.5 %all-gather.3.cloned.1.call-start = ((), (), s32[]{:S(2)}) async-start(), calls=%async_computation | async-start | bytes 3932160 | tf_op jit(solution)/shard_map/all_gather | solution.py:188
  8.3 11.4 %copy-start = (bf16[1,384,1536]{2,1,0:T(8,128)(2,1)S(1)}, bf16[1,384,1536]{2,1,0:T(8,128)(2,1)}, u32[]{:S(2)}) copy-start(bf16[1,384,1536]{2,1,0:T(8,128)(2,1)} %param.9) | copy-start | bytes 3538948
  8.3 11.4 %copy-start.1 = (bf16[1,384,1536]{2,1,0:T(8,128)(2,1)S(1)}, bf16[1,384,1536]{2,1,0:T(8,128)(2,1)}, u32[]{:S(2)}) copy-start(bf16[1,384,1536]{2,1,0:T(8,128)(2,1)} %param.10) | copy-start | bytes 3538948
  10.5 159.9 %all-gather.5.cloned.1.call-start = ((), (), s32[]{:S(2)}) async-start(), calls=%async_computation.1 | async-start | bytes 1966080 | tf_op jit(solution)/shard_map/all_gather | solution.py:188
  11.5 93.2 %collective-permute-start = (bf16[256,1536]{1,0:T(8,128)(2,1)}, bf16[256,1536]{1,0:T(8,128)(2,1)}, u32[]{:S(2)}, u32[]{:S(2)}) collective-permute-start(bf16[256,1536]{1,0:T(8,128)(2,1)} %pad_maximum_fusion.4.refs_2_), channel_id=1, source_target_pairs={{0,8},{4,12},{1,9},{5,13},{2,10},{6,14},{3,11},{7,15},{16,24},{20,... | collective-permute-start | bytes 2359304 | tf_op jit(solution)/shard_map/ppermute | solution.py:14
  18.4 86.3 %collective-permute-start.3 = (bf16[256,1536]{1,0:T(8,128)(2,1)}, bf16[256,1536]{1,0:T(8,128)(2,1)}, u32[]{:S(2)}, u32[]{:S(2)}) collective-permute-start(bf16[256,1536]{1,0:T(8,128)(2,1)} %pad_maximum_fusion.4.refs_2_), channel_id=1, source_target_pairs={{8,0},{12,4},{9,1},{13,5},{10,2},{14,6},{11,3},{15,7},{24,16},{28,... | collective-permute-start | bytes 2359304 | tf_op jit(solution)/shard_map/ppermute | solution.py:14
  21.1 79.6 %collective-permute-start.1 = (bf16[272,1536]{1,0:T(8,128)(2,1)}, bf16[272,1536]{1,0:T(8,128)(2,1)}, u32[]{:S(2)}, u32[]{:S(2)}) collective-permute-start(bf16[272,1536]{1,0:T(8,128)(2,1)} %get-tuple-element.47), channel_id=1, source_target_pairs={{0,4},{4,8},{8,12},{1,5},{5,9},{9,13},{2,6},{6,10},{10,14},{3,7},{... | collective-permute-start | bytes 2506760 | tf_op jit(solution)/shard_map/ppermute | solution.py:14
  25.5 74.4 %collective-permute-start.2 = (bf16[272,1536]{1,0:T(8,128)(2,1)}, bf16[272,1536]{1,0:T(8,128)(2,1)}, u32[]{:S(2)}, u32[]{:S(2)}) collective-permute-start(bf16[272,1536]{1,0:T(8,128)(2,1)} %get-tuple-element.46), channel_id=1, source_target_pairs={{4,0},{8,4},{12,8},{5,1},{9,5},{13,9},{6,2},{10,6},{14,10},{7,3},{... | collective-permute-start | bytes 2506760 | tf_op jit(solution)/shard_map/ppermute | solution.py:14
  28.3 124.7 %collective-permute-start.8 = (bf16[768,1536]{1,0:T(8,128)(2,1)}, bf16[768,1536]{1,0:T(8,128)(2,1)}, u32[]{:S(2)}, u32[]{:S(2)}) collective-permute-start(bf16[768,1536]{1,0:T(8,128)(2,1)} %pad_maximum_fusion), channel_id=1, source_target_pairs={{0,16},{16,0},{1,17},{17,1},{2,18},{18,2},{3,19},{19,3},{4,20},{20... | collective-permute-start | bytes 7077896 | tf_op jit(solution)/shard_map/ppermute | solution.py:22
  30.1 4.2 %copy-start.51 = (pred[384]{0:T(512)(128)(4,1)}, pred[384]{0:T(512)(128)(4,1)S(1)}, u32[]{:S(2)}) copy-start(pred[384]{0:T(512)(128)(4,1)S(1)} %compare_reduce_fusion) | copy-start | bytes 1156
  31.2 73.5 %copy-start.2 = (bf16[1,384,1536]{2,1,0:T(8,128)(2,1)S(1)}, bf16[1,384,1536]{2,1,0:T(8,128)(2,1)}, u32[]{:S(2)}) copy-start(bf16[1,384,1536]{2,1,0:T(8,128)(2,1)} %param.8) | copy-start | bytes 3538948
  102.0 12.9 %collective-permute-start.7 = (bf16[2,1536]{1,0:T(2,128)(2,1)}, bf16[2,1536]{1,0:T(2,128)(2,1)}, u32[]{:S(2)}, u32[]{:S(2)}) collective-permute-start(bf16[2,1536]{1,0:T(2,128)(2,1)} %pad_maximum_fusion.10), channel_id=1, source_target_pairs={{0,16},{16,0},{1,17},{17,1},{2,18},{18,2},{3,19},{19,3},{4,20},{20... | collective-permute-start | bytes 18440 | tf_op jit(solution)/shard_map/ppermute | solution.py:22
  109.3 7.7 %collective-permute-start.4 = (f32[8,384]{1,0:T(8,128)S(1)}, f32[8,384]{1,0:T(8,128)}, u32[]{:S(2)}, u32[]{:S(2)}) collective-permute-start(f32[8,384]{1,0:T(8,128)S(1)} %byte_sums.1), channel_id=1, source_target_pairs={{0,2},{2,0},{1,3},{3,1},{4,6},{6,4},{5,7},{7,5},{8,10},{10,8},{9,1... | collective-permute-start | bytes 36872 | tf_op jit(solution)/shard_map/ppermute | solution.py:22
  110.9 6.8 %copy-start.50 = (f32[384]{0:T(512)S(1)}, f32[384]{0:T(512)}, u32[]{:S(2)}) copy-start(f32[384]{0:T(512)} %select_multiply_fusion) | copy-start | bytes 4612
  110.9 8.9 %copy-start.52 = (pred[384]{0:T(512)(128)(4,1)S(1)}, pred[384]{0:T(512)(128)(4,1)}, u32[]{:S(2)}) copy-start(pred[384]{0:T(512)(128)(4,1)} %copy-done.51) | copy-start | bytes 1156
  110.9 9.5 %copy-start.39 = (s32[384]{0:T(512)S(1)}, s32[384]{0:T(512)}, u32[]{:S(2)}) copy-start(s32[384]{0:T(512)} %add_subtract_fusion) | copy-start | bytes 4612
  114.9 6.8 %copy-start.3 = (f32[384,1536]{1,0:T(8,128)}, f32[384,1536]{1,0:T(8,128)S(1)}, u32[]{:S(2)}) copy-start(f32[384,1536]{1,0:T(8,128)S(1)} %base.1) | copy-start | bytes 7077892
  118.3 30.3 %collective-permute-start.5 = (f32[3,1]{1,0:T(4,128)}, f32[3,1]{1,0:T(4,128)}, u32[]{:S(2)}, u32[]{:S(2)}) collective-permute-start(f32[3,1]{1,0:T(4,128)} %pad_maximum_fusion.11), channel_id=1, source_target_pairs={{4,0},{8,4},{12,8},{5,1},{9,5},{13,9},{6,2},{10,6},{14,10},{7,3},{... | collective-permute-start | bytes 44 | tf_op jit(solution)/shard_map/ppermute | solution.py:14
  125.7 34.7 %collective-permute-start.9 = (bf16[1024,1536]{1,0:T(8,128)(2,1)}, bf16[1024,1536]{1,0:T(8,128)(2,1)S(1)}, u32[]{:S(2)}, u32[]{:S(2)}) collective-permute-start(bf16[1024,1536]{1,0:T(8,128)(2,1)} %all-gather.3.cloned.1.call-done), channel_id=1, source_target_pairs={{0,1},{1,0},{2,3},{3,2},{4,5},{5,4},{6,7},{7,6},{8,9},{9,8},{10,11... | collective-permute-start | bytes 9437192 | tf_op jit(solution)/shard_map/ppermute | solution.py:22
  127.0 23.0 %copy-start.12 = (bf16[383,768]{1,0:T(8,128)(2,1)S(1)}, bf16[383,768]{1,0:T(8,128)(2,1)}, u32[]{:S(2)}) copy-start(bf16[383,768]{1,0:T(8,128)(2,1)} %get-tuple-element.34) | copy-start | bytes 1764868
  127.0 23.0 %copy-start.13 = (bf16[383,768]{1,0:T(8,128)(2,1)S(1)}, bf16[383,768]{1,0:T(8,128)(2,1)}, u32[]{:S(2)}) copy-start(bf16[383,768]{1,0:T(8,128)(2,1)} %get-tuple-element.35) | copy-start | bytes 1764868
  127.0 23.0 %copy-start.42 = (bf16[1,768]{1,0:T(2,128)(2,1)S(1)}, bf16[1,768]{1,0:T(2,128)(2,1)}, u32[]{:S(2)}) copy-start(bf16[1,768]{1,0:T(2,128)(2,1)} %get-tuple-element.57) | copy-start | bytes 4612
  127.0 23.0 %copy-start.43 = (bf16[1,768]{1,0:T(2,128)(2,1)S(1)}, bf16[1,768]{1,0:T(2,128)(2,1)}, u32[]{:S(2)}) copy-start(bf16[1,768]{1,0:T(2,128)(2,1)} %get-tuple-element.58) | copy-start | bytes 4612
  128.7 31.7 %copy-start.20 = (bf16[384,768]{1,0:T(8,128)(2,1)}, bf16[384,768]{1,0:T(8,128)(2,1)S(1)}, u32[]{:S(2)}) copy-start(bf16[384,768]{1,0:T(8,128)(2,1)S(1)} %get-tuple-element.24) | copy-start | bytes 1769476
  128.7 34.0 %copy-start.18 = (bf16[384,768]{1,0:T(8,128)(2,1)}, bf16[384,768]{1,0:T(8,128)(2,1)S(1)}, u32[]{:S(2)}) copy-start(bf16[384,768]{1,0:T(8,128)(2,1)S(1)} %get-tuple-element.25) | copy-start | bytes 1769476
  149.3 3.7 %collective-permute-start.6 = (f32[3,385]{1,0:T(4,128)S(1)}, f32[3,385]{1,0:T(4,128)S(1)}, u32[]{:S(2)}, u32[]{:S(2)}) collective-permute-start(f32[3,385]{1,0:T(4,128)S(1)} %pad_maximum_fusion.9), channel_id=1, source_target_pairs={{0,16},{16,0},{1,17},{17,1},{2,18},{18,2},{3,19},{19,3},{4,20},{20... | collective-permute-start | bytes 13868 | tf_op jit(solution)/shard_map/ppermute | solution.py:22
  150.6 12.1 %copy-start.22 = (bf16[384,768]{1,0:T(8,128)(2,1)}, bf16[384,768]{1,0:T(8,128)(2,1)S(1)}, u32[]{:S(2)}) copy-start(bf16[384,768]{1,0:T(8,128)(2,1)S(1)} %get-tuple-element.27) | copy-start | bytes 1769476
  150.6 28.0 %copy-start.25 = (bf16[384,768]{1,0:T(8,128)(2,1)}, bf16[384,768]{1,0:T(8,128)(2,1)S(1)}, u32[]{:S(2)}) copy-start(bf16[384,768]{1,0:T(8,128)(2,1)S(1)} %get-tuple-element.26) | copy-start | bytes 1769476
  156.2 4.2 %copy-start.30 = (bf16[384,768]{1,0:T(8,128)(2,1)}, bf16[384,768]{1,0:T(8,128)(2,1)S(1)}, u32[]{:S(2)}) copy-start(bf16[384,768]{1,0:T(8,128)(2,1)S(1)} %get-tuple-element.30) | copy-start | bytes 1769476
  156.2 6.5 %copy-start.27 = (bf16[384,768]{1,0:T(8,128)(2,1)}, bf16[384,768]{1,0:T(8,128)(2,1)S(1)}, u32[]{:S(2)}) copy-start(bf16[384,768]{1,0:T(8,128)(2,1)S(1)} %get-tuple-element.31) | copy-start | bytes 1769476
  157.0 5.7 %copy-start.33 = (bf16[384,768]{1,0:T(8,128)(2,1)}, bf16[384,768]{1,0:T(8,128)(2,1)S(1)}, u32[]{:S(2)}) copy-start(bf16[384,768]{1,0:T(8,128)(2,1)S(1)} %get-tuple-element.29) | copy-start | bytes 1769476
  162.1 16.6 %collective-permute-start.10 = (bf16[768,512]{1,0:T(8,128)(2,1)S(1)}, bf16[768,512]{1,0:T(8,128)(2,1)}, u32[]{:S(2)}, u32[]{:S(2)}) collective-permute-start(bf16[768,512]{1,0:T(8,128)(2,1)S(1)} %add_convert_fusion.1.refs_1_), channel_id=1, source_target_pairs={{0,2},{2,0},{1,3},{3,1},{4,6},{6,4},{5,7},{7,5},{8,10},{10,8},{9,1... | collective-permute-start | bytes 2359304 | tf_op jit(solution)/shard_map/ppermute | solution.py:22
  170.5 8.2 %copy-start.21 = (bf16[384,768]{1,0:T(8,128)(2,1)S(1)}, bf16[384,768]{1,0:T(8,128)(2,1)}, u32[]{:S(2)}) copy-start(bf16[384,768]{1,0:T(8,128)(2,1)} %copy-done.20) | copy-start | bytes 1769476
  170.5 8.2 %copy-start.31 = (bf16[384,768]{1,0:T(8,128)(2,1)S(1)}, bf16[384,768]{1,0:T(8,128)(2,1)}, u32[]{:S(2)}) copy-start(bf16[384,768]{1,0:T(8,128)(2,1)} %copy-done.30) | copy-start | bytes 1769476
  170.5 8.2 %copy-start.37 = (bf16[384,768]{1,0:T(8,128)(2,1)S(1)}, bf16[384,768]{1,0:T(8,128)(2,1)}, u32[]{:S(2)}) copy-start(bf16[384,768]{1,0:T(8,128)(2,1)} %copy-done.36) | copy-start | bytes 1769476
  170.5 22.7 %collective-permute-start.12 = (bf16[512,1536]{1,0:T(8,128)(2,1)}, bf16[512,1536]{1,0:T(8,128)(2,1)}, u32[]{:S(2)}, u32[]{:S(2)}) collective-permute-start(bf16[512,1536]{1,0:T(8,128)(2,1)} %after.5), channel_id=1, source_target_pairs={{0,1},{1,0},{2,3},{3,2},{4,5},{5,4},{6,7},{7,6},{8,9},{9,8},{10,11... | collective-permute-start | bytes 4718600 | tf_op jit(solution)/shard_map/ppermute | solution.py:22
  171.8 11.5 %collective-permute-start.15 = (bf16[128,1536]{1,0:T(8,128)(2,1)S(1)}, bf16[128,1536]{1,0:T(8,128)(2,1)S(1)}, u32[]{:S(2)}, u32[]{:S(2)}) collective-permute-start(bf16[128,1536]{1,0:T(8,128)(2,1)S(1)} %get-tuple-element.44), channel_id=1, source_target_pairs={{8,4},{12,8},{9,5},{13,9},{10,6},{14,10},{11,7},{15,11},{24,20},{2... | collective-permute-start | bytes 1179656 | tf_op jit(solution)/shard_map/ppermute | solution.py:30
  172.5 13.6 %collective-permute-start.16 = (bf16[128,1536]{1,0:T(8,128)(2,1)S(1)}, bf16[128,1536]{1,0:T(8,128)(2,1)S(1)}, u32[]{:S(2)}, u32[]{:S(2)}) collective-permute-start(bf16[128,1536]{1,0:T(8,128)(2,1)S(1)} %get-tuple-element.45), channel_id=1, source_target_pairs={{0,4},{4,8},{1,5},{5,9},{2,6},{6,10},{3,7},{7,11},{16,20},{20,24},... | collective-permute-start | bytes 1179656 | tf_op jit(solution)/shard_map/ppermute | solution.py:30
  182.3 9.8 %collective-permute-start.11 = (bf16[384,512]{1,0:T(8,128)(2,1)S(1)}, bf16[384,512]{1,0:T(8,128)(2,1)S(1)}, u32[]{:S(2)}, u32[]{:S(2)}) collective-permute-start(bf16[384,512]{1,0:T(8,128)(2,1)S(1)} %slice.305), channel_id=1, source_target_pairs={{0,16},{16,0},{1,17},{17,1},{2,18},{18,2},{3,19},{19,3},{4,20},{20... | collective-permute-start | bytes 1179656 | tf_op jit(solution)/shard_map/ppermute | solution.py:22
  187.6 5.5 %copy-start.26 = (bf16[384,768]{1,0:T(8,128)(2,1)S(1)}, bf16[384,768]{1,0:T(8,128)(2,1)}, u32[]{:S(2)}) copy-start(bf16[384,768]{1,0:T(8,128)(2,1)} %copy-done.25) | copy-start | bytes 1769476
  187.6 5.5 %copy-start.32 = (bf16[384,768]{1,0:T(8,128)(2,1)S(1)}, bf16[384,768]{1,0:T(8,128)(2,1)}, u32[]{:S(2)}) copy-start(bf16[384,768]{1,0:T(8,128)(2,1)} %copy-done.30) | copy-start | bytes 1769476
  187.6 5.5 %copy-start.38 = (bf16[384,768]{1,0:T(8,128)(2,1)S(1)}, bf16[384,768]{1,0:T(8,128)(2,1)}, u32[]{:S(2)}) copy-start(bf16[384,768]{1,0:T(8,128)(2,1)} %copy-done.36) | copy-start | bytes 1769476
  197.0 17.8 %collective-permute-start.13 = (bf16[768,256]{1,0:T(8,128)(2,1)}, bf16[768,256]{1,0:T(8,128)(2,1)}, u32[]{:S(2)}, u32[]{:S(2)}) collective-permute-start(bf16[768,256]{1,0:T(8,128)(2,1)} %fusion.17.refs_1_), channel_id=1, source_target_pairs={{0,2},{2,0},{1,3},{3,1},{4,6},{6,4},{5,7},{7,5},{8,10},{10,8},{9,1... | collective-permute-start | bytes 1179656 | tf_op jit(solution)/shard_map/ppermute | solution.py:22
  199.6 17.6 %collective-permute-start.18 = (bf16[128,1536]{1,0:T(8,128)(2,1)S(1)}, bf16[128,1536]{1,0:T(8,128)(2,1)S(1)}, u32[]{:S(2)}, u32[]{:S(2)}) collective-permute-start(bf16[128,1536]{1,0:T(8,128)(2,1)S(1)} %get-tuple-element.43), channel_id=1, source_target_pairs={{0,4},{4,8},{8,12},{1,5},{5,9},{9,13},{2,6},{6,10},{10,14},{3,7},{... | collective-permute-start | bytes 1179656 | tf_op jit(solution)/shard_map/ppermute | solution.py:14
  210.7 10.7 %collective-permute-start.17 = (bf16[128,1536]{1,0:T(8,128)(2,1)S(1)}, bf16[128,1536]{1,0:T(8,128)(2,1)S(1)}, u32[]{:S(2)}, u32[]{:S(2)}) collective-permute-start(bf16[128,1536]{1,0:T(8,128)(2,1)S(1)} %get-tuple-element.42), channel_id=1, source_target_pairs={{4,0},{8,4},{12,8},{5,1},{9,5},{13,9},{6,2},{10,6},{14,10},{7,3},{... | collective-permute-start | bytes 1179656 | tf_op jit(solution)/shard_map/ppermute | solution.py:14
  216.6 6.9 %copy-start.6 = (f32[384,1536]{1,0:T(8,128)S(1)}, f32[384,1536]{1,0:T(8,128)}, u32[]{:S(2)}) copy-start(f32[384,1536]{1,0:T(8,128)} %slice_dynamic-update-slice_fusion.3) | copy-start | bytes 7077892
  216.7 6.9 %copy-start.8 = (f32[384,512]{1,0:T(8,128)S(1)}, f32[384,512]{1,0:T(8,128)}, u32[]{:S(2)}) copy-start(f32[384,512]{1,0:T(8,128)} %copy-done.7) | copy-start | bytes 2359300
  216.7 6.8 %collective-permute-start.14 = (bf16[384,256]{1,0:T(8,128)(2,1)S(1)}, bf16[384,256]{1,0:T(8,128)(2,1)S(1)}, u32[]{:S(2)}, u32[]{:S(2)}) collective-permute-start(bf16[384,256]{1,0:T(8,128)(2,1)S(1)} %slice.306), channel_id=1, source_target_pairs={{0,16},{16,0},{1,17},{17,1},{2,18},{18,2},{3,19},{19,3},{4,20},{20... | collective-permute-start | bytes 589832 | tf_op jit(solution)/shard_map/ppermute | solution.py:22
  (30 other events, 76.1 us)
Sparse Core Ops, SparseCore 0:
  10.6 107.0 all-gather.2
  119.9 50.5 all-gather.4

commit v9 on v5

--- a/solution.py
+++ b/solution.py
@@ -245,7 +245,8 @@
         return total.astype(jnp.bfloat16)
 
     pieces = []
-    far_part, main_grad = None, None
+    main_grad = span_part(factors_other)
+    far_part = None
     for own_weight in own_weights:
         if far_part is not None:
             own_weight = after(own_weight, far_part)
@@ -268,8 +269,6 @@
             ).astype(jnp.float32)
         own = total[:row_count]
         returned = total[row_count:].astype(jnp.bfloat16)
-        if main_grad is None:
-            main_grad = span_part(returned)
         arrived = swapped(returned, "groups").astype(jnp.float32)
         pieces.append(
             [jnp.where(group_index == 0, own, arrived), jnp.where(group_index == 0, arrived, own)]

time: 211 us -> 205 us (0.972)
  waiting for transfers between devices: 89.2 us -> 82.2 us
  starting transfers between devices: 40.8 us -> 38.3 us
  matrix products: 23.1 us -> 25.5 us
  local copies, waits for them, and re-layouts: 19.3 us -> 21.7 us
    ppermute x6, waiting for transfers between devices: 33.9 us -> 20.8 us  [passed_on(): return lax.ppermute(x, axis, pairs)]
    ppermute x3, waiting for transfers between devices: 9.93 us -> 22.6 us  [passed_along(): return lax.ppermute(x, axis, pairs)]
    all_gather x2, waiting for transfers between devices: 9.56 us -> 0.01 us  [shards(): own_weights.append(lax.all_gather(piece, 'seq', axis=0, tiled=True))]
    ppermute x11, waiting for transfers between devices: 35.7 us -> 38.7 us  [swapped(): return lax.ppermute(x, axis, [(i, length - 1 - i) for i in range(length)])]
    unnamed x96 -> x100, local copies, waits for them, and re-layouts: 4.35 us -> 6.19 us
  transfers between devices with their start and end apart: 23 -> 23, of which waited for: 11 -> 13; matrix products, arithmetic and copies ran while one was open for 24% -> 26% of each run, Pallas kernels for 2% -> 2%
where the time goes in v9:
time: 205 us; the launch traced here: 204 us
  waiting for transfers between devices  82.2 us (40%)
  starting transfers between devices  38.3 us (19%)
  matrix products  25.5 us (12%)
  local copies, waits for them, and re-layouts  21.7 us (11%)
  other arithmetic  17.7 us (9%)
  between operations  14.6 us (7%)
  Pallas kernels  3.62 us (2%)
    ppermute x11, waiting for transfers between devices, swapped(): return lax.ppermute(x, axis, [(i, length - 1 - i) for i in range(length)])  38.7 us
    ppermute x3, waiting for transfers between devices, passed_along(): return lax.ppermute(x, axis, pairs)  22.6 us
    ppermute x6, waiting for transfers between devices, passed_on(): return lax.ppermute(x, axis, pairs)  20.8 us
    ppermute x6, starting transfers between devices, passed_on(): return lax.ppermute(x, axis, pairs)  18.8 us
    dot_general x8, matrix products, product(): lax.dot_general(rows, weight, (((1,), (1,)), ((), ())), preferred_element...  17 us
    ppermute x11, starting transfers between devices, swapped(): return lax.ppermute(x, axis, [(i, length - 1 - i) for i in range(length)])  11 us
    ppermute x3, starting transfers between devices, passed_along(): return lax.ppermute(x, axis, pairs)  8.28 us
    unnamed x100, local copies, waits for them, and re-layouts  6.19 us
  transfers between devices with their start and end apart: 23, of which 13 were waited for; matrix products, arithmetic and copies ran while one was open for 26% of the time, Pallas kernels for 2%

profile of v9, /device:TPU:0, one launch (start us, length us, event | category | flops | bytes accessed | tf_op | source)
XLA Modules:
  0.0 203.6 jit_solution(17060584757256432363)
XLA Ops:
  7.2 1.9 copy.38
  13.3 5.7 %collective-permute-start = (bf16[144,1536]{1,0:T(8,128)(2,1)}, bf16[144,1536]{1,0:T(8,128)(2,1)}, u32[]{:S(2)}, u32[]{:S(2)}) collective-permute-start(bf16[144,1536]{1,0:T(8,128)(2,1)} %get-tuple-element.42), channel_id=1, source_target_pairs={{0,4},{4,8},{8,12},{1,5},{5,9},{9,13},{2,6},{6,10},{10,14},{3,7},{... | collective-permute-start | bytes 1327112 | tf_op jit(solution)/shard_map/ppermute | solution.py:14
  19.0 1.3 collective-permute-start.2
  20.3 1.6 collective-permute-start.9
  22.9 1.1 dynamic-slice_bitcast_fusion.1
  24.0 1.6 dynamic-slice_bitcast_fusion
  27.6 5.6 %collective-permute-done.refs_1_ = bf16[144,1536]{1,0:T(8,128)(2,1)} collective-permute-done((bf16[144,1536]{1,0:T(8,128)(2,1)}, bf16[144,1536]{1,0:T(8,128)(2,1)}, u32[]{:S(2)}, u32[]{:S(2)}) %collective-permute-start) | collective-permute-done | bytes 442400 | tf_op jit(solution)/shard_map/ppermute | solution.py:14
  34.0 14.8 %collective-permute-done.2.refs_3_ = bf16[144,1536]{1,0:T(8,128)(2,1)} collective-permute-done((bf16[144,1536]{1,0:T(8,128)(2,1)}, bf16[144,1536]{1,0:T(8,128)(2,1)}, u32[]{:S(2)}, u32[]{:S(2)}) %collective-permute-start.2) | collective-permute-done | bytes 442400 | tf_op jit(solution)/shard_map/ppermute | solution.py:14
  50.1 1.6 collective-permute-start.7
  53.7 1.3 collective-permute-start.3
  55.0 18.3 %collective-permute-done.7 = bf16[2,1536]{1,0:T(2,128)(2,1)S(1)} collective-permute-done((bf16[2,1536]{1,0:T(2,128)(2,1)}, bf16[2,1536]{1,0:T(2,128)(2,1)S(1)}, u32[]{:S(2)}, u32[]{:S(2)}) %collective-permute-start.7) | collective-permute-done | bytes 6176 | tf_op jit(solution)/shard_map/ppermute | solution.py:22
  73.9 8.4 %collective-permute-done.3.refs_4_ = bf16[144,1536]{1,0:T(8,128)(2,1)S(1)} collective-permute-done((bf16[144,1536]{1,0:T(8,128)(2,1)}, bf16[144,1536]{1,0:T(8,128)(2,1)S(1)}, u32[]{:S(2)}, u32[]{:S(2)}) %collective-permute-start.3) | collective-permute-done | bytes 442400 | tf_op jit(solution)/shard_map/ppermute | solution.py:30
  83.3 3.6 %byte_sums.1 = f32[8,384]{1,0:T(8,128)S(1)} custom-call(s32[1]{0:T(128)} %bitcast.3.shard_ref, s32[1,512]{1,0:T(1,128)S(1)} %copy-done.5, bf16[384,1536]{1,0:T(8,128)(2,1)S(1)} %bitcast.51, bf16[384,1536]{1,0:T(8,128)(2,1)S(1)} %bitcast.53, bf16[384,1536]{1,0:T(8,128)(2,1)S(1)} %bitcast.55, bf16[144,1536]{1,0:T(8,128)(2,1)S(1)} %collective-permute-done.1.refs_0_, ...), custom_call_target="tpu_custom_call" | custom-call | tf_op jit(solution)/shard_map/byte_sums/pallas_call | solution.py:93
  86.9 1.6 collective-permute-start.4
  89.1 1.6 collective-permute-done.4
  91.9 1.3 collective-permute-start.5
  93.2 1.3 fusion.43
  94.5 3.9 %fusion.76 = (bf16[640,1536]{1,0:T(8,128)(2,1)}, f32[640,1536]{1,0:T(8,128)}) fusion(f32[640,1536]{1,0:T(8,128)S(1)} %fusion.43, bf16[1,384,1536]{2,1,0:T(8,128)(2,1)S(1)} %copy-done, s32[384]{0:T(512)S(1)} %get-tuple-element.61, bf16[384]{0:T(512)(128)(2,1)S(1)} %get-tuple-element.12), kind=kOutput, calls=%fused_computation.160 | convolution fusion | flops 757432320 | bytes 11012352 | tf_op jit(solution)/shard_map/dot_general | solution.py:222
  98.6 1.3 slice_bitcast_fusion.3
  100.8 2.2 %collective-permute-done.5 = f32[3,1]{1,0:T(4,128)} collective-permute-done((f32[3,1]{1,0:T(4,128)}, f32[3,1]{1,0:T(4,128)}, u32[]{:S(2)}, u32[]{:S(2)}) %collective-permute-start.5) | collective-permute-done | bytes 44 | tf_op jit(solution)/shard_map/ppermute | solution.py:14
  104.4 2.8 %fusion.22 = (bf16[384,768]{1,0:T(8,128)(2,1)}, bf16[384,768]{1,0:T(8,128)(2,1)}, bf16[384,768]{1,0:T(8,128)(2,1)}, bf16[384,768]{1,0:T(8,128)(2,1)}) fusion(bf16[1,768]{1,0:T(2,128)(2,1)S(1)} %copy-done.37, bf16[383,768]{1,0:T(8,128)(2,1)S(1)} %copy-done.9, bf16[1,384,1536]{2,1,0:T(8,128)(2,1)S(1)} %copy-done.2, s32[]{:T(128)S(6)} %select_n.148, ...), kind=kLoop, calls=%fused_computation.26 | loop fusion | flops 10616832 | bytes 7084040 | tf_op jit(solution)/shard_map/convert_element_type | solution.py:196
  108.1 1.2 slice_bitcast_fusion.1
  109.2 7.8 %collective-permute-start.16 = (bf16[128,1536]{1,0:T(8,128)(2,1)S(1)}, bf16[128,1536]{1,0:T(8,128)(2,1)S(1)}, u32[]{:S(2)}, u32[]{:S(2)}) collective-permute-start(bf16[128,1536]{1,0:T(8,128)(2,1)S(1)} %get-tuple-element.40), channel_id=1, source_target_pairs={{0,4},{4,8},{1,5},{5,9},{2,6},{6,10},{3,7},{7,11},{16,20},{20,24},... | collective-permute-start | bytes 1179656 | tf_op jit(solution)/shard_map/ppermute | solution.py:30
  118.7 1.9 fusion.74
  120.6 1.3 constant_dynamic-slice_fusion
  122.0 3.2 %subtract_convert_fusion = (bf16[384,768]{1,0:T(8,128)(2,1)S(1)}, bf16[384,768]{1,0:T(8,128)(2,1)S(1)}, bf16[384,768]{1,0:T(8,128)(2,1)S(1)}, bf16[384,768]{1,0:T(8,128)(2,1)S(1)}) fusion(bf16[1,768]{1,0:T(2,128)(2,1)S(1)} %copy-done.33, bf16[383,768]{1,0:T(8,128)(2,1)S(1)} %get-tuple-element.36, bf16[384,1536]{1,0:T(8,128)(2,1)} %collective-permute-done.8, ...), kind=kLoop, calls=%fused_computation.36 | loop fusion | flops 10616832 | bytes 7084040 | tf_op jit(solution)/shard_map/convert_element_type | solution.py:196
  125.2 9.3 %collective-permute-done.16 = bf16[128,1536]{1,0:T(8,128)(2,1)S(1)} collective-permute-done((bf16[128,1536]{1,0:T(8,128)(2,1)S(1)}, bf16[128,1536]{1,0:T(8,128)(2,1)S(1)}, u32[]{:S(2)}, u32[]{:S(2)}) %collective-permute-start.16) | collective-permute-done | bytes 393248 | tf_op jit(solution)/shard_map/ppermute | solution.py:30
  134.5 1.6 fusion.32
  136.0 6.9 %collective-permute-start.17 = (bf16[128,1536]{1,0:T(8,128)(2,1)S(1)}, bf16[128,1536]{1,0:T(8,128)(2,1)S(1)}, u32[]{:S(2)}, u32[]{:S(2)}) collective-permute-start(bf16[128,1536]{1,0:T(8,128)(2,1)S(1)} %get-tuple-element.16), channel_id=1, source_target_pairs={{0,4},{4,8},{8,12},{1,5},{5,9},{9,13},{2,6},{6,10},{10,14},{3,7},{... | collective-permute-start | bytes 1179656 | tf_op jit(solution)/shard_map/ppermute | solution.py:30
  143.0 1.5 collective-permute-start.19
  144.5 1.4 fusion.5
  146.0 3.7 %add_convert_fusion.refs_1_ = bf16[768,512]{1,0:T(8,128)(2,1)} fusion(f32[768,512]{1,0:T(8,128)S(1)} %fusion.5, bf16[1024,1536]{1,0:T(8,128)(2,1)} %collective-permute-done.10, s32[]{:T(128)S(6)} %select_n.149, bf16[384,768]{1,0:T(8,128)(2,1)S(1)} %get-tuple-element.28, bf16[384,768]{1,0:T(8,128)(2,1)S(1)} %get-tuple-element.68, ...), kind=kOutput, calls=%fused_computation.8 | convolution fusion | flops 1218183168 | bytes 6291460 | tf_op jit(solution)/shard_map/dot_general | solution.py:104
  149.7 1.1 copy-done.12
  150.8 1.5 collective-permute-start.11
  152.3 3.1 %collective-permute-done.19 = bf16[128,1536]{1,0:T(8,128)(2,1)} collective-permute-done((bf16[128,1536]{1,0:T(8,128)(2,1)S(1)}, bf16[128,1536]{1,0:T(8,128)(2,1)}, u32[]{:S(2)}, u32[]{:S(2)}) %collective-permute-start.19) | collective-permute-done | bytes 393248 | tf_op jit(solution)/shard_map/ppermute | solution.py:30
  155.5 2.1 %fusion.48 = bf16[1,128,1536]{2,1,0:T(8,128)(2,1)} fusion(bf16[128,1536]{1,0:T(8,128)(2,1)} %collective-permute-done.19, bf16[128,1536]{1,0:T(8,128)(2,1)S(1)} %collective-permute-done.17, f32[640,1536]{1,0:T(8,128)} %get-tuple-element.64), kind=kLoop, calls=%fused_computation.76 | loop fusion | flops 983040 | bytes 1966080 | tf_op jit(solution)/shard_map/broadcast_in_dim | solution.py:234
  157.6 1.0 copy-done.14
  158.8 3.3 %fusion.9 = f32[768,512]{1,0:T(8,128)S(1)} fusion(bf16[1024,1536]{1,0:T(8,128)(2,1)} %all-gather.4.cloned.1.call-done.refs_1_, s32[]{:T(128)S(6)} %select_n.147, bf16[384,768]{1,0:T(8,128)(2,1)} %copy-done.22, bf16[384,768]{1,0:T(8,128)(2,1)} %copy-done.24, bf16[384,768]{1,0:T(8,128)(2,1)S(1)} %copy-done.14, bf16[384,768]{1,0:T(8,128)(2,1)S(1)} %copy-done.16), kind=kOutput, calls=%fused_computation.16 | convolution fusion | flops 1217396736 | bytes 5505028 | tf_op jit(solution)/shard_map/dot_general | solution.py:104
  162.2 7.7 %collective-permute-done.11 = bf16[768,512]{1,0:T(8,128)(2,1)} collective-permute-done((bf16[768,512]{1,0:T(8,128)(2,1)S(1)}, bf16[768,512]{1,0:T(8,128)(2,1)}, u32[]{:S(2)}, u32[]{:S(2)}) %collective-permute-start.11) | collective-permute-done | bytes 786464 | tf_op jit(solution)/shard_map/ppermute | solution.py:22
  169.9 3.0 %convert_add_fusion = f32[768,512]{1,0:T(8,128)S(1)} fusion(bf16[768,512]{1,0:T(8,128)(2,1)} %collective-permute-done.11, f32[768,512]{1,0:T(8,128)S(1)} %fusion.9, bf16[1024,1536]{1,0:T(8,128)(2,1)} %collective-permute-done.10, s32[]{:T(128)S(6)} %select_n.147, bf16[384,768]{1,0:T(8,128)(2,1)S(1)} %copy-done.27, bf16[384,768]{1,0:T(8,128)(2,1)S(1)} %copy-done.29, ...), kind=kOutput, calls=%fused_computation.7 | convolution fusion | flops 1219362816 | bytes 7864324 | tf_op jit(solution)/shard_map/dot_general | solution.py:104
  173.0 1.7 collective-permute-start.12
  174.7 1.9 fusion.35
  177.5 1.6 collective-permute-start.14
  179.0 3.6 %collective-permute-done.12 = bf16[384,512]{1,0:T(8,128)(2,1)S(1)} collective-permute-done((bf16[384,512]{1,0:T(8,128)(2,1)S(1)}, bf16[384,512]{1,0:T(8,128)(2,1)S(1)}, u32[]{:S(2)}, u32[]{:S(2)}) %collective-permute-start.12) | collective-permute-done | bytes 393248 | tf_op jit(solution)/shard_map/ppermute | solution.py:22
  182.8 1.9 fusion.38
  184.8 2.2 %collective-permute-done.14 = bf16[768,256]{1,0:T(8,128)(2,1)S(1)} collective-permute-done((bf16[768,256]{1,0:T(8,128)(2,1)S(1)}, bf16[768,256]{1,0:T(8,128)(2,1)S(1)}, u32[]{:S(2)}, u32[]{:S(2)}) %collective-permute-start.14) | collective-permute-done | bytes 393248 | tf_op jit(solution)/shard_map/ppermute | solution.py:22
  188.4 5.1 %collective-permute-done.15 = bf16[384,256]{1,0:T(8,128)(2,1)S(1)} collective-permute-done((bf16[384,256]{1,0:T(8,128)(2,1)S(1)}, bf16[384,256]{1,0:T(8,128)(2,1)S(1)}, u32[]{:S(2)}, u32[]{:S(2)}) %collective-permute-start.15) | collective-permute-done | bytes 196640 | tf_op jit(solution)/shard_map/ppermute | solution.py:22
  193.8 3.3 %fusion.2 = bf16[1,384,1536]{2,1,0:T(8,128)(2,1)} fusion(f32[384,1536]{1,0:T(8,128)S(1)} %slice_dynamic-update-slice_fusion.4, bf16[512,1536]{1,0:T(8,128)(2,1)} %all-gather.6.cloned.1.call-done, s32[384]{0:T(512)S(1)} %copy-done.41, pred[384]{0:T(512)(128)(4,1)S(1)} %copy-done.44, bf16[1,384,1536]{2,1,0:T(8,128)(2,1)S(1)} %copy-done), kind=kOutput, calls=%fused_computation.4 | convolution fusion | flops 606732288 | bytes 6293376 | tf_op jit(solution)/shard_map/dot_general | solution.py:241
  (166 shorter events, 22.4 us)
Async XLA Ops:
  7.2 91.2 %all-gather.4.cloned.1.call-start = ((), (), s32[]{:S(2)}) async-start(), calls=%async_computation | async-start | bytes 3932160 | tf_op jit(solution)/shard_map/all_gather | solution.py:149
  11.2 11.2 %copy-start.5 = (s32[1,512]{1,0:T(1,128)S(1)}, s32[1,512]{1,0:T(1,128)}, u32[]{:S(2)}) copy-start(s32[1,512]{1,0:T(1,128)} %bounds_ref.1) | copy-start | bytes 6148
  12.2 137.5 %all-gather.8.cloned.1.call-start = ((), (), s32[]{:S(2)}) async-start(), calls=%async_computation.2 | async-start | bytes 1966080 | tf_op jit(solution)/shard_map/all_gather | solution.py:149
  13.3 19.9 %collective-permute-start = (bf16[144,1536]{1,0:T(8,128)(2,1)}, bf16[144,1536]{1,0:T(8,128)(2,1)}, u32[]{:S(2)}, u32[]{:S(2)}) collective-permute-start(bf16[144,1536]{1,0:T(8,128)(2,1)} %get-tuple-element.42), channel_id=1, source_target_pairs={{0,4},{4,8},{8,12},{1,5},{5,9},{9,13},{2,6},{6,10},{10,14},{3,7},{... | collective-permute-start | bytes 1327112 | tf_op jit(solution)/shard_map/ppermute | solution.py:14
  19.0 29.8 %collective-permute-start.2 = (bf16[144,1536]{1,0:T(8,128)(2,1)}, bf16[144,1536]{1,0:T(8,128)(2,1)}, u32[]{:S(2)}, u32[]{:S(2)}) collective-permute-start(bf16[144,1536]{1,0:T(8,128)(2,1)} %get-tuple-element.43), channel_id=1, source_target_pairs={{4,0},{8,4},{12,8},{5,1},{9,5},{13,9},{6,2},{10,6},{14,10},{7,3},{... | collective-permute-start | bytes 1327112 | tf_op jit(solution)/shard_map/ppermute | solution.py:14
  20.3 98.3 %collective-permute-start.9 = (bf16[384,1536]{1,0:T(8,128)(2,1)S(1)}, bf16[384,1536]{1,0:T(8,128)(2,1)}, u32[]{:S(2)}, u32[]{:S(2)}) collective-permute-start(bf16[384,1536]{1,0:T(8,128)(2,1)S(1)} %bitcast.52), channel_id=1, source_target_pairs={{0,16},{16,0},{1,17},{17,1},{2,18},{18,2},{3,19},{19,3},{4,20},{20... | collective-permute-start | bytes 3538952 | tf_op jit(solution)/shard_map/ppermute | solution.py:22
  21.9 98.7 %collective-permute-start.8 = (bf16[384,1536]{1,0:T(8,128)(2,1)S(1)}, bf16[384,1536]{1,0:T(8,128)(2,1)}, u32[]{:S(2)}, u32[]{:S(2)}) collective-permute-start(bf16[384,1536]{1,0:T(8,128)(2,1)S(1)} %bitcast.54), channel_id=1, source_target_pairs={{0,16},{16,0},{1,17},{17,1},{2,18},{18,2},{3,19},{19,3},{4,20},{20... | collective-permute-start | bytes 3538952 | tf_op jit(solution)/shard_map/ppermute | solution.py:22
  24.0 58.2 %copy-start = (bf16[1,384,1536]{2,1,0:T(8,128)(2,1)S(1)}, bf16[1,384,1536]{2,1,0:T(8,128)(2,1)}, u32[]{:S(2)}) copy-start(bf16[1,384,1536]{2,1,0:T(8,128)(2,1)} %param.8) | copy-start | bytes 3538948
  50.1 23.1 %collective-permute-start.7 = (bf16[2,1536]{1,0:T(2,128)(2,1)}, bf16[2,1536]{1,0:T(2,128)(2,1)S(1)}, u32[]{:S(2)}, u32[]{:S(2)}) collective-permute-start(bf16[2,1536]{1,0:T(2,128)(2,1)} %pad_maximum_fusion.6), channel_id=1, source_target_pairs={{0,16},{16,0},{1,17},{17,1},{2,18},{18,2},{3,19},{19,3},{4,20},{20... | collective-permute-start | bytes 18440 | tf_op jit(solution)/shard_map/ppermute | solution.py:22
  52.9 140.9 %all-gather.6.cloned.1.call-start = ((), (), s32[]{:S(2)}) async-start(), calls=%async_computation.1 | async-start | bytes 1966080 | tf_op jit(solution)/shard_map/all_gather | solution.py:236
  53.0 20.9 %collective-permute-start.1 = (bf16[144,1536]{1,0:T(8,128)(2,1)}, bf16[144,1536]{1,0:T(8,128)(2,1)S(1)}, u32[]{:S(2)}, u32[]{:S(2)}) collective-permute-start(bf16[144,1536]{1,0:T(8,128)(2,1)} %collective-permute-done.refs_1_), channel_id=1, source_target_pairs={{4,8},{8,12},{5,9},{9,13},{6,10},{10,14},{7,11},{11,15},{20,24},{2... | collective-permute-start | bytes 1327112 | tf_op jit(solution)/shard_map/ppermute | solution.py:30
  53.7 28.6 %collective-permute-start.3 = (bf16[144,1536]{1,0:T(8,128)(2,1)}, bf16[144,1536]{1,0:T(8,128)(2,1)S(1)}, u32[]{:S(2)}, u32[]{:S(2)}) collective-permute-start(bf16[144,1536]{1,0:T(8,128)(2,1)} %collective-permute-done.2.refs_3_), channel_id=1, source_target_pairs={{4,0},{8,4},{5,1},{9,5},{6,2},{10,6},{7,3},{11,7},{20,16},{24,20},... | collective-permute-start | bytes 1327112 | tf_op jit(solution)/shard_map/ppermute | solution.py:30
  83.3 7.4 %copy-start.45 = (f32[384]{0:T(512)S(1)}, f32[384]{0:T(512)}, u32[]{:S(2)}) copy-start(f32[384]{0:T(512)} %select_multiply_fusion) | copy-start | bytes 4612
  83.3 7.4 %copy-start.43 = (pred[384]{0:T(512)(128)(4,1)S(1)}, pred[384]{0:T(512)(128)(4,1)}, u32[]{:S(2)}) copy-start(pred[384]{0:T(512)(128)(4,1)} %copy-done.42) | copy-start | bytes 1156
  86.9 3.8 %collective-permute-start.4 = (f32[8,384]{1,0:T(8,128)S(1)}, f32[8,384]{1,0:T(8,128)S(1)}, u32[]{:S(2)}, u32[]{:S(2)}) collective-permute-start(f32[8,384]{1,0:T(8,128)S(1)} %byte_sums.1), channel_id=1, source_target_pairs={{0,2},{2,0},{1,3},{3,1},{4,6},{6,4},{5,7},{7,5},{8,10},{10,8},{9,1... | collective-permute-start | bytes 36872 | tf_op jit(solution)/shard_map/ppermute | solution.py:22
  91.9 11.2 %collective-permute-start.5 = (f32[3,1]{1,0:T(4,128)}, f32[3,1]{1,0:T(4,128)}, u32[]{:S(2)}, u32[]{:S(2)}) collective-permute-start(f32[3,1]{1,0:T(4,128)} %pad_maximum_fusion.7), channel_id=1, source_target_pairs={{4,0},{8,4},{12,8},{5,1},{9,5},{13,9},{6,2},{10,6},{14,10},{7,3},{... | collective-permute-start | bytes 44 | tf_op jit(solution)/shard_map/ppermute | solution.py:14
  98.4 5.9 %copy-start.7 = (bf16[383,768]{1,0:T(8,128)(2,1)S(1)}, bf16[383,768]{1,0:T(8,128)(2,1)}, u32[]{:S(2)}) copy-start(bf16[383,768]{1,0:T(8,128)(2,1)} %get-tuple-element.30) | copy-start | bytes 1764868
  98.4 5.9 %copy-start.8 = (bf16[383,768]{1,0:T(8,128)(2,1)S(1)}, bf16[383,768]{1,0:T(8,128)(2,1)}, u32[]{:S(2)}) copy-start(bf16[383,768]{1,0:T(8,128)(2,1)} %get-tuple-element.31) | copy-start | bytes 1764868
  98.4 5.9 %copy-start.9 = (bf16[383,768]{1,0:T(8,128)(2,1)S(1)}, bf16[383,768]{1,0:T(8,128)(2,1)}, u32[]{:S(2)}) copy-start(bf16[383,768]{1,0:T(8,128)(2,1)} %get-tuple-element.32) | copy-start | bytes 1764868
  98.4 5.9 %copy-start.10 = (bf16[383,768]{1,0:T(8,128)(2,1)S(1)}, bf16[383,768]{1,0:T(8,128)(2,1)}, u32[]{:S(2)}) copy-start(bf16[383,768]{1,0:T(8,128)(2,1)} %get-tuple-element.33) | copy-start | bytes 1764868
  98.4 5.9 %copy-start.35 = (bf16[1,768]{1,0:T(2,128)(2,1)S(1)}, bf16[1,768]{1,0:T(2,128)(2,1)}, u32[]{:S(2)}) copy-start(bf16[1,768]{1,0:T(2,128)(2,1)} %get-tuple-element.51) | copy-start | bytes 4612
  98.5 5.9 %copy-start.36 = (bf16[1,768]{1,0:T(2,128)(2,1)S(1)}, bf16[1,768]{1,0:T(2,128)(2,1)}, u32[]{:S(2)}) copy-start(bf16[1,768]{1,0:T(2,128)(2,1)} %get-tuple-element.52) | copy-start | bytes 4612
  98.5 5.9 %copy-start.37 = (bf16[1,768]{1,0:T(2,128)(2,1)S(1)}, bf16[1,768]{1,0:T(2,128)(2,1)}, u32[]{:S(2)}) copy-start(bf16[1,768]{1,0:T(2,128)(2,1)} %get-tuple-element.53) | copy-start | bytes 4612
  98.5 5.9 %copy-start.38 = (bf16[1,768]{1,0:T(2,128)(2,1)S(1)}, bf16[1,768]{1,0:T(2,128)(2,1)}, u32[]{:S(2)}) copy-start(bf16[1,768]{1,0:T(2,128)(2,1)} %get-tuple-element.54) | copy-start | bytes 4612
  98.5 5.9 %copy-start.39 = (f32[384]{0:T(512)S(1)}, f32[384]{0:T(512)}, u32[]{:S(2)}) copy-start(f32[384]{0:T(512)} %get-tuple-element.49) | copy-start | bytes 4612
  98.5 5.9 %copy-start.40 = (f32[384]{0:T(512)S(1)}, f32[384]{0:T(512)}, u32[]{:S(2)}) copy-start(f32[384]{0:T(512)} %get-tuple-element.50) | copy-start | bytes 4612
  98.5 47.5 %collective-permute-start.10 = (bf16[1024,1536]{1,0:T(8,128)(2,1)}, bf16[1024,1536]{1,0:T(8,128)(2,1)}, u32[]{:S(2)}, u32[]{:S(2)}) collective-permute-start(bf16[1024,1536]{1,0:T(8,128)(2,1)} %all-gather.4.cloned.1.call-done.refs_1_), channel_id=1, source_target_pairs={{0,1},{1,0},{2,3},{3,2},{4,5},{5,4},{6,7},{7,6},{8,9},{9,8},{10,11... | collective-permute-start | bytes 9437192 | tf_op jit(solution)/shard_map/ppermute | solution.py:22
  103.7 3.7 %collective-permute-start.6 = (f32[3,385]{1,0:T(4,128)S(1)}, f32[3,385]{1,0:T(4,128)S(1)}, u32[]{:S(2)}, u32[]{:S(2)}) collective-permute-start(f32[3,385]{1,0:T(4,128)S(1)} %pad_maximum_fusion.5), channel_id=1, source_target_pairs={{0,16},{16,0},{1,17},{17,1},{2,18},{18,2},{3,19},{19,3},{4,20},{20... | collective-permute-start | bytes 13868 | tf_op jit(solution)/shard_map/ppermute | solution.py:22
  109.2 25.2 %collective-permute-start.16 = (bf16[128,1536]{1,0:T(8,128)(2,1)S(1)}, bf16[128,1536]{1,0:T(8,128)(2,1)S(1)}, u32[]{:S(2)}, u32[]{:S(2)}) collective-permute-start(bf16[128,1536]{1,0:T(8,128)(2,1)S(1)} %get-tuple-element.40), channel_id=1, source_target_pairs={{0,4},{4,8},{1,5},{5,9},{2,6},{6,10},{3,7},{7,11},{16,20},{20,24},... | collective-permute-start | bytes 1179656 | tf_op jit(solution)/shard_map/ppermute | solution.py:30
  117.0 17.5 %collective-permute-start.18 = (bf16[128,1536]{1,0:T(8,128)(2,1)S(1)}, bf16[128,1536]{1,0:T(8,128)(2,1)S(1)}, u32[]{:S(2)}, u32[]{:S(2)}) collective-permute-start(bf16[128,1536]{1,0:T(8,128)(2,1)S(1)} %get-tuple-element.41), channel_id=1, source_target_pairs={{8,4},{12,8},{9,5},{13,9},{10,6},{14,10},{11,7},{15,11},{24,20},{2... | collective-permute-start | bytes 1179656 | tf_op jit(solution)/shard_map/ppermute | solution.py:30
  121.9 22.5 %copy-start.13 = (bf16[384,768]{1,0:T(8,128)(2,1)S(1)}, bf16[384,768]{1,0:T(8,128)(2,1)}, u32[]{:S(2)}) copy-start(bf16[384,768]{1,0:T(8,128)(2,1)} %get-tuple-element.25) | copy-start | bytes 1769476
  122.0 22.5 %copy-start.15 = (bf16[384,768]{1,0:T(8,128)(2,1)S(1)}, bf16[384,768]{1,0:T(8,128)(2,1)}, u32[]{:S(2)}) copy-start(bf16[384,768]{1,0:T(8,128)(2,1)} %get-tuple-element.65) | copy-start | bytes 1769476
  125.2 20.8 %copy-start.22 = (bf16[384,768]{1,0:T(8,128)(2,1)}, bf16[384,768]{1,0:T(8,128)(2,1)S(1)}, u32[]{:S(2)}) copy-start(bf16[384,768]{1,0:T(8,128)(2,1)S(1)} %get-tuple-element.29) | copy-start | bytes 1769476
  125.2 20.8 %copy-start.24 = (bf16[384,768]{1,0:T(8,128)(2,1)}, bf16[384,768]{1,0:T(8,128)(2,1)S(1)}, u32[]{:S(2)}) copy-start(bf16[384,768]{1,0:T(8,128)(2,1)S(1)} %get-tuple-element.67) | copy-start | bytes 1769476
  125.2 20.8 %copy-start.26 = (bf16[384,768]{1,0:T(8,128)(2,1)}, bf16[384,768]{1,0:T(8,128)(2,1)S(1)}, u32[]{:S(2)}) copy-start(bf16[384,768]{1,0:T(8,128)(2,1)S(1)} %get-tuple-element.28) | copy-start | bytes 1769476
  125.2 20.8 %copy-start.28 = (bf16[384,768]{1,0:T(8,128)(2,1)}, bf16[384,768]{1,0:T(8,128)(2,1)S(1)}, u32[]{:S(2)}) copy-start(bf16[384,768]{1,0:T(8,128)(2,1)S(1)} %get-tuple-element.68) | copy-start | bytes 1769476
  125.2 19.3 %copy-start.6 = (bf16[1024,1536]{1,0:T(8,128)(2,1)S(1)}, bf16[1024,1536]{1,0:T(8,128)(2,1)}, u32[]{:S(2)}) copy-start(bf16[1024,1536]{1,0:T(8,128)(2,1)} %all-gather.4.cloned.1.call-done.refs_1_) | copy-start | bytes 9437188
  136.0 16.3 %collective-permute-start.17 = (bf16[128,1536]{1,0:T(8,128)(2,1)S(1)}, bf16[128,1536]{1,0:T(8,128)(2,1)S(1)}, u32[]{:S(2)}, u32[]{:S(2)}) collective-permute-start(bf16[128,1536]{1,0:T(8,128)(2,1)S(1)} %get-tuple-element.16), channel_id=1, source_target_pairs={{0,4},{4,8},{8,12},{1,5},{5,9},{9,13},{2,6},{6,10},{10,14},{3,7},{... | collective-permute-start | bytes 1179656 | tf_op jit(solution)/shard_map/ppermute | solution.py:30
  143.0 12.5 %collective-permute-start.19 = (bf16[128,1536]{1,0:T(8,128)(2,1)S(1)}, bf16[128,1536]{1,0:T(8,128)(2,1)}, u32[]{:S(2)}, u32[]{:S(2)}) collective-permute-start(bf16[128,1536]{1,0:T(8,128)(2,1)S(1)} %get-tuple-element.17), channel_id=1, source_target_pairs={{4,0},{8,4},{12,8},{5,1},{9,5},{13,9},{6,2},{10,6},{14,10},{7,3},{... | collective-permute-start | bytes 1179656 | tf_op jit(solution)/shard_map/ppermute | solution.py:30
  149.7 25.0 %collective-permute-start.13 = (bf16[512,1536]{1,0:T(8,128)(2,1)}, bf16[512,1536]{1,0:T(8,128)(2,1)}, u32[]{:S(2)}, u32[]{:S(2)}) collective-permute-start(bf16[512,1536]{1,0:T(8,128)(2,1)} %after.6), channel_id=1, source_target_pairs={{0,1},{1,0},{2,3},{3,2},{4,5},{5,4},{6,7},{7,6},{8,9},{9,8},{10,11... | collective-permute-start | bytes 4718600 | tf_op jit(solution)/shard_map/ppermute | solution.py:22
  150.8 19.0 %collective-permute-start.11 = (bf16[768,512]{1,0:T(8,128)(2,1)S(1)}, bf16[768,512]{1,0:T(8,128)(2,1)}, u32[]{:S(2)}, u32[]{:S(2)}) collective-permute-start(bf16[768,512]{1,0:T(8,128)(2,1)S(1)} %copy-done.12), channel_id=1, source_target_pairs={{0,2},{2,0},{1,3},{3,1},{4,6},{6,4},{5,7},{7,5},{8,10},{10,8},{9,1... | collective-permute-start | bytes 2359304 | tf_op jit(solution)/shard_map/ppermute | solution.py:22
  158.8 11.0 %copy-start.19 = (bf16[384,768]{1,0:T(8,128)(2,1)S(1)}, bf16[384,768]{1,0:T(8,128)(2,1)}, u32[]{:S(2)}) copy-start(bf16[384,768]{1,0:T(8,128)(2,1)} %get-tuple-element.24) | copy-start | bytes 1769476
  158.8 11.0 %copy-start.21 = (bf16[384,768]{1,0:T(8,128)(2,1)S(1)}, bf16[384,768]{1,0:T(8,128)(2,1)}, u32[]{:S(2)}) copy-start(bf16[384,768]{1,0:T(8,128)(2,1)} %get-tuple-element.66) | copy-start | bytes 1769476
  158.8 11.0 %copy-start.27 = (bf16[384,768]{1,0:T(8,128)(2,1)S(1)}, bf16[384,768]{1,0:T(8,128)(2,1)}, u32[]{:S(2)}) copy-start(bf16[384,768]{1,0:T(8,128)(2,1)} %copy-done.26) | copy-start | bytes 1769476
  158.8 11.0 %copy-start.29 = (bf16[384,768]{1,0:T(8,128)(2,1)S(1)}, bf16[384,768]{1,0:T(8,128)(2,1)}, u32[]{:S(2)}) copy-start(bf16[384,768]{1,0:T(8,128)(2,1)} %copy-done.28) | copy-start | bytes 1769476
  173.0 9.6 %collective-permute-start.12 = (bf16[384,512]{1,0:T(8,128)(2,1)S(1)}, bf16[384,512]{1,0:T(8,128)(2,1)S(1)}, u32[]{:S(2)}, u32[]{:S(2)}) collective-permute-start(bf16[384,512]{1,0:T(8,128)(2,1)S(1)} %slice.279), channel_id=1, source_target_pairs={{0,16},{16,0},{1,17},{17,1},{2,18},{18,2},{3,19},{19,3},{4,20},{20... | collective-permute-start | bytes 1179656 | tf_op jit(solution)/shard_map/ppermute | solution.py:22
  177.5 9.4 %collective-permute-start.14 = (bf16[768,256]{1,0:T(8,128)(2,1)S(1)}, bf16[768,256]{1,0:T(8,128)(2,1)S(1)}, u32[]{:S(2)}, u32[]{:S(2)}) collective-permute-start(bf16[768,256]{1,0:T(8,128)(2,1)S(1)} %fusion.20), channel_id=1, source_target_pairs={{0,2},{2,0},{1,3},{3,1},{4,6},{6,4},{5,7},{7,5},{8,10},{10,8},{9,1... | collective-permute-start | bytes 1179656 | tf_op jit(solution)/shard_map/ppermute | solution.py:22
  187.8 5.7 %collective-permute-start.15 = (bf16[384,256]{1,0:T(8,128)(2,1)S(1)}, bf16[384,256]{1,0:T(8,128)(2,1)S(1)}, u32[]{:S(2)}, u32[]{:S(2)}) collective-permute-start(bf16[384,256]{1,0:T(8,128)(2,1)S(1)} %slice.280), channel_id=1, source_target_pairs={{0,16},{16,0},{1,17},{17,1},{2,18},{18,2},{3,19},{19,3},{4,20},{20... | collective-permute-start | bytes 589832 | tf_op jit(solution)/shard_map/ppermute | solution.py:22
  (23 other events, 73.6 us)
Sparse Core Ops, SparseCore 0:
  12.3 81.0 all-gather.3
  95.5 40.1 all-gather.7
  157.7 35.3 all-gather.5

commit v10 on v9

--- a/solution.py
+++ b/solution.py
@@ -224,14 +224,13 @@
         )
         terms = [span_terms[i * span_rows : (i + 1) * span_rows] for i in range(2 * reach + 1)]
 
-        def moved(block, by, further):
-            moved_block = passed_on(block.astype(jnp.bfloat16), "seq", by, further)
-            return moved_block.astype(jnp.float32)
-
-        outer = after(jnp.stack([terms[0], terms[4]]).astype(jnp.bfloat16), ready)
-        span_sums = terms[2] + moved(terms[3] + moved(outer[1], 1, 2), 1, 1)
-        span_sums = span_sums + moved(terms[1] + moved(outer[0], -1, -2), -1, -1)
-        return span_sums.astype(jnp.bfloat16)[None]
+        parts = after(jnp.concatenate(terms, 0).astype(jnp.bfloat16), ready)
+        received = [
+            passed_along(parts[i * span_rows : (i + 1) * span_rows], "seq", i - reach)
+            for i in range(2 * reach + 1)
+            if i != reach
+        ]
+        return terms[reach], received
 
     window_grad = lax.all_gather(
         after(main_in_grad[0], own_weights[0]), "seq", axis=0, tiled=True
@@ -245,7 +244,7 @@
         return total.astype(jnp.bfloat16)
 
     pieces = []
-    main_grad = span_part(factors_other)
+    span_sums, received = span_part(factors_other)
     far_part = None
     for own_weight in own_weights:
         if far_part is not None:
@@ -264,8 +263,9 @@
             incoming = swapped(far_part, "tensor").astype(jnp.float32)
             total = partial(*half(tensor_index)).astype(jnp.float32) + incoming
         else:
+            far_part = partial(own_weight, other_weight)
             total = lax.psum_scatter(
-                partial(own_weight, other_weight), "tensor", scatter_dimension=1, tiled=True
+                far_part, "tensor", scatter_dimension=1, tiled=True
             ).astype(jnp.float32)
         own = total[:row_count]
         returned = total[row_count:].astype(jnp.bfloat16)
@@ -273,6 +273,10 @@
         pieces.append(
             [jnp.where(group_index == 0, own, arrived), jnp.where(group_index == 0, arrived, own)]
         )
+    span_sums = after(span_sums, far_part)
+    for block in received:
+        span_sums = span_sums + block.astype(jnp.float32)
+    main_grad = span_sums.astype(jnp.bfloat16)[None]
     widths = [high - low for low, high in cuts]
     routing = jnp.concatenate(
         [

time: 205 us -> 217 us (1.059)
  waiting for transfers between devices: 82.2 us -> 102 us
  other arithmetic: 17.7 us -> 14.6 us
    all_gather x2, waiting for transfers between devices: 0.01 us -> 23.7 us  [shards(): own_weights.append(lax.all_gather(piece, 'seq', axis=0, tiled=True))]
    ppermute x6 -> x2, waiting for transfers between devices: 20.8 us -> 0.01 us  [passed_on(): return lax.ppermute(x, axis, pairs)]
    ppermute x3 -> x7, waiting for transfers between devices: 22.6 us -> 41 us  [passed_along(): return lax.ppermute(x, axis, pairs)]
    ppermute x6 -> x2, starting transfers between devices: 18.8 us -> 2.71 us  [passed_on(): return lax.ppermute(x, axis, pairs)]
    ppermute x3 -> x7, starting transfers between devices: 8.28 us -> 21.6 us  [passed_along(): return lax.ppermute(x, axis, pairs)]
    unnamed x100 -> x122, local copies, waits for them, and re-layouts: 6.19 us -> 3.89 us
    slice x0 -> x2, local copies, waits for them, and re-layouts: none -> 2.17 us  [the longest x1 1.18 us: span_part(): parts[i * span_rows:(i + 1) * span_rows]]
  transfers between devices with their start and end apart: 23 -> 23, of which waited for: 13 -> 11; matrix products, arithmetic and copies ran while one was open for 26% -> 23% of each run, Pallas kernels for 2% -> 2%
where the time goes in v10:
time: 217 us; the launch traced here: 216 us
  waiting for transfers between devices  102 us (47%)
  starting transfers between devices  37.2 us (17%)
  matrix products  24.4 us (11%)
  local copies, waits for them, and re-layouts  19.8 us (9%)
  between operations  14.8 us (7%)
  other arithmetic  14.6 us (7%)
  Pallas kernels  3.9 us (2%)
    ppermute x7, waiting for transfers between devices, passed_along(): return lax.ppermute(x, axis, pairs)  41 us
    ppermute x11, waiting for transfers between devices, swapped(): return lax.ppermute(x, axis, [(i, length - 1 - i) for i in range(length)])  36.9 us
    all_gather x2, waiting for transfers between devices, shards(): own_weights.append(lax.all_gather(piece, 'seq', axis=0, tiled=True))  23.7 us
    ppermute x7, starting transfers between devices, passed_along(): return lax.ppermute(x, axis, pairs)  21.6 us
    dot_general x8, matrix products, product(): lax.dot_general(rows, weight, (((1,), (1,)), ((), ())), preferred_element...  17.2 us
    ppermute x11, starting transfers between devices, swapped(): return lax.ppermute(x, axis, [(i, length - 1 - i) for i in range(length)])  12.7 us
    convert_element_type x2, other arithmetic, grads(): key_grad.astype(jnp.bfloat16)  5.1 us
  transfers between devices with their start and end apart: 23, of which 11 were waited for; matrix products, arithmetic and copies ran while one was open for 23% of the time, Pallas kernels for 2%

profile of v10, /device:TPU:0, one launch (start us, length us, event | category | flops | bytes accessed | tf_op | source)
XLA Modules:
  0.0 216.2 jit_solution(16866392986713088478)
XLA Ops:
  7.2 1.9 copy.40
  9.2 1.0 dynamic_slice.89
  10.2 1.0 dynamic_slice.88
  13.3 1.3 collective-permute-start.2
  14.6 6.3 %collective-permute-start = (bf16[144,1536]{1,0:T(8,128)(2,1)}, bf16[144,1536]{1,0:T(8,128)(2,1)}, u32[]{:S(2)}, u32[]{:S(2)}) collective-permute-start(bf16[144,1536]{1,0:T(8,128)(2,1)} %get-tuple-element.40), channel_id=1, source_target_pairs={{0,4},{4,8},{8,12},{1,5},{5,9},{9,13},{2,6},{6,10},{10,14},{3,7},{... | collective-permute-start | bytes 1327112 | tf_op jit(solution)/shard_map/ppermute | solution.py:14
  20.9 2.0 collective-permute-start.9
  23.4 1.1 dynamic-slice_bitcast_fusion.1
  24.6 1.6 dynamic-slice_bitcast_fusion
  28.2 7.4 %collective-permute-done.2.refs_3_ = bf16[144,1536]{1,0:T(8,128)(2,1)} collective-permute-done((bf16[144,1536]{1,0:T(8,128)(2,1)}, bf16[144,1536]{1,0:T(8,128)(2,1)}, u32[]{:S(2)}, u32[]{:S(2)}) %collective-permute-start.2) | collective-permute-done | bytes 442400 | tf_op jit(solution)/shard_map/ppermute | solution.py:14
  38.5 2.0 collective-permute-start.7
  41.7 1.4 collective-permute-start.1
  43.1 1.3 collective-permute-start.3
  44.4 29.4 %collective-permute-done.7 = bf16[2,1536]{1,0:T(2,128)(2,1)S(1)} collective-permute-done((bf16[2,1536]{1,0:T(2,128)(2,1)}, bf16[2,1536]{1,0:T(2,128)(2,1)S(1)}, u32[]{:S(2)}, u32[]{:S(2)}) %collective-permute-start.7) | collective-permute-done | bytes 6176 | tf_op jit(solution)/shard_map/ppermute | solution.py:22
  74.4 15.9 %all-gather.4.cloned.1.call-done.refs_1_ = bf16[1024,1536]{1,0:T(8,128)(2,1)} async-done(((bf16[256,1536]{1,0:T(8,128)(2,1)}), bf16[1024,1536]{1,0:T(8,128)(2,1)}) %all-gather.4.cloned.1.call-update) | async-done | bytes 3145744 | tf_op jit(solution)/shard_map/all_gather | solution.py:149
  92.1 3.9 %byte_sums.1 = f32[8,384]{1,0:T(8,128)S(1)} custom-call(s32[1]{0:T(128)} %bitcast.3.shard_ref, s32[1,512]{1,0:T(1,128)S(1)} %copy-done.5, bf16[384,1536]{1,0:T(8,128)(2,1)S(1)} %bitcast.43, bf16[384,1536]{1,0:T(8,128)(2,1)S(1)} %bitcast.45, bf16[384,1536]{1,0:T(8,128)(2,1)S(1)} %bitcast.47, bf16[144,1536]{1,0:T(8,128)(2,1)} %collective-permute-done.1.refs_0_, ...), custom_call_target="tpu_custom_call" | custom-call | tf_op jit(solution)/shard_map/byte_sums/pallas_call | solution.py:93
  96.0 1.6 collective-permute-start.4
  97.5 2.2 %collective-permute-done.4 = f32[8,384]{1,0:T(8,128)S(1)} collective-permute-done((f32[8,384]{1,0:T(8,128)S(1)}, f32[8,384]{1,0:T(8,128)S(1)}, u32[]{:S(2)}, u32[]{:S(2)}) %collective-permute-start.4) | collective-permute-done | bytes 12320 | tf_op jit(solution)/shard_map/ppermute | solution.py:22
  99.8 1.5 collective-permute-start.5
  101.4 1.3 fusion.39
  102.7 2.5 %collective-permute-done.5 = f32[3,1]{1,0:T(4,128)S(1)} collective-permute-done((f32[3,1]{1,0:T(4,128)S(1)}, f32[3,1]{1,0:T(4,128)S(1)}, u32[]{:S(2)}, u32[]{:S(2)}) %collective-permute-start.5) | collective-permute-done | bytes 44 | tf_op jit(solution)/shard_map/ppermute | solution.py:14
  105.3 1.6 collective-permute-start.6
  107.1 1.9 fusion.22
  109.1 2.5 %fusion.71 = (bf16[383,768]{1,0:T(8,128)(2,1)S(1)}, bf16[383,768]{1,0:T(8,128)(2,1)S(1)}) fusion(bf16[384,1536]{1,0:T(8,128)(2,1)} %collective-permute-done.9, s32[]{:T(128)S(6)} %add.223, s32[]{:T(128)S(6)} %select_n.148, s32[]{:T(128)} %select_n.142), kind=kLoop, calls=%fused_computation.148 | loop fusion | bytes 2353164 | tf_op jit(solution)/shard_map/slice | solution.py:190
  111.7 1.3 constant_dynamic-slice_fusion
  113.0 3.2 %subtract_convert_fusion = (bf16[384,768]{1,0:T(8,128)(2,1)S(1)}, bf16[384,768]{1,0:T(8,128)(2,1)S(1)}, bf16[384,768]{1,0:T(8,128)(2,1)S(1)}, bf16[384,768]{1,0:T(8,128)(2,1)S(1)}) fusion(bf16[1,768]{1,0:T(2,128)(2,1)S(1)} %get-tuple-element.55, bf16[383,768]{1,0:T(8,128)(2,1)S(1)} %get-tuple-element.36, bf16[384,1536]{1,0:T(8,128)(2,1)} %collective-permute-done.8, ...), kind=kLoop, calls=%fused_computation.36 | loop fusion | flops 10616832 | bytes 7084040 | tf_op jit(solution)/shard_map/convert_element_type | solution.py:196
  116.3 1.4 fusion.5
  117.8 1.4 add_convert_fusion.refs_1_
  119.5 1.5 collective-permute-start.11
  121.0 2.7 %fusion.73 = (bf16[640,1536]{1,0:T(8,128)(2,1)}, f32[640,1536]{1,0:T(8,128)S(1)}) fusion(f32[640,1536]{1,0:T(8,128)S(1)} %fusion.39, bf16[1,384,1536]{2,1,0:T(8,128)(2,1)S(1)} %copy-done, s32[384]{0:T(512)S(1)} %get-tuple-element.59, bf16[384]{0:T(512)(128)(2,1)S(1)} %get-tuple-element.12), kind=kOutput, calls=%fused_computation.150 | convolution fusion | flops 757432320 | bytes 11012352 | tf_op jit(solution)/shard_map/dot_general | solution.py:222
  124.7 7.8 %all-gather.8.cloned.1.call-done.refs_0_ = bf16[512,1536]{1,0:T(8,128)(2,1)} async-done(((bf16[128,1536]{1,0:T(8,128)(2,1)}), bf16[512,1536]{1,0:T(8,128)(2,1)}) %all-gather.8.cloned.1.call-update) | async-done | bytes 1572880 | tf_op jit(solution)/shard_map/all_gather | solution.py:149
  132.6 3.3 %fusion.9 = f32[768,512]{1,0:T(8,128)S(1)} fusion(bf16[1024,1536]{1,0:T(8,128)(2,1)} %all-gather.4.cloned.1.call-done.refs_1_, s32[]{:T(128)S(6)} %select_n.147, bf16[384,768]{1,0:T(8,128)(2,1)} %copy-done.32, bf16[384,768]{1,0:T(8,128)(2,1)} %copy-done.35, bf16[384,768]{1,0:T(8,128)(2,1)S(1)} %copy-done.20, bf16[384,768]{1,0:T(8,128)(2,1)S(1)} %copy-done.23), kind=kOutput, calls=%fused_computation.16 | convolution fusion | flops 1217396736 | bytes 5505028 | tf_op jit(solution)/shard_map/dot_general | solution.py:104
  136.9 2.6 %convert_add_fusion = f32[768,512]{1,0:T(8,128)S(1)} fusion(bf16[768,512]{1,0:T(8,128)(2,1)} %collective-permute-done.11, f32[768,512]{1,0:T(8,128)S(1)} %fusion.9, bf16[1024,1536]{1,0:T(8,128)(2,1)S(1)} %copy-done.56, s32[]{:T(128)S(6)} %select_n.147, bf16[384,768]{1,0:T(8,128)(2,1)S(1)} %copy-done.39, bf16[384,768]{1,0:T(8,128)(2,1)S(1)} %copy-done.42, ...), kind=kOutput, calls=%fused_computation.7 | convolution fusion | flops 1219362816 | bytes 7864324 | tf_op jit(solution)/shard_map/dot_general | solution.py:104
  141.0 1.2 fusion.70
  142.2 5.9 %collective-permute-start.19 = (bf16[128,1536]{1,0:T(8,128)(2,1)}, bf16[128,1536]{1,0:T(8,128)(2,1)}, u32[]{:S(2)}, u32[]{:S(2)}) collective-permute-start(bf16[128,1536]{1,0:T(8,128)(2,1)} %get-tuple-element.17), channel_id=1, source_target_pairs={{0,8},{4,12},{1,9},{5,13},{2,10},{6,14},{3,11},{7,15},{16,24},{20,... | collective-permute-start | bytes 1179656 | tf_op jit(solution)/shard_map/ppermute | solution.py:14
  148.1 3.6 %collective-permute-start.18 = (bf16[128,1536]{1,0:T(8,128)(2,1)}, bf16[128,1536]{1,0:T(8,128)(2,1)}, u32[]{:S(2)}, u32[]{:S(2)}) collective-permute-start(bf16[128,1536]{1,0:T(8,128)(2,1)} %get-tuple-element.18), channel_id=1, source_target_pairs={{0,4},{4,8},{8,12},{1,5},{5,9},{9,13},{2,6},{6,10},{10,14},{3,7},{... | collective-permute-start | bytes 1179656 | tf_op jit(solution)/shard_map/ppermute | solution.py:14
  151.8 1.3 collective-permute-start.17
  153.1 1.6 collective-permute-start.16
  154.8 2.0 convert_select_fusion
  156.8 2.3 %fusion.31 = f32[768,256]{1,0:T(8,128)S(1)} fusion(bf16[512,1536]{1,0:T(8,128)(2,1)} %collective-permute-done.13, s32[]{:T(128)S(6)} %select_n.154, bf16[384,768]{1,0:T(8,128)(2,1)S(1)} %copy-done.40, bf16[384,768]{1,0:T(8,128)(2,1)S(1)} %copy-done.43, bf16[384,768]{1,0:T(8,128)(2,1)S(1)} %copy-done.28, bf16[384,768]{1,0:T(8,128)(2,1)S(1)} %copy-done.31), kind=kOutput, calls=%fused_computation.48 | convolution fusion | flops 613416960 | bytes 3932164 | tf_op jit(solution)/shard_map/dot_general | solution.py:104
  159.2 1.6 fusion.20.refs_1_
  160.8 1.5 collective-permute-start.14
  162.3 2.8 %fusion.34 = f32[768,256]{1,0:T(8,128)S(1)} fusion(bf16[512,1536]{1,0:T(8,128)(2,1)} %collective-permute-done.13, s32[]{:T(128)S(6)} %select_n.153, bf16[384,768]{1,0:T(8,128)(2,1)} %copy-done.38, bf16[384,768]{1,0:T(8,128)(2,1)} %copy-done.41, bf16[384,768]{1,0:T(8,128)(2,1)} %copy-done.26, bf16[384,768]{1,0:T(8,128)(2,1)} %copy-done.29), kind=kOutput, calls=%fused_computation.51 | convolution fusion | flops 613416960 | bytes 3932164 | tf_op jit(solution)/shard_map/dot_general | solution.py:104
  165.1 4.3 %collective-permute-done.14 = bf16[768,256]{1,0:T(8,128)(2,1)} collective-permute-done((bf16[768,256]{1,0:T(8,128)(2,1)}, bf16[768,256]{1,0:T(8,128)(2,1)}, u32[]{:S(2)}, u32[]{:S(2)}) %collective-permute-start.14) | collective-permute-done | bytes 393248 | tf_op jit(solution)/shard_map/ppermute | solution.py:22
  169.4 1.8 fusion.19
  171.3 1.8 collective-permute-start.15
  173.2 30.3 %collective-permute-done.16 = bf16[128,1536]{1,0:T(8,128)(2,1)} collective-permute-done((bf16[128,1536]{1,0:T(8,128)(2,1)}, bf16[128,1536]{1,0:T(8,128)(2,1)}, u32[]{:S(2)}, u32[]{:S(2)}) %collective-permute-start.16) | collective-permute-done | bytes 393248 | tf_op jit(solution)/shard_map/ppermute | solution.py:14
  203.4 2.4 %fusion.44 = bf16[1,128,1536]{2,1,0:T(8,128)(2,1)} fusion(bf16[128,1536]{1,0:T(8,128)(2,1)} %collective-permute-done.19, bf16[128,1536]{1,0:T(8,128)(2,1)} %collective-permute-done.18, bf16[128,1536]{1,0:T(8,128)(2,1)} %collective-permute-done.17, f32[128,1536]{1,0:T(8,128)S(1)} %copy-done.7, bf16[128,1536]{1,0:T(8,128)(2,1)} %collective-permute-done.16), kind=kLoop, calls=%fused_computation.69 | loop fusion | flops 1769472 | bytes 2752512 | tf_op jit(solution)/shard_map/broadcast_in_dim | solution.py:279
  206.5 3.2 %fusion.2 = bf16[1,384,1536]{2,1,0:T(8,128)(2,1)} fusion(f32[384,1536]{1,0:T(8,128)S(1)} %slice_dynamic-update-slice_fusion.4, bf16[512,1536]{1,0:T(8,128)(2,1)} %all-gather.6.cloned.1.call-done, s32[384]{0:T(512)S(1)} %copy-done.50, pred[384]{0:T(512)(128)(4,1)S(1)} %copy-done.53, bf16[1,384,1536]{2,1,0:T(8,128)(2,1)S(1)} %copy-done), kind=kOutput, calls=%fused_computation.4 | convolution fusion | flops 606732288 | bytes 6293376 | tf_op jit(solution)/shard_map/dot_general | solution.py:240
  (187 shorter events, 16.0 us)
Async XLA Ops:
  7.2 83.1 %all-gather.4.cloned.1.call-start = ((), (), s32[]{:S(2)}) async-start(), calls=%async_computation | async-start | bytes 3932160 | tf_op jit(solution)/shard_map/all_gather | solution.py:149
  11.2 11.7 %copy-start.5 = (s32[1,512]{1,0:T(1,128)S(1)}, s32[1,512]{1,0:T(1,128)}, u32[]{:S(2)}) copy-start(s32[1,512]{1,0:T(1,128)} %bounds_ref.1) | copy-start | bytes 6148
  12.2 120.3 %all-gather.8.cloned.1.call-start = ((), (), s32[]{:S(2)}) async-start(), calls=%async_computation.2 | async-start | bytes 1966080 | tf_op jit(solution)/shard_map/all_gather | solution.py:149
  13.3 22.3 %collective-permute-start.2 = (bf16[144,1536]{1,0:T(8,128)(2,1)}, bf16[144,1536]{1,0:T(8,128)(2,1)}, u32[]{:S(2)}, u32[]{:S(2)}) collective-permute-start(bf16[144,1536]{1,0:T(8,128)(2,1)} %get-tuple-element.41), channel_id=1, source_target_pairs={{4,0},{8,4},{12,8},{5,1},{9,5},{13,9},{6,2},{10,6},{14,10},{7,3},{... | collective-permute-start | bytes 1327112 | tf_op jit(solution)/shard_map/ppermute | solution.py:14
  14.6 22.5 %collective-permute-start = (bf16[144,1536]{1,0:T(8,128)(2,1)}, bf16[144,1536]{1,0:T(8,128)(2,1)}, u32[]{:S(2)}, u32[]{:S(2)}) collective-permute-start(bf16[144,1536]{1,0:T(8,128)(2,1)} %get-tuple-element.40), channel_id=1, source_target_pairs={{0,4},{4,8},{8,12},{1,5},{5,9},{9,13},{2,6},{6,10},{10,14},{3,7},{... | collective-permute-start | bytes 1327112 | tf_op jit(solution)/shard_map/ppermute | solution.py:14
  20.9 88.2 %collective-permute-start.9 = (bf16[384,1536]{1,0:T(8,128)(2,1)S(1)}, bf16[384,1536]{1,0:T(8,128)(2,1)}, u32[]{:S(2)}, u32[]{:S(2)}) collective-permute-start(bf16[384,1536]{1,0:T(8,128)(2,1)S(1)} %bitcast.44), channel_id=1, source_target_pairs={{0,16},{16,0},{1,17},{17,1},{2,18},{18,2},{3,19},{19,3},{4,20},{20... | collective-permute-start | bytes 3538952 | tf_op jit(solution)/shard_map/ppermute | solution.py:22
  22.9 88.8 %collective-permute-start.8 = (bf16[384,1536]{1,0:T(8,128)(2,1)S(1)}, bf16[384,1536]{1,0:T(8,128)(2,1)}, u32[]{:S(2)}, u32[]{:S(2)}) collective-permute-start(bf16[384,1536]{1,0:T(8,128)(2,1)S(1)} %bitcast.46), channel_id=1, source_target_pairs={{0,16},{16,0},{1,17},{17,1},{2,18},{18,2},{3,19},{19,3},{4,20},{20... | collective-permute-start | bytes 3538952 | tf_op jit(solution)/shard_map/ppermute | solution.py:22
  24.6 66.5 %copy-start = (bf16[1,384,1536]{2,1,0:T(8,128)(2,1)S(1)}, bf16[1,384,1536]{2,1,0:T(8,128)(2,1)}, u32[]{:S(2)}) copy-start(bf16[1,384,1536]{2,1,0:T(8,128)(2,1)} %param.8) | copy-start | bytes 3538948
  38.5 35.3 %collective-permute-start.7 = (bf16[2,1536]{1,0:T(2,128)(2,1)}, bf16[2,1536]{1,0:T(2,128)(2,1)S(1)}, u32[]{:S(2)}, u32[]{:S(2)}) collective-permute-start(bf16[2,1536]{1,0:T(2,128)(2,1)} %pad_maximum_fusion.5), channel_id=1, source_target_pairs={{0,16},{16,0},{1,17},{17,1},{2,18},{18,2},{3,19},{19,3},{4,20},{20... | collective-permute-start | bytes 18440 | tf_op jit(solution)/shard_map/ppermute | solution.py:22
  41.6 164.5 %all-gather.6.cloned.1.call-start = ((), (), s32[]{:S(2)}) async-start(), calls=%async_computation.1 | async-start | bytes 1966080 | tf_op jit(solution)/shard_map/all_gather | solution.py:235
  41.7 49.4 %collective-permute-start.1 = (bf16[144,1536]{1,0:T(8,128)(2,1)}, bf16[144,1536]{1,0:T(8,128)(2,1)}, u32[]{:S(2)}, u32[]{:S(2)}) collective-permute-start(bf16[144,1536]{1,0:T(8,128)(2,1)} %collective-permute-done.refs_1_), channel_id=1, source_target_pairs={{4,8},{8,12},{5,9},{9,13},{6,10},{10,14},{7,11},{11,15},{20,24},{2... | collective-permute-start | bytes 1327112 | tf_op jit(solution)/shard_map/ppermute | solution.py:30
  43.1 47.9 %collective-permute-start.3 = (bf16[144,1536]{1,0:T(8,128)(2,1)}, bf16[144,1536]{1,0:T(8,128)(2,1)}, u32[]{:S(2)}, u32[]{:S(2)}) collective-permute-start(bf16[144,1536]{1,0:T(8,128)(2,1)} %collective-permute-done.2.refs_3_), channel_id=1, source_target_pairs={{4,0},{8,4},{5,1},{9,5},{6,2},{10,6},{7,3},{11,7},{20,16},{24,20},... | collective-permute-start | bytes 1327112 | tf_op jit(solution)/shard_map/ppermute | solution.py:30
  90.3 27.5 %collective-permute-start.10 = (bf16[1024,1536]{1,0:T(8,128)(2,1)}, bf16[1024,1536]{1,0:T(8,128)(2,1)S(1)}, u32[]{:S(2)}, u32[]{:S(2)}) collective-permute-start(bf16[1024,1536]{1,0:T(8,128)(2,1)} %all-gather.4.cloned.1.call-done.refs_1_), channel_id=1, source_target_pairs={{0,1},{1,0},{2,3},{3,2},{4,5},{5,4},{6,7},{7,6},{8,9},{9,8},{10,11... | collective-permute-start | bytes 9437192 | tf_op jit(solution)/shard_map/ppermute | solution.py:22
  92.1 7.7 %copy-start.54 = (f32[384]{0:T(512)S(1)}, f32[384]{0:T(512)}, u32[]{:S(2)}) copy-start(f32[384]{0:T(512)} %select_multiply_fusion) | copy-start | bytes 4612
  92.1 9.2 %copy-start.52 = (pred[384]{0:T(512)(128)(4,1)S(1)}, pred[384]{0:T(512)(128)(4,1)}, u32[]{:S(2)}) copy-start(pred[384]{0:T(512)(128)(4,1)} %copy-done.51) | copy-start | bytes 1156
  96.0 3.8 %collective-permute-start.4 = (f32[8,384]{1,0:T(8,128)S(1)}, f32[8,384]{1,0:T(8,128)S(1)}, u32[]{:S(2)}, u32[]{:S(2)}) collective-permute-start(f32[8,384]{1,0:T(8,128)S(1)} %byte_sums.1), channel_id=1, source_target_pairs={{0,2},{2,0},{1,3},{3,1},{4,6},{6,4},{5,7},{7,5},{8,10},{10,8},{9,1... | collective-permute-start | bytes 36872 | tf_op jit(solution)/shard_map/ppermute | solution.py:22
  99.8 5.5 %collective-permute-start.5 = (f32[3,1]{1,0:T(4,128)S(1)}, f32[3,1]{1,0:T(4,128)S(1)}, u32[]{:S(2)}, u32[]{:S(2)}) collective-permute-start(f32[3,1]{1,0:T(4,128)S(1)} %pad_maximum_fusion.6), channel_id=1, source_target_pairs={{4,0},{8,4},{12,8},{5,1},{9,5},{13,9},{6,2},{10,6},{14,10},{7,3},{... | collective-permute-start | bytes 44 | tf_op jit(solution)/shard_map/ppermute | solution.py:14
  101.3 5.6 %copy-start.12 = (bf16[383,768]{1,0:T(8,128)(2,1)S(1)}, bf16[383,768]{1,0:T(8,128)(2,1)}, u32[]{:S(2)}) copy-start(bf16[383,768]{1,0:T(8,128)(2,1)} %get-tuple-element.30) | copy-start | bytes 1764868
  101.3 5.6 %copy-start.13 = (bf16[383,768]{1,0:T(8,128)(2,1)S(1)}, bf16[383,768]{1,0:T(8,128)(2,1)}, u32[]{:S(2)}) copy-start(bf16[383,768]{1,0:T(8,128)(2,1)} %get-tuple-element.31) | copy-start | bytes 1764868
  101.3 5.6 %copy-start.14 = (bf16[383,768]{1,0:T(8,128)(2,1)S(1)}, bf16[383,768]{1,0:T(8,128)(2,1)}, u32[]{:S(2)}) copy-start(bf16[383,768]{1,0:T(8,128)(2,1)} %get-tuple-element.32) | copy-start | bytes 1764868
  101.4 5.6 %copy-start.15 = (bf16[383,768]{1,0:T(8,128)(2,1)S(1)}, bf16[383,768]{1,0:T(8,128)(2,1)}, u32[]{:S(2)}) copy-start(bf16[383,768]{1,0:T(8,128)(2,1)} %get-tuple-element.33) | copy-start | bytes 1764868
  101.4 5.6 %copy-start.46 = (bf16[1,768]{1,0:T(2,128)(2,1)S(1)}, bf16[1,768]{1,0:T(2,128)(2,1)}, u32[]{:S(2)}) copy-start(bf16[1,768]{1,0:T(2,128)(2,1)} %get-tuple-element.51) | copy-start | bytes 4612
  101.4 5.6 %copy-start.47 = (bf16[1,768]{1,0:T(2,128)(2,1)S(1)}, bf16[1,768]{1,0:T(2,128)(2,1)}, u32[]{:S(2)}) copy-start(bf16[1,768]{1,0:T(2,128)(2,1)} %get-tuple-element.52) | copy-start | bytes 4612
  101.4 5.6 %copy-start.48 = (bf16[1,768]{1,0:T(2,128)(2,1)S(1)}, bf16[1,768]{1,0:T(2,128)(2,1)}, u32[]{:S(2)}) copy-start(bf16[1,768]{1,0:T(2,128)(2,1)} %get-tuple-element.49) | copy-start | bytes 4612
  105.3 3.7 %collective-permute-start.6 = (f32[3,385]{1,0:T(4,128)S(1)}, f32[3,385]{1,0:T(4,128)S(1)}, u32[]{:S(2)}, u32[]{:S(2)}) collective-permute-start(f32[3,385]{1,0:T(4,128)S(1)} %pad_maximum_fusion.4), channel_id=1, source_target_pairs={{0,16},{16,0},{1,17},{17,1},{2,18},{18,2},{3,19},{19,3},{4,20},{20... | collective-permute-start | bytes 13868 | tf_op jit(solution)/shard_map/ppermute | solution.py:22
  108.9 7.4 %copy-start.19 = (bf16[384,768]{1,0:T(8,128)(2,1)}, bf16[384,768]{1,0:T(8,128)(2,1)S(1)}, u32[]{:S(2)}) copy-start(bf16[384,768]{1,0:T(8,128)(2,1)S(1)} %get-tuple-element.25) | copy-start | bytes 1769476
  108.9 7.4 %copy-start.22 = (bf16[384,768]{1,0:T(8,128)(2,1)}, bf16[384,768]{1,0:T(8,128)(2,1)S(1)}, u32[]{:S(2)}) copy-start(bf16[384,768]{1,0:T(8,128)(2,1)S(1)} %get-tuple-element.63) | copy-start | bytes 1769476
  108.9 8.9 %copy-start.26 = (bf16[384,768]{1,0:T(8,128)(2,1)}, bf16[384,768]{1,0:T(8,128)(2,1)S(1)}, u32[]{:S(2)}) copy-start(bf16[384,768]{1,0:T(8,128)(2,1)S(1)} %get-tuple-element.24) | copy-start | bytes 1769476
  109.0 8.9 %copy-start.29 = (bf16[384,768]{1,0:T(8,128)(2,1)}, bf16[384,768]{1,0:T(8,128)(2,1)S(1)}, u32[]{:S(2)}) copy-start(bf16[384,768]{1,0:T(8,128)(2,1)S(1)} %get-tuple-element.64) | copy-start | bytes 1769476
  119.5 17.4 %collective-permute-start.11 = (bf16[768,512]{1,0:T(8,128)(2,1)S(1)}, bf16[768,512]{1,0:T(8,128)(2,1)}, u32[]{:S(2)}, u32[]{:S(2)}) collective-permute-start(bf16[768,512]{1,0:T(8,128)(2,1)S(1)} %add_convert_fusion.refs_1_), channel_id=1, source_target_pairs={{0,2},{2,0},{1,3},{3,1},{4,6},{6,4},{5,7},{7,5},{8,10},{10,8},{9,1... | collective-permute-start | bytes 2359304 | tf_op jit(solution)/shard_map/ppermute | solution.py:22
  124.7 7.9 %copy-start.20 = (bf16[384,768]{1,0:T(8,128)(2,1)S(1)}, bf16[384,768]{1,0:T(8,128)(2,1)}, u32[]{:S(2)}) copy-start(bf16[384,768]{1,0:T(8,128)(2,1)} %copy-done.19) | copy-start | bytes 1769476
  124.7 8.0 %copy-start.23 = (bf16[384,768]{1,0:T(8,128)(2,1)S(1)}, bf16[384,768]{1,0:T(8,128)(2,1)}, u32[]{:S(2)}) copy-start(bf16[384,768]{1,0:T(8,128)(2,1)} %copy-done.22) | copy-start | bytes 1769476
  132.5 24.3 %collective-permute-start.13 = (bf16[512,1536]{1,0:T(8,128)(2,1)}, bf16[512,1536]{1,0:T(8,128)(2,1)}, u32[]{:S(2)}, u32[]{:S(2)}) collective-permute-start(bf16[512,1536]{1,0:T(8,128)(2,1)} %after.7), channel_id=1, source_target_pairs={{0,1},{1,0},{2,3},{3,2},{4,5},{5,4},{6,7},{7,6},{8,9},{9,8},{10,11... | collective-permute-start | bytes 4718600 | tf_op jit(solution)/shard_map/ppermute | solution.py:22
  140.3 12.8 %collective-permute-start.12 = (bf16[384,512]{1,0:T(8,128)(2,1)}, bf16[384,512]{1,0:T(8,128)(2,1)}, u32[]{:S(2)}, u32[]{:S(2)}) collective-permute-start(bf16[384,512]{1,0:T(8,128)(2,1)} %slice.255), channel_id=1, source_target_pairs={{0,16},{16,0},{1,17},{17,1},{2,18},{18,2},{3,19},{19,3},{4,20},{20... | collective-permute-start | bytes 1179656 | tf_op jit(solution)/shard_map/ppermute | solution.py:22
  142.2 31.0 %collective-permute-start.19 = (bf16[128,1536]{1,0:T(8,128)(2,1)}, bf16[128,1536]{1,0:T(8,128)(2,1)}, u32[]{:S(2)}, u32[]{:S(2)}) collective-permute-start(bf16[128,1536]{1,0:T(8,128)(2,1)} %get-tuple-element.17), channel_id=1, source_target_pairs={{0,8},{4,12},{1,9},{5,13},{2,10},{6,14},{3,11},{7,15},{16,24},{20,... | collective-permute-start | bytes 1179656 | tf_op jit(solution)/shard_map/ppermute | solution.py:14
  148.1 25.1 %collective-permute-start.18 = (bf16[128,1536]{1,0:T(8,128)(2,1)}, bf16[128,1536]{1,0:T(8,128)(2,1)}, u32[]{:S(2)}, u32[]{:S(2)}) collective-permute-start(bf16[128,1536]{1,0:T(8,128)(2,1)} %get-tuple-element.18), channel_id=1, source_target_pairs={{0,4},{4,8},{8,12},{1,5},{5,9},{9,13},{2,6},{6,10},{10,14},{3,7},{... | collective-permute-start | bytes 1179656 | tf_op jit(solution)/shard_map/ppermute | solution.py:14
  151.8 21.4 %collective-permute-start.17 = (bf16[128,1536]{1,0:T(8,128)(2,1)}, bf16[128,1536]{1,0:T(8,128)(2,1)}, u32[]{:S(2)}, u32[]{:S(2)}) collective-permute-start(bf16[128,1536]{1,0:T(8,128)(2,1)} %get-tuple-element.19), channel_id=1, source_target_pairs={{4,0},{8,4},{12,8},{5,1},{9,5},{13,9},{6,2},{10,6},{14,10},{7,3},{... | collective-permute-start | bytes 1179656 | tf_op jit(solution)/shard_map/ppermute | solution.py:14
  153.1 50.3 %collective-permute-start.16 = (bf16[128,1536]{1,0:T(8,128)(2,1)}, bf16[128,1536]{1,0:T(8,128)(2,1)}, u32[]{:S(2)}, u32[]{:S(2)}) collective-permute-start(bf16[128,1536]{1,0:T(8,128)(2,1)} %get-tuple-element.16), channel_id=1, source_target_pairs={{8,0},{12,4},{9,1},{13,5},{10,2},{14,6},{11,3},{15,7},{24,16},{28,... | collective-permute-start | bytes 1179656 | tf_op jit(solution)/shard_map/ppermute | solution.py:14
  160.8 8.7 %collective-permute-start.14 = (bf16[768,256]{1,0:T(8,128)(2,1)}, bf16[768,256]{1,0:T(8,128)(2,1)}, u32[]{:S(2)}, u32[]{:S(2)}) collective-permute-start(bf16[768,256]{1,0:T(8,128)(2,1)} %fusion.20.refs_1_), channel_id=1, source_target_pairs={{0,2},{2,0},{1,3},{3,1},{4,6},{6,4},{5,7},{7,5},{8,10},{10,8},{9,1... | collective-permute-start | bytes 1179656 | tf_op jit(solution)/shard_map/ppermute | solution.py:22
  162.3 7.2 %copy-start.17 = (bf16[512,1536]{1,0:T(8,128)(2,1)S(1)}, bf16[512,1536]{1,0:T(8,128)(2,1)}, u32[]{:S(2)}) copy-start(bf16[512,1536]{1,0:T(8,128)(2,1)} %after.7) | copy-start | bytes 4718596
  162.3 7.2 %copy-start.21 = (bf16[384,768]{1,0:T(8,128)(2,1)S(1)}, bf16[384,768]{1,0:T(8,128)(2,1)}, u32[]{:S(2)}) copy-start(bf16[384,768]{1,0:T(8,128)(2,1)} %copy-done.19) | copy-start | bytes 1769476
  162.3 7.1 %copy-start.25 = (bf16[384,768]{1,0:T(8,128)(2,1)S(1)}, bf16[384,768]{1,0:T(8,128)(2,1)}, u32[]{:S(2)}) copy-start(bf16[384,768]{1,0:T(8,128)(2,1)} %copy-done.22) | copy-start | bytes 1769476
  162.3 7.1 %copy-start.34 = (bf16[384,768]{1,0:T(8,128)(2,1)S(1)}, bf16[384,768]{1,0:T(8,128)(2,1)}, u32[]{:S(2)}) copy-start(bf16[384,768]{1,0:T(8,128)(2,1)} %copy-done.32) | copy-start | bytes 1769476
  162.3 7.1 %copy-start.37 = (bf16[384,768]{1,0:T(8,128)(2,1)S(1)}, bf16[384,768]{1,0:T(8,128)(2,1)}, u32[]{:S(2)}) copy-start(bf16[384,768]{1,0:T(8,128)(2,1)} %copy-done.35) | copy-start | bytes 1769476
  165.1 38.3 %copy-start.7 = (f32[128,1536]{1,0:T(8,128)S(1)}, f32[128,1536]{1,0:T(8,128)}, u32[]{:S(2)}) copy-start(f32[128,1536]{1,0:T(8,128)} %after.8) | copy-start | bytes 2359300
  171.3 34.6 %copy-start.8 = (f32[384,512]{1,0:T(8,128)S(1)}, f32[384,512]{1,0:T(8,128)}, u32[]{:S(2)}) copy-start(f32[384,512]{1,0:T(8,128)} %get-tuple-element.20) | copy-start | bytes 2359300
  171.3 34.6 %copy-start.10 = (f32[384,512]{1,0:T(8,128)S(1)}, f32[384,512]{1,0:T(8,128)}, u32[]{:S(2)}) copy-start(f32[384,512]{1,0:T(8,128)} %copy-done.9) | copy-start | bytes 2359300
  171.3 34.5 %collective-permute-start.15 = (bf16[384,256]{1,0:T(8,128)(2,1)S(1)}, bf16[384,256]{1,0:T(8,128)(2,1)S(1)}, u32[]{:S(2)}, u32[]{:S(2)}) collective-permute-start(bf16[384,256]{1,0:T(8,128)(2,1)S(1)} %slice.256), channel_id=1, source_target_pairs={{0,16},{16,0},{1,17},{17,1},{2,18},{18,2},{3,19},{19,3},{4,20},{20... | collective-permute-start | bytes 589832 | tf_op jit(solution)/shard_map/ppermute | solution.py:22
  (34 other events, 116.6 us)
Sparse Core Ops, SparseCore 0:
  12.3 77.9 all-gather.3
  92.4 40.0 all-gather.7
  153.2 50.2 all-gather.5

commit v11 on v10

--- a/solution.py
+++ b/solution.py
@@ -269,6 +269,8 @@
             ).astype(jnp.float32)
         own = total[:row_count]
         returned = total[row_count:].astype(jnp.bfloat16)
+        if not pieces:
+            returned = after(returned, *received)
         arrived = swapped(returned, "groups").astype(jnp.float32)
         pieces.append(
             [jnp.where(group_index == 0, own, arrived), jnp.where(group_index == 0, arrived, own)]

time: 217 us -> 218 us (level)
  waiting for transfers between devices: 102 us -> 94 us
  local copies, waits for them, and re-layouts: 19.8 us -> 27.5 us
  starting transfers between devices: 37.2 us -> 31.2 us
  matrix products: 24.4 us -> 29.4 us
    all_gather x2, waiting for transfers between devices: 23.7 us -> 9.42 us  [shards(): own_weights.append(lax.all_gather(piece, 'seq', axis=0, tiled=True))]
    ppermute x2, waiting for transfers between devices: 0.01 us -> 8.34 us  [passed_on(): return lax.ppermute(x, axis, pairs)]
    unnamed x122 -> x128, local copies, waits for them, and re-layouts: 3.89 us -> 10.6 us
    ppermute x7, starting transfers between devices: 21.6 us -> 17.3 us  [passed_along(): return lax.ppermute(x, axis, pairs)]
    dot_general x8, matrix products: 17.2 us -> 20 us  [product(): lax.dot_general(rows, weight, (((1,), (1,)), ((), ())), preferred_element...]
  transfers between devices with their start and end apart: 23 -> 23, of which waited for: 11 -> 14; matrix products, arithmetic and copies ran while one was open for 23% -> 28% of each run, Pallas kernels for 2% -> 2%
where the time goes in v11:
time: 218 us; the launch traced here: 217 us
  waiting for transfers between devices  94 us (43%)
  starting transfers between devices  31.2 us (14%)
  matrix products  29.4 us (13%)
  local copies, waits for them, and re-layouts  27.5 us (13%)
  other arithmetic  16.6 us (8%)
  between operations  14.7 us (7%)
  Pallas kernels  3.62 us (2%)
    ppermute x7, waiting for transfers between devices, passed_along(): return lax.ppermute(x, axis, pairs)  41.1 us
    ppermute x11, waiting for transfers between devices, swapped(): return lax.ppermute(x, axis, [(i, length - 1 - i) for i in range(length)])  35 us
    dot_general x8, matrix products, product(): lax.dot_general(rows, weight, (((1,), (1,)), ((), ())), preferred_element...  20 us
    ppermute x7, starting transfers between devices, passed_along(): return lax.ppermute(x, axis, pairs)  17.3 us
    ppermute x11, starting transfers between devices, swapped(): return lax.ppermute(x, axis, [(i, length - 1 - i) for i in range(length)])  11.8 us
    unnamed x128, local copies, waits for them, and re-layouts  10.6 us
    all_gather x2, waiting for transfers between devices, shards(): own_weights.append(lax.all_gather(piece, 'seq', axis=0, tiled=True))  9.42 us
    ppermute x2, waiting for transfers between devices, passed_on(): return lax.ppermute(x, axis, pairs)  8.34 us
  transfers between devices with their start and end apart: 23, of which 14 were waited for; matrix products, arithmetic and copies ran while one was open for 28% of the time, Pallas kernels for 2%

profile of v11, /device:TPU:0, one launch (start us, length us, event | category | flops | bytes accessed | tf_op | source)
XLA Modules:
  0.0 216.9 jit_solution(18270357740859049385)
XLA Ops:
  7.2 1.9 copy.42
  13.3 5.7 %collective-permute-start = (bf16[144,1536]{1,0:T(8,128)(2,1)}, bf16[144,1536]{1,0:T(8,128)(2,1)}, u32[]{:S(2)}, u32[]{:S(2)}) collective-permute-start(bf16[144,1536]{1,0:T(8,128)(2,1)} %get-tuple-element.40), channel_id=1, source_target_pairs={{0,4},{4,8},{8,12},{1,5},{5,9},{9,13},{2,6},{6,10},{10,14},{3,7},{... | collective-permute-start | bytes 1327112 | tf_op jit(solution)/shard_map/ppermute | solution.py:14
  19.0 1.3 collective-permute-start.2
  20.3 1.6 collective-permute-start.8
  24.0 1.7 dynamic-slice_bitcast_fusion
  27.6 5.6 %collective-permute-done.refs_1_ = bf16[144,1536]{1,0:T(8,128)(2,1)} collective-permute-done((bf16[144,1536]{1,0:T(8,128)(2,1)}, bf16[144,1536]{1,0:T(8,128)(2,1)}, u32[]{:S(2)}, u32[]{:S(2)}) %collective-permute-start) | collective-permute-done | bytes 442400 | tf_op jit(solution)/shard_map/ppermute | solution.py:14
  33.9 14.7 %collective-permute-done.2.refs_3_ = bf16[144,1536]{1,0:T(8,128)(2,1)} collective-permute-done((bf16[144,1536]{1,0:T(8,128)(2,1)}, bf16[144,1536]{1,0:T(8,128)(2,1)}, u32[]{:S(2)}, u32[]{:S(2)}) %collective-permute-start.2) | collective-permute-done | bytes 442400 | tf_op jit(solution)/shard_map/ppermute | solution.py:14
  50.0 1.6 collective-permute-start.7
  53.6 1.3 collective-permute-start.3
  54.9 18.4 %collective-permute-done.7 = bf16[2,1536]{1,0:T(2,128)(2,1)S(1)} collective-permute-done((bf16[2,1536]{1,0:T(2,128)(2,1)}, bf16[2,1536]{1,0:T(2,128)(2,1)S(1)}, u32[]{:S(2)}, u32[]{:S(2)}) %collective-permute-start.7) | collective-permute-done | bytes 6176 | tf_op jit(solution)/shard_map/ppermute | solution.py:22
  73.8 8.3 %collective-permute-done.3.refs_4_ = bf16[144,1536]{1,0:T(8,128)(2,1)S(1)} collective-permute-done((bf16[144,1536]{1,0:T(8,128)(2,1)}, bf16[144,1536]{1,0:T(8,128)(2,1)S(1)}, u32[]{:S(2)}, u32[]{:S(2)}) %collective-permute-start.3) | collective-permute-done | bytes 442400 | tf_op jit(solution)/shard_map/ppermute | solution.py:30
  83.2 3.6 %byte_sums.1 = f32[8,384]{1,0:T(8,128)S(1)} custom-call(s32[1]{0:T(128)} %bitcast.3.shard_ref, s32[1,512]{1,0:T(1,128)S(1)} %copy-done.5, bf16[384,1536]{1,0:T(8,128)(2,1)S(1)} %bitcast.43, bf16[384,1536]{1,0:T(8,128)(2,1)S(1)} %bitcast.47, bf16[384,1536]{1,0:T(8,128)(2,1)S(1)} %bitcast.45, bf16[144,1536]{1,0:T(8,128)(2,1)S(1)} %collective-permute-done.1.refs_0_, ...), custom_call_target="tpu_custom_call" | custom-call | tf_op jit(solution)/shard_map/byte_sums/pallas_call | solution.py:93
  86.8 1.6 collective-permute-start.4
  89.0 1.6 collective-permute-done.4
  91.8 1.6 all-gather.4.cloned.1.call-done.refs_1_
  94.7 1.5 collective-permute-start.5
  96.9 1.3 fusion.39
  98.3 4.1 %fusion.73 = (bf16[640,1536]{1,0:T(8,128)(2,1)}, f32[640,1536]{1,0:T(8,128)}) fusion(f32[640,1536]{1,0:T(8,128)S(1)} %fusion.39, bf16[1,384,1536]{2,1,0:T(8,128)(2,1)S(1)} %copy-done, s32[384]{0:T(512)S(1)} %get-tuple-element.60, bf16[384]{0:T(512)(128)(2,1)S(1)} %get-tuple-element.12), kind=kOutput, calls=%fused_computation.150 | convolution fusion | flops 757432320 | bytes 11012352 | tf_op jit(solution)/shard_map/dot_general | solution.py:222
  102.4 1.4 collective-permute-done.5
  104.5 2.8 %fusion.22 = (bf16[384,768]{1,0:T(8,128)(2,1)}, bf16[384,768]{1,0:T(8,128)(2,1)}, bf16[384,768]{1,0:T(8,128)(2,1)}, bf16[384,768]{1,0:T(8,128)(2,1)}) fusion(bf16[1,768]{1,0:T(2,128)(2,1)S(1)} %copy-done.52, bf16[383,768]{1,0:T(8,128)(2,1)S(1)} %copy-done.12, bf16[1,384,1536]{2,1,0:T(8,128)(2,1)S(1)} %copy-done.1, s32[]{:T(128)S(6)} %select_n.148, ...), kind=kLoop, calls=%fused_computation.26 | loop fusion | flops 10616832 | bytes 7084040 | tf_op jit(solution)/shard_map/convert_element_type | solution.py:196
  109.1 1.3 constant_dynamic-slice_fusion
  110.4 1.9 fusion.71
  112.4 3.3 %subtract_convert_fusion = (bf16[384,768]{1,0:T(8,128)(2,1)S(1)}, bf16[384,768]{1,0:T(8,128)(2,1)S(1)}, bf16[384,768]{1,0:T(8,128)(2,1)S(1)}, bf16[384,768]{1,0:T(8,128)(2,1)S(1)}) fusion(bf16[1,768]{1,0:T(2,128)(2,1)S(1)} %copy-done.54, bf16[383,768]{1,0:T(8,128)(2,1)S(1)} %get-tuple-element.36, bf16[384,1536]{1,0:T(8,128)(2,1)} %collective-permute-done.8, ...), kind=kLoop, calls=%fused_computation.36 | loop fusion | flops 10616832 | bytes 7084040 | tf_op jit(solution)/shard_map/convert_element_type | solution.py:196
  115.8 1.4 fusion.5
  117.8 3.7 %add_convert_fusion.refs_1_ = bf16[768,512]{1,0:T(8,128)(2,1)} fusion(f32[768,512]{1,0:T(8,128)S(1)} %fusion.5, bf16[1024,1536]{1,0:T(8,128)(2,1)} %collective-permute-done.10, s32[]{:T(128)S(6)} %select_n.149, bf16[384,768]{1,0:T(8,128)(2,1)S(1)} %get-tuple-element.28, bf16[384,768]{1,0:T(8,128)(2,1)S(1)} %get-tuple-element.66, ...), kind=kOutput, calls=%fused_computation.8 | convolution fusion | flops 1218183168 | bytes 6291460 | tf_op jit(solution)/shard_map/dot_general | solution.py:104
  121.5 1.6 collective-permute-start.11
  123.0 7.8 %all-gather.8.cloned.1.call-done.refs_0_ = bf16[512,1536]{1,0:T(8,128)(2,1)} async-done(((bf16[128,1536]{1,0:T(8,128)(2,1)}), bf16[512,1536]{1,0:T(8,128)(2,1)}) %all-gather.8.cloned.1.call-update) | async-done | bytes 1572880 | tf_op jit(solution)/shard_map/all_gather | solution.py:149
  131.0 3.5 %collective-permute-start.15 = (bf16[128,1536]{1,0:T(8,128)(2,1)S(1)}, bf16[128,1536]{1,0:T(8,128)(2,1)S(1)}, u32[]{:S(2)}, u32[]{:S(2)}) collective-permute-start(bf16[128,1536]{1,0:T(8,128)(2,1)S(1)} %get-tuple-element.18), channel_id=1, source_target_pairs={{0,8},{4,12},{1,9},{5,13},{2,10},{6,14},{3,11},{7,15},{16,24},{20,... | collective-permute-start | bytes 1179656 | tf_op jit(solution)/shard_map/ppermute | solution.py:14
  134.4 2.5 %collective-permute-start.14 = (bf16[128,1536]{1,0:T(8,128)(2,1)S(1)}, bf16[128,1536]{1,0:T(8,128)(2,1)S(1)}, u32[]{:S(2)}, u32[]{:S(2)}) collective-permute-start(bf16[128,1536]{1,0:T(8,128)(2,1)S(1)} %get-tuple-element.19), channel_id=1, source_target_pairs={{0,4},{4,8},{8,12},{1,5},{5,9},{9,13},{2,6},{6,10},{10,14},{3,7},{... | collective-permute-start | bytes 1179656 | tf_op jit(solution)/shard_map/ppermute | solution.py:14
  137.0 1.4 collective-permute-start.13
  138.4 3.0 %fusion.9 = f32[768,512]{1,0:T(8,128)S(1)} fusion(bf16[1024,1536]{1,0:T(8,128)(2,1)S(1)} %copy-done.9, s32[]{:T(128)S(6)} %select_n.147, bf16[384,768]{1,0:T(8,128)(2,1)} %copy-done.36, bf16[384,768]{1,0:T(8,128)(2,1)} %copy-done.39, bf16[384,768]{1,0:T(8,128)(2,1)} %get-tuple-element.25, bf16[384,768]{1,0:T(8,128)(2,1)} %get-tuple-element.63), kind=kOutput, calls=%fused_computation.16 | convolution fusion | flops 1217396736 | bytes 5505028 | tf_op jit(solution)/shard_map/dot_general | solution.py:104
  141.5 1.5 collective-permute-start.12
  143.0 3.0 %convert_add_fusion = f32[768,512]{1,0:T(8,128)S(1)} fusion(bf16[768,512]{1,0:T(8,128)(2,1)} %collective-permute-done.11, f32[768,512]{1,0:T(8,128)S(1)} %fusion.9, bf16[1024,1536]{1,0:T(8,128)(2,1)} %collective-permute-done.10, s32[]{:T(128)S(6)} %select_n.147, bf16[384,768]{1,0:T(8,128)(2,1)S(1)} %copy-done.43, bf16[384,768]{1,0:T(8,128)(2,1)S(1)} %copy-done.45, ...), kind=kOutput, calls=%fused_computation.7 | convolution fusion | flops 1219362816 | bytes 7864324 | tf_op jit(solution)/shard_map/dot_general | solution.py:104
  146.9 4.8 %collective-permute-done.14.refs_3_ = bf16[128,1536]{1,0:T(8,128)(2,1)S(1)} collective-permute-done((bf16[128,1536]{1,0:T(8,128)(2,1)S(1)}, bf16[128,1536]{1,0:T(8,128)(2,1)S(1)}, u32[]{:S(2)}, u32[]{:S(2)}) %collective-permute-start.14) | collective-permute-done | bytes 393248 | tf_op jit(solution)/shard_map/ppermute | solution.py:14
  151.8 14.6 %collective-permute-done.12.refs_1_ = bf16[128,1536]{1,0:T(8,128)(2,1)S(1)} collective-permute-done((bf16[128,1536]{1,0:T(8,128)(2,1)S(1)}, bf16[128,1536]{1,0:T(8,128)(2,1)S(1)}, u32[]{:S(2)}, u32[]{:S(2)}) %collective-permute-start.12) | collective-permute-done | bytes 393248 | tf_op jit(solution)/shard_map/ppermute | solution.py:14
  167.2 1.5 collective-permute-start.16
  168.6 2.1 slice.232.refs_0_
  170.7 6.9 %collective-permute-done.16 = bf16[384,512]{1,0:T(8,128)(2,1)S(1)} collective-permute-done((bf16[384,512]{1,0:T(8,128)(2,1)}, bf16[384,512]{1,0:T(8,128)(2,1)S(1)}, u32[]{:S(2)}, u32[]{:S(2)}) %collective-permute-start.16) | collective-permute-done | bytes 393248 | tf_op jit(solution)/shard_map/ppermute | solution.py:22
  177.6 1.3 convert_select_fusion
  179.0 2.8 %fusion.31 = f32[768,256]{1,0:T(8,128)S(1)} fusion(bf16[512,1536]{1,0:T(8,128)(2,1)} %collective-permute-done.17, s32[]{:T(128)S(6)} %select_n.158, bf16[384,768]{1,0:T(8,128)(2,1)} %copy-done.42, bf16[384,768]{1,0:T(8,128)(2,1)} %copy-done.44, bf16[384,768]{1,0:T(8,128)(2,1)} %get-tuple-element.24, bf16[384,768]{1,0:T(8,128)(2,1)} %get-tuple-element.64), kind=kOutput, calls=%fused_computation.48 | convolution fusion | flops 613416960 | bytes 3932164 | tf_op jit(solution)/shard_map/dot_general | solution.py:104
  182.0 1.6 fusion.20.refs_1_
  183.5 1.5 collective-permute-start.18
  185.8 2.6 %fusion.34 = f32[768,256]{1,0:T(8,128)S(1)} fusion(bf16[512,1536]{1,0:T(8,128)(2,1)} %collective-permute-done.17, s32[]{:T(128)S(6)} %select_n.157, bf16[384,768]{1,0:T(8,128)(2,1)} %copy-done.42, bf16[384,768]{1,0:T(8,128)(2,1)} %copy-done.44, bf16[384,768]{1,0:T(8,128)(2,1)S(1)} %copy-done.33, bf16[384,768]{1,0:T(8,128)(2,1)} %get-tuple-element.64), kind=kOutput, calls=%fused_computation.51 | convolution fusion | flops 613416960 | bytes 3932164 | tf_op jit(solution)/shard_map/dot_general | solution.py:104
  188.5 4.7 %collective-permute-done.18 = bf16[768,256]{1,0:T(8,128)(2,1)} collective-permute-done((bf16[768,256]{1,0:T(8,128)(2,1)}, bf16[768,256]{1,0:T(8,128)(2,1)}, u32[]{:S(2)}, u32[]{:S(2)}) %collective-permute-start.18) | collective-permute-done | bytes 393248 | tf_op jit(solution)/shard_map/ppermute | solution.py:22
  193.2 1.8 fusion.19
  195.1 1.5 collective-permute-start.19
  197.6 3.2 %collective-permute-done.19 = bf16[384,256]{1,0:T(8,128)(2,1)S(1)} collective-permute-done((bf16[384,256]{1,0:T(8,128)(2,1)S(1)}, bf16[384,256]{1,0:T(8,128)(2,1)S(1)}, u32[]{:S(2)}, u32[]{:S(2)}) %collective-permute-start.19) | collective-permute-done | bytes 196640 | tf_op jit(solution)/shard_map/ppermute | solution.py:22
  206.3 4.0 %fusion.2 = bf16[1,384,1536]{2,1,0:T(8,128)(2,1)} fusion(f32[384,1536]{1,0:T(8,128)} %slice_dynamic-update-slice_fusion.4, bf16[512,1536]{1,0:T(8,128)(2,1)} %all-gather.6.cloned.1.call-done, s32[384]{0:T(512)S(1)} %copy-done.56, pred[384]{0:T(512)(128)(4,1)S(1)} %copy-done.58, bf16[1,384,1536]{2,1,0:T(8,128)(2,1)S(1)} %copy-done), kind=kOutput, calls=%fused_computation.4 | convolution fusion | flops 606732288 | bytes 6293376 | tf_op jit(solution)/shard_map/dot_general | solution.py:240
  (194 shorter events, 30.0 us)
Async XLA Ops:
  7.2 86.2 %all-gather.4.cloned.1.call-start = ((), (), s32[]{:S(2)}) async-start(), calls=%async_computation | async-start | bytes 3932160 | tf_op jit(solution)/shard_map/all_gather | solution.py:149
  11.2 11.1 %copy-start.5 = (s32[1,512]{1,0:T(1,128)S(1)}, s32[1,512]{1,0:T(1,128)}, u32[]{:S(2)}) copy-start(s32[1,512]{1,0:T(1,128)} %bounds_ref.1) | copy-start | bytes 6148
  12.2 118.6 %all-gather.8.cloned.1.call-start = ((), (), s32[]{:S(2)}) async-start(), calls=%async_computation.2 | async-start | bytes 1966080 | tf_op jit(solution)/shard_map/all_gather | solution.py:149
  13.3 19.9 %collective-permute-start = (bf16[144,1536]{1,0:T(8,128)(2,1)}, bf16[144,1536]{1,0:T(8,128)(2,1)}, u32[]{:S(2)}, u32[]{:S(2)}) collective-permute-start(bf16[144,1536]{1,0:T(8,128)(2,1)} %get-tuple-element.40), channel_id=1, source_target_pairs={{0,4},{4,8},{8,12},{1,5},{5,9},{9,13},{2,6},{6,10},{10,14},{3,7},{... | collective-permute-start | bytes 1327112 | tf_op jit(solution)/shard_map/ppermute | solution.py:14
  19.0 29.7 %collective-permute-start.2 = (bf16[144,1536]{1,0:T(8,128)(2,1)}, bf16[144,1536]{1,0:T(8,128)(2,1)}, u32[]{:S(2)}, u32[]{:S(2)}) collective-permute-start(bf16[144,1536]{1,0:T(8,128)(2,1)} %get-tuple-element.41), channel_id=1, source_target_pairs={{4,0},{8,4},{12,8},{5,1},{9,5},{13,9},{6,2},{10,6},{14,10},{7,3},{... | collective-permute-start | bytes 1327112 | tf_op jit(solution)/shard_map/ppermute | solution.py:14
  20.3 88.8 %collective-permute-start.8 = (bf16[384,1536]{1,0:T(8,128)(2,1)S(1)}, bf16[384,1536]{1,0:T(8,128)(2,1)}, u32[]{:S(2)}, u32[]{:S(2)}) collective-permute-start(bf16[384,1536]{1,0:T(8,128)(2,1)S(1)} %bitcast.44), channel_id=1, source_target_pairs={{0,16},{16,0},{1,17},{17,1},{2,18},{18,2},{3,19},{19,3},{4,20},{20... | collective-permute-start | bytes 3538952 | tf_op jit(solution)/shard_map/ppermute | solution.py:22
  21.9 88.6 %collective-permute-start.9 = (bf16[384,1536]{1,0:T(8,128)(2,1)S(1)}, bf16[384,1536]{1,0:T(8,128)(2,1)}, u32[]{:S(2)}, u32[]{:S(2)}) collective-permute-start(bf16[384,1536]{1,0:T(8,128)(2,1)S(1)} %bitcast.46), channel_id=1, source_target_pairs={{0,16},{16,0},{1,17},{17,1},{2,18},{18,2},{3,19},{19,3},{4,20},{20... | collective-permute-start | bytes 3538952 | tf_op jit(solution)/shard_map/ppermute | solution.py:22
  24.0 58.2 %copy-start = (bf16[1,384,1536]{2,1,0:T(8,128)(2,1)S(1)}, bf16[1,384,1536]{2,1,0:T(8,128)(2,1)}, u32[]{:S(2)}) copy-start(bf16[1,384,1536]{2,1,0:T(8,128)(2,1)} %param.8) | copy-start | bytes 3538948
  50.0 23.2 %collective-permute-start.7 = (bf16[2,1536]{1,0:T(2,128)(2,1)}, bf16[2,1536]{1,0:T(2,128)(2,1)S(1)}, u32[]{:S(2)}, u32[]{:S(2)}) collective-permute-start(bf16[2,1536]{1,0:T(2,128)(2,1)} %pad_maximum_fusion.5), channel_id=1, source_target_pairs={{0,16},{16,0},{1,17},{17,1},{2,18},{18,2},{3,19},{19,3},{4,20},{20... | collective-permute-start | bytes 18440 | tf_op jit(solution)/shard_map/ppermute | solution.py:22
  52.8 153.5 %all-gather.6.cloned.1.call-start = ((), (), s32[]{:S(2)}) async-start(), calls=%async_computation.1 | async-start | bytes 1966080 | tf_op jit(solution)/shard_map/all_gather | solution.py:235
  52.9 21.0 %collective-permute-start.1 = (bf16[144,1536]{1,0:T(8,128)(2,1)}, bf16[144,1536]{1,0:T(8,128)(2,1)S(1)}, u32[]{:S(2)}, u32[]{:S(2)}) collective-permute-start(bf16[144,1536]{1,0:T(8,128)(2,1)} %collective-permute-done.refs_1_), channel_id=1, source_target_pairs={{4,8},{8,12},{5,9},{9,13},{6,10},{10,14},{7,11},{11,15},{20,24},{2... | collective-permute-start | bytes 1327112 | tf_op jit(solution)/shard_map/ppermute | solution.py:30
  53.6 28.6 %collective-permute-start.3 = (bf16[144,1536]{1,0:T(8,128)(2,1)}, bf16[144,1536]{1,0:T(8,128)(2,1)S(1)}, u32[]{:S(2)}, u32[]{:S(2)}) collective-permute-start(bf16[144,1536]{1,0:T(8,128)(2,1)} %collective-permute-done.2.refs_3_), channel_id=1, source_target_pairs={{4,0},{8,4},{5,1},{9,5},{6,2},{10,6},{7,3},{11,7},{20,16},{24,20},... | collective-permute-start | bytes 1327112 | tf_op jit(solution)/shard_map/ppermute | solution.py:30
  83.2 7.4 %copy-start.59 = (f32[384]{0:T(512)S(1)}, f32[384]{0:T(512)}, u32[]{:S(2)}) copy-start(f32[384]{0:T(512)} %select_multiply_fusion) | copy-start | bytes 4612
  86.8 3.8 %collective-permute-start.4 = (f32[8,384]{1,0:T(8,128)S(1)}, f32[8,384]{1,0:T(8,128)S(1)}, u32[]{:S(2)}, u32[]{:S(2)}) collective-permute-start(f32[8,384]{1,0:T(8,128)S(1)} %byte_sums.1), channel_id=1, source_target_pairs={{0,2},{2,0},{1,3},{3,1},{4,6},{6,4},{5,7},{7,5},{8,10},{10,8},{9,1... | collective-permute-start | bytes 36872 | tf_op jit(solution)/shard_map/ppermute | solution.py:22
  93.4 23.8 %collective-permute-start.10 = (bf16[1024,1536]{1,0:T(8,128)(2,1)}, bf16[1024,1536]{1,0:T(8,128)(2,1)}, u32[]{:S(2)}, u32[]{:S(2)}) collective-permute-start(bf16[1024,1536]{1,0:T(8,128)(2,1)} %all-gather.4.cloned.1.call-done.refs_1_), channel_id=1, source_target_pairs={{0,1},{1,0},{2,3},{3,2},{4,5},{5,4},{6,7},{7,6},{8,9},{9,8},{10,11... | collective-permute-start | bytes 9437192 | tf_op jit(solution)/shard_map/ppermute | solution.py:22
  94.7 9.1 %collective-permute-start.5 = (f32[3,1]{1,0:T(4,128)S(1)}, f32[3,1]{1,0:T(4,128)S(1)}, u32[]{:S(2)}, u32[]{:S(2)}) collective-permute-start(f32[3,1]{1,0:T(4,128)S(1)} %pad_maximum_fusion.6), channel_id=1, source_target_pairs={{4,0},{8,4},{12,8},{5,1},{9,5},{13,9},{6,2},{10,6},{14,10},{7,3},{... | collective-permute-start | bytes 44 | tf_op jit(solution)/shard_map/ppermute | solution.py:14
  98.3 6.1 %copy-start.10 = (bf16[383,768]{1,0:T(8,128)(2,1)S(1)}, bf16[383,768]{1,0:T(8,128)(2,1)}, u32[]{:S(2)}) copy-start(bf16[383,768]{1,0:T(8,128)(2,1)} %get-tuple-element.30) | copy-start | bytes 1764868
  98.3 6.1 %copy-start.11 = (bf16[383,768]{1,0:T(8,128)(2,1)S(1)}, bf16[383,768]{1,0:T(8,128)(2,1)}, u32[]{:S(2)}) copy-start(bf16[383,768]{1,0:T(8,128)(2,1)} %get-tuple-element.31) | copy-start | bytes 1764868
  98.3 6.1 %copy-start.12 = (bf16[383,768]{1,0:T(8,128)(2,1)S(1)}, bf16[383,768]{1,0:T(8,128)(2,1)}, u32[]{:S(2)}) copy-start(bf16[383,768]{1,0:T(8,128)(2,1)} %get-tuple-element.32) | copy-start | bytes 1764868
  98.3 6.1 %copy-start.13 = (bf16[383,768]{1,0:T(8,128)(2,1)S(1)}, bf16[383,768]{1,0:T(8,128)(2,1)}, u32[]{:S(2)}) copy-start(bf16[383,768]{1,0:T(8,128)(2,1)} %get-tuple-element.33) | copy-start | bytes 1764868
  98.3 6.1 %copy-start.50 = (bf16[1,768]{1,0:T(2,128)(2,1)S(1)}, bf16[1,768]{1,0:T(2,128)(2,1)}, u32[]{:S(2)}) copy-start(bf16[1,768]{1,0:T(2,128)(2,1)} %get-tuple-element.49) | copy-start | bytes 4612
  103.8 3.7 %collective-permute-start.6 = (f32[3,385]{1,0:T(4,128)S(1)}, f32[3,385]{1,0:T(4,128)S(1)}, u32[]{:S(2)}, u32[]{:S(2)}) collective-permute-start(f32[3,385]{1,0:T(4,128)S(1)} %pad_maximum_fusion.4), channel_id=1, source_target_pairs={{0,16},{16,0},{1,17},{17,1},{2,18},{18,2},{3,19},{19,3},{4,20},{20... | collective-permute-start | bytes 13868 | tf_op jit(solution)/shard_map/ppermute | solution.py:22
  121.5 9.4 %copy-start.6 = (bf16[640,1536]{1,0:T(8,128)(2,1)S(1)}, bf16[640,1536]{1,0:T(8,128)(2,1)}, u32[]{:S(2)}) copy-start(bf16[640,1536]{1,0:T(8,128)(2,1)} %after.7) | copy-start | bytes 5898244
  121.5 20.0 %collective-permute-start.11 = (bf16[768,512]{1,0:T(8,128)(2,1)}, bf16[768,512]{1,0:T(8,128)(2,1)}, u32[]{:S(2)}, u32[]{:S(2)}) collective-permute-start(bf16[768,512]{1,0:T(8,128)(2,1)} %add_convert_fusion.refs_1_), channel_id=1, source_target_pairs={{0,2},{2,0},{1,3},{3,1},{4,6},{6,4},{5,7},{7,5},{8,10},{10,8},{9,1... | collective-permute-start | bytes 2359304 | tf_op jit(solution)/shard_map/ppermute | solution.py:22
  130.9 7.6 %copy-start.9 = (bf16[1024,1536]{1,0:T(8,128)(2,1)S(1)}, bf16[1024,1536]{1,0:T(8,128)(2,1)}, u32[]{:S(2)}) copy-start(bf16[1024,1536]{1,0:T(8,128)(2,1)} %all-gather.4.cloned.1.call-done.refs_1_) | copy-start | bytes 9437188
  130.9 48.2 %collective-permute-start.17 = (bf16[512,1536]{1,0:T(8,128)(2,1)}, bf16[512,1536]{1,0:T(8,128)(2,1)}, u32[]{:S(2)}, u32[]{:S(2)}) collective-permute-start(bf16[512,1536]{1,0:T(8,128)(2,1)} %after.10), channel_id=1, source_target_pairs={{0,1},{1,0},{2,3},{3,2},{4,5},{5,4},{6,7},{7,6},{8,9},{9,8},{10,11... | collective-permute-start | bytes 4718600 | tf_op jit(solution)/shard_map/ppermute | solution.py:22
  131.0 16.0 %collective-permute-start.15 = (bf16[128,1536]{1,0:T(8,128)(2,1)S(1)}, bf16[128,1536]{1,0:T(8,128)(2,1)S(1)}, u32[]{:S(2)}, u32[]{:S(2)}) collective-permute-start(bf16[128,1536]{1,0:T(8,128)(2,1)S(1)} %get-tuple-element.18), channel_id=1, source_target_pairs={{0,8},{4,12},{1,9},{5,13},{2,10},{6,14},{3,11},{7,15},{16,24},{20,... | collective-permute-start | bytes 1179656 | tf_op jit(solution)/shard_map/ppermute | solution.py:14
  134.4 17.3 %collective-permute-start.14 = (bf16[128,1536]{1,0:T(8,128)(2,1)S(1)}, bf16[128,1536]{1,0:T(8,128)(2,1)S(1)}, u32[]{:S(2)}, u32[]{:S(2)}) collective-permute-start(bf16[128,1536]{1,0:T(8,128)(2,1)S(1)} %get-tuple-element.19), channel_id=1, source_target_pairs={{0,4},{4,8},{8,12},{1,5},{5,9},{9,13},{2,6},{6,10},{10,14},{3,7},{... | collective-permute-start | bytes 1179656 | tf_op jit(solution)/shard_map/ppermute | solution.py:14
  137.0 14.8 %collective-permute-start.13 = (bf16[128,1536]{1,0:T(8,128)(2,1)S(1)}, bf16[128,1536]{1,0:T(8,128)(2,1)S(1)}, u32[]{:S(2)}, u32[]{:S(2)}) collective-permute-start(bf16[128,1536]{1,0:T(8,128)(2,1)S(1)} %get-tuple-element.20), channel_id=1, source_target_pairs={{4,0},{8,4},{12,8},{5,1},{9,5},{13,9},{6,2},{10,6},{14,10},{7,3},{... | collective-permute-start | bytes 1179656 | tf_op jit(solution)/shard_map/ppermute | solution.py:14
  141.5 24.9 %collective-permute-start.12 = (bf16[128,1536]{1,0:T(8,128)(2,1)S(1)}, bf16[128,1536]{1,0:T(8,128)(2,1)S(1)}, u32[]{:S(2)}, u32[]{:S(2)}) collective-permute-start(bf16[128,1536]{1,0:T(8,128)(2,1)S(1)} %get-tuple-element.21), channel_id=1, source_target_pairs={{8,0},{12,4},{9,1},{13,5},{10,2},{14,6},{11,3},{15,7},{24,16},{28,... | collective-permute-start | bytes 1179656 | tf_op jit(solution)/shard_map/ppermute | solution.py:14
  146.9 19.5 %copy-start.16 = (bf16[128,1536]{1,0:T(8,128)(2,1)}, bf16[128,1536]{1,0:T(8,128)(2,1)S(1)}, u32[]{:S(2)}) copy-start(bf16[128,1536]{1,0:T(8,128)(2,1)S(1)} %collective-permute-done.15.refs_4_) | copy-start | bytes 1179652
  151.8 14.6 %copy-start.18 = (bf16[128,1536]{1,0:T(8,128)(2,1)}, bf16[128,1536]{1,0:T(8,128)(2,1)S(1)}, u32[]{:S(2)}) copy-start(bf16[128,1536]{1,0:T(8,128)(2,1)S(1)} %collective-permute-done.14.refs_3_) | copy-start | bytes 1179652
  151.8 14.6 %copy-start.20 = (bf16[128,1536]{1,0:T(8,128)(2,1)}, bf16[128,1536]{1,0:T(8,128)(2,1)S(1)}, u32[]{:S(2)}) copy-start(bf16[128,1536]{1,0:T(8,128)(2,1)S(1)} %collective-permute-done.13.refs_2_) | copy-start | bytes 1179652
  167.2 10.5 %collective-permute-start.16 = (bf16[384,512]{1,0:T(8,128)(2,1)}, bf16[384,512]{1,0:T(8,128)(2,1)S(1)}, u32[]{:S(2)}, u32[]{:S(2)}) collective-permute-start(bf16[384,512]{1,0:T(8,128)(2,1)} %after.8), channel_id=1, source_target_pairs={{0,16},{16,0},{1,17},{17,1},{2,18},{18,2},{3,19},{19,3},{4,20},{20... | collective-permute-start | bytes 1179656 | tf_op jit(solution)/shard_map/ppermute | solution.py:22
  183.5 9.7 %collective-permute-start.18 = (bf16[768,256]{1,0:T(8,128)(2,1)}, bf16[768,256]{1,0:T(8,128)(2,1)}, u32[]{:S(2)}, u32[]{:S(2)}) collective-permute-start(bf16[768,256]{1,0:T(8,128)(2,1)} %fusion.20.refs_1_), channel_id=1, source_target_pairs={{0,2},{2,0},{1,3},{3,1},{4,6},{6,4},{5,7},{7,5},{8,10},{10,8},{9,1... | collective-permute-start | bytes 1179656 | tf_op jit(solution)/shard_map/ppermute | solution.py:22
  185.8 7.4 %copy-start.15 = (bf16[512,1536]{1,0:T(8,128)(2,1)S(1)}, bf16[512,1536]{1,0:T(8,128)(2,1)}, u32[]{:S(2)}) copy-start(bf16[512,1536]{1,0:T(8,128)(2,1)} %after.10) | copy-start | bytes 4718596
  185.8 7.4 %copy-start.27 = (bf16[384,768]{1,0:T(8,128)(2,1)S(1)}, bf16[384,768]{1,0:T(8,128)(2,1)}, u32[]{:S(2)}) copy-start(bf16[384,768]{1,0:T(8,128)(2,1)} %get-tuple-element.25) | copy-start | bytes 1769476
  185.8 7.4 %copy-start.30 = (bf16[384,768]{1,0:T(8,128)(2,1)S(1)}, bf16[384,768]{1,0:T(8,128)(2,1)}, u32[]{:S(2)}) copy-start(bf16[384,768]{1,0:T(8,128)(2,1)} %get-tuple-element.63) | copy-start | bytes 1769476
  185.8 7.4 %copy-start.38 = (bf16[384,768]{1,0:T(8,128)(2,1)S(1)}, bf16[384,768]{1,0:T(8,128)(2,1)}, u32[]{:S(2)}) copy-start(bf16[384,768]{1,0:T(8,128)(2,1)} %copy-done.36) | copy-start | bytes 1769476
  185.8 7.4 %copy-start.41 = (bf16[384,768]{1,0:T(8,128)(2,1)S(1)}, bf16[384,768]{1,0:T(8,128)(2,1)}, u32[]{:S(2)}) copy-start(bf16[384,768]{1,0:T(8,128)(2,1)} %copy-done.39) | copy-start | bytes 1769476
  188.5 8.1 %copy-start.7 = (f32[128,1536]{1,0:T(8,128)S(1)}, f32[128,1536]{1,0:T(8,128)}, u32[]{:S(2)}) copy-start(f32[128,1536]{1,0:T(8,128)} %after.11) | copy-start | bytes 2359300
  188.5 8.1 %copy-start.17 = (bf16[128,1536]{1,0:T(8,128)(2,1)S(1)}, bf16[128,1536]{1,0:T(8,128)(2,1)}, u32[]{:S(2)}) copy-start(bf16[128,1536]{1,0:T(8,128)(2,1)} %copy-done.16) | copy-start | bytes 1179652
  188.5 8.1 %copy-start.19 = (bf16[128,1536]{1,0:T(8,128)(2,1)S(1)}, bf16[128,1536]{1,0:T(8,128)(2,1)}, u32[]{:S(2)}) copy-start(bf16[128,1536]{1,0:T(8,128)(2,1)} %copy-done.18) | copy-start | bytes 1179652
  188.5 8.1 %copy-start.21 = (bf16[128,1536]{1,0:T(8,128)(2,1)S(1)}, bf16[128,1536]{1,0:T(8,128)(2,1)}, u32[]{:S(2)}) copy-start(bf16[128,1536]{1,0:T(8,128)(2,1)} %copy-done.20) | copy-start | bytes 1179652
  188.5 8.1 %copy-start.23 = (bf16[128,1536]{1,0:T(8,128)(2,1)S(1)}, bf16[128,1536]{1,0:T(8,128)(2,1)}, u32[]{:S(2)}) copy-start(bf16[128,1536]{1,0:T(8,128)(2,1)} %copy-done.22) | copy-start | bytes 1179652
  195.1 5.7 %collective-permute-start.19 = (bf16[384,256]{1,0:T(8,128)(2,1)S(1)}, bf16[384,256]{1,0:T(8,128)(2,1)S(1)}, u32[]{:S(2)}, u32[]{:S(2)}) collective-permute-start(bf16[384,256]{1,0:T(8,128)(2,1)S(1)} %slice.256), channel_id=1, source_target_pairs={{0,16},{16,0},{1,17},{17,1},{2,18},{18,2},{3,19},{19,3},{4,20},{20... | collective-permute-start | bytes 589832 | tf_op jit(solution)/shard_map/ppermute | solution.py:22
  197.6 8.7 %copy-start.56 = (s32[384]{0:T(512)S(1)}, s32[384]{0:T(512)}, u32[]{:S(2)}) copy-start(s32[384]{0:T(512)} %get-tuple-element.59) | copy-start | bytes 4612
  197.6 8.7 %copy-start.58 = (pred[384]{0:T(512)(128)(4,1)S(1)}, pred[384]{0:T(512)(128)(4,1)}, u32[]{:S(2)}) copy-start(pred[384]{0:T(512)(128)(4,1)} %copy-done.57) | copy-start | bytes 1156
  (37 other events, 132.5 us)
Sparse Core Ops, SparseCore 0:
  12.3 81.0 all-gather.3
  95.5 35.2 all-gather.7
  170.8 34.3 all-gather.5

commit v12 on v10

--- a/solution.py
+++ b/solution.py
@@ -248,7 +248,7 @@
     far_part = None
     for own_weight in own_weights:
         if far_part is not None:
-            own_weight = after(own_weight, far_part)
+            own_weight = after(own_weight, far_part, *received)
         other_weight = swapped(own_weight, "pipe")
         block_rows = own_weight.shape[0] // tensor_count
         if tensor_count == 2:

time: 217 us -> 222 us (1.023)
  local copies, waits for them, and re-layouts: 19.8 us -> 26.5 us
  waiting for transfers between devices: 102 us -> 95.5 us
  matrix products: 24.4 us -> 29.3 us
  starting transfers between devices: 37.2 us -> 34.4 us
    all_gather x2, waiting for transfers between devices: 23.7 us -> 1.64 us  [shards(): own_weights.append(lax.all_gather(piece, 'seq', axis=0, tiled=True))]
    ppermute x2, waiting for transfers between devices: 0.01 us -> 8.34 us  [passed_on(): return lax.ppermute(x, axis, pairs)]
    ppermute x7, waiting for transfers between devices: 41 us -> 47.3 us  [passed_along(): return lax.ppermute(x, axis, pairs)]
    unnamed x122 -> x138, local copies, waits for them, and re-layouts: 3.89 us -> 9.97 us
    dot_general x8, matrix products: 17.2 us -> 19.9 us  [product(): lax.dot_general(rows, weight, (((1,), (1,)), ((), ())), preferred_element...]
  transfers between devices with their start and end apart: 23 -> 23, of which waited for: 11 -> 14; matrix products, arithmetic and copies ran while one was open for 23% -> 28% of each run, Pallas kernels for 2% -> 2%
where the time goes in v12:
time: 222 us; the launch traced here: 221 us
  waiting for transfers between devices  95.5 us (43%)
  starting transfers between devices  34.4 us (15%)
  matrix products  29.3 us (13%)
  local copies, waits for them, and re-layouts  26.5 us (12%)
  other arithmetic  16.7 us (8%)
  between operations  14.7 us (7%)
  Pallas kernels  3.62 us (2%)
    ppermute x7, waiting for transfers between devices, passed_along(): return lax.ppermute(x, axis, pairs)  47.3 us
    ppermute x11, waiting for transfers between devices, swapped(): return lax.ppermute(x, axis, [(i, length - 1 - i) for i in range(length)])  38.2 us
    ppermute x7, starting transfers between devices, passed_along(): return lax.ppermute(x, axis, pairs)  21.1 us
    dot_general x8, matrix products, product(): lax.dot_general(rows, weight, (((1,), (1,)), ((), ())), preferred_element...  19.9 us
    ppermute x11, starting transfers between devices, swapped(): return lax.ppermute(x, axis, [(i, length - 1 - i) for i in range(length)])  11.2 us
    unnamed x138, local copies, waits for them, and re-layouts  9.97 us
    ppermute x2, waiting for transfers between devices, passed_on(): return lax.ppermute(x, axis, pairs)  8.34 us
    convert_element_type x2, other arithmetic, grads(): key_grad.astype(jnp.bfloat16)  6.03 us
  transfers between devices with their start and end apart: 23, of which 14 were waited for; matrix products, arithmetic and copies ran while one was open for 28% of the time, Pallas kernels for 2%

profile of v12, /device:TPU:0, one launch (start us, length us, event | category | flops | bytes accessed | tf_op | source)
XLA Modules:
  0.0 220.8 jit_solution(6219735817370753573)
XLA Ops:
  7.2 1.9 copy.40
  13.3 5.7 %collective-permute-start = (bf16[144,1536]{1,0:T(8,128)(2,1)}, bf16[144,1536]{1,0:T(8,128)(2,1)}, u32[]{:S(2)}, u32[]{:S(2)}) collective-permute-start(bf16[144,1536]{1,0:T(8,128)(2,1)} %get-tuple-element.40), channel_id=1, source_target_pairs={{0,4},{4,8},{8,12},{1,5},{5,9},{9,13},{2,6},{6,10},{10,14},{3,7},{... | collective-permute-start | bytes 1327112 | tf_op jit(solution)/shard_map/ppermute | solution.py:14
  19.0 1.3 collective-permute-start.2
  20.3 1.6 collective-permute-start.8
  24.0 1.6 dynamic-slice_bitcast_fusion
  27.6 5.6 %collective-permute-done.refs_1_ = bf16[144,1536]{1,0:T(8,128)(2,1)} collective-permute-done((bf16[144,1536]{1,0:T(8,128)(2,1)}, bf16[144,1536]{1,0:T(8,128)(2,1)}, u32[]{:S(2)}, u32[]{:S(2)}) %collective-permute-start) | collective-permute-done | bytes 442400 | tf_op jit(solution)/shard_map/ppermute | solution.py:14
  33.9 14.7 %collective-permute-done.2.refs_3_ = bf16[144,1536]{1,0:T(8,128)(2,1)} collective-permute-done((bf16[144,1536]{1,0:T(8,128)(2,1)}, bf16[144,1536]{1,0:T(8,128)(2,1)}, u32[]{:S(2)}, u32[]{:S(2)}) %collective-permute-start.2) | collective-permute-done | bytes 442400 | tf_op jit(solution)/shard_map/ppermute | solution.py:14
  50.0 1.6 collective-permute-start.7
  53.5 1.3 collective-permute-start.3
  54.8 18.4 %collective-permute-done.7 = bf16[2,1536]{1,0:T(2,128)(2,1)S(1)} collective-permute-done((bf16[2,1536]{1,0:T(2,128)(2,1)}, bf16[2,1536]{1,0:T(2,128)(2,1)S(1)}, u32[]{:S(2)}, u32[]{:S(2)}) %collective-permute-start.7) | collective-permute-done | bytes 6176 | tf_op jit(solution)/shard_map/ppermute | solution.py:22
  73.8 8.3 %collective-permute-done.3.refs_4_ = bf16[144,1536]{1,0:T(8,128)(2,1)S(1)} collective-permute-done((bf16[144,1536]{1,0:T(8,128)(2,1)}, bf16[144,1536]{1,0:T(8,128)(2,1)S(1)}, u32[]{:S(2)}, u32[]{:S(2)}) %collective-permute-start.3) | collective-permute-done | bytes 442400 | tf_op jit(solution)/shard_map/ppermute | solution.py:30
  83.2 3.6 %byte_sums.1 = f32[8,384]{1,0:T(8,128)S(1)} custom-call(s32[1]{0:T(128)} %bitcast.3.shard_ref, s32[1,512]{1,0:T(1,128)S(1)} %copy-done.5, bf16[384,1536]{1,0:T(8,128)(2,1)S(1)} %bitcast.43, bf16[384,1536]{1,0:T(8,128)(2,1)S(1)} %bitcast.47, bf16[384,1536]{1,0:T(8,128)(2,1)S(1)} %bitcast.45, bf16[144,1536]{1,0:T(8,128)(2,1)S(1)} %collective-permute-done.1.refs_0_, ...), custom_call_target="tpu_custom_call" | custom-call | tf_op jit(solution)/shard_map/byte_sums/pallas_call | solution.py:93
  86.8 1.6 collective-permute-start.4
  89.0 1.6 collective-permute-done.4
  90.6 1.2 slice_reduce_fusion.7
  91.7 1.6 all-gather.4.cloned.1.call-done.refs_1_
  94.7 1.5 collective-permute-start.5
  96.9 1.3 fusion.39
  98.3 4.1 %fusion.73 = (bf16[640,1536]{1,0:T(8,128)(2,1)}, f32[640,1536]{1,0:T(8,128)}) fusion(f32[640,1536]{1,0:T(8,128)S(1)} %fusion.39, bf16[1,384,1536]{2,1,0:T(8,128)(2,1)S(1)} %copy-done, s32[384]{0:T(512)S(1)} %get-tuple-element.60, bf16[384]{0:T(512)(128)(2,1)S(1)} %get-tuple-element.12), kind=kOutput, calls=%fused_computation.150 | convolution fusion | flops 757432320 | bytes 11012352 | tf_op jit(solution)/shard_map/dot_general | solution.py:222
  102.4 1.4 collective-permute-done.5
  104.5 2.8 %fusion.22 = (bf16[384,768]{1,0:T(8,128)(2,1)}, bf16[384,768]{1,0:T(8,128)(2,1)}, bf16[384,768]{1,0:T(8,128)(2,1)}, bf16[384,768]{1,0:T(8,128)(2,1)}) fusion(bf16[1,768]{1,0:T(2,128)(2,1)S(1)} %copy-done.55, bf16[383,768]{1,0:T(8,128)(2,1)S(1)} %copy-done.11, bf16[1,384,1536]{2,1,0:T(8,128)(2,1)S(1)} %copy-done.1, s32[]{:T(128)S(6)} %select_n.148, ...), kind=kLoop, calls=%fused_computation.26 | loop fusion | flops 10616832 | bytes 7084040 | tf_op jit(solution)/shard_map/convert_element_type | solution.py:196
  108.2 1.3 constant_dynamic-slice_fusion
  109.6 1.9 fusion.71
  111.6 3.2 %subtract_convert_fusion = (bf16[384,768]{1,0:T(8,128)(2,1)S(1)}, bf16[384,768]{1,0:T(8,128)(2,1)S(1)}, bf16[384,768]{1,0:T(8,128)(2,1)S(1)}, bf16[384,768]{1,0:T(8,128)(2,1)S(1)}) fusion(bf16[1,768]{1,0:T(2,128)(2,1)S(1)} %copy-done.57, bf16[383,768]{1,0:T(8,128)(2,1)S(1)} %get-tuple-element.36, bf16[384,1536]{1,0:T(8,128)(2,1)} %collective-permute-done.8, ...), kind=kLoop, calls=%fused_computation.36 | loop fusion | flops 10616832 | bytes 7084040 | tf_op jit(solution)/shard_map/convert_element_type | solution.py:196
  114.9 1.4 fusion.5
  116.9 3.9 %add_convert_fusion.refs_1_ = bf16[768,512]{1,0:T(8,128)(2,1)} fusion(f32[768,512]{1,0:T(8,128)S(1)} %fusion.5, bf16[1024,1536]{1,0:T(8,128)(2,1)} %collective-permute-done.10, s32[]{:T(128)S(6)} %select_n.149, bf16[384,768]{1,0:T(8,128)(2,1)S(1)} %get-tuple-element.28, bf16[384,768]{1,0:T(8,128)(2,1)S(1)} %get-tuple-element.66, ...), kind=kOutput, calls=%fused_computation.8 | convolution fusion | flops 1218183168 | bytes 6291460 | tf_op jit(solution)/shard_map/dot_general | solution.py:104
  120.8 1.6 collective-permute-start.11
  122.4 8.1 %collective-permute-start.16 = (bf16[128,1536]{1,0:T(8,128)(2,1)S(1)}, bf16[128,1536]{1,0:T(8,128)(2,1)S(1)}, u32[]{:S(2)}, u32[]{:S(2)}) collective-permute-start(bf16[128,1536]{1,0:T(8,128)(2,1)S(1)} %get-tuple-element.18), channel_id=1, source_target_pairs={{0,8},{4,12},{1,9},{5,13},{2,10},{6,14},{3,11},{7,15},{16,24},{20,... | collective-permute-start | bytes 1179656 | tf_op jit(solution)/shard_map/ppermute | solution.py:14
  130.6 1.6 collective-permute-start.15
  132.2 1.3 collective-permute-start.14
  133.5 1.6 collective-permute-start.13
  135.1 5.0 %collective-permute-done.16.refs_5_ = bf16[128,1536]{1,0:T(8,128)(2,1)S(1)} collective-permute-done((bf16[128,1536]{1,0:T(8,128)(2,1)S(1)}, bf16[128,1536]{1,0:T(8,128)(2,1)S(1)}, u32[]{:S(2)}, u32[]{:S(2)}) %collective-permute-start.16) | collective-permute-done | bytes 393248 | tf_op jit(solution)/shard_map/ppermute | solution.py:14
  140.1 6.8 %collective-permute-done.15.refs_4_ = bf16[128,1536]{1,0:T(8,128)(2,1)S(1)} collective-permute-done((bf16[128,1536]{1,0:T(8,128)(2,1)S(1)}, bf16[128,1536]{1,0:T(8,128)(2,1)S(1)}, u32[]{:S(2)}, u32[]{:S(2)}) %collective-permute-start.15) | collective-permute-done | bytes 393248 | tf_op jit(solution)/shard_map/ppermute | solution.py:14
  146.9 13.8 %collective-permute-done.13.refs_2_ = bf16[128,1536]{1,0:T(8,128)(2,1)S(1)} collective-permute-done((bf16[128,1536]{1,0:T(8,128)(2,1)S(1)}, bf16[128,1536]{1,0:T(8,128)(2,1)S(1)}, u32[]{:S(2)}, u32[]{:S(2)}) %collective-permute-start.13) | collective-permute-done | bytes 393248 | tf_op jit(solution)/shard_map/ppermute | solution.py:14
  161.5 3.5 %fusion.9 = f32[768,512]{1,0:T(8,128)S(1)} fusion(bf16[1024,1536]{1,0:T(8,128)(2,1)} %all-gather.4.cloned.1.call-done.refs_1_, s32[]{:T(128)S(6)} %select_n.147, bf16[384,768]{1,0:T(8,128)(2,1)} %copy-done.37, bf16[384,768]{1,0:T(8,128)(2,1)} %copy-done.40, bf16[384,768]{1,0:T(8,128)(2,1)S(1)} %copy-done.25, bf16[384,768]{1,0:T(8,128)(2,1)} %get-tuple-element.63), kind=kOutput, calls=%fused_computation.16 | convolution fusion | flops 1217396736 | bytes 5505028 | tf_op jit(solution)/shard_map/dot_general | solution.py:104
  165.1 3.0 %convert_add_fusion = f32[768,512]{1,0:T(8,128)S(1)} fusion(bf16[768,512]{1,0:T(8,128)(2,1)} %collective-permute-done.11, f32[768,512]{1,0:T(8,128)S(1)} %fusion.9, bf16[1024,1536]{1,0:T(8,128)(2,1)} %collective-permute-done.10, s32[]{:T(128)S(6)} %select_n.147, bf16[384,768]{1,0:T(8,128)(2,1)S(1)} %copy-done.44, bf16[384,768]{1,0:T(8,128)(2,1)S(1)} %copy-done.47, ...), kind=kOutput, calls=%fused_computation.7 | convolution fusion | flops 1219362816 | bytes 7864324 | tf_op jit(solution)/shard_map/dot_general | solution.py:104
  169.0 1.6 collective-permute-start.12
  170.7 2.1 slice.232.refs_0_
  172.8 8.0 %collective-permute-done.12 = bf16[384,512]{1,0:T(8,128)(2,1)} collective-permute-done((bf16[384,512]{1,0:T(8,128)(2,1)}, bf16[384,512]{1,0:T(8,128)(2,1)}, u32[]{:S(2)}, u32[]{:S(2)}) %collective-permute-start.12) | collective-permute-done | bytes 393248 | tf_op jit(solution)/shard_map/ppermute | solution.py:22
  180.8 1.5 convert_select_fusion
  182.4 2.1 fusion.31
  184.5 1.6 fusion.20.refs_1_
  187.5 2.7 %fusion.34 = f32[768,256]{1,0:T(8,128)S(1)} fusion(bf16[512,1536]{1,0:T(8,128)(2,1)} %collective-permute-done.17, s32[]{:T(128)S(6)} %select_n.157, bf16[384,768]{1,0:T(8,128)(2,1)} %copy-done.43, bf16[384,768]{1,0:T(8,128)(2,1)} %copy-done.46, bf16[384,768]{1,0:T(8,128)(2,1)S(1)} %copy-done.33, bf16[384,768]{1,0:T(8,128)(2,1)} %get-tuple-element.64), kind=kOutput, calls=%fused_computation.51 | convolution fusion | flops 613416960 | bytes 3932164 | tf_op jit(solution)/shard_map/dot_general | solution.py:104
  190.2 7.0 %collective-permute-done.18 = bf16[768,256]{1,0:T(8,128)(2,1)} collective-permute-done((bf16[768,256]{1,0:T(8,128)(2,1)}, bf16[768,256]{1,0:T(8,128)(2,1)}, u32[]{:S(2)}, u32[]{:S(2)}) %collective-permute-start.18) | collective-permute-done | bytes 393248 | tf_op jit(solution)/shard_map/ppermute | solution.py:22
  197.2 1.8 fusion.19
  199.0 1.7 collective-permute-start.19
  201.8 3.0 %collective-permute-done.19 = bf16[384,256]{1,0:T(8,128)(2,1)S(1)} collective-permute-done((bf16[384,256]{1,0:T(8,128)(2,1)S(1)}, bf16[384,256]{1,0:T(8,128)(2,1)S(1)}, u32[]{:S(2)}, u32[]{:S(2)}) %collective-permute-start.19) | collective-permute-done | bytes 196640 | tf_op jit(solution)/shard_map/ppermute | solution.py:22
  210.3 4.0 %fusion.2 = bf16[1,384,1536]{2,1,0:T(8,128)(2,1)} fusion(f32[384,1536]{1,0:T(8,128)} %slice_dynamic-update-slice_fusion.4, bf16[512,1536]{1,0:T(8,128)(2,1)} %all-gather.6.cloned.1.call-done, s32[384]{0:T(512)S(1)} %copy-done.61, pred[384]{0:T(512)(128)(4,1)S(1)} %copy-done.63, bf16[1,384,1536]{2,1,0:T(8,128)(2,1)S(1)} %copy-done), kind=kOutput, calls=%fused_computation.4 | convolution fusion | flops 606732288 | bytes 6293376 | tf_op jit(solution)/shard_map/dot_general | solution.py:240
  (203 shorter events, 28.4 us)
Async XLA Ops:
  7.2 86.2 %all-gather.4.cloned.1.call-start = ((), (), s32[]{:S(2)}) async-start(), calls=%async_computation | async-start | bytes 3932160 | tf_op jit(solution)/shard_map/all_gather | solution.py:149
  11.2 11.2 %copy-start.5 = (s32[1,512]{1,0:T(1,128)S(1)}, s32[1,512]{1,0:T(1,128)}, u32[]{:S(2)}) copy-start(s32[1,512]{1,0:T(1,128)} %bounds_ref.1) | copy-start | bytes 6148
  12.2 148.5 %all-gather.8.cloned.1.call-start = ((), (), s32[]{:S(2)}) async-start(), calls=%async_computation.2 | async-start | bytes 1966080 | tf_op jit(solution)/shard_map/all_gather | solution.py:149
  13.3 19.9 %collective-permute-start = (bf16[144,1536]{1,0:T(8,128)(2,1)}, bf16[144,1536]{1,0:T(8,128)(2,1)}, u32[]{:S(2)}, u32[]{:S(2)}) collective-permute-start(bf16[144,1536]{1,0:T(8,128)(2,1)} %get-tuple-element.40), channel_id=1, source_target_pairs={{0,4},{4,8},{8,12},{1,5},{5,9},{9,13},{2,6},{6,10},{10,14},{3,7},{... | collective-permute-start | bytes 1327112 | tf_op jit(solution)/shard_map/ppermute | solution.py:14
  19.0 29.7 %collective-permute-start.2 = (bf16[144,1536]{1,0:T(8,128)(2,1)}, bf16[144,1536]{1,0:T(8,128)(2,1)}, u32[]{:S(2)}, u32[]{:S(2)}) collective-permute-start(bf16[144,1536]{1,0:T(8,128)(2,1)} %get-tuple-element.41), channel_id=1, source_target_pairs={{4,0},{8,4},{12,8},{5,1},{9,5},{13,9},{6,2},{10,6},{14,10},{7,3},{... | collective-permute-start | bytes 1327112 | tf_op jit(solution)/shard_map/ppermute | solution.py:14
  20.3 88.0 %collective-permute-start.8 = (bf16[384,1536]{1,0:T(8,128)(2,1)S(1)}, bf16[384,1536]{1,0:T(8,128)(2,1)}, u32[]{:S(2)}, u32[]{:S(2)}) collective-permute-start(bf16[384,1536]{1,0:T(8,128)(2,1)S(1)} %bitcast.44), channel_id=1, source_target_pairs={{0,16},{16,0},{1,17},{17,1},{2,18},{18,2},{3,19},{19,3},{4,20},{20... | collective-permute-start | bytes 3538952 | tf_op jit(solution)/shard_map/ppermute | solution.py:22
  21.8 87.7 %collective-permute-start.9 = (bf16[384,1536]{1,0:T(8,128)(2,1)S(1)}, bf16[384,1536]{1,0:T(8,128)(2,1)}, u32[]{:S(2)}, u32[]{:S(2)}) collective-permute-start(bf16[384,1536]{1,0:T(8,128)(2,1)S(1)} %bitcast.46), channel_id=1, source_target_pairs={{0,16},{16,0},{1,17},{17,1},{2,18},{18,2},{3,19},{19,3},{4,20},{20... | collective-permute-start | bytes 3538952 | tf_op jit(solution)/shard_map/ppermute | solution.py:22
  24.0 58.2 %copy-start = (bf16[1,384,1536]{2,1,0:T(8,128)(2,1)S(1)}, bf16[1,384,1536]{2,1,0:T(8,128)(2,1)}, u32[]{:S(2)}) copy-start(bf16[1,384,1536]{2,1,0:T(8,128)(2,1)} %param.8) | copy-start | bytes 3538948
  50.0 23.2 %collective-permute-start.7 = (bf16[2,1536]{1,0:T(2,128)(2,1)}, bf16[2,1536]{1,0:T(2,128)(2,1)S(1)}, u32[]{:S(2)}, u32[]{:S(2)}) collective-permute-start(bf16[2,1536]{1,0:T(2,128)(2,1)} %pad_maximum_fusion.5), channel_id=1, source_target_pairs={{0,16},{16,0},{1,17},{17,1},{2,18},{18,2},{3,19},{19,3},{4,20},{20... | collective-permute-start | bytes 18440 | tf_op jit(solution)/shard_map/ppermute | solution.py:22
  52.8 157.5 %all-gather.6.cloned.1.call-start = ((), (), s32[]{:S(2)}) async-start(), calls=%async_computation.1 | async-start | bytes 1966080 | tf_op jit(solution)/shard_map/all_gather | solution.py:235
  52.8 21.0 %collective-permute-start.1 = (bf16[144,1536]{1,0:T(8,128)(2,1)}, bf16[144,1536]{1,0:T(8,128)(2,1)S(1)}, u32[]{:S(2)}, u32[]{:S(2)}) collective-permute-start(bf16[144,1536]{1,0:T(8,128)(2,1)} %collective-permute-done.refs_1_), channel_id=1, source_target_pairs={{4,8},{8,12},{5,9},{9,13},{6,10},{10,14},{7,11},{11,15},{20,24},{2... | collective-permute-start | bytes 1327112 | tf_op jit(solution)/shard_map/ppermute | solution.py:30
  53.5 28.6 %collective-permute-start.3 = (bf16[144,1536]{1,0:T(8,128)(2,1)}, bf16[144,1536]{1,0:T(8,128)(2,1)S(1)}, u32[]{:S(2)}, u32[]{:S(2)}) collective-permute-start(bf16[144,1536]{1,0:T(8,128)(2,1)} %collective-permute-done.2.refs_3_), channel_id=1, source_target_pairs={{4,0},{8,4},{5,1},{9,5},{6,2},{10,6},{7,3},{11,7},{20,16},{24,20},... | collective-permute-start | bytes 1327112 | tf_op jit(solution)/shard_map/ppermute | solution.py:30
  83.2 7.4 %copy-start.64 = (f32[384]{0:T(512)S(1)}, f32[384]{0:T(512)}, u32[]{:S(2)}) copy-start(f32[384]{0:T(512)} %select_multiply_fusion) | copy-start | bytes 4612
  86.8 3.8 %collective-permute-start.4 = (f32[8,384]{1,0:T(8,128)S(1)}, f32[8,384]{1,0:T(8,128)S(1)}, u32[]{:S(2)}, u32[]{:S(2)}) collective-permute-start(f32[8,384]{1,0:T(8,128)S(1)} %byte_sums.1), channel_id=1, source_target_pairs={{0,2},{2,0},{1,3},{3,1},{4,6},{6,4},{5,7},{7,5},{8,10},{10,8},{9,1... | collective-permute-start | bytes 36872 | tf_op jit(solution)/shard_map/ppermute | solution.py:22
  93.4 23.0 %collective-permute-start.10 = (bf16[1024,1536]{1,0:T(8,128)(2,1)}, bf16[1024,1536]{1,0:T(8,128)(2,1)}, u32[]{:S(2)}, u32[]{:S(2)}) collective-permute-start(bf16[1024,1536]{1,0:T(8,128)(2,1)} %all-gather.4.cloned.1.call-done.refs_1_), channel_id=1, source_target_pairs={{0,1},{1,0},{2,3},{3,2},{4,5},{5,4},{6,7},{7,6},{8,9},{9,8},{10,11... | collective-permute-start | bytes 9437192 | tf_op jit(solution)/shard_map/ppermute | solution.py:22
  94.7 9.0 %collective-permute-start.5 = (f32[3,1]{1,0:T(4,128)S(1)}, f32[3,1]{1,0:T(4,128)S(1)}, u32[]{:S(2)}, u32[]{:S(2)}) collective-permute-start(f32[3,1]{1,0:T(4,128)S(1)} %pad_maximum_fusion.6), channel_id=1, source_target_pairs={{4,0},{8,4},{12,8},{5,1},{9,5},{13,9},{6,2},{10,6},{14,10},{7,3},{... | collective-permute-start | bytes 44 | tf_op jit(solution)/shard_map/ppermute | solution.py:14
  98.3 6.1 %copy-start.9 = (bf16[383,768]{1,0:T(8,128)(2,1)S(1)}, bf16[383,768]{1,0:T(8,128)(2,1)}, u32[]{:S(2)}) copy-start(bf16[383,768]{1,0:T(8,128)(2,1)} %get-tuple-element.30) | copy-start | bytes 1764868
  98.3 6.1 %copy-start.10 = (bf16[383,768]{1,0:T(8,128)(2,1)S(1)}, bf16[383,768]{1,0:T(8,128)(2,1)}, u32[]{:S(2)}) copy-start(bf16[383,768]{1,0:T(8,128)(2,1)} %get-tuple-element.31) | copy-start | bytes 1764868
  103.8 3.7 %collective-permute-start.6 = (f32[3,385]{1,0:T(4,128)S(1)}, f32[3,385]{1,0:T(4,128)S(1)}, u32[]{:S(2)}, u32[]{:S(2)}) collective-permute-start(f32[3,385]{1,0:T(4,128)S(1)} %pad_maximum_fusion.4), channel_id=1, source_target_pairs={{0,16},{16,0},{1,17},{17,1},{2,18},{18,2},{3,19},{19,3},{4,20},{20... | collective-permute-start | bytes 13868 | tf_op jit(solution)/shard_map/ppermute | solution.py:22
  120.8 44.3 %collective-permute-start.11 = (bf16[768,512]{1,0:T(8,128)(2,1)}, bf16[768,512]{1,0:T(8,128)(2,1)}, u32[]{:S(2)}, u32[]{:S(2)}) collective-permute-start(bf16[768,512]{1,0:T(8,128)(2,1)} %add_convert_fusion.refs_1_), channel_id=1, source_target_pairs={{0,2},{2,0},{1,3},{3,1},{4,6},{6,4},{5,7},{7,5},{8,10},{10,8},{9,1... | collective-permute-start | bytes 2359304 | tf_op jit(solution)/shard_map/ppermute | solution.py:22
  122.4 17.7 %collective-permute-start.16 = (bf16[128,1536]{1,0:T(8,128)(2,1)S(1)}, bf16[128,1536]{1,0:T(8,128)(2,1)S(1)}, u32[]{:S(2)}, u32[]{:S(2)}) collective-permute-start(bf16[128,1536]{1,0:T(8,128)(2,1)S(1)} %get-tuple-element.18), channel_id=1, source_target_pairs={{0,8},{4,12},{1,9},{5,13},{2,10},{6,14},{3,11},{7,15},{16,24},{20,... | collective-permute-start | bytes 1179656 | tf_op jit(solution)/shard_map/ppermute | solution.py:14
  130.6 16.3 %collective-permute-start.15 = (bf16[128,1536]{1,0:T(8,128)(2,1)S(1)}, bf16[128,1536]{1,0:T(8,128)(2,1)S(1)}, u32[]{:S(2)}, u32[]{:S(2)}) collective-permute-start(bf16[128,1536]{1,0:T(8,128)(2,1)S(1)} %get-tuple-element.19), channel_id=1, source_target_pairs={{0,4},{4,8},{8,12},{1,5},{5,9},{9,13},{2,6},{6,10},{10,14},{3,7},{... | collective-permute-start | bytes 1179656 | tf_op jit(solution)/shard_map/ppermute | solution.py:14
  132.2 14.8 %collective-permute-start.14 = (bf16[128,1536]{1,0:T(8,128)(2,1)S(1)}, bf16[128,1536]{1,0:T(8,128)(2,1)S(1)}, u32[]{:S(2)}, u32[]{:S(2)}) collective-permute-start(bf16[128,1536]{1,0:T(8,128)(2,1)S(1)} %get-tuple-element.20), channel_id=1, source_target_pairs={{4,0},{8,4},{12,8},{5,1},{9,5},{13,9},{6,2},{10,6},{14,10},{7,3},{... | collective-permute-start | bytes 1179656 | tf_op jit(solution)/shard_map/ppermute | solution.py:14
  133.5 28.0 %copy-start.25 = (bf16[384,768]{1,0:T(8,128)(2,1)S(1)}, bf16[384,768]{1,0:T(8,128)(2,1)}, u32[]{:S(2)}) copy-start(bf16[384,768]{1,0:T(8,128)(2,1)} %get-tuple-element.25) | copy-start | bytes 1769476
  133.5 27.2 %collective-permute-start.13 = (bf16[128,1536]{1,0:T(8,128)(2,1)S(1)}, bf16[128,1536]{1,0:T(8,128)(2,1)S(1)}, u32[]{:S(2)}, u32[]{:S(2)}) collective-permute-start(bf16[128,1536]{1,0:T(8,128)(2,1)S(1)} %get-tuple-element.21), channel_id=1, source_target_pairs={{8,0},{12,4},{9,1},{13,5},{10,2},{14,6},{11,3},{15,7},{24,16},{28,... | collective-permute-start | bytes 1179656 | tf_op jit(solution)/shard_map/ppermute | solution.py:14
  140.1 20.6 %copy-start.15 = (bf16[128,1536]{1,0:T(8,128)(2,1)}, bf16[128,1536]{1,0:T(8,128)(2,1)S(1)}, u32[]{:S(2)}) copy-start(bf16[128,1536]{1,0:T(8,128)(2,1)S(1)} %collective-permute-done.16.refs_5_) | copy-start | bytes 1179652
  146.9 13.8 %copy-start.17 = (bf16[128,1536]{1,0:T(8,128)(2,1)}, bf16[128,1536]{1,0:T(8,128)(2,1)S(1)}, u32[]{:S(2)}) copy-start(bf16[128,1536]{1,0:T(8,128)(2,1)S(1)} %collective-permute-done.15.refs_4_) | copy-start | bytes 1179652
  146.9 13.8 %copy-start.19 = (bf16[128,1536]{1,0:T(8,128)(2,1)}, bf16[128,1536]{1,0:T(8,128)(2,1)S(1)}, u32[]{:S(2)}) copy-start(bf16[128,1536]{1,0:T(8,128)(2,1)S(1)} %collective-permute-done.14.refs_3_) | copy-start | bytes 1179652
  161.5 20.9 %collective-permute-start.17 = (bf16[512,1536]{1,0:T(8,128)(2,1)}, bf16[512,1536]{1,0:T(8,128)(2,1)}, u32[]{:S(2)}, u32[]{:S(2)}) collective-permute-start(bf16[512,1536]{1,0:T(8,128)(2,1)} %after.8), channel_id=1, source_target_pairs={{0,1},{1,0},{2,3},{3,2},{4,5},{5,4},{6,7},{7,6},{8,9},{9,8},{10,11... | collective-permute-start | bytes 4718600 | tf_op jit(solution)/shard_map/ppermute | solution.py:22
  169.0 11.8 %collective-permute-start.12 = (bf16[384,512]{1,0:T(8,128)(2,1)}, bf16[384,512]{1,0:T(8,128)(2,1)}, u32[]{:S(2)}, u32[]{:S(2)}) collective-permute-start(bf16[384,512]{1,0:T(8,128)(2,1)} %slice.255), channel_id=1, source_target_pairs={{0,16},{16,0},{1,17},{17,1},{2,18},{18,2},{3,19},{19,3},{4,20},{20... | collective-permute-start | bytes 1179656 | tf_op jit(solution)/shard_map/ppermute | solution.py:22
  172.8 9.6 %copy-start.32 = (bf16[384,768]{1,0:T(8,128)(2,1)S(1)}, bf16[384,768]{1,0:T(8,128)(2,1)}, u32[]{:S(2)}) copy-start(bf16[384,768]{1,0:T(8,128)(2,1)} %get-tuple-element.24) | copy-start | bytes 1769476
  172.8 9.6 %copy-start.36 = (bf16[384,768]{1,0:T(8,128)(2,1)S(1)}, bf16[384,768]{1,0:T(8,128)(2,1)}, u32[]{:S(2)}) copy-start(bf16[384,768]{1,0:T(8,128)(2,1)} %get-tuple-element.64) | copy-start | bytes 1769476
  172.8 9.6 %copy-start.45 = (bf16[384,768]{1,0:T(8,128)(2,1)S(1)}, bf16[384,768]{1,0:T(8,128)(2,1)}, u32[]{:S(2)}) copy-start(bf16[384,768]{1,0:T(8,128)(2,1)} %copy-done.43) | copy-start | bytes 1769476
  172.8 9.6 %copy-start.48 = (bf16[384,768]{1,0:T(8,128)(2,1)S(1)}, bf16[384,768]{1,0:T(8,128)(2,1)}, u32[]{:S(2)}) copy-start(bf16[384,768]{1,0:T(8,128)(2,1)} %copy-done.46) | copy-start | bytes 1769476
  186.1 11.0 %collective-permute-start.18 = (bf16[768,256]{1,0:T(8,128)(2,1)}, bf16[768,256]{1,0:T(8,128)(2,1)}, u32[]{:S(2)}, u32[]{:S(2)}) collective-permute-start(bf16[768,256]{1,0:T(8,128)(2,1)} %fusion.20.refs_1_), channel_id=1, source_target_pairs={{0,2},{2,0},{1,3},{3,1},{4,6},{6,4},{5,7},{7,5},{8,10},{10,8},{9,1... | collective-permute-start | bytes 1179656 | tf_op jit(solution)/shard_map/ppermute | solution.py:22
  187.5 9.7 %copy-start.14 = (bf16[512,1536]{1,0:T(8,128)(2,1)S(1)}, bf16[512,1536]{1,0:T(8,128)(2,1)}, u32[]{:S(2)}) copy-start(bf16[512,1536]{1,0:T(8,128)(2,1)} %after.8) | copy-start | bytes 4718596
  187.5 9.7 %copy-start.26 = (bf16[384,768]{1,0:T(8,128)(2,1)S(1)}, bf16[384,768]{1,0:T(8,128)(2,1)}, u32[]{:S(2)}) copy-start(bf16[384,768]{1,0:T(8,128)(2,1)} %get-tuple-element.25) | copy-start | bytes 1769476
  187.5 9.7 %copy-start.29 = (bf16[384,768]{1,0:T(8,128)(2,1)S(1)}, bf16[384,768]{1,0:T(8,128)(2,1)}, u32[]{:S(2)}) copy-start(bf16[384,768]{1,0:T(8,128)(2,1)} %get-tuple-element.63) | copy-start | bytes 1769476
  187.5 9.7 %copy-start.39 = (bf16[384,768]{1,0:T(8,128)(2,1)S(1)}, bf16[384,768]{1,0:T(8,128)(2,1)}, u32[]{:S(2)}) copy-start(bf16[384,768]{1,0:T(8,128)(2,1)} %copy-done.37) | copy-start | bytes 1769476
  187.5 9.7 %copy-start.42 = (bf16[384,768]{1,0:T(8,128)(2,1)S(1)}, bf16[384,768]{1,0:T(8,128)(2,1)}, u32[]{:S(2)}) copy-start(bf16[384,768]{1,0:T(8,128)(2,1)} %copy-done.40) | copy-start | bytes 1769476
  190.2 10.6 %copy-start.7 = (f32[128,1536]{1,0:T(8,128)S(1)}, f32[128,1536]{1,0:T(8,128)}, u32[]{:S(2)}) copy-start(f32[128,1536]{1,0:T(8,128)} %after.9) | copy-start | bytes 2359300
  190.2 10.6 %copy-start.16 = (bf16[128,1536]{1,0:T(8,128)(2,1)S(1)}, bf16[128,1536]{1,0:T(8,128)(2,1)}, u32[]{:S(2)}) copy-start(bf16[128,1536]{1,0:T(8,128)(2,1)} %copy-done.15) | copy-start | bytes 1179652
  190.2 10.6 %copy-start.18 = (bf16[128,1536]{1,0:T(8,128)(2,1)S(1)}, bf16[128,1536]{1,0:T(8,128)(2,1)}, u32[]{:S(2)}) copy-start(bf16[128,1536]{1,0:T(8,128)(2,1)} %copy-done.17) | copy-start | bytes 1179652
  190.2 10.6 %copy-start.20 = (bf16[128,1536]{1,0:T(8,128)(2,1)S(1)}, bf16[128,1536]{1,0:T(8,128)(2,1)}, u32[]{:S(2)}) copy-start(bf16[128,1536]{1,0:T(8,128)(2,1)} %copy-done.19) | copy-start | bytes 1179652
  190.2 10.6 %copy-start.22 = (bf16[128,1536]{1,0:T(8,128)(2,1)S(1)}, bf16[128,1536]{1,0:T(8,128)(2,1)}, u32[]{:S(2)}) copy-start(bf16[128,1536]{1,0:T(8,128)(2,1)} %copy-done.21) | copy-start | bytes 1179652
  199.0 5.7 %collective-permute-start.19 = (bf16[384,256]{1,0:T(8,128)(2,1)S(1)}, bf16[384,256]{1,0:T(8,128)(2,1)S(1)}, u32[]{:S(2)}, u32[]{:S(2)}) collective-permute-start(bf16[384,256]{1,0:T(8,128)(2,1)S(1)} %slice.256), channel_id=1, source_target_pairs={{0,16},{16,0},{1,17},{17,1},{2,18},{18,2},{3,19},{19,3},{4,20},{20... | collective-permute-start | bytes 589832 | tf_op jit(solution)/shard_map/ppermute | solution.py:22
  201.8 8.5 %copy-start.61 = (s32[384]{0:T(512)S(1)}, s32[384]{0:T(512)}, u32[]{:S(2)}) copy-start(s32[384]{0:T(512)} %get-tuple-element.59) | copy-start | bytes 4612
  201.8 8.5 %copy-start.63 = (pred[384]{0:T(512)(128)(4,1)S(1)}, pred[384]{0:T(512)(128)(4,1)}, u32[]{:S(2)}) copy-start(pred[384]{0:T(512)(128)(4,1)} %copy-done.62) | copy-start | bytes 1156
  (42 other events, 145.2 us)
Sparse Core Ops, SparseCore 0:
  12.3 81.0 all-gather.3
  95.5 35.2 all-gather.7
  172.9 33.3 all-gather.5

commit v13 on v9

--- a/solution.py
+++ b/solution.py
@@ -229,9 +229,10 @@
             return moved_block.astype(jnp.float32)
 
         outer = after(jnp.stack([terms[0], terms[4]]).astype(jnp.bfloat16), ready)
-        span_sums = terms[2] + moved(terms[3] + moved(outer[1], 1, 2), 1, 1)
-        span_sums = span_sums + moved(terms[1] + moved(outer[0], -1, -2), -1, -1)
-        return span_sums.astype(jnp.bfloat16)[None]
+        inner = jnp.stack(
+            [terms[1] + moved(outer[0], -1, -2), terms[3] + moved(outer[1], 1, 2)]
+        )
+        return terms[reach], inner.astype(jnp.bfloat16)
 
     window_grad = lax.all_gather(
         after(main_in_grad[0], own_weights[0]), "seq", axis=0, tiled=True
@@ -245,7 +246,7 @@
         return total.astype(jnp.bfloat16)
 
     pieces = []
-    main_grad = span_part(factors_other)
+    span_sums, span_inner = span_part(factors_other)
     far_part = None
     for own_weight in own_weights:
         if far_part is not None:
@@ -264,8 +265,9 @@
             incoming = swapped(far_part, "tensor").astype(jnp.float32)
             total = partial(*half(tensor_index)).astype(jnp.float32) + incoming
         else:
+            far_part = partial(own_weight, other_weight)
             total = lax.psum_scatter(
-                partial(own_weight, other_weight), "tensor", scatter_dimension=1, tiled=True
+                far_part, "tensor", scatter_dimension=1, tiled=True
             ).astype(jnp.float32)
         own = total[:row_count]
         returned = total[row_count:].astype(jnp.bfloat16)
@@ -273,6 +275,10 @@
         pieces.append(
             [jnp.where(group_index == 0, own, arrived), jnp.where(group_index == 0, arrived, own)]
         )
+    span_inner = after(span_inner, far_part)
+    span_sums = span_sums + passed_along(span_inner[0], "seq", -1).astype(jnp.float32)
+    span_sums = span_sums + passed_along(span_inner[1], "seq", 1).astype(jnp.float32)
+    main_grad = span_sums.astype(jnp.bfloat16)[None]
     widths = [high - low for low, high in cuts]
     routing = jnp.concatenate(
         [

time: 205 us -> 211 us (1.029)
  waiting for transfers between devices: 82.2 us -> 77.9 us
  starting transfers between devices: 38.3 us -> 42.4 us
  other arithmetic: 17.7 us -> 21.4 us
  matrix products: 25.5 us -> 28.4 us
    ppermute x6 -> x4, waiting for transfers between devices: 20.8 us -> 10.1 us  [passed_on(): return lax.ppermute(x, axis, pairs)]
    ppermute x3 -> x5, starting transfers between devices: 8.28 us -> 18.4 us  [passed_along(): return lax.ppermute(x, axis, pairs)]
    ppermute x6 -> x4, starting transfers between devices: 18.8 us -> 11.9 us  [passed_on(): return lax.ppermute(x, axis, pairs)]
    ppermute x11, waiting for transfers between devices: 38.7 us -> 42.4 us  [swapped(): return lax.ppermute(x, axis, [(i, length - 1 - i) for i in range(length)])]
    dot_general x8, matrix products: 17 us -> 19.8 us  [product(): lax.dot_general(rows, weight, (((1,), (1,)), ((), ())), preferred_element...]
    another operation x0 -> x2, other arithmetic: none -> 2.78 us  [span_part(): jnp.stack([terms[1] + moved(outer[0], -1, -2), terms[3] + moved(outer[1],...]
    ppermute x3 -> x5, waiting for transfers between devices: 22.6 us -> 25.4 us  [passed_along(): return lax.ppermute(x, axis, pairs)]
    unnamed x100 -> x112, local copies, waits for them, and re-layouts: 6.19 us -> 5.94 us
  transfers between devices with their start and end apart: 23 -> 23, of which waited for: 13 -> 9; matrix products, arithmetic and copies ran while one was open for 26% -> 28% of each run, Pallas kernels for 2% -> 2%
where the time goes in v13:
time: 211 us; the launch traced here: 210 us
  waiting for transfers between devices  77.9 us (37%)
  starting transfers between devices  42.4 us (20%)
  matrix products  28.4 us (13%)
  local copies, waits for them, and re-layouts  21.9 us (10%)
  other arithmetic  21.4 us (10%)
  between operations  14.7 us (7%)
  Pallas kernels  3.62 us (2%)
    ppermute x11, waiting for transfers between devices, swapped(): return lax.ppermute(x, axis, [(i, length - 1 - i) for i in range(length)])  42.4 us
    ppermute x5, waiting for transfers between devices, passed_along(): return lax.ppermute(x, axis, pairs)  25.4 us
    dot_general x8, matrix products, product(): lax.dot_general(rows, weight, (((1,), (1,)), ((), ())), preferred_element...  19.8 us
    ppermute x5, starting transfers between devices, passed_along(): return lax.ppermute(x, axis, pairs)  18.4 us
    ppermute x11, starting transfers between devices, swapped(): return lax.ppermute(x, axis, [(i, length - 1 - i) for i in range(length)])  12 us
    ppermute x4, starting transfers between devices, passed_on(): return lax.ppermute(x, axis, pairs)  11.9 us
    ppermute x4, waiting for transfers between devices, passed_on(): return lax.ppermute(x, axis, pairs)  10.1 us
    convert_element_type x2, other arithmetic, grads(): key_grad.astype(jnp.bfloat16)  6.03 us
  transfers between devices with their start and end apart: 23, of which 9 were waited for; matrix products, arithmetic and copies ran while one was open for 28% of the time, Pallas kernels for 2%

profile of v13, /device:TPU:0, one launch (start us, length us, event | category | flops | bytes accessed | tf_op | source)
XLA Modules:
  0.0 210.3 jit_solution(4117511119190053651)
XLA Ops:
  7.2 1.9 copy.40
  9.2 1.0 dynamic_slice.89
  10.2 1.0 dynamic_slice.88
  12.3 1.0 pad_maximum_fusion.3
  13.3 1.3 collective-permute-start.2
  14.6 6.4 %collective-permute-start = (bf16[144,1536]{1,0:T(8,128)(2,1)}, bf16[144,1536]{1,0:T(8,128)(2,1)}, u32[]{:S(2)}, u32[]{:S(2)}) collective-permute-start(bf16[144,1536]{1,0:T(8,128)(2,1)} %get-tuple-element.44), channel_id=1, source_target_pairs={{0,4},{4,8},{8,12},{1,5},{5,9},{9,13},{2,6},{6,10},{10,14},{3,7},{... | collective-permute-start | bytes 1327112 | tf_op jit(solution)/shard_map/ppermute | solution.py:14
  21.0 2.0 collective-permute-start.9
  23.5 1.1 dynamic-slice_bitcast_fusion.1
  24.7 1.7 dynamic-slice_bitcast_fusion
  28.2 7.5 %collective-permute-done.2.refs_3_ = bf16[144,1536]{1,0:T(8,128)(2,1)} collective-permute-done((bf16[144,1536]{1,0:T(8,128)(2,1)}, bf16[144,1536]{1,0:T(8,128)(2,1)}, u32[]{:S(2)}, u32[]{:S(2)}) %collective-permute-start.2) | collective-permute-done | bytes 442400 | tf_op jit(solution)/shard_map/ppermute | solution.py:14
  38.5 2.0 collective-permute-start.7
  42.5 1.3 collective-permute-start.3
  43.8 30.1 %collective-permute-done.7 = bf16[2,1536]{1,0:T(2,128)(2,1)S(1)} collective-permute-done((bf16[2,1536]{1,0:T(2,128)(2,1)}, bf16[2,1536]{1,0:T(2,128)(2,1)S(1)}, u32[]{:S(2)}, u32[]{:S(2)}) %collective-permute-start.7) | collective-permute-done | bytes 6176 | tf_op jit(solution)/shard_map/ppermute | solution.py:22
  74.5 10.1 %collective-permute-done.3.refs_4_ = bf16[144,1536]{1,0:T(8,128)(2,1)S(1)} collective-permute-done((bf16[144,1536]{1,0:T(8,128)(2,1)}, bf16[144,1536]{1,0:T(8,128)(2,1)S(1)}, u32[]{:S(2)}, u32[]{:S(2)}) %collective-permute-start.3) | collective-permute-done | bytes 442400 | tf_op jit(solution)/shard_map/ppermute | solution.py:30
  85.5 3.6 %byte_sums.1 = f32[8,384]{1,0:T(8,128)S(1)} custom-call(s32[1]{0:T(128)} %bitcast.3.shard_ref, s32[1,512]{1,0:T(1,128)S(1)} %copy-done.5, bf16[384,1536]{1,0:T(8,128)(2,1)S(1)} %bitcast.59, bf16[384,1536]{1,0:T(8,128)(2,1)S(1)} %bitcast.61, bf16[384,1536]{1,0:T(8,128)(2,1)S(1)} %bitcast.63, bf16[144,1536]{1,0:T(8,128)(2,1)S(1)} %collective-permute-done.1.refs_0_, ...), custom_call_target="tpu_custom_call" | custom-call | tf_op jit(solution)/shard_map/byte_sums/pallas_call | solution.py:93
  89.2 1.5 collective-permute-start.4
  91.3 1.6 collective-permute-done.4
  93.6 1.5 collective-permute-start.5
  96.2 2.0 fusion.43
  98.2 3.3 %fusion.78 = (bf16[640,1536]{1,0:T(8,128)(2,1)S(1)}, f32[640,1536]{1,0:T(8,128)}) fusion(f32[640,1536]{1,0:T(8,128)S(1)} %fusion.43, bf16[1,384,1536]{2,1,0:T(8,128)(2,1)S(1)} %copy-done, s32[384]{0:T(512)S(1)} %get-tuple-element.63, bf16[384]{0:T(512)(128)(2,1)S(1)} %copy-done.51), kind=kOutput, calls=%fused_computation.165 | convolution fusion | flops 757432320 | bytes 11012352 | tf_op jit(solution)/shard_map/dot_general | solution.py:222
  104.5 2.8 %fusion.22 = (bf16[384,768]{1,0:T(8,128)(2,1)}, bf16[384,768]{1,0:T(8,128)(2,1)}, bf16[384,768]{1,0:T(8,128)(2,1)}, bf16[384,768]{1,0:T(8,128)(2,1)}) fusion(bf16[1,768]{1,0:T(2,128)(2,1)S(1)} %copy-done.38, bf16[383,768]{1,0:T(8,128)(2,1)S(1)} %copy-done.13, bf16[1,384,1536]{2,1,0:T(8,128)(2,1)S(1)} %copy-done.2, s32[]{:T(128)S(6)} %select_n.148, ...), kind=kLoop, calls=%fused_computation.26 | loop fusion | flops 10616832 | bytes 7084040 | tf_op jit(solution)/shard_map/convert_element_type | solution.py:196
  108.8 1.9 fusion.76
  110.7 1.3 constant_dynamic-slice_fusion
  112.1 3.3 %subtract_convert_fusion = (bf16[384,768]{1,0:T(8,128)(2,1)S(1)}, bf16[384,768]{1,0:T(8,128)(2,1)S(1)}, bf16[384,768]{1,0:T(8,128)(2,1)S(1)}, bf16[384,768]{1,0:T(8,128)(2,1)S(1)}) fusion(bf16[1,768]{1,0:T(2,128)(2,1)S(1)} %copy-done.36, bf16[383,768]{1,0:T(8,128)(2,1)S(1)} %get-tuple-element.36, bf16[384,1536]{1,0:T(8,128)(2,1)} %collective-permute-done.8, ...), kind=kLoop, calls=%fused_computation.36 | loop fusion | flops 10616832 | bytes 7084040 | tf_op jit(solution)/shard_map/convert_element_type | solution.py:196
  115.5 1.4 fusion.5
  117.5 2.9 %add_convert_fusion.refs_1_ = bf16[768,512]{1,0:T(8,128)(2,1)S(1)} fusion(f32[768,512]{1,0:T(8,128)S(1)} %fusion.5, bf16[1024,1536]{1,0:T(8,128)(2,1)} %collective-permute-done.10, s32[]{:T(128)S(6)} %select_n.149, bf16[384,768]{1,0:T(8,128)(2,1)S(1)} %get-tuple-element.28, bf16[384,768]{1,0:T(8,128)(2,1)S(1)} %get-tuple-element.70, ...), kind=kOutput, calls=%fused_computation.8 | convolution fusion | flops 1218183168 | bytes 6291460 | tf_op jit(solution)/shard_map/dot_general | solution.py:104
  120.4 1.6 collective-permute-start.11
  122.9 1.4 collective-permute-start.16
  124.3 8.5 %collective-permute-start.17 = (bf16[128,1536]{1,0:T(8,128)(2,1)}, bf16[128,1536]{1,0:T(8,128)(2,1)}, u32[]{:S(2)}, u32[]{:S(2)}) collective-permute-start(bf16[128,1536]{1,0:T(8,128)(2,1)} %get-tuple-element.43), channel_id=1, source_target_pairs={{0,4},{4,8},{1,5},{5,9},{2,6},{6,10},{3,7},{7,11},{16,20},{20,24},... | collective-permute-start | bytes 1179656 | tf_op jit(solution)/shard_map/ppermute | solution.py:30
  132.9 2.6 %fusion.9 = f32[768,512]{1,0:T(8,128)} fusion(bf16[1024,1536]{1,0:T(8,128)(2,1)S(1)} %copy-done.10, s32[]{:T(128)S(6)} %select_n.147, bf16[384,768]{1,0:T(8,128)(2,1)S(1)} %get-tuple-element.29, bf16[384,768]{1,0:T(8,128)(2,1)S(1)} %get-tuple-element.69, bf16[384,768]{1,0:T(8,128)(2,1)S(1)} %copy-done.18, bf16[384,768]{1,0:T(8,128)(2,1)S(1)} %copy-done.21), kind=kOutput, calls=%fused_computation.16 | convolution fusion | flops 1217396736 | bytes 5505028 | tf_op jit(solution)/shard_map/dot_general | solution.py:104
  135.5 4.5 %collective-permute-done.11 = bf16[768,512]{1,0:T(8,128)(2,1)} collective-permute-done((bf16[768,512]{1,0:T(8,128)(2,1)S(1)}, bf16[768,512]{1,0:T(8,128)(2,1)}, u32[]{:S(2)}, u32[]{:S(2)}) %collective-permute-start.11) | collective-permute-done | bytes 786464 | tf_op jit(solution)/shard_map/ppermute | solution.py:22
  140.0 4.1 %convert_add_fusion = f32[768,512]{1,0:T(8,128)S(1)} fusion(bf16[768,512]{1,0:T(8,128)(2,1)} %collective-permute-done.11, f32[768,512]{1,0:T(8,128)} %fusion.9, bf16[1024,1536]{1,0:T(8,128)(2,1)} %collective-permute-done.10, s32[]{:T(128)S(6)} %select_n.147, bf16[384,768]{1,0:T(8,128)(2,1)} %copy-done.33, bf16[384,768]{1,0:T(8,128)(2,1)} %copy-done.34, ...), kind=kOutput, calls=%fused_computation.7 | convolution fusion | flops 1219362816 | bytes 7864324 | tf_op jit(solution)/shard_map/dot_general | solution.py:104
  144.9 1.4 collective-permute-start.12
  146.3 1.8 fusion.49
  149.1 6.2 %collective-permute-done.12 = bf16[384,512]{1,0:T(8,128)(2,1)} collective-permute-done((bf16[384,512]{1,0:T(8,128)(2,1)}, bf16[384,512]{1,0:T(8,128)(2,1)}, u32[]{:S(2)}, u32[]{:S(2)}) %collective-permute-start.12) | collective-permute-done | bytes 393248 | tf_op jit(solution)/shard_map/ppermute | solution.py:22
  155.3 2.1 %convert_select_fusion = (f32[384,512]{1,0:T(8,128)}, f32[384,512]{1,0:T(8,128)S(1)}) fusion(bf16[384,512]{1,0:T(8,128)(2,1)} %collective-permute-done.12, f32[768,512]{1,0:T(8,128)S(1)} %convert_add_fusion, pred[]{:T(512)S(6)} %eq.73), kind=kLoop, calls=%fused_computation.43 | loop fusion | flops 589824 | bytes 2752513 | tf_op jit(solution)/shard_map/jit(_where)/select_n | solution.py:276
  158.4 2.8 %fusion.35 = f32[768,256]{1,0:T(8,128)S(1)} fusion(bf16[512,1536]{1,0:T(8,128)(2,1)} %collective-permute-done.13, s32[]{:T(128)S(6)} %select_n.154, bf16[384,768]{1,0:T(8,128)(2,1)} %copy-done.33, bf16[384,768]{1,0:T(8,128)(2,1)} %copy-done.34, bf16[384,768]{1,0:T(8,128)(2,1)} %get-tuple-element.24, bf16[384,768]{1,0:T(8,128)(2,1)} %get-tuple-element.68), kind=kOutput, calls=%fused_computation.56 | convolution fusion | flops 613416960 | bytes 3932164 | tf_op jit(solution)/shard_map/dot_general | solution.py:104
  161.6 1.6 fusion.20.refs_1_
  163.1 2.0 collective-permute-start.14
  165.1 1.2 slice_bitcast_fusion.1
  166.3 7.7 %collective-permute-start.19 = (bf16[128,1536]{1,0:T(8,128)(2,1)S(1)}, bf16[128,1536]{1,0:T(8,128)(2,1)S(1)}, u32[]{:S(2)}, u32[]{:S(2)}) collective-permute-start(bf16[128,1536]{1,0:T(8,128)(2,1)S(1)} %get-tuple-element.41), channel_id=1, source_target_pairs={{0,4},{4,8},{8,12},{1,5},{5,9},{9,13},{2,6},{6,10},{10,14},{3,7},{... | collective-permute-start | bytes 1179656 | tf_op jit(solution)/shard_map/ppermute | solution.py:14
  174.0 1.6 collective-permute-start.18
  175.6 2.7 %fusion.38 = f32[768,256]{1,0:T(8,128)S(1)} fusion(bf16[512,1536]{1,0:T(8,128)(2,1)} %collective-permute-done.13, s32[]{:T(128)S(6)} %select_n.153, bf16[384,768]{1,0:T(8,128)(2,1)} %copy-done.33, bf16[384,768]{1,0:T(8,128)(2,1)} %copy-done.34, bf16[384,768]{1,0:T(8,128)(2,1)} %get-tuple-element.24, bf16[384,768]{1,0:T(8,128)(2,1)} %get-tuple-element.68), kind=kOutput, calls=%fused_computation.59 | convolution fusion | flops 613416960 | bytes 3932164 | tf_op jit(solution)/shard_map/dot_general | solution.py:104
  178.3 1.8 fusion.19
  180.7 10.2 %collective-permute-done.19 = bf16[128,1536]{1,0:T(8,128)(2,1)S(1)} collective-permute-done((bf16[128,1536]{1,0:T(8,128)(2,1)S(1)}, bf16[128,1536]{1,0:T(8,128)(2,1)S(1)}, u32[]{:S(2)}, u32[]{:S(2)}) %collective-permute-start.19) | collective-permute-done | bytes 393248 | tf_op jit(solution)/shard_map/ppermute | solution.py:14
  191.0 6.9 %collective-permute-done.18 = bf16[128,1536]{1,0:T(8,128)(2,1)S(1)} collective-permute-done((bf16[128,1536]{1,0:T(8,128)(2,1)S(1)}, bf16[128,1536]{1,0:T(8,128)(2,1)S(1)}, u32[]{:S(2)}, u32[]{:S(2)}) %collective-permute-start.18) | collective-permute-done | bytes 393248 | tf_op jit(solution)/shard_map/ppermute | solution.py:14
  197.9 2.0 fusion.48
  200.6 3.2 %fusion.2 = bf16[1,384,1536]{2,1,0:T(8,128)(2,1)} fusion(f32[384,1536]{1,0:T(8,128)S(1)} %slice_dynamic-update-slice_fusion.4, bf16[512,1536]{1,0:T(8,128)(2,1)} %all-gather.6.cloned.1.call-done, s32[384]{0:T(512)S(1)} %copy-done.46, pred[384]{0:T(512)(128)(4,1)S(1)} %copy-done.49, bf16[1,384,1536]{2,1,0:T(8,128)(2,1)S(1)} %copy-done), kind=kOutput, calls=%fused_computation.4 | convolution fusion | flops 606732288 | bytes 6293376 | tf_op jit(solution)/shard_map/dot_general | solution.py:242
  (181 shorter events, 22.5 us)
Async XLA Ops:
  7.2 5.1 %copy-start.1 = (bf16[1,384,1536]{2,1,0:T(8,128)(2,1)S(1)}, bf16[1,384,1536]{2,1,0:T(8,128)(2,1)}, u32[]{:S(2)}) copy-start(bf16[1,384,1536]{2,1,0:T(8,128)(2,1)} %param.9) | copy-start | bytes 3538948
  7.2 5.1 %copy-start.2 = (bf16[1,384,1536]{2,1,0:T(8,128)(2,1)S(1)}, bf16[1,384,1536]{2,1,0:T(8,128)(2,1)}, u32[]{:S(2)}) copy-start(bf16[1,384,1536]{2,1,0:T(8,128)(2,1)} %param.10) | copy-start | bytes 3538948
  7.2 5.1 %copy-start.3 = (bf16[1,128,1536]{2,1,0:T(8,128)(2,1)S(1)}, bf16[1,128,1536]{2,1,0:T(8,128)(2,1)}, u32[]{:S(2)}) copy-start(bf16[1,128,1536]{2,1,0:T(8,128)(2,1)} %param.11) | copy-start | bytes 1179652
  7.2 89.0 %all-gather.4.cloned.1.call-start = ((), (), s32[]{:S(2)}) async-start(), calls=%async_computation | async-start | bytes 3932160 | tf_op jit(solution)/shard_map/all_gather | solution.py:149
  11.2 11.8 %copy-start.5 = (s32[1,512]{1,0:T(1,128)S(1)}, s32[1,512]{1,0:T(1,128)}, u32[]{:S(2)}) copy-start(s32[1,512]{1,0:T(1,128)} %bounds_ref.1) | copy-start | bytes 6148
  12.2 123.3 %all-gather.8.cloned.1.call-start = ((), (), s32[]{:S(2)}) async-start(), calls=%async_computation.2 | async-start | bytes 1966080 | tf_op jit(solution)/shard_map/all_gather | solution.py:149
  13.3 22.3 %collective-permute-start.2 = (bf16[144,1536]{1,0:T(8,128)(2,1)}, bf16[144,1536]{1,0:T(8,128)(2,1)}, u32[]{:S(2)}, u32[]{:S(2)}) collective-permute-start(bf16[144,1536]{1,0:T(8,128)(2,1)} %get-tuple-element.45), channel_id=1, source_target_pairs={{4,0},{8,4},{12,8},{5,1},{9,5},{13,9},{6,2},{10,6},{14,10},{7,3},{... | collective-permute-start | bytes 1327112 | tf_op jit(solution)/shard_map/ppermute | solution.py:14
  14.6 22.5 %collective-permute-start = (bf16[144,1536]{1,0:T(8,128)(2,1)}, bf16[144,1536]{1,0:T(8,128)(2,1)}, u32[]{:S(2)}, u32[]{:S(2)}) collective-permute-start(bf16[144,1536]{1,0:T(8,128)(2,1)} %get-tuple-element.44), channel_id=1, source_target_pairs={{0,4},{4,8},{8,12},{1,5},{5,9},{9,13},{2,6},{6,10},{10,14},{3,7},{... | collective-permute-start | bytes 1327112 | tf_op jit(solution)/shard_map/ppermute | solution.py:14
  21.0 87.8 %collective-permute-start.9 = (bf16[384,1536]{1,0:T(8,128)(2,1)S(1)}, bf16[384,1536]{1,0:T(8,128)(2,1)}, u32[]{:S(2)}, u32[]{:S(2)}) collective-permute-start(bf16[384,1536]{1,0:T(8,128)(2,1)S(1)} %bitcast.60), channel_id=1, source_target_pairs={{0,16},{16,0},{1,17},{17,1},{2,18},{18,2},{3,19},{19,3},{4,20},{20... | collective-permute-start | bytes 3538952 | tf_op jit(solution)/shard_map/ppermute | solution.py:22
  22.9 87.8 %collective-permute-start.8 = (bf16[384,1536]{1,0:T(8,128)(2,1)S(1)}, bf16[384,1536]{1,0:T(8,128)(2,1)}, u32[]{:S(2)}, u32[]{:S(2)}) collective-permute-start(bf16[384,1536]{1,0:T(8,128)(2,1)S(1)} %bitcast.62), channel_id=1, source_target_pairs={{0,16},{16,0},{1,17},{17,1},{2,18},{18,2},{3,19},{19,3},{4,20},{20... | collective-permute-start | bytes 3538952 | tf_op jit(solution)/shard_map/ppermute | solution.py:22
  23.2 3.6 %copy-start.47 = (pred[384]{0:T(512)(128)(4,1)}, pred[384]{0:T(512)(128)(4,1)S(1)}, u32[]{:S(2)}) copy-start(pred[384]{0:T(512)(128)(4,1)S(1)} %compare_reduce_fusion) | copy-start | bytes 1156
  23.5 3.9 %dynamic-slice-start = ((bf16[768,1536]{1,0:T(8,128)(2,1)}, s32[]{:T(128)}, s32[]{:T(128)}), bf16[128,768]{1,0:T(8,128)(2,1)S(1)}, s32[]{:S(2)}) async-start(bf16[768,1536]{1,0:T(8,128)(2,1)} %param.15, s32[]{:T(128)} %select_n.152, s32[]{:T(128)} %select_n.142), calls=%async_computation.3 | async-start | bytes 393728 | tf_op jit(solution)/shard_map/dynamic_slice | solution.py:138
  23.5 3.9 %dynamic-slice-start.1 = ((bf16[768,1536]{1,0:T(8,128)(2,1)}, s32[]{:T(128)}, s32[]{:T(128)}), bf16[128,768]{1,0:T(8,128)(2,1)S(1)}, s32[]{:S(2)}) async-start(bf16[768,1536]{1,0:T(8,128)(2,1)} %param.14, s32[]{:T(128)} %select_n.152, s32[]{:T(128)} %select_n.142), calls=%async_computation.4 | async-start | bytes 393728 | tf_op jit(solution)/shard_map/dynamic_slice | solution.py:138
  24.7 59.9 %copy-start = (bf16[1,384,1536]{2,1,0:T(8,128)(2,1)S(1)}, bf16[1,384,1536]{2,1,0:T(8,128)(2,1)}, u32[]{:S(2)}) copy-start(bf16[1,384,1536]{2,1,0:T(8,128)(2,1)} %param.8) | copy-start | bytes 3538948
  38.5 35.3 %collective-permute-start.7 = (bf16[2,1536]{1,0:T(2,128)(2,1)}, bf16[2,1536]{1,0:T(2,128)(2,1)S(1)}, u32[]{:S(2)}, u32[]{:S(2)}) collective-permute-start(bf16[2,1536]{1,0:T(2,128)(2,1)} %pad_maximum_fusion.7), channel_id=1, source_target_pairs={{0,16},{16,0},{1,17},{17,1},{2,18},{18,2},{3,19},{19,3},{4,20},{20... | collective-permute-start | bytes 18440 | tf_op jit(solution)/shard_map/ppermute | solution.py:22
  41.7 158.5 %all-gather.6.cloned.1.call-start = ((), (), s32[]{:S(2)}) async-start(), calls=%async_computation.1 | async-start | bytes 1966080 | tf_op jit(solution)/shard_map/all_gather | solution.py:237
  41.8 32.7 %collective-permute-start.1 = (bf16[144,1536]{1,0:T(8,128)(2,1)}, bf16[144,1536]{1,0:T(8,128)(2,1)S(1)}, u32[]{:S(2)}, u32[]{:S(2)}) collective-permute-start(bf16[144,1536]{1,0:T(8,128)(2,1)} %collective-permute-done.refs_1_), channel_id=1, source_target_pairs={{4,8},{8,12},{5,9},{9,13},{6,10},{10,14},{7,11},{11,15},{20,24},{2... | collective-permute-start | bytes 1327112 | tf_op jit(solution)/shard_map/ppermute | solution.py:30
  42.5 42.1 %collective-permute-start.3 = (bf16[144,1536]{1,0:T(8,128)(2,1)}, bf16[144,1536]{1,0:T(8,128)(2,1)S(1)}, u32[]{:S(2)}, u32[]{:S(2)}) collective-permute-start(bf16[144,1536]{1,0:T(8,128)(2,1)} %collective-permute-done.2.refs_3_), channel_id=1, source_target_pairs={{4,0},{8,4},{5,1},{9,5},{6,2},{10,6},{7,3},{11,7},{20,16},{24,20},... | collective-permute-start | bytes 1327112 | tf_op jit(solution)/shard_map/ppermute | solution.py:30
  85.5 7.4 %copy-start.50 = (f32[384]{0:T(512)S(1)}, f32[384]{0:T(512)}, u32[]{:S(2)}) copy-start(f32[384]{0:T(512)} %select_multiply_fusion) | copy-start | bytes 4612
  85.5 9.5 %copy-start.48 = (pred[384]{0:T(512)(128)(4,1)S(1)}, pred[384]{0:T(512)(128)(4,1)}, u32[]{:S(2)}) copy-start(pred[384]{0:T(512)(128)(4,1)} %copy-done.47) | copy-start | bytes 1156
  89.2 3.8 %collective-permute-start.4 = (f32[8,384]{1,0:T(8,128)S(1)}, f32[8,384]{1,0:T(8,128)S(1)}, u32[]{:S(2)}, u32[]{:S(2)}) collective-permute-start(f32[8,384]{1,0:T(8,128)S(1)} %byte_sums.1), channel_id=1, source_target_pairs={{0,2},{2,0},{1,3},{3,1},{4,6},{6,4},{5,7},{7,5},{8,10},{10,8},{9,1... | collective-permute-start | bytes 36872 | tf_op jit(solution)/shard_map/ppermute | solution.py:22
  93.6 9.1 %collective-permute-start.5 = (f32[3,1]{1,0:T(4,128)}, f32[3,1]{1,0:T(4,128)}, u32[]{:S(2)}, u32[]{:S(2)}) collective-permute-start(f32[3,1]{1,0:T(4,128)} %pad_maximum_fusion.8), channel_id=1, source_target_pairs={{4,0},{8,4},{12,8},{5,1},{9,5},{13,9},{6,2},{10,6},{14,10},{7,3},{... | collective-permute-start | bytes 44 | tf_op jit(solution)/shard_map/ppermute | solution.py:14
  96.2 20.6 %collective-permute-start.10 = (bf16[1024,1536]{1,0:T(8,128)(2,1)}, bf16[1024,1536]{1,0:T(8,128)(2,1)}, u32[]{:S(2)}, u32[]{:S(2)}) collective-permute-start(bf16[1024,1536]{1,0:T(8,128)(2,1)} %all-gather.4.cloned.1.call-done.refs_1_), channel_id=1, source_target_pairs={{0,1},{1,0},{2,3},{3,2},{4,5},{5,4},{6,7},{7,6},{8,9},{9,8},{10,11... | collective-permute-start | bytes 9437192 | tf_op jit(solution)/shard_map/ppermute | solution.py:22
  103.4 3.9 %collective-permute-start.6 = (f32[3,385]{1,0:T(4,128)S(1)}, f32[3,385]{1,0:T(4,128)S(1)}, u32[]{:S(2)}, u32[]{:S(2)}) collective-permute-start(f32[3,385]{1,0:T(4,128)S(1)} %pad_maximum_fusion.6), channel_id=1, source_target_pairs={{0,16},{16,0},{1,17},{17,1},{2,18},{18,2},{3,19},{19,3},{4,20},{20... | collective-permute-start | bytes 13868 | tf_op jit(solution)/shard_map/ppermute | solution.py:22
  112.1 3.3 %copy-start.10 = (bf16[1024,1536]{1,0:T(8,128)(2,1)S(1)}, bf16[1024,1536]{1,0:T(8,128)(2,1)}, u32[]{:S(2)}) copy-start(bf16[1024,1536]{1,0:T(8,128)(2,1)} %all-gather.4.cloned.1.call-done.refs_1_) | copy-start | bytes 9437188
  112.1 3.3 %copy-start.18 = (bf16[384,768]{1,0:T(8,128)(2,1)S(1)}, bf16[384,768]{1,0:T(8,128)(2,1)}, u32[]{:S(2)}) copy-start(bf16[384,768]{1,0:T(8,128)(2,1)} %get-tuple-element.25) | copy-start | bytes 1769476
  112.1 3.3 %copy-start.21 = (bf16[384,768]{1,0:T(8,128)(2,1)S(1)}, bf16[384,768]{1,0:T(8,128)(2,1)}, u32[]{:S(2)}) copy-start(bf16[384,768]{1,0:T(8,128)(2,1)} %get-tuple-element.67) | copy-start | bytes 1769476
  115.4 17.5 %copy-start.27 = (bf16[384,768]{1,0:T(8,128)(2,1)}, bf16[384,768]{1,0:T(8,128)(2,1)S(1)}, u32[]{:S(2)}) copy-start(bf16[384,768]{1,0:T(8,128)(2,1)S(1)} %get-tuple-element.29) | copy-start | bytes 1769476
  115.4 17.5 %copy-start.30 = (bf16[384,768]{1,0:T(8,128)(2,1)}, bf16[384,768]{1,0:T(8,128)(2,1)S(1)}, u32[]{:S(2)}) copy-start(bf16[384,768]{1,0:T(8,128)(2,1)S(1)} %get-tuple-element.69) | copy-start | bytes 1769476
  117.5 4.5 %copy-start.6 = (bf16[2,128,1536]{2,1,0:T(8,128)(2,1)S(1)}, bf16[2,128,1536]{2,1,0:T(8,128)(2,1)}, u32[]{:S(2)}) copy-start(bf16[2,128,1536]{2,1,0:T(8,128)(2,1)} %after.8) | copy-start | bytes 2359300
  120.4 15.1 %copy-start.17 = (bf16[768,512]{1,0:T(8,128)(2,1)}, bf16[768,512]{1,0:T(8,128)(2,1)S(1)}, u32[]{:S(2)}) copy-start(bf16[768,512]{1,0:T(8,128)(2,1)S(1)} %add_convert_fusion.refs_1_) | copy-start | bytes 2359300
  120.4 19.6 %collective-permute-start.11 = (bf16[768,512]{1,0:T(8,128)(2,1)S(1)}, bf16[768,512]{1,0:T(8,128)(2,1)}, u32[]{:S(2)}, u32[]{:S(2)}) collective-permute-start(bf16[768,512]{1,0:T(8,128)(2,1)S(1)} %add_convert_fusion.refs_1_), channel_id=1, source_target_pairs={{0,2},{2,0},{1,3},{3,1},{4,6},{6,4},{5,7},{7,5},{8,10},{10,8},{9,1... | collective-permute-start | bytes 2359304 | tf_op jit(solution)/shard_map/ppermute | solution.py:22
  122.9 23.4 %collective-permute-start.16 = (bf16[128,1536]{1,0:T(8,128)(2,1)}, bf16[128,1536]{1,0:T(8,128)(2,1)}, u32[]{:S(2)}, u32[]{:S(2)}) collective-permute-start(bf16[128,1536]{1,0:T(8,128)(2,1)} %get-tuple-element.42), channel_id=1, source_target_pairs={{8,4},{12,8},{9,5},{13,9},{10,6},{14,10},{11,7},{15,11},{24,20},{2... | collective-permute-start | bytes 1179656 | tf_op jit(solution)/shard_map/ppermute | solution.py:30
  124.3 22.0 %collective-permute-start.17 = (bf16[128,1536]{1,0:T(8,128)(2,1)}, bf16[128,1536]{1,0:T(8,128)(2,1)}, u32[]{:S(2)}, u32[]{:S(2)}) collective-permute-start(bf16[128,1536]{1,0:T(8,128)(2,1)} %get-tuple-element.43), channel_id=1, source_target_pairs={{0,4},{4,8},{1,5},{5,9},{2,6},{6,10},{3,7},{7,11},{16,20},{20,24},... | collective-permute-start | bytes 1179656 | tf_op jit(solution)/shard_map/ppermute | solution.py:30
  135.5 4.5 %copy-start.25 = (bf16[384,768]{1,0:T(8,128)(2,1)S(1)}, bf16[384,768]{1,0:T(8,128)(2,1)}, u32[]{:S(2)}) copy-start(bf16[384,768]{1,0:T(8,128)(2,1)} %get-tuple-element.24) | copy-start | bytes 1769476
  135.5 22.9 %collective-permute-start.13 = (bf16[512,1536]{1,0:T(8,128)(2,1)}, bf16[512,1536]{1,0:T(8,128)(2,1)}, u32[]{:S(2)}, u32[]{:S(2)}) collective-permute-start(bf16[512,1536]{1,0:T(8,128)(2,1)} %after.7), channel_id=1, source_target_pairs={{0,1},{1,0},{2,3},{3,2},{4,5},{5,4},{6,7},{7,6},{8,9},{9,8},{10,11... | collective-permute-start | bytes 4718600 | tf_op jit(solution)/shard_map/ppermute | solution.py:22
  144.9 10.5 %collective-permute-start.12 = (bf16[384,512]{1,0:T(8,128)(2,1)}, bf16[384,512]{1,0:T(8,128)(2,1)}, u32[]{:S(2)}, u32[]{:S(2)}) collective-permute-start(bf16[384,512]{1,0:T(8,128)(2,1)} %slice.295), channel_id=1, source_target_pairs={{0,16},{16,0},{1,17},{17,1},{2,18},{18,2},{3,19},{19,3},{4,20},{20... | collective-permute-start | bytes 1179656 | tf_op jit(solution)/shard_map/ppermute | solution.py:22
  163.1 15.1 %collective-permute-start.14 = (bf16[768,256]{1,0:T(8,128)(2,1)}, bf16[768,256]{1,0:T(8,128)(2,1)}, u32[]{:S(2)}, u32[]{:S(2)}) collective-permute-start(bf16[768,256]{1,0:T(8,128)(2,1)} %fusion.20.refs_1_), channel_id=1, source_target_pairs={{0,2},{2,0},{1,3},{3,1},{4,6},{6,4},{5,7},{7,5},{8,10},{10,8},{9,1... | collective-permute-start | bytes 1179656 | tf_op jit(solution)/shard_map/ppermute | solution.py:22
  166.3 24.7 %collective-permute-start.19 = (bf16[128,1536]{1,0:T(8,128)(2,1)S(1)}, bf16[128,1536]{1,0:T(8,128)(2,1)S(1)}, u32[]{:S(2)}, u32[]{:S(2)}) collective-permute-start(bf16[128,1536]{1,0:T(8,128)(2,1)S(1)} %get-tuple-element.41), channel_id=1, source_target_pairs={{0,4},{4,8},{8,12},{1,5},{5,9},{9,13},{2,6},{6,10},{10,14},{3,7},{... | collective-permute-start | bytes 1179656 | tf_op jit(solution)/shard_map/ppermute | solution.py:14
  174.0 4.3 %copy-start.16 = (bf16[512,1536]{1,0:T(8,128)(2,1)S(1)}, bf16[512,1536]{1,0:T(8,128)(2,1)}, u32[]{:S(2)}) copy-start(bf16[512,1536]{1,0:T(8,128)(2,1)} %after.7) | copy-start | bytes 4718596
  174.0 4.3 %copy-start.20 = (bf16[384,768]{1,0:T(8,128)(2,1)S(1)}, bf16[384,768]{1,0:T(8,128)(2,1)}, u32[]{:S(2)}) copy-start(bf16[384,768]{1,0:T(8,128)(2,1)} %get-tuple-element.25) | copy-start | bytes 1769476
  174.0 4.3 %copy-start.23 = (bf16[384,768]{1,0:T(8,128)(2,1)S(1)}, bf16[384,768]{1,0:T(8,128)(2,1)}, u32[]{:S(2)}) copy-start(bf16[384,768]{1,0:T(8,128)(2,1)} %get-tuple-element.67) | copy-start | bytes 1769476
  174.0 4.3 %copy-start.29 = (bf16[384,768]{1,0:T(8,128)(2,1)S(1)}, bf16[384,768]{1,0:T(8,128)(2,1)}, u32[]{:S(2)}) copy-start(bf16[384,768]{1,0:T(8,128)(2,1)} %copy-done.27) | copy-start | bytes 1769476
  174.0 4.3 %copy-start.32 = (bf16[384,768]{1,0:T(8,128)(2,1)S(1)}, bf16[384,768]{1,0:T(8,128)(2,1)}, u32[]{:S(2)}) copy-start(bf16[384,768]{1,0:T(8,128)(2,1)} %copy-done.30) | copy-start | bytes 1769476
  174.0 23.8 %collective-permute-start.18 = (bf16[128,1536]{1,0:T(8,128)(2,1)S(1)}, bf16[128,1536]{1,0:T(8,128)(2,1)S(1)}, u32[]{:S(2)}, u32[]{:S(2)}) collective-permute-start(bf16[128,1536]{1,0:T(8,128)(2,1)S(1)} %get-tuple-element.40), channel_id=1, source_target_pairs={{4,0},{8,4},{12,8},{5,1},{9,5},{13,9},{6,2},{10,6},{14,10},{7,3},{... | collective-permute-start | bytes 1179656 | tf_op jit(solution)/shard_map/ppermute | solution.py:14
  180.1 19.9 %copy-start.7 = (f32[384,512]{1,0:T(8,128)S(1)}, f32[384,512]{1,0:T(8,128)}, u32[]{:S(2)}) copy-start(f32[384,512]{1,0:T(8,128)} %get-tuple-element.20) | copy-start | bytes 2359300
  180.2 19.9 %copy-start.9 = (f32[384,512]{1,0:T(8,128)S(1)}, f32[384,512]{1,0:T(8,128)}, u32[]{:S(2)}) copy-start(f32[384,512]{1,0:T(8,128)} %copy-done.8) | copy-start | bytes 2359300
  180.2 19.7 %collective-permute-start.15 = (bf16[384,256]{1,0:T(8,128)(2,1)S(1)}, bf16[384,256]{1,0:T(8,128)(2,1)S(1)}, u32[]{:S(2)}, u32[]{:S(2)}) collective-permute-start(bf16[384,256]{1,0:T(8,128)(2,1)S(1)} %slice.296), channel_id=1, source_target_pairs={{0,16},{16,0},{1,17},{17,1},{2,18},{18,2},{3,19},{19,3},{4,20},{20... | collective-permute-start | bytes 589832 | tf_op jit(solution)/shard_map/ppermute | solution.py:22
  (29 other events, 68.7 us)
Sparse Core Ops, SparseCore 0:
  12.3 77.9 all-gather.3
  92.5 40.0 all-gather.7
  149.2 46.5 all-gather.5

commit v14 on v9

--- a/solution.py
+++ b/solution.py
@@ -245,7 +245,7 @@
         return total.astype(jnp.bfloat16)
 
     pieces = []
-    main_grad = span_part(factors_other)
+    main_grad = span_part(sums)
     far_part = None
     for own_weight in own_weights:
         if far_part is not None:

time: 205 us -> 204 us (level)
  waiting for transfers between devices: 82.2 us -> 74.7 us
  starting transfers between devices: 38.3 us -> 45.5 us
  other arithmetic: 17.7 us -> 20.2 us
    ppermute x6, waiting for transfers between devices: 20.8 us -> 11.5 us  [passed_on(): return lax.ppermute(x, axis, pairs)]
    ppermute x6, starting transfers between devices: 18.8 us -> 26.1 us  [passed_on(): return lax.ppermute(x, axis, pairs)]
    ppermute x3, waiting for transfers between devices: 22.6 us -> 24.7 us  [passed_along(): return lax.ppermute(x, axis, pairs)]
    unnamed x100 -> x86, local copies, waits for them, and re-layouts: 6.19 us -> 5.55 us
  transfers between devices with their start and end apart: 23 -> 23, of which waited for: 13 -> 12; matrix products, arithmetic and copies ran while one was open for 26% -> 26% of each run, Pallas kernels for 2% -> 2%
where the time goes in v14:
time: 204 us; the launch traced here: 203 us
  waiting for transfers between devices  74.7 us (37%)
  starting transfers between devices  45.5 us (22%)
  matrix products  24.9 us (12%)
  other arithmetic  20.2 us (10%)
  local copies, waits for them, and re-layouts  19.9 us (10%)
  between operations  14.5 us (7%)
  Pallas kernels  3.62 us (2%)
    ppermute x11, waiting for transfers between devices, swapped(): return lax.ppermute(x, axis, [(i, length - 1 - i) for i in range(length)])  38.4 us
    ppermute x6, starting transfers between devices, passed_on(): return lax.ppermute(x, axis, pairs)  26.1 us
    ppermute x3, waiting for transfers between devices, passed_along(): return lax.ppermute(x, axis, pairs)  24.7 us
    dot_general x8, matrix products, product(): lax.dot_general(rows, weight, (((1,), (1,)), ((), ())), preferred_element...  17 us
    ppermute x6, waiting for transfers between devices, passed_on(): return lax.ppermute(x, axis, pairs)  11.5 us
    ppermute x11, starting transfers between devices, swapped(): return lax.ppermute(x, axis, [(i, length - 1 - i) for i in range(length)])  11 us
    ppermute x3, starting transfers between devices, passed_along(): return lax.ppermute(x, axis, pairs)  8.29 us
    convert_element_type x2, other arithmetic, grads(): key_grad.astype(jnp.bfloat16)  6.27 us
  transfers between devices with their start and end apart: 23, of which 12 were waited for; matrix products, arithmetic and copies ran while one was open for 26% of the time, Pallas kernels for 2%

profile of v14, /device:TPU:0, one launch (start us, length us, event | category | flops | bytes accessed | tf_op | source)
XLA Modules:
  0.0 203.3 jit_solution(9112971045822796198)
XLA Ops:
  7.2 1.9 copy.38
  12.3 1.1 pad_maximum_fusion.2
  13.3 5.7 %collective-permute-start = (bf16[144,1536]{1,0:T(8,128)(2,1)}, bf16[144,1536]{1,0:T(8,128)(2,1)}, u32[]{:S(2)}, u32[]{:S(2)}) collective-permute-start(bf16[144,1536]{1,0:T(8,128)(2,1)} %get-tuple-element.42), channel_id=1, source_target_pairs={{0,4},{4,8},{8,12},{1,5},{5,9},{9,13},{2,6},{6,10},{10,14},{3,7},{... | collective-permute-start | bytes 1327112 | tf_op jit(solution)/shard_map/ppermute | solution.py:14
  19.1 1.3 collective-permute-start.2
  20.4 1.6 collective-permute-start.9
  23.0 1.1 dynamic-slice_bitcast_fusion.1
  24.1 1.7 dynamic-slice_bitcast_fusion
  27.7 5.7 %collective-permute-done.refs_1_ = bf16[144,1536]{1,0:T(8,128)(2,1)} collective-permute-done((bf16[144,1536]{1,0:T(8,128)(2,1)}, bf16[144,1536]{1,0:T(8,128)(2,1)}, u32[]{:S(2)}, u32[]{:S(2)}) %collective-permute-start) | collective-permute-done | bytes 442400 | tf_op jit(solution)/shard_map/ppermute | solution.py:14
  34.1 14.9 %collective-permute-done.2.refs_3_ = bf16[144,1536]{1,0:T(8,128)(2,1)} collective-permute-done((bf16[144,1536]{1,0:T(8,128)(2,1)}, bf16[144,1536]{1,0:T(8,128)(2,1)}, u32[]{:S(2)}, u32[]{:S(2)}) %collective-permute-start.2) | collective-permute-done | bytes 442400 | tf_op jit(solution)/shard_map/ppermute | solution.py:14
  50.3 1.5 collective-permute-start.7
  53.8 1.3 collective-permute-start.3
  55.1 18.2 %collective-permute-done.7 = bf16[2,1536]{1,0:T(2,128)(2,1)S(1)} collective-permute-done((bf16[2,1536]{1,0:T(2,128)(2,1)}, bf16[2,1536]{1,0:T(2,128)(2,1)S(1)}, u32[]{:S(2)}, u32[]{:S(2)}) %collective-permute-start.7) | collective-permute-done | bytes 6176 | tf_op jit(solution)/shard_map/ppermute | solution.py:22
  73.9 8.5 %collective-permute-done.3.refs_4_ = bf16[144,1536]{1,0:T(8,128)(2,1)S(1)} collective-permute-done((bf16[144,1536]{1,0:T(8,128)(2,1)}, bf16[144,1536]{1,0:T(8,128)(2,1)S(1)}, u32[]{:S(2)}, u32[]{:S(2)}) %collective-permute-start.3) | collective-permute-done | bytes 442400 | tf_op jit(solution)/shard_map/ppermute | solution.py:30
  83.4 3.6 %byte_sums.1 = f32[8,384]{1,0:T(8,128)S(1)} custom-call(s32[1]{0:T(128)} %bitcast.3.shard_ref, s32[1,512]{1,0:T(1,128)S(1)} %copy-done.5, bf16[384,1536]{1,0:T(8,128)(2,1)S(1)} %bitcast.51, bf16[384,1536]{1,0:T(8,128)(2,1)S(1)} %bitcast.53, bf16[384,1536]{1,0:T(8,128)(2,1)S(1)} %bitcast.55, bf16[144,1536]{1,0:T(8,128)(2,1)S(1)} %collective-permute-done.1.refs_0_, ...), custom_call_target="tpu_custom_call" | custom-call | tf_op jit(solution)/shard_map/byte_sums/pallas_call | solution.py:93
  87.0 1.6 collective-permute-start.4
  89.2 1.6 collective-permute-done.4
  92.0 1.3 fusion.43
  93.3 3.3 %fusion.76 = (bf16[640,1536]{1,0:T(8,128)(2,1)S(1)}, f32[640,1536]{1,0:T(8,128)}) fusion(f32[640,1536]{1,0:T(8,128)S(1)} %fusion.43, bf16[1,384,1536]{2,1,0:T(8,128)(2,1)S(1)} %copy-done, s32[384]{0:T(512)S(1)} %get-tuple-element.61, bf16[384]{0:T(512)(128)(2,1)S(1)} %get-tuple-element.12), kind=kOutput, calls=%fused_computation.160 | convolution fusion | flops 757432320 | bytes 11012352 | tf_op jit(solution)/shard_map/dot_general | solution.py:222
  97.6 2.1 %pad_maximum_fusion.1.refs_0_ = bf16[2,128,1536]{2,1,0:T(8,128)(2,1)} fusion(bf16[1,128,1536]{2,1,0:T(8,128)(2,1)} %get-tuple-element.19, bf16[1,128,1536]{2,1,0:T(8,128)(2,1)} %get-tuple-element.18), kind=kLoop, calls=%fused_computation.54 | loop fusion | flops 393216 | bytes 1572864 | tf_op jit(solution)/shard_map/stack | solution.py:231
  99.6 1.2 slice_bitcast_fusion.1
  100.8 9.4 %collective-permute-start.16 = (bf16[128,1536]{1,0:T(8,128)(2,1)S(1)}, bf16[128,1536]{1,0:T(8,128)(2,1)S(1)}, u32[]{:S(2)}, u32[]{:S(2)}) collective-permute-start(bf16[128,1536]{1,0:T(8,128)(2,1)S(1)} %get-tuple-element.40), channel_id=1, source_target_pairs={{0,4},{4,8},{1,5},{5,9},{2,6},{6,10},{3,7},{7,11},{16,20},{20,24},... | collective-permute-start | bytes 1179656 | tf_op jit(solution)/shard_map/ppermute | solution.py:30
  111.1 1.3 collective-permute-start.5
  112.4 4.2 %collective-permute-done.5 = f32[3,1]{1,0:T(4,128)S(1)} collective-permute-done((f32[3,1]{1,0:T(4,128)S(1)}, f32[3,1]{1,0:T(4,128)S(1)}, u32[]{:S(2)}, u32[]{:S(2)}) %collective-permute-start.5) | collective-permute-done | bytes 44 | tf_op jit(solution)/shard_map/ppermute | solution.py:14
  117.3 3.2 %fusion.22 = (bf16[384,768]{1,0:T(8,128)(2,1)S(1)}, bf16[384,768]{1,0:T(8,128)(2,1)S(1)}, bf16[384,768]{1,0:T(8,128)(2,1)S(1)}, bf16[384,768]{1,0:T(8,128)(2,1)S(1)}) fusion(bf16[1,768]{1,0:T(2,128)(2,1)S(1)} %copy-done.31, bf16[383,768]{1,0:T(8,128)(2,1)} %get-tuple-element.32, bf16[1,384,1536]{2,1,0:T(8,128)(2,1)S(1)} %copy-done.2, s32[]{:T(128)S(6)} %select_n.148, ...), kind=kLoop, calls=%fused_computation.26 | loop fusion | flops 10616832 | bytes 7084040 | tf_op jit(solution)/shard_map/convert_element_type | solution.py:196
  121.3 1.9 fusion.74
  123.2 1.3 constant_dynamic-slice_fusion
  124.6 3.1 %subtract_convert_fusion = (bf16[384,768]{1,0:T(8,128)(2,1)S(1)}, bf16[384,768]{1,0:T(8,128)(2,1)S(1)}, bf16[384,768]{1,0:T(8,128)(2,1)S(1)}, bf16[384,768]{1,0:T(8,128)(2,1)S(1)}) fusion(bf16[1,768]{1,0:T(2,128)(2,1)S(1)} %copy-done.32, bf16[383,768]{1,0:T(8,128)(2,1)S(1)} %get-tuple-element.36, bf16[384,1536]{1,0:T(8,128)(2,1)} %collective-permute-done.8, ...), kind=kLoop, calls=%fused_computation.36 | loop fusion | flops 10616832 | bytes 7084040 | tf_op jit(solution)/shard_map/convert_element_type | solution.py:196
  127.9 2.5 %fusion.32 = (bf16[128,1536]{1,0:T(8,128)(2,1)S(1)}, bf16[128,1536]{1,0:T(8,128)(2,1)S(1)}) fusion(f32[640,1536]{1,0:T(8,128)} %get-tuple-element.64, bf16[128,1536]{1,0:T(8,128)(2,1)S(1)} %collective-permute-done.16, bf16[128,1536]{1,0:T(8,128)(2,1)S(1)} %collective-permute-done.18), kind=kLoop, calls=%fused_computation.48 | loop fusion | flops 1179648 | bytes 3145728 | tf_op jit(solution)/shard_map/convert_element_type | solution.py:228
  130.4 12.6 %collective-permute-start.17 = (bf16[128,1536]{1,0:T(8,128)(2,1)S(1)}, bf16[128,1536]{1,0:T(8,128)(2,1)S(1)}, u32[]{:S(2)}, u32[]{:S(2)}) collective-permute-start(bf16[128,1536]{1,0:T(8,128)(2,1)S(1)} %get-tuple-element.16), channel_id=1, source_target_pairs={{0,4},{4,8},{8,12},{1,5},{5,9},{9,13},{2,6},{6,10},{10,14},{3,7},{... | collective-permute-start | bytes 1179656 | tf_op jit(solution)/shard_map/ppermute | solution.py:30
  143.1 1.5 collective-permute-start.19
  144.6 1.4 fusion.5
  146.1 3.7 %add_convert_fusion.refs_1_ = bf16[768,512]{1,0:T(8,128)(2,1)} fusion(f32[768,512]{1,0:T(8,128)S(1)} %fusion.5, bf16[1024,1536]{1,0:T(8,128)(2,1)} %collective-permute-done.10, s32[]{:T(128)S(6)} %select_n.149, bf16[384,768]{1,0:T(8,128)(2,1)S(1)} %get-tuple-element.28, bf16[384,768]{1,0:T(8,128)(2,1)S(1)} %get-tuple-element.68, ...), kind=kOutput, calls=%fused_computation.8 | convolution fusion | flops 1218183168 | bytes 6291460 | tf_op jit(solution)/shard_map/dot_general | solution.py:104
  149.8 1.1 copy-done.8
  150.9 1.5 collective-permute-start.11
  152.4 2.9 %collective-permute-done.19 = bf16[128,1536]{1,0:T(8,128)(2,1)S(1)} collective-permute-done((bf16[128,1536]{1,0:T(8,128)(2,1)S(1)}, bf16[128,1536]{1,0:T(8,128)(2,1)S(1)}, u32[]{:S(2)}, u32[]{:S(2)}) %collective-permute-start.19) | collective-permute-done | bytes 393248 | tf_op jit(solution)/shard_map/ppermute | solution.py:30
  155.2 2.0 fusion.48
  157.3 1.0 copy-done.10
  158.5 3.3 %fusion.9 = f32[768,512]{1,0:T(8,128)S(1)} fusion(bf16[1024,1536]{1,0:T(8,128)(2,1)} %all-gather.4.cloned.1.call-done.refs_1_, s32[]{:T(128)S(6)} %select_n.147, bf16[384,768]{1,0:T(8,128)(2,1)} %copy-done.17, bf16[384,768]{1,0:T(8,128)(2,1)} %copy-done.19, bf16[384,768]{1,0:T(8,128)(2,1)S(1)} %copy-done.10, bf16[384,768]{1,0:T(8,128)(2,1)S(1)} %copy-done.12), kind=kOutput, calls=%fused_computation.16 | convolution fusion | flops 1217396736 | bytes 5505028 | tf_op jit(solution)/shard_map/dot_general | solution.py:104
  161.8 8.0 %collective-permute-done.11 = bf16[768,512]{1,0:T(8,128)(2,1)} collective-permute-done((bf16[768,512]{1,0:T(8,128)(2,1)S(1)}, bf16[768,512]{1,0:T(8,128)(2,1)}, u32[]{:S(2)}, u32[]{:S(2)}) %collective-permute-start.11) | collective-permute-done | bytes 786464 | tf_op jit(solution)/shard_map/ppermute | solution.py:22
  169.9 3.0 %convert_add_fusion = f32[768,512]{1,0:T(8,128)S(1)} fusion(bf16[768,512]{1,0:T(8,128)(2,1)} %collective-permute-done.11, f32[768,512]{1,0:T(8,128)S(1)} %fusion.9, bf16[1024,1536]{1,0:T(8,128)(2,1)} %collective-permute-done.10, s32[]{:T(128)S(6)} %select_n.147, bf16[384,768]{1,0:T(8,128)(2,1)S(1)} %copy-done.22, bf16[384,768]{1,0:T(8,128)(2,1)S(1)} %copy-done.24, ...), kind=kOutput, calls=%fused_computation.7 | convolution fusion | flops 1219362816 | bytes 7864324 | tf_op jit(solution)/shard_map/dot_general | solution.py:104
  173.0 1.6 collective-permute-start.12
  174.6 1.9 fusion.35
  177.4 1.5 collective-permute-start.14
  178.9 3.7 %collective-permute-done.12 = bf16[384,512]{1,0:T(8,128)(2,1)S(1)} collective-permute-done((bf16[384,512]{1,0:T(8,128)(2,1)S(1)}, bf16[384,512]{1,0:T(8,128)(2,1)S(1)}, u32[]{:S(2)}, u32[]{:S(2)}) %collective-permute-start.12) | collective-permute-done | bytes 393248 | tf_op jit(solution)/shard_map/ppermute | solution.py:22
  182.7 1.9 fusion.38
  184.7 2.0 collective-permute-done.14
  188.3 5.0 %collective-permute-done.15 = bf16[384,256]{1,0:T(8,128)(2,1)S(1)} collective-permute-done((bf16[384,256]{1,0:T(8,128)(2,1)S(1)}, bf16[384,256]{1,0:T(8,128)(2,1)S(1)}, u32[]{:S(2)}, u32[]{:S(2)}) %collective-permute-start.15) | collective-permute-done | bytes 196640 | tf_op jit(solution)/shard_map/ppermute | solution.py:22
  193.6 3.3 %fusion.2 = bf16[1,384,1536]{2,1,0:T(8,128)(2,1)} fusion(f32[384,1536]{1,0:T(8,128)S(1)} %slice_dynamic-update-slice_fusion.4, bf16[512,1536]{1,0:T(8,128)(2,1)} %all-gather.6.cloned.1.call-done, s32[384]{0:T(512)S(1)} %copy-done.34, pred[384]{0:T(512)(128)(4,1)S(1)} %copy-done.37, bf16[1,384,1536]{2,1,0:T(8,128)(2,1)S(1)} %copy-done), kind=kOutput, calls=%fused_computation.4 | convolution fusion | flops 606732288 | bytes 6293376 | tf_op jit(solution)/shard_map/dot_general | solution.py:241
  (152 shorter events, 20.1 us)
Async XLA Ops:
  7.2 5.1 %copy-start.2 = (bf16[1,384,1536]{2,1,0:T(8,128)(2,1)S(1)}, bf16[1,384,1536]{2,1,0:T(8,128)(2,1)}, u32[]{:S(2)}) copy-start(bf16[1,384,1536]{2,1,0:T(8,128)(2,1)} %param.10) | copy-start | bytes 3538948
  7.2 5.1 %copy-start.3 = (bf16[1,128,1536]{2,1,0:T(8,128)(2,1)S(1)}, bf16[1,128,1536]{2,1,0:T(8,128)(2,1)}, u32[]{:S(2)}) copy-start(bf16[1,128,1536]{2,1,0:T(8,128)(2,1)} %param.11) | copy-start | bytes 1179652
  7.2 90.3 %all-gather.4.cloned.1.call-start = ((), (), s32[]{:S(2)}) async-start(), calls=%async_computation | async-start | bytes 3932160 | tf_op jit(solution)/shard_map/all_gather | solution.py:149
  11.2 11.2 %copy-start.5 = (s32[1,512]{1,0:T(1,128)S(1)}, s32[1,512]{1,0:T(1,128)}, u32[]{:S(2)}) copy-start(s32[1,512]{1,0:T(1,128)} %bounds_ref.1) | copy-start | bytes 6148
  12.2 137.6 %all-gather.8.cloned.1.call-start = ((), (), s32[]{:S(2)}) async-start(), calls=%async_computation.2 | async-start | bytes 1966080 | tf_op jit(solution)/shard_map/all_gather | solution.py:149
  13.3 20.0 %collective-permute-start = (bf16[144,1536]{1,0:T(8,128)(2,1)}, bf16[144,1536]{1,0:T(8,128)(2,1)}, u32[]{:S(2)}, u32[]{:S(2)}) collective-permute-start(bf16[144,1536]{1,0:T(8,128)(2,1)} %get-tuple-element.42), channel_id=1, source_target_pairs={{0,4},{4,8},{8,12},{1,5},{5,9},{9,13},{2,6},{6,10},{10,14},{3,7},{... | collective-permute-start | bytes 1327112 | tf_op jit(solution)/shard_map/ppermute | solution.py:14
  19.1 29.9 %collective-permute-start.2 = (bf16[144,1536]{1,0:T(8,128)(2,1)}, bf16[144,1536]{1,0:T(8,128)(2,1)}, u32[]{:S(2)}, u32[]{:S(2)}) collective-permute-start(bf16[144,1536]{1,0:T(8,128)(2,1)} %get-tuple-element.43), channel_id=1, source_target_pairs={{4,0},{8,4},{12,8},{5,1},{9,5},{13,9},{6,2},{10,6},{14,10},{7,3},{... | collective-permute-start | bytes 1327112 | tf_op jit(solution)/shard_map/ppermute | solution.py:14
  20.4 101.0 %collective-permute-start.9 = (bf16[384,1536]{1,0:T(8,128)(2,1)S(1)}, bf16[384,1536]{1,0:T(8,128)(2,1)}, u32[]{:S(2)}, u32[]{:S(2)}) collective-permute-start(bf16[384,1536]{1,0:T(8,128)(2,1)S(1)} %bitcast.52), channel_id=1, source_target_pairs={{0,16},{16,0},{1,17},{17,1},{2,18},{18,2},{3,19},{19,3},{4,20},{20... | collective-permute-start | bytes 3538952 | tf_op jit(solution)/shard_map/ppermute | solution.py:22
  21.9 101.3 %collective-permute-start.8 = (bf16[384,1536]{1,0:T(8,128)(2,1)S(1)}, bf16[384,1536]{1,0:T(8,128)(2,1)}, u32[]{:S(2)}, u32[]{:S(2)}) collective-permute-start(bf16[384,1536]{1,0:T(8,128)(2,1)S(1)} %bitcast.54), channel_id=1, source_target_pairs={{0,16},{16,0},{1,17},{17,1},{2,18},{18,2},{3,19},{19,3},{4,20},{20... | collective-permute-start | bytes 3538952 | tf_op jit(solution)/shard_map/ppermute | solution.py:22
  24.1 58.3 %copy-start = (bf16[1,384,1536]{2,1,0:T(8,128)(2,1)S(1)}, bf16[1,384,1536]{2,1,0:T(8,128)(2,1)}, u32[]{:S(2)}) copy-start(bf16[1,384,1536]{2,1,0:T(8,128)(2,1)} %param.8) | copy-start | bytes 3538948
  50.3 23.0 %collective-permute-start.7 = (bf16[2,1536]{1,0:T(2,128)(2,1)}, bf16[2,1536]{1,0:T(2,128)(2,1)S(1)}, u32[]{:S(2)}, u32[]{:S(2)}) collective-permute-start(bf16[2,1536]{1,0:T(2,128)(2,1)} %pad_maximum_fusion.6), channel_id=1, source_target_pairs={{0,16},{16,0},{1,17},{17,1},{2,18},{18,2},{3,19},{19,3},{4,20},{20... | collective-permute-start | bytes 18440 | tf_op jit(solution)/shard_map/ppermute | solution.py:22
  53.0 140.5 %all-gather.6.cloned.1.call-start = ((), (), s32[]{:S(2)}) async-start(), calls=%async_computation.1 | async-start | bytes 1966080 | tf_op jit(solution)/shard_map/all_gather | solution.py:236
  53.1 20.8 %collective-permute-start.1 = (bf16[144,1536]{1,0:T(8,128)(2,1)}, bf16[144,1536]{1,0:T(8,128)(2,1)S(1)}, u32[]{:S(2)}, u32[]{:S(2)}) collective-permute-start(bf16[144,1536]{1,0:T(8,128)(2,1)} %collective-permute-done.refs_1_), channel_id=1, source_target_pairs={{4,8},{8,12},{5,9},{9,13},{6,10},{10,14},{7,11},{11,15},{20,24},{2... | collective-permute-start | bytes 1327112 | tf_op jit(solution)/shard_map/ppermute | solution.py:30
  53.8 28.6 %collective-permute-start.3 = (bf16[144,1536]{1,0:T(8,128)(2,1)}, bf16[144,1536]{1,0:T(8,128)(2,1)S(1)}, u32[]{:S(2)}, u32[]{:S(2)}) collective-permute-start(bf16[144,1536]{1,0:T(8,128)(2,1)} %collective-permute-done.2.refs_3_), channel_id=1, source_target_pairs={{4,0},{8,4},{5,1},{9,5},{6,2},{10,6},{7,3},{11,7},{20,16},{24,20},... | collective-permute-start | bytes 1327112 | tf_op jit(solution)/shard_map/ppermute | solution.py:30
  83.4 7.4 %copy-start.38 = (f32[384]{0:T(512)S(1)}, f32[384]{0:T(512)}, u32[]{:S(2)}) copy-start(f32[384]{0:T(512)} %select_multiply_fusion) | copy-start | bytes 4612
  83.4 8.0 %copy-start.36 = (pred[384]{0:T(512)(128)(4,1)S(1)}, pred[384]{0:T(512)(128)(4,1)}, u32[]{:S(2)}) copy-start(pred[384]{0:T(512)(128)(4,1)} %copy-done.35) | copy-start | bytes 1156
  87.0 3.8 %collective-permute-start.4 = (f32[8,384]{1,0:T(8,128)S(1)}, f32[8,384]{1,0:T(8,128)S(1)}, u32[]{:S(2)}, u32[]{:S(2)}) collective-permute-start(f32[8,384]{1,0:T(8,128)S(1)} %byte_sums.1), channel_id=1, source_target_pairs={{0,2},{2,0},{1,3},{3,1},{4,6},{6,4},{5,7},{7,5},{8,10},{10,8},{9,1... | collective-permute-start | bytes 36872 | tf_op jit(solution)/shard_map/ppermute | solution.py:22
  97.5 48.5 %collective-permute-start.10 = (bf16[1024,1536]{1,0:T(8,128)(2,1)}, bf16[1024,1536]{1,0:T(8,128)(2,1)}, u32[]{:S(2)}, u32[]{:S(2)}) collective-permute-start(bf16[1024,1536]{1,0:T(8,128)(2,1)} %all-gather.4.cloned.1.call-done.refs_1_), channel_id=1, source_target_pairs={{0,1},{1,0},{2,3},{3,2},{4,5},{5,4},{6,7},{7,6},{8,9},{9,8},{10,11... | collective-permute-start | bytes 9437192 | tf_op jit(solution)/shard_map/ppermute | solution.py:22
  97.5 13.5 %copy-start.26 = (f32[1,384]{1,0:T(1,128)S(1)}, f32[1,384]{1,0:T(1,128)}, u32[]{:S(2)}) copy-start(f32[1,384]{1,0:T(1,128)} %get-tuple-element.46) | copy-start | bytes 4612
  97.5 19.7 %copy-start.29 = (bf16[1,768]{1,0:T(2,128)(2,1)S(1)}, bf16[1,768]{1,0:T(2,128)(2,1)}, u32[]{:S(2)}) copy-start(bf16[1,768]{1,0:T(2,128)(2,1)} %get-tuple-element.51) | copy-start | bytes 4612
  97.6 19.7 %copy-start.30 = (bf16[1,768]{1,0:T(2,128)(2,1)S(1)}, bf16[1,768]{1,0:T(2,128)(2,1)}, u32[]{:S(2)}) copy-start(bf16[1,768]{1,0:T(2,128)(2,1)} %get-tuple-element.52) | copy-start | bytes 4612
  97.6 19.7 %copy-start.31 = (bf16[1,768]{1,0:T(2,128)(2,1)S(1)}, bf16[1,768]{1,0:T(2,128)(2,1)}, u32[]{:S(2)}) copy-start(bf16[1,768]{1,0:T(2,128)(2,1)} %get-tuple-element.53) | copy-start | bytes 4612
  100.8 27.1 %collective-permute-start.16 = (bf16[128,1536]{1,0:T(8,128)(2,1)S(1)}, bf16[128,1536]{1,0:T(8,128)(2,1)S(1)}, u32[]{:S(2)}, u32[]{:S(2)}) collective-permute-start(bf16[128,1536]{1,0:T(8,128)(2,1)S(1)} %get-tuple-element.40), channel_id=1, source_target_pairs={{0,4},{4,8},{1,5},{5,9},{2,6},{6,10},{3,7},{7,11},{16,20},{20,24},... | collective-permute-start | bytes 1179656 | tf_op jit(solution)/shard_map/ppermute | solution.py:30
  111.1 5.5 %collective-permute-start.5 = (f32[3,1]{1,0:T(4,128)S(1)}, f32[3,1]{1,0:T(4,128)S(1)}, u32[]{:S(2)}, u32[]{:S(2)}) collective-permute-start(f32[3,1]{1,0:T(4,128)S(1)} %pad_maximum_fusion.7), channel_id=1, source_target_pairs={{4,0},{8,4},{12,8},{5,1},{9,5},{13,9},{6,2},{10,6},{14,10},{7,3},{... | collective-permute-start | bytes 44 | tf_op jit(solution)/shard_map/ppermute | solution.py:14
  116.6 3.9 %collective-permute-start.6 = (f32[3,385]{1,0:T(4,128)S(1)}, f32[3,385]{1,0:T(4,128)S(1)}, u32[]{:S(2)}, u32[]{:S(2)}) collective-permute-start(f32[3,385]{1,0:T(4,128)S(1)} %pad_maximum_fusion.5), channel_id=1, source_target_pairs={{0,16},{16,0},{1,17},{17,1},{2,18},{18,2},{3,19},{19,3},{4,20},{20... | collective-permute-start | bytes 13868 | tf_op jit(solution)/shard_map/ppermute | solution.py:22
  120.4 24.1 %copy-start.9 = (bf16[384,768]{1,0:T(8,128)(2,1)}, bf16[384,768]{1,0:T(8,128)(2,1)S(1)}, u32[]{:S(2)}) copy-start(bf16[384,768]{1,0:T(8,128)(2,1)S(1)} %get-tuple-element.25) | copy-start | bytes 1769476
  120.5 24.1 %copy-start.11 = (bf16[384,768]{1,0:T(8,128)(2,1)}, bf16[384,768]{1,0:T(8,128)(2,1)S(1)}, u32[]{:S(2)}) copy-start(bf16[384,768]{1,0:T(8,128)(2,1)S(1)} %get-tuple-element.65) | copy-start | bytes 1769476
  120.5 25.6 %copy-start.13 = (bf16[384,768]{1,0:T(8,128)(2,1)}, bf16[384,768]{1,0:T(8,128)(2,1)S(1)}, u32[]{:S(2)}) copy-start(bf16[384,768]{1,0:T(8,128)(2,1)S(1)} %get-tuple-element.24) | copy-start | bytes 1769476
  120.5 25.6 %copy-start.15 = (bf16[384,768]{1,0:T(8,128)(2,1)}, bf16[384,768]{1,0:T(8,128)(2,1)S(1)}, u32[]{:S(2)}) copy-start(bf16[384,768]{1,0:T(8,128)(2,1)S(1)} %get-tuple-element.66) | copy-start | bytes 1769476
  120.5 7.4 %collective-permute-start.18 = (bf16[128,1536]{1,0:T(8,128)(2,1)S(1)}, bf16[128,1536]{1,0:T(8,128)(2,1)S(1)}, u32[]{:S(2)}, u32[]{:S(2)}) collective-permute-start(bf16[128,1536]{1,0:T(8,128)(2,1)S(1)} %get-tuple-element.41), channel_id=1, source_target_pairs={{8,4},{12,8},{9,5},{13,9},{10,6},{14,10},{11,7},{15,11},{24,20},{2... | collective-permute-start | bytes 1179656 | tf_op jit(solution)/shard_map/ppermute | solution.py:30
  127.7 18.3 %copy-start.17 = (bf16[384,768]{1,0:T(8,128)(2,1)}, bf16[384,768]{1,0:T(8,128)(2,1)S(1)}, u32[]{:S(2)}) copy-start(bf16[384,768]{1,0:T(8,128)(2,1)S(1)} %get-tuple-element.29) | copy-start | bytes 1769476
  127.7 18.3 %copy-start.19 = (bf16[384,768]{1,0:T(8,128)(2,1)}, bf16[384,768]{1,0:T(8,128)(2,1)S(1)}, u32[]{:S(2)}) copy-start(bf16[384,768]{1,0:T(8,128)(2,1)S(1)} %get-tuple-element.67) | copy-start | bytes 1769476
  127.7 18.3 %copy-start.21 = (bf16[384,768]{1,0:T(8,128)(2,1)}, bf16[384,768]{1,0:T(8,128)(2,1)S(1)}, u32[]{:S(2)}) copy-start(bf16[384,768]{1,0:T(8,128)(2,1)S(1)} %get-tuple-element.28) | copy-start | bytes 1769476
  127.7 18.3 %copy-start.23 = (bf16[384,768]{1,0:T(8,128)(2,1)}, bf16[384,768]{1,0:T(8,128)(2,1)S(1)}, u32[]{:S(2)}) copy-start(bf16[384,768]{1,0:T(8,128)(2,1)S(1)} %get-tuple-element.68) | copy-start | bytes 1769476
  127.7 16.8 %copy-start.6 = (bf16[1024,1536]{1,0:T(8,128)(2,1)S(1)}, bf16[1024,1536]{1,0:T(8,128)(2,1)}, u32[]{:S(2)}) copy-start(bf16[1024,1536]{1,0:T(8,128)(2,1)} %all-gather.4.cloned.1.call-done.refs_1_) | copy-start | bytes 9437188
  130.4 21.9 %collective-permute-start.17 = (bf16[128,1536]{1,0:T(8,128)(2,1)S(1)}, bf16[128,1536]{1,0:T(8,128)(2,1)S(1)}, u32[]{:S(2)}, u32[]{:S(2)}) collective-permute-start(bf16[128,1536]{1,0:T(8,128)(2,1)S(1)} %get-tuple-element.16), channel_id=1, source_target_pairs={{0,4},{4,8},{8,12},{1,5},{5,9},{9,13},{2,6},{6,10},{10,14},{3,7},{... | collective-permute-start | bytes 1179656 | tf_op jit(solution)/shard_map/ppermute | solution.py:30
  143.1 12.2 %collective-permute-start.19 = (bf16[128,1536]{1,0:T(8,128)(2,1)S(1)}, bf16[128,1536]{1,0:T(8,128)(2,1)S(1)}, u32[]{:S(2)}, u32[]{:S(2)}) collective-permute-start(bf16[128,1536]{1,0:T(8,128)(2,1)S(1)} %get-tuple-element.17), channel_id=1, source_target_pairs={{4,0},{8,4},{12,8},{5,1},{9,5},{13,9},{6,2},{10,6},{14,10},{7,3},{... | collective-permute-start | bytes 1179656 | tf_op jit(solution)/shard_map/ppermute | solution.py:30
  149.8 24.8 %collective-permute-start.13 = (bf16[512,1536]{1,0:T(8,128)(2,1)}, bf16[512,1536]{1,0:T(8,128)(2,1)}, u32[]{:S(2)}, u32[]{:S(2)}) collective-permute-start(bf16[512,1536]{1,0:T(8,128)(2,1)} %after.6), channel_id=1, source_target_pairs={{0,1},{1,0},{2,3},{3,2},{4,5},{5,4},{6,7},{7,6},{8,9},{9,8},{10,11... | collective-permute-start | bytes 4718600 | tf_op jit(solution)/shard_map/ppermute | solution.py:22
  150.9 18.9 %collective-permute-start.11 = (bf16[768,512]{1,0:T(8,128)(2,1)S(1)}, bf16[768,512]{1,0:T(8,128)(2,1)}, u32[]{:S(2)}, u32[]{:S(2)}) collective-permute-start(bf16[768,512]{1,0:T(8,128)(2,1)S(1)} %copy-done.8), channel_id=1, source_target_pairs={{0,2},{2,0},{1,3},{3,1},{4,6},{6,4},{5,7},{7,5},{8,10},{10,8},{9,1... | collective-permute-start | bytes 2359304 | tf_op jit(solution)/shard_map/ppermute | solution.py:22
  158.5 11.4 %copy-start.14 = (bf16[384,768]{1,0:T(8,128)(2,1)S(1)}, bf16[384,768]{1,0:T(8,128)(2,1)}, u32[]{:S(2)}) copy-start(bf16[384,768]{1,0:T(8,128)(2,1)} %copy-done.13) | copy-start | bytes 1769476
  158.5 11.4 %copy-start.16 = (bf16[384,768]{1,0:T(8,128)(2,1)S(1)}, bf16[384,768]{1,0:T(8,128)(2,1)}, u32[]{:S(2)}) copy-start(bf16[384,768]{1,0:T(8,128)(2,1)} %copy-done.15) | copy-start | bytes 1769476
  158.5 11.4 %copy-start.22 = (bf16[384,768]{1,0:T(8,128)(2,1)S(1)}, bf16[384,768]{1,0:T(8,128)(2,1)}, u32[]{:S(2)}) copy-start(bf16[384,768]{1,0:T(8,128)(2,1)} %copy-done.21) | copy-start | bytes 1769476
  158.5 11.4 %copy-start.24 = (bf16[384,768]{1,0:T(8,128)(2,1)S(1)}, bf16[384,768]{1,0:T(8,128)(2,1)}, u32[]{:S(2)}) copy-start(bf16[384,768]{1,0:T(8,128)(2,1)} %copy-done.23) | copy-start | bytes 1769476
  173.0 9.6 %collective-permute-start.12 = (bf16[384,512]{1,0:T(8,128)(2,1)S(1)}, bf16[384,512]{1,0:T(8,128)(2,1)S(1)}, u32[]{:S(2)}, u32[]{:S(2)}) collective-permute-start(bf16[384,512]{1,0:T(8,128)(2,1)S(1)} %slice.279), channel_id=1, source_target_pairs={{0,16},{16,0},{1,17},{17,1},{2,18},{18,2},{3,19},{19,3},{4,20},{20... | collective-permute-start | bytes 1179656 | tf_op jit(solution)/shard_map/ppermute | solution.py:22
  177.4 9.3 %collective-permute-start.14 = (bf16[768,256]{1,0:T(8,128)(2,1)S(1)}, bf16[768,256]{1,0:T(8,128)(2,1)S(1)}, u32[]{:S(2)}, u32[]{:S(2)}) collective-permute-start(bf16[768,256]{1,0:T(8,128)(2,1)S(1)} %fusion.20), channel_id=1, source_target_pairs={{0,2},{2,0},{1,3},{3,1},{4,6},{6,4},{5,7},{7,5},{8,10},{10,8},{9,1... | collective-permute-start | bytes 1179656 | tf_op jit(solution)/shard_map/ppermute | solution.py:22
  187.5 5.7 %collective-permute-start.15 = (bf16[384,256]{1,0:T(8,128)(2,1)S(1)}, bf16[384,256]{1,0:T(8,128)(2,1)S(1)}, u32[]{:S(2)}, u32[]{:S(2)}) collective-permute-start(bf16[384,256]{1,0:T(8,128)(2,1)S(1)} %slice.280), channel_id=1, source_target_pairs={{0,16},{16,0},{1,17},{17,1},{2,18},{18,2},{3,19},{19,3},{4,20},{20... | collective-permute-start | bytes 589832 | tf_op jit(solution)/shard_map/ppermute | solution.py:22
  188.3 5.3 %copy-start.34 = (s32[384]{0:T(512)S(1)}, s32[384]{0:T(512)}, u32[]{:S(2)}) copy-start(s32[384]{0:T(512)} %get-tuple-element.62) | copy-start | bytes 4612
  188.3 5.3 %copy-start.37 = (pred[384]{0:T(512)(128)(4,1)S(1)}, pred[384]{0:T(512)(128)(4,1)}, u32[]{:S(2)}) copy-start(pred[384]{0:T(512)(128)(4,1)} %copy-done.35) | copy-start | bytes 1156
  (16 other events, 47.4 us)
Sparse Core Ops, SparseCore 0:
  12.3 81.0 all-gather.3
  95.6 40.1 all-gather.7
  157.4 36.0 all-gather.5
